TPU v7x, 32 devices: a whole 2x2x4 slice. The times are simulated.
32 devices in a mesh: groups: 2 (over x), curve: 16 (over z, y, core).
Axes of the slice: x: 2, y: 2, z: 4, core: 2. Of those that a mesh axis runs over, the one named last changes fastest.
Arguments:
- latlon_cotangent: bfloat16 [2, 69, 24576], P('groups', None, 'curve'), parts along dimension 0, may hold values from -6 to 6
- healpix_cotangent: bfloat16 [2, 69, 24576], P('groups', None, 'curve'), parts along dimension 0, may hold values from -6 to 6
- outward_weights: bfloat16 [2304, 128, 128], P('curve'), may hold values from -0.15625 to 0.15625
- outward_source: int32 [2304], P('curve'), may hold values from 0 to 11
- outward_target: int32 [2304], P('curve'), may hold values from 0 to 11
- outward_counts: int32 [16, 16], P('curve'), may hold values from 1 to 18, 144 in all within a row
- inward_weights: bfloat16 [2304, 128, 128], P('curve'), may hold values from -0.15625 to 0.15625
- inward_source: int32 [2304], P('curve'), may hold values from 0 to 11
- inward_target: int32 [2304], P('curve'), may hold values from 0 to 11
- inward_counts: int32 [16, 16], P('curve'), may hold values from 1 to 18, 144 in all within a row
Outputs:
- healpix_gradient: bfloat16 [2, 69, 24576], P('groups', None, 'curve'), parts along dimension 0
- latlon_gradient: bfloat16 [2, 69, 24576], P('groups', None, 'curve'), parts along dimension 0
There are 2 independent parts, one for each index of `groups`. A program takes and returns all parts, laid end to end along the dimension named above; an argument that names none is the same for every part. Nothing has to cross between parts.
Inputs may be any that keep to these rules, and one draw needn't show every extreme that they name: `outward_counts`: each row sums to 144; its largest entry is exactly 18. `inward_counts`: each row sums to 144; its largest entry is exactly 18.
All inputs are finite; a program needn't handle non-finite values.
Results may differ from a plain program's by a relative error of at most 0.005.
Values may be sent and summed in bfloat16 or wider, within the bound.
No kernel may reach another device: no remote copies, remote signals or barrier semaphores. Data moves between devices by JAX's collectives and lax.ppermute only.
A program may use at most 128 MiB of HBM per device.

v0:
```python
import jax
import jax.numpy as jnp
from jax import lax
from jax.sharding import PartitionSpec as P


def block_products(cotangent, weights, source):
    width = weights.shape[1]
    lead = cotangent.shape[0] * cotangent.shape[1]
    tiled = cotangent.reshape(lead, cotangent.shape[2] // width, width)
    picked = jnp.take(tiled, source, axis=1)
    products = jnp.einsum("kbi,bij->bkj", picked, weights, preferred_element_type=jnp.float32)
    return products.astype(jnp.bfloat16)


def pack_slots(products, target, count_row):
    blocks = products.shape[0]
    devices = count_row.shape[0]
    per_device = 2 * blocks // devices
    inclusive = jnp.cumsum(count_row)
    exclusive = inclusive - count_row
    positions = jnp.arange(blocks, dtype=jnp.int32)
    owner = jnp.sum((positions[:, None] >= inclusive[None, :]).astype(jnp.int32), axis=1)
    chosen = owner[:, None] == jnp.arange(devices, dtype=jnp.int32)[None, :]
    first = jnp.sum(jnp.where(chosen, exclusive[None, :], 0), axis=1)
    slot_index = owner * per_device + positions - first
    buffer = (
        jnp.zeros((devices * per_device,) + products.shape[1:], jnp.bfloat16)
        .at[slot_index]
        .set(products)
    )
    labels = jnp.full((devices * per_device,), -1, jnp.int32).at[slot_index].set(target)
    return (buffer, labels)


def sum_slots(received, labels, tiles_out, like_shape):
    selector = (labels[None, :] == jnp.arange(tiles_out, dtype=jnp.int32)[:, None]).astype(
        jnp.bfloat16
    )
    summed = jnp.einsum("ts,skc->ktc", selector, received, preferred_element_type=jnp.float32)
    return summed.reshape(like_shape[0], like_shape[1], -1).astype(jnp.bfloat16)


def on_device(
    latlon_cotangent,
    healpix_cotangent,
    outward_weights,
    outward_source,
    outward_target,
    outward_counts,
    inward_weights,
    inward_source,
    inward_target,
    inward_counts,
):
    width = outward_weights.shape[1]
    tiles_latlon = latlon_cotangent.shape[2] // width
    tiles_healpix = healpix_cotangent.shape[2] // width
    outward_products = block_products(latlon_cotangent, outward_weights, outward_source)
    outward_buffer, outward_labels = pack_slots(outward_products, outward_target, outward_counts[0])
    inward_products = block_products(healpix_cotangent, inward_weights, inward_source)
    inward_buffer, inward_labels = pack_slots(inward_products, inward_target, inward_counts[0])
    outward_arrived, outward_arrived_labels = (
        lax.all_to_all(outward_buffer, "curve", split_axis=0, concat_axis=0, tiled=True),
        lax.all_to_all(outward_labels, "curve", split_axis=0, concat_axis=0, tiled=True),
    )
    inward_arrived, inward_arrived_labels = (
        lax.all_to_all(inward_buffer, "curve", split_axis=0, concat_axis=0, tiled=True),
        lax.all_to_all(inward_labels, "curve", split_axis=0, concat_axis=0, tiled=True),
    )
    healpix_gradient = sum_slots(
        outward_arrived, outward_arrived_labels, tiles_healpix, healpix_cotangent.shape
    )
    latlon_gradient = sum_slots(
        inward_arrived, inward_arrived_labels, tiles_latlon, latlon_cotangent.shape
    )
    return (healpix_gradient, latlon_gradient)


def solution(mesh):
    in_specs = (
        P("groups", None, "curve"),
        P("groups", None, "curve"),
        P("curve", None, None),
        P("curve"),
        P("curve"),
        P("curve", None),
        P("curve", None, None),
        P("curve"),
        P("curve"),
        P("curve", None),
    )
    out_specs = (P("groups", None, "curve"), P("groups", None, "curve"))
    return jax.shard_map(
        on_device, mesh=mesh, in_specs=in_specs, out_specs=out_specs, check_vma=False
    )
```

profile of v0, /device:TPU:13, one launch (start us, length us, event | category | flops | bytes accessed | tf_op | source)
XLA Modules:
  0.0 299.2 jit_solution(17780577935863267117)
XLA Ops:
  0.6 0.7 copy.28
  1.4 0.1 reduce
  1.5 0.7 fusion.43
  2.2 0.1 convert_reduce_fusion.1
  2.3 0.1 select_reduce_fusion.1
  2.4 1.2 scatter_custom_fusion.1
  3.6 0.7 all_to_all.19
  4.3 6.6 %all-to-all-start.1 = ((s32[16,18,1]{1,2,0:T(1,128)}), s32[16,18,1]{1,2,0:T(1,128)S(1)}, u32[]{:S(2)}, u32[]{:S(2)}) async-start(s32[16,18,1]{1,2,0:T(1,128)} %bitcast.6), calls=%async_computation.1 | async-start | bytes 16384 | tf_op jit(solution)/shard_map/all_to_all | solution.py:65
  10.8 0.7 compare_select_fusion.3
  11.5 0.7 compare_and_fusion.1
  12.2 0.7 copy.32
  13.0 0.1 reduce.3
  13.1 0.7 fusion.42
  13.7 0.1 convert_reduce_fusion
  13.8 0.1 select_reduce_fusion
  14.0 1.1 reshape.139
  15.1 0.1 copy.29
  15.1 1.2 scatter_custom_fusion.3
  16.3 0.7 all_to_all.22
  17.0 2.7 gather_fusion
  19.7 0.0 all-to-all-done.1
  19.7 6.0 %all-to-all-start.3 = ((s32[16,18,1]{1,2,0:T(1,128)}), s32[16,18,1]{1,2,0:T(1,128)S(1)}, u32[]{:S(2)}, u32[]{:S(2)}) async-start(s32[16,18,1]{1,2,0:T(1,128)} %bitcast.15), calls=%async_computation.3 | async-start | bytes 16384 | tf_op jit(solution)/shard_map/all_to_all | solution.py:69
  25.7 4.7 %fusion.12 = bf16[144,69,128]{2,1,0:T(8,128)(2,1)S(1)} fusion(bf16[144,128,128]{2,1,0:T(8,128)(2,1)} %param.14, bf16[144,69,128]{2,1,0:T(8,128)(2,1)} %gather_fusion, pred[144]{0:T(512)(128)(4,1)S(1)} %compare_and_fusion.1), kind=kOutput, calls=%fused_computation.18 | convolution fusion | flops 328126464 | bytes 9805968 | tf_op jit(solution)/shard_map/kbi,bij->bkj/dot_general | solution.py:12
  30.5 3.0 %broadcast.65.clone = bf16[288,69,128]{2,1,0:T(8,128)(2,1)} broadcast(bf16[]{:T(256)} %constant.3.clone.1), dimensions={} | broadcast | bytes 5087234 | tf_op jit(solution)/shard_map/broadcast.8
  33.5 17.8 %scatter_fusion = bf16[288,69,128]{2,1,0:T(8,128)(2,1)} fusion(bf16[288,69,128]{2,1,0:T(8,128)(2,1)} %broadcast.65.clone, s32[144]{0:T(256)S(1)} %bitcast.49, bf16[144,69,128]{2,1,0:T(8,128)(2,1)S(1)} %fusion.12), kind=kCustom, calls=%fused_computation.2 | custom fusion | bytes 7631424 | tf_op jit(solution)/shard_map/scatter | solution.py:30
  51.3 0.0 copy-start
  51.3 0.0 all-to-all-done.3
  51.3 6.2 %all-to-all-start = ((bf16[288,69,128]{2,1,0:T(8,128)(2,1)}), bf16[288,69,128]{2,1,0:T(8,128)(2,1)}, u32[]{:S(2)}, u32[]{:S(2)}) async-start(bf16[288,69,128]{2,1,0:T(8,128)(2,1)} %scatter_fusion), calls=%async_computation | async-start | bytes 10616832 | tf_op jit(solution)/shard_map/all_to_all | solution.py:64
  57.5 0.0 copy-done
  57.5 0.2 reshape.142
  57.7 0.1 copy.33
  57.7 0.0 copy-done.1
  57.8 2.7 gather_fusion.1
  60.5 4.7 %fusion.15 = bf16[144,69,128]{2,1,0:T(8,128)(2,1)S(1)} fusion(bf16[144,128,128]{2,1,0:T(8,128)(2,1)} %param.18, bf16[144,69,128]{2,1,0:T(8,128)(2,1)} %gather_fusion.1, pred[144]{0:T(512)(128)(4,1)S(1)} %compare_and_fusion), kind=kOutput, calls=%fused_computation.19 | convolution fusion | flops 328126464 | bytes 9805968 | tf_op jit(solution)/shard_map/kbi,bij->bkj/dot_general | solution.py:12
  65.2 3.1 %broadcast.65.clone.1 = bf16[288,69,128]{2,1,0:T(8,128)(2,1)} broadcast(bf16[]{:T(256)} %constant.3.clone.1), dimensions={} | broadcast | bytes 5087234 | tf_op jit(solution)/shard_map/broadcast.8
  68.3 17.7 %scatter_fusion.1 = bf16[288,69,128]{2,1,0:T(8,128)(2,1)} fusion(bf16[288,69,128]{2,1,0:T(8,128)(2,1)} %broadcast.65.clone.1, s32[144]{0:T(256)S(1)} %bitcast.47, bf16[144,69,128]{2,1,0:T(8,128)(2,1)S(1)} %fusion.15), kind=kCustom, calls=%fused_computation.4 | custom fusion | bytes 7631424 | tf_op jit(solution)/shard_map/scatter | solution.py:30
  86.0 87.8 %all-to-all-done = bf16[288,69,128]{2,1,0:T(8,128)(2,1)} async-done(((bf16[288,69,128]{2,1,0:T(8,128)(2,1)}), bf16[288,69,128]{2,1,0:T(8,128)(2,1)}, u32[]{:S(2)}, u32[]{:S(2)}) %all-to-all-start) | async-done | bytes 5087264 | tf_op jit(solution)/shard_map/all_to_all | solution.py:64
  173.8 4.9 %all-to-all-start.2 = ((bf16[288,69,128]{2,1,0:T(8,128)(2,1)}), bf16[288,69,128]{2,1,0:T(8,128)(2,1)}, u32[]{:S(2)}, u32[]{:S(2)}) async-start(bf16[288,69,128]{2,1,0:T(8,128)(2,1)} %scatter_fusion.1), calls=%async_computation.2 | async-start | bytes 10616832 | tf_op jit(solution)/shard_map/all_to_all | solution.py:68
  178.7 0.5 broadcast.128
  179.2 0.7 reduce.10
  179.9 0.1 eq.59
  180.0 0.7 reduce.11
  180.7 0.1 eq.66
  180.8 3.3 %fusion.29 = bf16[69,12,128]{2,1,0:T(8,128)(2,1)S(1)} fusion(bf16[288,69,128]{2,1,0:T(8,128)(2,1)} %all-to-all-done, s32[288]{0:T(512)S(1)} %eq.59), kind=kOutput, calls=%fused_computation.25 | convolution fusion | flops 61156224 | bytes 5300352 | tf_op jit(solution)/shard_map/ts,skc->ktc/dot_general | solution.py:40
  184.1 0.9 convert_element_type.52
  184.9 110.1 %all-to-all-done.2 = bf16[288,69,128]{2,1,0:T(8,128)(2,1)} async-done(((bf16[288,69,128]{2,1,0:T(8,128)(2,1)}), bf16[288,69,128]{2,1,0:T(8,128)(2,1)}, u32[]{:S(2)}, u32[]{:S(2)}) %all-to-all-start.2) | async-done | bytes 5087264 | tf_op jit(solution)/shard_map/all_to_all | solution.py:68
  295.1 3.3 %fusion.26 = bf16[69,12,128]{2,1,0:T(8,128)(2,1)S(1)} fusion(bf16[288,69,128]{2,1,0:T(8,128)(2,1)} %all-to-all-done.2, s32[288]{0:T(512)S(1)} %eq.66), kind=kOutput, calls=%fused_computation.24 | convolution fusion | flops 61156224 | bytes 5300352 | tf_op jit(solution)/shard_map/ts,skc->ktc/dot_general | solution.py:40
  298.4 0.9 convert_element_type.57
  (11 shorter events, 0.1 us)
Async XLA Ops:
  4.3 15.5 %all-to-all-start.1 = ((s32[16,18,1]{1,2,0:T(1,128)}), s32[16,18,1]{1,2,0:T(1,128)S(1)}, u32[]{:S(2)}, u32[]{:S(2)}) async-start(s32[16,18,1]{1,2,0:T(1,128)} %bitcast.6), calls=%async_computation.1 | async-start | bytes 16384 | tf_op jit(solution)/shard_map/all_to_all | solution.py:65
  19.7 31.6 %all-to-all-start.3 = ((s32[16,18,1]{1,2,0:T(1,128)}), s32[16,18,1]{1,2,0:T(1,128)S(1)}, u32[]{:S(2)}, u32[]{:S(2)}) async-start(s32[16,18,1]{1,2,0:T(1,128)} %bitcast.15), calls=%async_computation.3 | async-start | bytes 16384 | tf_op jit(solution)/shard_map/all_to_all | solution.py:69
  51.3 6.2 %copy-start = (bf16[1,69,1536]{2,1,0:T(8,128)(2,1)S(1)}, bf16[1,69,1536]{2,1,0:T(8,128)(2,1)}, u32[]{:S(2)}) copy-start(bf16[1,69,1536]{2,1,0:T(8,128)(2,1)} %param.13) | copy-start | bytes 635908
  51.3 6.4 %copy-start.1 = (s32[144]{0:T(256)S(1)}, s32[144]{0:T(256)}, u32[]{:S(2)}) copy-start(s32[144]{0:T(256)} %param.19) | copy-start | bytes 1732
  51.3 122.5 %all-to-all-start = ((bf16[288,69,128]{2,1,0:T(8,128)(2,1)}), bf16[288,69,128]{2,1,0:T(8,128)(2,1)}, u32[]{:S(2)}, u32[]{:S(2)}) async-start(bf16[288,69,128]{2,1,0:T(8,128)(2,1)} %scatter_fusion), calls=%async_computation | async-start | bytes 10616832 | tf_op jit(solution)/shard_map/all_to_all | solution.py:64
  173.8 121.2 %all-to-all-start.2 = ((bf16[288,69,128]{2,1,0:T(8,128)(2,1)}), bf16[288,69,128]{2,1,0:T(8,128)(2,1)}, u32[]{:S(2)}, u32[]{:S(2)}) async-start(bf16[288,69,128]{2,1,0:T(8,128)(2,1)} %scatter_fusion.1), calls=%async_computation.2 | async-start | bytes 10616832 | tf_op jit(solution)/shard_map/all_to_all | solution.py:68
where the time goes:
time: 301 us; the launch traced here: 299 us
  waiting for transfers between devices  198 us (66%)
  local copies, waits for them, and re-layouts  56.1 us (19%)
  starting transfers between devices  23.6 us (8%)
  matrix products  16.1 us (5%)
  other arithmetic  4.74 us (2%)
    all_to_all x1, waiting for transfers between devices, on_device(): lax.all_to_all(inward_buffer, 'curve', split_axis=0, concat_axis=0, tiled...  110 us
    all_to_all x1, waiting for transfers between devices, on_device(): lax.all_to_all(outward_buffer, 'curve', split_axis=0, concat_axis=0, tile...  87.8 us
    scatter x2, local copies, waits for them, and re-layouts, pack_slots(): buffer = jnp.zeros((devices * per_device,) + products.shape[1:], jnp.bflo...  35.5 us
    dot_general x2, matrix products, block_products(): jnp.einsum('kbi,bij->bkj', picked, weights, preferred_element_type=jnp.fl...  9.48 us
    another operation x3, local copies, waits for them, and re-layouts  6.83 us
    dot_general x2, matrix products, sum_slots(): jnp.einsum('ts,skc->ktc', selector, received, preferred_element_type=jnp....  6.6 us
    all_to_all x1, starting transfers between devices, on_device(): lax.all_to_all(outward_labels, 'curve', split_axis=0, concat_axis=0, tile...  6.55 us
    all_to_all x1, starting transfers between devices, on_device(): lax.all_to_all(outward_buffer, 'curve', split_axis=0, concat_axis=0, tile...  6.17 us
  transfers between devices with their start and end apart: 4, of which 2 were waited for; matrix products, arithmetic and copies ran while one was open for 23% of the time, Pallas kernels for 0%

commit v1 on v0

v1 whole, which is shorter than its diff:
```python
import functools

import jax
import jax.numpy as jnp
from jax import lax
from jax.experimental import pallas as pl
from jax.experimental.pallas import tpu as pltpu
from jax.sharding import PartitionSpec as P

LANES = 128
HALVES = 2
ACC_LIMIT = 16 * 1024 * 1024


def round_up(value, unit):
    return -(-value // unit) * unit


def block_products(cotangent, weights, source):
    width = weights.shape[1]
    lead = cotangent.shape[0] * cotangent.shape[1]
    tiled = cotangent.reshape(lead, cotangent.shape[2] // width, width)
    picked = jnp.take(tiled, source, axis=1)
    products = jnp.einsum("kbi,bij->bkj", picked, weights, preferred_element_type=jnp.float32)
    return products.astype(jnp.bfloat16)


def pack_slots(products, target, count_row):
    blocks = products.shape[0]
    devices = count_row.shape[0]
    per_device = 2 * blocks // devices
    inclusive = jnp.cumsum(count_row)
    exclusive = inclusive - count_row
    positions = jnp.arange(blocks, dtype=jnp.int32)
    owner = jnp.sum((positions[:, None] >= inclusive[None, :]).astype(jnp.int32), axis=1)
    chosen = owner[:, None] == jnp.arange(devices, dtype=jnp.int32)[None, :]
    first = jnp.sum(jnp.where(chosen, exclusive[None, :], 0), axis=1)
    slot_index = owner * per_device + positions - first
    buffer = (
        jnp.zeros((devices * per_device,) + products.shape[1:], jnp.bfloat16)
        .at[slot_index]
        .set(products)
    )
    labels = jnp.full((devices * per_device,), -1, jnp.int32).at[slot_index].set(target)
    return (buffer, labels)


def sum_slots(received, labels, tiles_out, like_shape):
    selector = (labels[None, :] == jnp.arange(tiles_out, dtype=jnp.int32)[:, None]).astype(
        jnp.bfloat16
    )
    summed = jnp.einsum("ts,skc->ktc", selector, received, preferred_element_type=jnp.float32)
    return summed.reshape(like_shape[0], like_shape[1], -1).astype(jnp.bfloat16)


def slot_remap(cotangent, weights, source, target, counts, like_shape):
    products = block_products(cotangent, weights, source)
    buffer, labels = pack_slots(products, target, counts[0])
    arrived = lax.all_to_all(buffer, "curve", split_axis=0, concat_axis=0, tiled=True)
    arrived_labels = lax.all_to_all(labels, "curve", split_axis=0, concat_axis=0, tiled=True)
    return sum_slots(arrived, arrived_labels, like_shape[2] // weights.shape[1], like_shape)


def place_of(owner, me, bits):
    differ = jnp.bitwise_xor(owner, me)
    place = jnp.bitwise_and(differ, 1)
    for bit in range(1, bits):
        place = place * 2 + jnp.bitwise_and(jnp.right_shift(differ, bit), 1)
    return place


def product_kernel(
    bits, channels, pitch, tiles, step_blocks,
    source, target, counts, x_ref, w_ref, *rest,
):
    sends, keeps = rest[:HALVES], rest[HALVES:2 * HALVES]
    acc, xs, stage, state, sems = rest[2 * HALVES:]
    devices = 1 << bits
    part = tiles // HALVES
    rows = devices * part * pitch
    half_rows = rows // 2
    step = pl.program_id(0)
    me = lax.axis_index("curve")

    @pl.when(step == 0)
    def start():
        @pl.loop(0, HALVES * devices)
        def clear(index):
            at = pl.multiple_of(index * (part * pitch), part * pitch)
            acc[pl.ds(at, part * pitch), :] = jnp.zeros((part * pitch, LANES), jnp.float32)

        for tile in range(xs.shape[0]):
            xs[tile] = jnp.zeros(xs.shape[1:], xs.dtype)
            xs[tile, :channels, :] = x_ref[0, :, tile * LANES:(tile + 1) * LANES]
        state[0] = 0
        state[1] = counts[0]

    owner, end = state[0], state[1]
    places = []
    for index in range(step_blocks):
        block = step * step_blocks + index
        passed = (block >= end).astype(jnp.int32)
        owner = jnp.minimum(owner + passed, devices - 1)
        end = end + passed * counts[owner]
        tile = target[block]
        half = (tile >= part).astype(jnp.int32)
        place = (half * devices + place_of(owner, me, bits)) * part + tile - half * part
        places.append(pl.multiple_of(place * pitch, 8))
    state[0] = owner
    state[1] = end
    for index in range(step_blocks):
        x = xs[source[step * step_blocks + index], :pitch, :]
        product = jnp.dot(x, w_ref[index], preferred_element_type=jnp.float32)
        acc[pl.ds(places[index], pitch), :] += product

    @pl.when(step == pl.num_programs(0) - 1)
    def finish():
        copies = []
        for half in range(HALVES):
            base = half * rows

            @pl.loop(0, devices // 2)
            def convert(index):
                unit = part * pitch
                at = pl.multiple_of(index * unit, unit)
                stage[half, pl.ds(at, unit), :] = acc[
                    pl.ds(base + half_rows + at, unit), :
                ].astype(jnp.bfloat16)

            copies.append(pltpu.make_async_copy(stage.at[half], sends[half], sems.at[2 * half]))
            copies[-1].start()
            copies.append(
                pltpu.make_async_copy(
                    acc.at[pl.ds(base, half_rows)], keeps[half], sems.at[2 * half + 1]
                )
            )
            copies[-1].start()
        for copy in copies:
            copy.wait()


def products(cotangent, weights, source, target, counts, tiles, bits):
    devices = 1 << bits
    channels = cotangent.shape[1]
    pitch = round_up(channels, 8)
    tiles_in = cotangent.shape[2] // LANES
    blocks = weights.shape[0]
    step_blocks = max(size for size in range(1, 17) if blocks % size == 0)
    part = tiles // HALVES
    half_rows = devices * part * pitch // 2
    send = jax.ShapeDtypeStruct((half_rows, LANES), jnp.bfloat16)
    keep = jax.ShapeDtypeStruct((half_rows, LANES), jnp.float32)
    return pl.pallas_call(
        functools.partial(product_kernel, bits, channels, pitch, tiles, step_blocks),
        out_shape=[send] * HALVES + [keep] * HALVES,
        grid_spec=pltpu.PrefetchScalarGridSpec(
            num_scalar_prefetch=3,
            grid=(blocks // step_blocks,),
            in_specs=[
                pl.BlockSpec(cotangent.shape, lambda step, *_: (0, 0, 0)),
                pl.BlockSpec((step_blocks, LANES, LANES), lambda step, *_: (step, 0, 0)),
            ],
            out_specs=[pl.BlockSpec(memory_space=pl.ANY)] * (2 * HALVES),
            scratch_shapes=[
                pltpu.VMEM((HALVES * 2 * half_rows, LANES), jnp.float32),
                pltpu.VMEM((tiles_in, round_up(pitch, 16), LANES), jnp.bfloat16),
                pltpu.VMEM((HALVES, half_rows, LANES), jnp.bfloat16),
                pltpu.SMEM((2,), jnp.int32),
                pltpu.SemaphoreType.DMA((2 * HALVES,)),
            ],
        ),
        compiler_params=pltpu.CompilerParams(vmem_limit_bytes=32 * 1024 * 1024),
        cost_estimate=pl.CostEstimate(
            flops=2 * blocks * channels * LANES * LANES,
            bytes_accessed=2 * weights.size + 6 * HALVES * half_rows * LANES,
            transcendentals=0,
        ),
    )(source, target, counts.reshape(-1), cotangent, weights)


def exchange(value, bit, devices):
    return lax.ppermute(value, "curve", [(at, at ^ (1 << bit)) for at in range(devices)])


def reduce_halves(send, keep, bits):
    devices = 1 << bits
    terms = [keep]
    length = keep.shape[0]
    for bit in range(bits):
        terms.append(exchange(send, bit, devices))
        length //= 2
        if bit + 1 < bits:
            total = sum(term[length:2 * length].astype(jnp.float32) for term in terms)
            send = total.astype(jnp.bfloat16)
    return terms


def final_kernel(channels, pitch, part, count, *refs):
    out = refs[-1]
    for half in range(HALVES):
        terms = refs[half * count:(half + 1) * count]
        for tile in range(part):
            total = sum(
                term[tile * pitch:(tile + 1) * pitch, :].astype(jnp.float32) for term in terms
            )
            at = (half * part + tile) * LANES
            out[0, :, at:at + LANES] = total[:channels].astype(jnp.bfloat16)


def final_sum(terms, like_shape, pitch, part):
    rows = part * pitch
    flat = [term for half in terms for term in half]
    return pl.pallas_call(
        functools.partial(final_kernel, like_shape[1], pitch, part, len(terms[0])),
        out_shape=jax.ShapeDtypeStruct(like_shape, jnp.bfloat16),
        grid=(1,),
        in_specs=[pl.BlockSpec((rows, LANES), lambda step: (0, 0)) for _ in flat],
        out_specs=pl.BlockSpec(like_shape, lambda step: (0, 0, 0)),
        compiler_params=pltpu.CompilerParams(vmem_limit_bytes=32 * 1024 * 1024),
    )(*flat)


def bit_remaps(remaps, bits):
    made = []
    for cotangent, weights, source, target, counts, like_shape in remaps:
        tiles = like_shape[2] // LANES
        made.append(products(cotangent, weights, source, target, counts, tiles, bits))
    results = []
    for arrays, remap in zip(made, remaps):
        like_shape = remap[-1]
        terms = [reduce_halves(arrays[half], arrays[HALVES + half], bits) for half in range(HALVES)]
        part = like_shape[2] // LANES // HALVES
        results.append(final_sum(terms, like_shape, round_up(like_shape[1], 8), part))
    return results


def on_device(devices, *args):
    latlon, healpix = args[:2]
    remaps = [
        (latlon, args[2], args[3], args[4], args[5], healpix.shape),
        (healpix, args[6], args[7], args[8], args[9], latlon.shape),
    ]
    bits = devices.bit_length() - 1
    tiles = max(latlon.shape[2], healpix.shape[2]) // LANES
    size = devices * tiles * round_up(latlon.shape[1], 8) * LANES * 4
    if devices == 1 << bits and bits > 0 and size <= ACC_LIMIT:
        return tuple(bit_remaps(remaps, bits))
    return tuple(slot_remap(*remap) for remap in remaps)


def solution(mesh):
    in_specs = (
        P("groups", None, "curve"),
        P("groups", None, "curve"),
        P("curve", None, None),
        P("curve"),
        P("curve"),
        P("curve", None),
        P("curve", None, None),
        P("curve"),
        P("curve"),
        P("curve", None),
    )
    out_specs = (P("groups", None, "curve"), P("groups", None, "curve"))
    return jax.shard_map(
        functools.partial(on_device, mesh.shape["curve"]),
        mesh=mesh, in_specs=in_specs, out_specs=out_specs, check_vma=False,
    )
```

time: 301 us -> 86.3 us (0.29)
  the two profiles are of different devices: /device:TPU:13 before, /device:TPU:0 now
where the time goes in v1:
time: 86.3 us; the launch traced here: 86.1 us
  waiting for transfers between devices  43 us (50%)
  starting transfers between devices  22.6 us (26%)
  Pallas kernels  13.5 us (16%)
  local copies, waits for them, and re-layouts  5.3 us (6%)
  other arithmetic  1.03 us (1%)
    ppermute x16, waiting for transfers between devices, exchange(): lax.ppermute(value, 'curve', [(at, at ^ 1 << bit) for at in range(devices)])  43 us
    ppermute x16, starting transfers between devices, exchange(): lax.ppermute(value, 'curve', [(at, at ^ 1 << bit) for at in range(devices)])  22.6 us
    pallas_call x2, Pallas kernels, products(): pl.pallas_call(functools.partial(product_kernel, bits, channels, pitch, t...  11.8 us
    unnamed x20, local copies, waits for them, and re-layouts  5.3 us
  transfers between devices with their start and end apart: 16, of which 8 were waited for; matrix products, arithmetic and copies ran while one was open for 1% of the time, Pallas kernels for 8%

profile of v1, /device:TPU:0, one launch (start us, length us, event | category | flops | bytes accessed | tf_op | source)
XLA Modules:
  0.0 86.1 jit_solution(11622583743573453479)
XLA Ops:
  0.6 2.3 %copy-done = bf16[144,128,128]{2,1,0:T(8,128)(2,1)S(1)} copy-done((bf16[144,128,128]{2,1,0:T(8,128)(2,1)S(1)}, bf16[144,128,128]{2,1,0:T(8,128)(2,1)}, u32[]{:S(2)}) %copy-start) | copy-done | bytes 4718616
  3.0 0.9 %copy-done.2 = bf16[1,69,1536]{2,1,0:T(8,128)(2,1)S(1)} copy-done((bf16[1,69,1536]{2,1,0:T(8,128)(2,1)S(1)}, bf16[1,69,1536]{2,1,0:T(8,128)(2,1)}, u32[]{:S(2)}) %copy-start.2) | copy-done | bytes 211992
  3.9 0.7 copy-done.4
  4.6 0.7 copy-done.5
  5.3 0.7 copy-done.8
  5.9 5.9 %shard_map.113 = (bf16[3456,128]{1,0:T(8,128)(2,1)S(1)}, bf16[3456,128]{1,0:T(8,128)(2,1)S(1)}, f32[3456,128]{1,0:T(8,128)S(1)}, f32[3456,128]{1,0:T(8,128)S(1)}) custom-call(s32[144]{0:T(256)S(1)} %copy-done.4, s32[144]{0:T(256)S(1)} %copy-done.5, s32[16]{0:T(128)S(1)} %bitcast.2, bf16[1,69,1536]{2,1,0:T(8,128)(2,1)S(1)} %copy-done.2, ...), custom_call_target="tpu_custom_call" | custom-call | flops 325582848 | bytes 10027008 | tf_op jit(solution)/shard_map/pallas_call | solution.py:153
  11.9 0.5 collective-permute-start
  12.4 0.1 collective-permute-start.4
  12.5 5.9 %shard_map.115 = (bf16[3456,128]{1,0:T(8,128)(2,1)S(1)}, bf16[3456,128]{1,0:T(8,128)(2,1)S(1)}, f32[3456,128]{1,0:T(8,128)S(1)}, f32[3456,128]{1,0:T(8,128)S(1)}) custom-call(s32[144]{0:T(256)S(1)} %copy-done.6, s32[144]{0:T(256)S(1)} %copy-done.7, s32[16]{0:T(128)S(1)} %bitcast.3, bf16[1,69,1536]{2,1,0:T(8,128)(2,1)S(1)} %copy-done.3, ...), custom_call_target="tpu_custom_call" | custom-call | flops 325582848 | bytes 10027008 | tf_op jit(solution)/shard_map/pallas_call | solution.py:153
  18.4 0.5 collective-permute-start.8
  18.9 0.1 collective-permute-start.12
  19.0 0.1 add_convert_fusion.3
  19.1 3.0 %collective-permute-start.1 = (bf16[1728,128]{1,0:T(8,128)(2,1)S(1)}, bf16[1728,128]{1,0:T(8,128)(2,1)S(1)}, u32[]{:S(2)}, u32[]{:S(2)}) collective-permute-start(bf16[1728,128]{1,0:T(8,128)(2,1)S(1)} %add_convert_fusion.3), channel_id=1, source_target_pairs={{0,2},{1,3},{2,0},{3,1},{4,6},{5,7},{6,4},{7,5},{8,10},{9,11},{10,... | collective-permute-start | bytes 1327112 | tf_op jit(solution)/shard_map/ppermute | solution.py:182
  22.1 0.0 collective-permute-done.4.refs_6_
  22.1 0.1 add_convert_fusion.2
  22.2 0.1 collective-permute-start.5
  22.3 0.0 collective-permute-done.8.refs_1_
  22.3 0.1 add_convert_fusion.1
  22.4 2.1 %collective-permute-start.9 = (bf16[1728,128]{1,0:T(8,128)(2,1)S(1)}, bf16[1728,128]{1,0:T(8,128)(2,1)S(1)}, u32[]{:S(2)}, u32[]{:S(2)}) collective-permute-start(bf16[1728,128]{1,0:T(8,128)(2,1)S(1)} %add_convert_fusion.1), channel_id=1, source_target_pairs={{0,2},{1,3},{2,0},{3,1},{4,6},{5,7},{6,4},{7,5},{8,10},{9,11},{10,... | collective-permute-start | bytes 1327112 | tf_op jit(solution)/shard_map/ppermute | solution.py:182
  24.5 0.1 add_convert_fusion
  24.6 0.7 collective-permute-start.13
  25.2 7.8 %collective-permute-done.1.refs_2_ = bf16[1728,128]{1,0:T(8,128)(2,1)S(1)} collective-permute-done((bf16[1728,128]{1,0:T(8,128)(2,1)S(1)}, bf16[1728,128]{1,0:T(8,128)(2,1)S(1)}, u32[]{:S(2)}, u32[]{:S(2)}) %collective-permute-start.1) | collective-permute-done | bytes 442400 | tf_op jit(solution)/shard_map/ppermute | solution.py:182
  33.0 0.1 add_convert_fusion.7
  33.1 2.2 %collective-permute-start.2 = (bf16[864,128]{1,0:T(8,128)(2,1)S(1)}, bf16[864,128]{1,0:T(8,128)(2,1)S(1)}, u32[]{:S(2)}, u32[]{:S(2)}) collective-permute-start(bf16[864,128]{1,0:T(8,128)(2,1)S(1)} %add_convert_fusion.7), channel_id=1, source_target_pairs={{0,4},{1,5},{2,6},{3,7},{4,0},{5,1},{6,2},{7,3},{8,12},{9,13},{10,... | collective-permute-start | bytes 663560 | tf_op jit(solution)/shard_map/ppermute | solution.py:182
  35.4 7.2 %collective-permute-done.5.refs_7_ = bf16[1728,128]{1,0:T(8,128)(2,1)S(1)} collective-permute-done((bf16[1728,128]{1,0:T(8,128)(2,1)S(1)}, bf16[1728,128]{1,0:T(8,128)(2,1)S(1)}, u32[]{:S(2)}, u32[]{:S(2)}) %collective-permute-start.5) | collective-permute-done | bytes 442400 | tf_op jit(solution)/shard_map/ppermute | solution.py:182
  42.5 0.1 add_convert_fusion.6
  42.6 2.2 %collective-permute-start.6 = (bf16[864,128]{1,0:T(8,128)(2,1)S(1)}, bf16[864,128]{1,0:T(8,128)(2,1)S(1)}, u32[]{:S(2)}, u32[]{:S(2)}) collective-permute-start(bf16[864,128]{1,0:T(8,128)(2,1)S(1)} %add_convert_fusion.6), channel_id=1, source_target_pairs={{0,4},{1,5},{2,6},{3,7},{4,0},{5,1},{6,2},{7,3},{8,12},{9,13},{10,... | collective-permute-start | bytes 663560 | tf_op jit(solution)/shard_map/ppermute | solution.py:182
  44.8 7.2 %collective-permute-done.9.refs_2_ = bf16[1728,128]{1,0:T(8,128)(2,1)S(1)} collective-permute-done((bf16[1728,128]{1,0:T(8,128)(2,1)S(1)}, bf16[1728,128]{1,0:T(8,128)(2,1)S(1)}, u32[]{:S(2)}, u32[]{:S(2)}) %collective-permute-start.9) | collective-permute-done | bytes 442400 | tf_op jit(solution)/shard_map/ppermute | solution.py:182
  52.0 0.1 add_convert_fusion.5
  52.1 2.2 %collective-permute-start.10 = (bf16[864,128]{1,0:T(8,128)(2,1)S(1)}, bf16[864,128]{1,0:T(8,128)(2,1)S(1)}, u32[]{:S(2)}, u32[]{:S(2)}) collective-permute-start(bf16[864,128]{1,0:T(8,128)(2,1)S(1)} %add_convert_fusion.5), channel_id=1, source_target_pairs={{0,4},{1,5},{2,6},{3,7},{4,0},{5,1},{6,2},{7,3},{8,12},{9,13},{10,... | collective-permute-start | bytes 663560 | tf_op jit(solution)/shard_map/ppermute | solution.py:182
  54.3 6.7 %collective-permute-done.13.refs_7_ = bf16[1728,128]{1,0:T(8,128)(2,1)S(1)} collective-permute-done((bf16[1728,128]{1,0:T(8,128)(2,1)S(1)}, bf16[1728,128]{1,0:T(8,128)(2,1)S(1)}, u32[]{:S(2)}, u32[]{:S(2)}) %collective-permute-start.13) | collective-permute-done | bytes 442400 | tf_op jit(solution)/shard_map/ppermute | solution.py:182
  61.0 0.1 add_convert_fusion.4
  61.1 1.9 %collective-permute-start.14 = (bf16[864,128]{1,0:T(8,128)(2,1)S(1)}, bf16[864,128]{1,0:T(8,128)(2,1)S(1)}, u32[]{:S(2)}, u32[]{:S(2)}) collective-permute-start(bf16[864,128]{1,0:T(8,128)(2,1)S(1)} %add_convert_fusion.4), channel_id=1, source_target_pairs={{0,4},{1,5},{2,6},{3,7},{4,0},{5,1},{6,2},{7,3},{8,12},{9,13},{10,... | collective-permute-start | bytes 663560 | tf_op jit(solution)/shard_map/ppermute | solution.py:182
  62.9 0.0 collective-permute-done.2.refs_3_
  62.9 0.1 add_convert_fusion.11
  63.0 2.7 %collective-permute-start.3 = (bf16[432,128]{1,0:T(8,128)(2,1)S(1)}, bf16[432,128]{1,0:T(8,128)(2,1)S(1)}, u32[]{:S(2)}, u32[]{:S(2)}) collective-permute-start(bf16[432,128]{1,0:T(8,128)(2,1)S(1)} %add_convert_fusion.11), channel_id=1, source_target_pairs={{0,8},{1,9},{2,10},{3,11},{4,12},{5,13},{6,14},{7,15},{8,0},{9,1},... | collective-permute-start | bytes 331784 | tf_op jit(solution)/shard_map/ppermute | solution.py:182
  65.6 0.1 add_convert_fusion.10
  65.7 0.4 collective-permute-start.7
  66.1 0.1 add_convert_fusion.9
  66.2 2.7 %collective-permute-start.11 = (bf16[432,128]{1,0:T(8,128)(2,1)S(1)}, bf16[432,128]{1,0:T(8,128)(2,1)S(1)}, u32[]{:S(2)}, u32[]{:S(2)}) collective-permute-start(bf16[432,128]{1,0:T(8,128)(2,1)S(1)} %add_convert_fusion.9), channel_id=1, source_target_pairs={{0,8},{1,9},{2,10},{3,11},{4,12},{5,13},{6,14},{7,15},{8,0},{9,1},... | collective-permute-start | bytes 331784 | tf_op jit(solution)/shard_map/ppermute | solution.py:182
  68.8 2.8 %collective-permute-done.14.refs_8_ = bf16[864,128]{1,0:T(8,128)(2,1)S(1)} collective-permute-done((bf16[864,128]{1,0:T(8,128)(2,1)S(1)}, bf16[864,128]{1,0:T(8,128)(2,1)S(1)}, u32[]{:S(2)}, u32[]{:S(2)}) %collective-permute-start.14) | collective-permute-done | bytes 221216 | tf_op jit(solution)/shard_map/ppermute | solution.py:182
  71.6 0.1 add_convert_fusion.8
  71.7 1.4 %collective-permute-start.15 = (bf16[432,128]{1,0:T(8,128)(2,1)S(1)}, bf16[432,128]{1,0:T(8,128)(2,1)S(1)}, u32[]{:S(2)}, u32[]{:S(2)}) collective-permute-start(bf16[432,128]{1,0:T(8,128)(2,1)S(1)} %add_convert_fusion.8), channel_id=1, source_target_pairs={{0,8},{1,9},{2,10},{3,11},{4,12},{5,13},{6,14},{7,15},{8,0},{9,1},... | collective-permute-start | bytes 331784 | tf_op jit(solution)/shard_map/ppermute | solution.py:182
  73.1 8.2 %collective-permute-done.7.refs_9_ = bf16[432,128]{1,0:T(8,128)(2,1)S(1)} collective-permute-done((bf16[432,128]{1,0:T(8,128)(2,1)S(1)}, bf16[432,128]{1,0:T(8,128)(2,1)S(1)}, u32[]{:S(2)}, u32[]{:S(2)}) %collective-permute-start.7) | collective-permute-done | bytes 110624 | tf_op jit(solution)/shard_map/ppermute | solution.py:182
  81.3 0.8 shard_map.114
  82.2 1.5 %collective-permute-done.11.refs_4_ = bf16[432,128]{1,0:T(8,128)(2,1)S(1)} collective-permute-done((bf16[432,128]{1,0:T(8,128)(2,1)S(1)}, bf16[432,128]{1,0:T(8,128)(2,1)S(1)}, u32[]{:S(2)}, u32[]{:S(2)}) %collective-permute-start.11) | collective-permute-done | bytes 110624 | tf_op jit(solution)/shard_map/ppermute | solution.py:182
  83.7 1.6 %collective-permute-done.15.refs_9_ = bf16[432,128]{1,0:T(8,128)(2,1)S(1)} collective-permute-done((bf16[432,128]{1,0:T(8,128)(2,1)S(1)}, bf16[432,128]{1,0:T(8,128)(2,1)S(1)}, u32[]{:S(2)}, u32[]{:S(2)}) %collective-permute-start.15) | collective-permute-done | bytes 110624 | tf_op jit(solution)/shard_map/ppermute | solution.py:182
  85.3 0.8 shard_map.116
  (20 shorter events, 0.0 us)
Async XLA Ops:
  0.6 2.3 %copy-start = (bf16[144,128,128]{2,1,0:T(8,128)(2,1)S(1)}, bf16[144,128,128]{2,1,0:T(8,128)(2,1)}, u32[]{:S(2)}) copy-start(bf16[144,128,128]{2,1,0:T(8,128)(2,1)} %w_ref.2) | copy-start | bytes 14155780
  3.0 0.9 %copy-start.2 = (bf16[1,69,1536]{2,1,0:T(8,128)(2,1)S(1)}, bf16[1,69,1536]{2,1,0:T(8,128)(2,1)}, u32[]{:S(2)}) copy-start(bf16[1,69,1536]{2,1,0:T(8,128)(2,1)} %x_ref.2) | copy-start | bytes 635908
  3.9 0.7 copy-start.4
  4.6 0.7 copy-start.5
  5.3 0.7 copy-start.8
  5.9 6.5 %copy-start.1 = (bf16[144,128,128]{2,1,0:T(8,128)(2,1)S(1)}, bf16[144,128,128]{2,1,0:T(8,128)(2,1)}, u32[]{:S(2)}) copy-start(bf16[144,128,128]{2,1,0:T(8,128)(2,1)} %w_ref.3) | copy-start | bytes 14155780
  5.9 6.5 %copy-start.3 = (bf16[1,69,1536]{2,1,0:T(8,128)(2,1)S(1)}, bf16[1,69,1536]{2,1,0:T(8,128)(2,1)}, u32[]{:S(2)}) copy-start(bf16[1,69,1536]{2,1,0:T(8,128)(2,1)} %x_ref.3) | copy-start | bytes 635908
  5.9 6.5 %copy-start.6 = (s32[144]{0:T(256)S(1)}, s32[144]{0:T(256)}, u32[]{:S(2)}) copy-start(s32[144]{0:T(256)} %source.3) | copy-start | bytes 1732
  5.9 6.5 %copy-start.7 = (s32[144]{0:T(256)S(1)}, s32[144]{0:T(256)}, u32[]{:S(2)}) copy-start(s32[144]{0:T(256)} %target.3) | copy-start | bytes 1732
  5.9 6.5 %copy-start.9 = (s32[1,16]{1,0:T(1,128)S(1)}, s32[1,16]{1,0:T(1,128)}, u32[]{:S(2)}) copy-start(s32[1,16]{1,0:T(1,128)} %param.19) | copy-start | bytes 196
  11.9 7.1 %collective-permute-start = (bf16[3456,128]{1,0:T(8,128)(2,1)S(1)}, bf16[3456,128]{1,0:T(8,128)(2,1)S(1)}, u32[]{:S(2)}, u32[]{:S(2)}) collective-permute-start(bf16[3456,128]{1,0:T(8,128)(2,1)S(1)} %get-tuple-element.11), channel_id=1, source_target_pairs={{0,1},{1,0},{2,3},{3,2},{4,5},{5,4},{6,7},{7,6},{8,9},{9,8},{10,11... | collective-permute-start | bytes 2654216 | tf_op jit(solution)/shard_map/ppermute | solution.py:182
  12.4 9.7 %collective-permute-start.4 = (bf16[3456,128]{1,0:T(8,128)(2,1)S(1)}, bf16[3456,128]{1,0:T(8,128)(2,1)S(1)}, u32[]{:S(2)}, u32[]{:S(2)}) collective-permute-start(bf16[3456,128]{1,0:T(8,128)(2,1)S(1)} %get-tuple-element.13), channel_id=1, source_target_pairs={{0,1},{1,0},{2,3},{3,2},{4,5},{5,4},{6,7},{7,6},{8,9},{9,8},{10,11... | collective-permute-start | bytes 2654216 | tf_op jit(solution)/shard_map/ppermute | solution.py:182
  18.4 3.9 %collective-permute-start.8 = (bf16[3456,128]{1,0:T(8,128)(2,1)S(1)}, bf16[3456,128]{1,0:T(8,128)(2,1)S(1)}, u32[]{:S(2)}, u32[]{:S(2)}) collective-permute-start(bf16[3456,128]{1,0:T(8,128)(2,1)S(1)} %get-tuple-element.15), channel_id=1, source_target_pairs={{0,1},{1,0},{2,3},{3,2},{4,5},{5,4},{6,7},{7,6},{8,9},{9,8},{10,11... | collective-permute-start | bytes 2654216 | tf_op jit(solution)/shard_map/ppermute | solution.py:182
  18.9 5.6 %collective-permute-start.12 = (bf16[3456,128]{1,0:T(8,128)(2,1)S(1)}, bf16[3456,128]{1,0:T(8,128)(2,1)S(1)}, u32[]{:S(2)}, u32[]{:S(2)}) collective-permute-start(bf16[3456,128]{1,0:T(8,128)(2,1)S(1)} %get-tuple-element.17), channel_id=1, source_target_pairs={{0,1},{1,0},{2,3},{3,2},{4,5},{5,4},{6,7},{7,6},{8,9},{9,8},{10,11... | collective-permute-start | bytes 2654216 | tf_op jit(solution)/shard_map/ppermute | solution.py:182
  19.1 14.0 %collective-permute-start.1 = (bf16[1728,128]{1,0:T(8,128)(2,1)S(1)}, bf16[1728,128]{1,0:T(8,128)(2,1)S(1)}, u32[]{:S(2)}, u32[]{:S(2)}) collective-permute-start(bf16[1728,128]{1,0:T(8,128)(2,1)S(1)} %add_convert_fusion.3), channel_id=1, source_target_pairs={{0,2},{1,3},{2,0},{3,1},{4,6},{5,7},{6,4},{7,5},{8,10},{9,11},{10,... | collective-permute-start | bytes 1327112 | tf_op jit(solution)/shard_map/ppermute | solution.py:182
  22.2 20.3 %collective-permute-start.5 = (bf16[1728,128]{1,0:T(8,128)(2,1)S(1)}, bf16[1728,128]{1,0:T(8,128)(2,1)S(1)}, u32[]{:S(2)}, u32[]{:S(2)}) collective-permute-start(bf16[1728,128]{1,0:T(8,128)(2,1)S(1)} %add_convert_fusion.2), channel_id=1, source_target_pairs={{0,2},{1,3},{2,0},{3,1},{4,6},{5,7},{6,4},{7,5},{8,10},{9,11},{10,... | collective-permute-start | bytes 1327112 | tf_op jit(solution)/shard_map/ppermute | solution.py:182
  22.4 29.6 %collective-permute-start.9 = (bf16[1728,128]{1,0:T(8,128)(2,1)S(1)}, bf16[1728,128]{1,0:T(8,128)(2,1)S(1)}, u32[]{:S(2)}, u32[]{:S(2)}) collective-permute-start(bf16[1728,128]{1,0:T(8,128)(2,1)S(1)} %add_convert_fusion.1), channel_id=1, source_target_pairs={{0,2},{1,3},{2,0},{3,1},{4,6},{5,7},{6,4},{7,5},{8,10},{9,11},{10,... | collective-permute-start | bytes 1327112 | tf_op jit(solution)/shard_map/ppermute | solution.py:182
  24.6 36.4 %collective-permute-start.13 = (bf16[1728,128]{1,0:T(8,128)(2,1)S(1)}, bf16[1728,128]{1,0:T(8,128)(2,1)S(1)}, u32[]{:S(2)}, u32[]{:S(2)}) collective-permute-start(bf16[1728,128]{1,0:T(8,128)(2,1)S(1)} %add_convert_fusion), channel_id=1, source_target_pairs={{0,2},{1,3},{2,0},{3,1},{4,6},{5,7},{6,4},{7,5},{8,10},{9,11},{10,... | collective-permute-start | bytes 1327112 | tf_op jit(solution)/shard_map/ppermute | solution.py:182
  33.1 29.8 %collective-permute-start.2 = (bf16[864,128]{1,0:T(8,128)(2,1)S(1)}, bf16[864,128]{1,0:T(8,128)(2,1)S(1)}, u32[]{:S(2)}, u32[]{:S(2)}) collective-permute-start(bf16[864,128]{1,0:T(8,128)(2,1)S(1)} %add_convert_fusion.7), channel_id=1, source_target_pairs={{0,4},{1,5},{2,6},{3,7},{4,0},{5,1},{6,2},{7,3},{8,12},{9,13},{10,... | collective-permute-start | bytes 663560 | tf_op jit(solution)/shard_map/ppermute | solution.py:182
  42.6 23.0 %collective-permute-start.6 = (bf16[864,128]{1,0:T(8,128)(2,1)S(1)}, bf16[864,128]{1,0:T(8,128)(2,1)S(1)}, u32[]{:S(2)}, u32[]{:S(2)}) collective-permute-start(bf16[864,128]{1,0:T(8,128)(2,1)S(1)} %add_convert_fusion.6), channel_id=1, source_target_pairs={{0,4},{1,5},{2,6},{3,7},{4,0},{5,1},{6,2},{7,3},{8,12},{9,13},{10,... | collective-permute-start | bytes 663560 | tf_op jit(solution)/shard_map/ppermute | solution.py:182
  52.1 14.0 %collective-permute-start.10 = (bf16[864,128]{1,0:T(8,128)(2,1)S(1)}, bf16[864,128]{1,0:T(8,128)(2,1)S(1)}, u32[]{:S(2)}, u32[]{:S(2)}) collective-permute-start(bf16[864,128]{1,0:T(8,128)(2,1)S(1)} %add_convert_fusion.5), channel_id=1, source_target_pairs={{0,4},{1,5},{2,6},{3,7},{4,0},{5,1},{6,2},{7,3},{8,12},{9,13},{10,... | collective-permute-start | bytes 663560 | tf_op jit(solution)/shard_map/ppermute | solution.py:182
  61.1 10.6 %collective-permute-start.14 = (bf16[864,128]{1,0:T(8,128)(2,1)S(1)}, bf16[864,128]{1,0:T(8,128)(2,1)S(1)}, u32[]{:S(2)}, u32[]{:S(2)}) collective-permute-start(bf16[864,128]{1,0:T(8,128)(2,1)S(1)} %add_convert_fusion.4), channel_id=1, source_target_pairs={{0,4},{1,5},{2,6},{3,7},{4,0},{5,1},{6,2},{7,3},{8,12},{9,13},{10,... | collective-permute-start | bytes 663560 | tf_op jit(solution)/shard_map/ppermute | solution.py:182
  63.0 10.1 %collective-permute-start.3 = (bf16[432,128]{1,0:T(8,128)(2,1)S(1)}, bf16[432,128]{1,0:T(8,128)(2,1)S(1)}, u32[]{:S(2)}, u32[]{:S(2)}) collective-permute-start(bf16[432,128]{1,0:T(8,128)(2,1)S(1)} %add_convert_fusion.11), channel_id=1, source_target_pairs={{0,8},{1,9},{2,10},{3,11},{4,12},{5,13},{6,14},{7,15},{8,0},{9,1},... | collective-permute-start | bytes 331784 | tf_op jit(solution)/shard_map/ppermute | solution.py:182
  65.7 15.6 %collective-permute-start.7 = (bf16[432,128]{1,0:T(8,128)(2,1)S(1)}, bf16[432,128]{1,0:T(8,128)(2,1)S(1)}, u32[]{:S(2)}, u32[]{:S(2)}) collective-permute-start(bf16[432,128]{1,0:T(8,128)(2,1)S(1)} %add_convert_fusion.10), channel_id=1, source_target_pairs={{0,8},{1,9},{2,10},{3,11},{4,12},{5,13},{6,14},{7,15},{8,0},{9,1},... | collective-permute-start | bytes 331784 | tf_op jit(solution)/shard_map/ppermute | solution.py:182
  66.2 17.5 %collective-permute-start.11 = (bf16[432,128]{1,0:T(8,128)(2,1)S(1)}, bf16[432,128]{1,0:T(8,128)(2,1)S(1)}, u32[]{:S(2)}, u32[]{:S(2)}) collective-permute-start(bf16[432,128]{1,0:T(8,128)(2,1)S(1)} %add_convert_fusion.9), channel_id=1, source_target_pairs={{0,8},{1,9},{2,10},{3,11},{4,12},{5,13},{6,14},{7,15},{8,0},{9,1},... | collective-permute-start | bytes 331784 | tf_op jit(solution)/shard_map/ppermute | solution.py:182
  71.7 13.6 %collective-permute-start.15 = (bf16[432,128]{1,0:T(8,128)(2,1)S(1)}, bf16[432,128]{1,0:T(8,128)(2,1)S(1)}, u32[]{:S(2)}, u32[]{:S(2)}) collective-permute-start(bf16[432,128]{1,0:T(8,128)(2,1)S(1)} %add_convert_fusion.8), channel_id=1, source_target_pairs={{0,8},{1,9},{2,10},{3,11},{4,12},{5,13},{6,14},{7,15},{8,0},{9,1},... | collective-permute-start | bytes 331784 | tf_op jit(solution)/shard_map/ppermute | solution.py:182

commit v2 on v0

v2 whole, which is shorter than its diff:
```python
import functools

import jax
import jax.numpy as jnp
from jax import lax
from jax.experimental import pallas as pl
from jax.experimental.pallas import tpu as pltpu
from jax.sharding import PartitionSpec as P

LANES = 128
ACC_LIMIT = 16 * 1024 * 1024
UNROLL = 8
PARTS = 4


def round_up(value, unit):
    return -(-value // unit) * unit


def block_products(cotangent, weights, source):
    width = weights.shape[1]
    lead = cotangent.shape[0] * cotangent.shape[1]
    tiled = cotangent.reshape(lead, cotangent.shape[2] // width, width)
    picked = jnp.take(tiled, source, axis=1)
    products = jnp.einsum("kbi,bij->bkj", picked, weights, preferred_element_type=jnp.float32)
    return products.astype(jnp.bfloat16)


def pack_slots(products, target, count_row):
    blocks = products.shape[0]
    devices = count_row.shape[0]
    per_device = 2 * blocks // devices
    inclusive = jnp.cumsum(count_row)
    exclusive = inclusive - count_row
    positions = jnp.arange(blocks, dtype=jnp.int32)
    owner = jnp.sum((positions[:, None] >= inclusive[None, :]).astype(jnp.int32), axis=1)
    chosen = owner[:, None] == jnp.arange(devices, dtype=jnp.int32)[None, :]
    first = jnp.sum(jnp.where(chosen, exclusive[None, :], 0), axis=1)
    slot_index = owner * per_device + positions - first
    buffer = (
        jnp.zeros((devices * per_device,) + products.shape[1:], jnp.bfloat16)
        .at[slot_index]
        .set(products)
    )
    labels = jnp.full((devices * per_device,), -1, jnp.int32).at[slot_index].set(target)
    return (buffer, labels)


def sum_slots(received, labels, tiles_out, like_shape):
    selector = (labels[None, :] == jnp.arange(tiles_out, dtype=jnp.int32)[:, None]).astype(
        jnp.bfloat16
    )
    summed = jnp.einsum("ts,skc->ktc", selector, received, preferred_element_type=jnp.float32)
    return summed.reshape(like_shape[0], like_shape[1], -1).astype(jnp.bfloat16)


def slot_remap(cotangent, weights, source, target, counts, like_shape):
    products = block_products(cotangent, weights, source)
    buffer, labels = pack_slots(products, target, counts[0])
    arrived = lax.all_to_all(buffer, "curve", split_axis=0, concat_axis=0, tiled=True)
    arrived_labels = lax.all_to_all(labels, "curve", split_axis=0, concat_axis=0, tiled=True)
    return sum_slots(arrived, arrived_labels, like_shape[2] // weights.shape[1], like_shape)


def slots_of(stages):
    return [[sum(((m >> i) & 1) << bit for i, bit in enumerate(stage)) for m in range(1 << len(stage))]
            for stage in stages]


def owners_in_order(stages):
    masks = [0]
    for stage in slots_of(stages):
        masks = [left + right for left in masks for right in stage]
    return masks


def product_kernel(
    bits, channels, pitch, chunks, first,
    source_hbm, target_hbm, counts_hbm, x_hbm, w_hbm, *rest,
):
    number = len(chunks)
    sends, keeps = rest[:number], rest[number:2 * number]
    acc, xs, x_in, w, source, target, counts, list_block, list_row, sems = rest[2 * number:]
    devices = 1 << bits
    blocks = w.shape[0]
    per_part = blocks // PARTS
    me = lax.axis_index("curve")

    scalars = [
        pltpu.make_async_copy(source_hbm, source, sems.at[0]),
        pltpu.make_async_copy(target_hbm, target, sems.at[1]),
        pltpu.make_async_copy(counts_hbm, counts, sems.at[2]),
    ]
    x_copy = pltpu.make_async_copy(x_hbm, x_in, sems.at[3])
    w_copies = [
        pltpu.make_async_copy(
            w_hbm.at[pl.ds(part * per_part, per_part)], w.at[pl.ds(part * per_part, per_part)],
            sems.at[4 + part],
        )
        for part in range(PARTS)
    ]
    for copy in scalars + [x_copy] + w_copies:
        copy.start()

    trash = acc.shape[0] - pitch

    @pl.loop(0, acc.shape[0] // pitch)
    def clear(index):
        acc[pl.ds(pl.multiple_of(index * pitch, pitch), pitch), :] = jnp.zeros((pitch, LANES), jnp.float32)

    for tile in range(xs.shape[0]):
        xs[tile] = jnp.zeros(xs.shape[1:], xs.dtype)
    for copy in scalars:
        copy.wait()

    bases, base = [], 0
    for low, high, stages in chunks:
        bases.append(base)
        base += devices // 2 * (high - low)
    length = jnp.int32(0)
    begin = jnp.int32(0)
    marks = [jnp.int32(0)] * (PARTS - 1)
    for owner in range(devices):
        differ = jnp.bitwise_xor(me, owner)
        count = counts[0, owner]
        starts, takes = [], []
        for base, (low, high, stages) in zip(bases, chunks):
            picked = jnp.bitwise_and(jnp.right_shift(differ, stages[1][0]), 1)
            takes.append(picked if first else 1 - picked)
            place = jnp.bitwise_and(jnp.right_shift(differ, stages[0][0]), 1)
            for stage in stages[2:]:
                for bit in reversed(stage):
                    place = place * 2 + jnp.bitwise_and(jnp.right_shift(differ, bit), 1)
            starts.append(base + place * (high - low) - low)

        def note(index, length, begin=begin, starts=starts, takes=takes):
            block = begin + index
            tile = target[block]
            place, take = starts[0], takes[0]
            for (low, high, stages), other, other_take in zip(chunks[1:], starts[1:], takes[1:]):
                place = jnp.where(tile >= low, other, place)
                take = jnp.where(tile >= low, other_take, take)
            list_block[length] = block
            list_row[length] = (place + tile) * pitch
            return length + take

        any_take = functools.reduce(jnp.maximum, takes)
        length = lax.fori_loop(0, count * any_take, note, length)
        begin = begin + count
        marks = [jnp.where(begin <= per_part * (part + 1), length, mark) for part, mark in enumerate(marks)]
    for index in range(UNROLL):
        list_block[length + index] = 0
        list_row[length + index] = trash

    x_copy.wait()
    for tile in range(xs.shape[0]):
        xs[tile, :channels, :] = x_in[0, :, tile * LANES:(tile + 1) * LANES]

    def some(step, carry):
        rows, found = [], []
        for index in range(UNROLL):
            at = step * UNROLL + index
            rows.append(pl.multiple_of(list_row[at], 8))
            found.append(list_block[at])
        for row, block in zip(rows, found):
            product = jnp.dot(xs[source[block], :pitch, :], w[block], preferred_element_type=jnp.float32)
            acc[pl.ds(row, pitch), :] += product
        return carry

    done = jnp.int32(0)
    for part in range(PARTS):
        w_copies[part].wait()
        upto = marks[part] // UNROLL if part + 1 < PARTS else (length + UNROLL - 1) // UNROLL
        lax.fori_loop(done, upto, some, jnp.int32(0))
        done = upto

    for base, (low, high, stages), send, keep in zip(bases, chunks, sends, keeps):
        unit = (high - low) * pitch
        places = devices // 4

        @pl.loop(0, places)
        def finish(index):
            at = pl.multiple_of(index * unit, 8)
            own = pl.multiple_of(base * pitch + index * unit, 8)
            other = pl.multiple_of((base + places * (high - low)) * pitch + index * unit, 8)
            send[pl.ds(at, unit), :] = acc[pl.ds(other, unit), :].astype(jnp.bfloat16)
            keep[pl.ds(at, unit), :] = acc[pl.ds(own, unit), :]


def products(remap, chunks, bits, first):
    cotangent, weights, source, target, counts = remap[:5]
    devices = 1 << bits
    channels = cotangent.shape[1]
    pitch = round_up(channels, 8)
    tiles_in = cotangent.shape[2] // LANES
    blocks = weights.shape[0]
    rows = [devices // 4 * (high - low) * pitch for low, high, stages in chunks]
    whole = pl.BlockSpec(memory_space=pltpu.VMEM)
    sums = sum(rows) * 2 + pitch
    return pl.pallas_call(
        functools.partial(product_kernel, bits, channels, pitch, chunks, first),
        out_shape=[jax.ShapeDtypeStruct((size, LANES), jnp.bfloat16) for size in rows]
        + [jax.ShapeDtypeStruct((size, LANES), jnp.float32) for size in rows],
        in_specs=[pl.BlockSpec(memory_space=pltpu.HBM)] * 5,
        out_specs=[whole] * (2 * len(rows)),
        scratch_shapes=[
            pltpu.VMEM((sums, LANES), jnp.float32),
            pltpu.VMEM((tiles_in, round_up(pitch, 16), LANES), jnp.bfloat16),
            pltpu.VMEM(cotangent.shape, jnp.bfloat16),
            pltpu.VMEM(weights.shape, jnp.bfloat16),
            pltpu.SMEM(source.shape, jnp.int32),
            pltpu.SMEM(target.shape, jnp.int32),
            pltpu.SMEM(counts.shape, jnp.int32),
            pltpu.SMEM((blocks + UNROLL,), jnp.int32),
            pltpu.SMEM((blocks + UNROLL,), jnp.int32),
            pltpu.SemaphoreType.DMA((4 + PARTS,)),
        ],
        compiler_params=pltpu.CompilerParams(vmem_limit_bytes=28 * 1024 * 1024),
        cost_estimate=pl.CostEstimate(
            flops=blocks * channels * LANES * LANES,
            bytes_accessed=2 * weights.size + 6 * sum(rows) * LANES,
            transcendentals=0,
        ),
    )(*[pltpu.with_memory_space_constraint(value, pltpu.HBM) for value in (source, target, counts, cotangent, weights)])


def exchange(value, mask, devices):
    return lax.ppermute(value, "curve", [(at, at ^ mask) for at in range(devices)])


def added(terms, low, high):
    return sum(term[low:high].astype(jnp.float32) for term in terms)


class Chain:
    def __init__(self, remap, chunk, bits):
        self.remap, self.chunk, self.devices = remap, chunk, 1 << bits
        self.slots = slots_of(chunk[2])
        self.stage = 2

    def take_first(self, send, keep):
        self.first_keep = keep
        self.first_got = exchange(send, self.slots[0][1], self.devices)

    def sum_first(self):
        total = added([self.first_keep, self.first_got], 0, self.first_keep.shape[0])
        self.total = total.astype(jnp.bfloat16)

    def send_second(self):
        self.got = [exchange(self.total, self.slots[1][1], self.devices)]

    def take_rest(self, send, keep):
        self.terms = [keep, exchange(send, self.slots[0][1], self.devices)]
        self.length = keep.shape[0]

    def send_next(self):
        self.terms = self.terms + self.got
        masks = self.slots[self.stage]
        self.length //= len(masks)
        self.got = []
        for place, mask in enumerate(masks[1:], 1):
            total = added(self.terms, place * self.length, (place + 1) * self.length)
            self.got.append(exchange(total.astype(jnp.bfloat16), mask, self.devices))
        self.stage += 1

    def finish(self):
        self.terms = self.terms + self.got
        return self.terms


def final_kernel(channels, pitch, parts, *refs):
    out = refs[-1]
    at = 0
    for low, high, count in parts:
        terms = refs[at:at + count]
        at += count
        for tile in range(high - low):
            total = sum(
                term[tile * pitch:(tile + 1) * pitch, :].astype(jnp.float32) for term in terms
            )
            lane = (low + tile) * LANES
            out[0, :, lane:lane + LANES] = total[:channels].astype(jnp.bfloat16)


def final_sum(chains, like_shape, pitch):
    parts = [(chain.chunk[0], chain.chunk[1], len(chain.terms)) for chain in chains]
    flat, specs = [], []
    for chain in chains:
        rows = (chain.chunk[1] - chain.chunk[0]) * pitch
        for term in chain.terms:
            flat.append(term)
            specs.append(pl.BlockSpec((rows, LANES), lambda step: (0, 0)))
    return pl.pallas_call(
        functools.partial(final_kernel, like_shape[1], pitch, parts),
        out_shape=jax.ShapeDtypeStruct(like_shape, jnp.bfloat16),
        grid=(1,),
        in_specs=specs,
        out_specs=pl.BlockSpec(like_shape, lambda step: (0, 0, 0)),
        compiler_params=pltpu.CompilerParams(vmem_limit_bytes=28 * 1024 * 1024),
    )(*flat)


def plan(tiles, bits):
    stages = tuple((bit,) for bit in range(bits))
    half = tiles // 2
    return [
        [(0, half, stages), (half, tiles, stages)],
        [(0, half, stages), (half, tiles, stages)],
    ]


def bit_remaps(remaps, bits):
    chunks = [plan(remap[-1][2] // LANES, bits)[index] for index, remap in enumerate(remaps)]
    chains = [[Chain(remap, chunk, bits) for chunk in own] for remap, own in zip(remaps, chunks)]
    for index, remap in enumerate(remaps):
        made = products(remap, chunks[index], bits, True)
        number = len(chunks[index])
        for chain, send, keep in zip(chains[index], made[:number], made[number:]):
            chain.take_first(send, keep)
            chain.sum_first()
    for index, remap in enumerate(remaps):
        sent = [chain.total for chain in chains[index]]
        tied = lax.optimization_barrier((remap[0], *sent))
        for chain, total in zip(chains[index], tied[1:]):
            chain.total = total
            chain.send_second()
        made = products((tied[0],) + remap[1:], chunks[index], bits, False)
        number = len(chunks[index])
        for chain, send, keep in zip(chains[index], made[:number], made[number:]):
            chain.take_rest(send, keep)
    line = [chain for own in chains for chain in own]
    for step in range(len(line) + bits - 3):
        ready = [chain for place, chain in enumerate(line)
                 if chain.stage == 2 + step - place and chain.stage < len(chain.slots)]
        tied = lax.optimization_barrier([chain.got for chain in ready])
        for chain, got in zip(ready, tied):
            chain.got = got
        for chain in reversed(ready):
            chain.send_next()
    results = []
    for index, remap in enumerate(remaps):
        for chain in chains[index]:
            chain.finish()
        results.append(final_sum(chains[index], remap[-1], round_up(remap[-1][1], 8)))
    return results


def on_device(devices, *args):
    latlon, healpix = args[:2]
    remaps = [
        (latlon, args[2], args[3], args[4], args[5], healpix.shape),
        (healpix, args[6], args[7], args[8], args[9], latlon.shape),
    ]
    bits = devices.bit_length() - 1
    tiles = max(latlon.shape[2], healpix.shape[2]) // LANES
    size = devices * tiles * round_up(latlon.shape[1], 8) * LANES * 4
    if devices == 1 << bits and bits > 2 and size <= ACC_LIMIT:
        return tuple(bit_remaps(remaps, bits))
    return tuple(slot_remap(*remap) for remap in remaps)


def solution(mesh):
    in_specs = (
        P("groups", None, "curve"),
        P("groups", None, "curve"),
        P("curve", None, None),
        P("curve"),
        P("curve"),
        P("curve", None),
        P("curve", None, None),
        P("curve"),
        P("curve"),
        P("curve", None),
    )
    out_specs = (P("groups", None, "curve"), P("groups", None, "curve"))
    return jax.shard_map(
        functools.partial(on_device, mesh.shape["curve"]),
        mesh=mesh, in_specs=in_specs, out_specs=out_specs, check_vma=False,
    )
```

time: 301 us -> 73.2 us (0.24)
  the two profiles are of different devices: /device:TPU:13 before, /device:TPU:0 now
where the time goes in v2:
time: 73.2 us; the launch traced here: 73 us
  waiting for transfers between devices  31.3 us (43%)
  starting transfers between devices  21.9 us (30%)
  Pallas kernels  18.2 us (25%)
  other arithmetic  0.94 us (1%)
  between operations  0.75 us (1%)
    ppermute x20, waiting for transfers between devices, exchange(): lax.ppermute(value, 'curve', [(at, at ^ mask) for at in range(devices)])  31.3 us
    ppermute x20, starting transfers between devices, exchange(): lax.ppermute(value, 'curve', [(at, at ^ mask) for at in range(devices)])  21.9 us
    pallas_call x4, Pallas kernels, products(): pl.pallas_call(functools.partial(product_kernel, bits, channels, pitch, c...  16.5 us
    pallas_call x2, Pallas kernels, final_sum(): pl.pallas_call(functools.partial(final_kernel, like_shape[1], pitch, part...  1.67 us
  transfers between devices with their start and end apart: 20, of which 7 were waited for; matrix products, arithmetic and copies ran while one was open for 1% of the time, Pallas kernels for 18%

profile of v2, /device:TPU:0, one launch (start us, length us, event | category | flops | bytes accessed | tf_op | source)
XLA Modules:
  0.0 73.0 jit_solution(11942539513907375975)
XLA Ops:
  0.6 4.4 %shard_map.113 = (bf16[1728,128]{1,0:T(8,128)(2,1)S(1)}, bf16[1728,128]{1,0:T(8,128)(2,1)S(1)}, f32[1728,128]{1,0:T(8,128)S(1)}, f32[1728,128]{1,0:T(8,128)S(1)}) custom-call(s32[144]{0:T(256)} %source_hbm.5, s32[144]{0:T(256)} %target_hbm.5, s32[1,16]{1,0:T(1,128)} %counts_hbm.5, bf16[1,69,1536]{2,1,0:T(8,128)(2,1)} %x_hbm.3, bf16[144,128,128]{2,1,0:T(8,128)(2,1)} %w_hbm.5), custom_call_target="tpu_custom_call" | custom-call | flops 162791424 | bytes 7372800 | tf_op jit(solution)/shard_map/pallas_call | solution.py:200
  5.0 0.1 collective-permute-start
  5.1 0.5 collective-permute-start.1
  5.6 4.0 %shard_map.115 = (bf16[1728,128]{1,0:T(8,128)(2,1)S(1)}, bf16[1728,128]{1,0:T(8,128)(2,1)S(1)}, f32[1728,128]{1,0:T(8,128)S(1)}, f32[1728,128]{1,0:T(8,128)S(1)}) custom-call(s32[144]{0:T(256)} %source_hbm.7, s32[144]{0:T(256)} %target_hbm.7, s32[1,16]{1,0:T(1,128)} %counts_hbm.7, bf16[1,69,1536]{2,1,0:T(8,128)(2,1)} %x_hbm.5, bf16[144,128,128]{2,1,0:T(8,128)(2,1)} %w_hbm.7), custom_call_target="tpu_custom_call" | custom-call | flops 162791424 | bytes 7372800 | tf_op jit(solution)/shard_map/pallas_call | solution.py:200
  9.6 0.7 collective-permute-start.9
  10.3 0.1 collective-permute-start.10
  10.4 0.1 add_convert_fusion.3
  10.5 0.0 collective-permute-done.1
  10.5 0.1 add_convert_fusion.2
  10.6 2.8 %collective-permute-start.3 = (bf16[1728,128]{1,0:T(8,128)(2,1)S(1)}, bf16[1728,128]{1,0:T(8,128)(2,1)S(1)}, u32[]{:S(2)}, u32[]{:S(2)}) collective-permute-start(bf16[1728,128]{1,0:T(8,128)(2,1)S(1)} %add_convert_fusion.3), channel_id=1, source_target_pairs={{0,2},{1,3},{2,0},{3,1},{4,6},{5,7},{6,4},{7,5},{8,10},{9,11},{10,... | collective-permute-start | bytes 1327112 | tf_op jit(solution)/shard_map/ppermute | solution.py:228
  13.4 0.1 collective-permute-start.5
  13.5 3.7 %shard_map.114 = (bf16[1728,128]{1,0:T(8,128)(2,1)S(1)}, bf16[1728,128]{1,0:T(8,128)(2,1)S(1)}, f32[1728,128]{1,0:T(8,128)S(1)}, f32[1728,128]{1,0:T(8,128)S(1)}) custom-call(s32[144]{0:T(256)} %source_hbm.5, s32[144]{0:T(256)} %target_hbm.5, s32[1,16]{1,0:T(1,128)} %counts_hbm.5, bf16[1,69,1536]{2,1,0:T(8,128)(2,1)} %x_hbm.3, bf16[144,128,128]{2,1,0:T(8,128)(2,1)} %w_hbm.5), custom_call_target="tpu_custom_call" | custom-call | flops 162791424 | bytes 7372800 | tf_op jit(solution)/shard_map/pallas_call | solution.py:200
  17.2 1.4 %collective-permute-start.2 = (bf16[1728,128]{1,0:T(8,128)(2,1)S(1)}, bf16[1728,128]{1,0:T(8,128)(2,1)S(1)}, u32[]{:S(2)}, u32[]{:S(2)}) collective-permute-start(bf16[1728,128]{1,0:T(8,128)(2,1)S(1)} %get-tuple-element.36), channel_id=1, source_target_pairs={{0,1},{1,0},{2,3},{3,2},{4,5},{5,4},{6,7},{7,6},{8,9},{9,8},{10,11... | collective-permute-start | bytes 1327112 | tf_op jit(solution)/shard_map/ppermute | solution.py:228
  18.6 0.0 collective-permute-done.9
  18.7 0.1 collective-permute-start.7
  18.7 0.1 add_convert_fusion.1
  18.8 5.6 %collective-permute-done.3.refs_2_ = bf16[1728,128]{1,0:T(8,128)(2,1)S(1)} collective-permute-done((bf16[1728,128]{1,0:T(8,128)(2,1)S(1)}, bf16[1728,128]{1,0:T(8,128)(2,1)S(1)}, u32[]{:S(2)}, u32[]{:S(2)}) %collective-permute-start.3) | collective-permute-done | bytes 442400 | tf_op jit(solution)/shard_map/ppermute | solution.py:228
  24.4 0.0 collective-permute-done.2.refs_1_
  24.4 0.1 add_convert_fusion.7
  24.5 2.0 %collective-permute-start.4 = (bf16[864,128]{1,0:T(8,128)(2,1)S(1)}, bf16[864,128]{1,0:T(8,128)(2,1)S(1)}, u32[]{:S(2)}, u32[]{:S(2)}) collective-permute-start(bf16[864,128]{1,0:T(8,128)(2,1)S(1)} %add_convert_fusion.7), channel_id=1, source_target_pairs={{0,4},{1,5},{2,6},{3,7},{4,0},{5,1},{6,2},{7,3},{8,12},{9,13},{10,... | collective-permute-start | bytes 663560 | tf_op jit(solution)/shard_map/ppermute | solution.py:228
  26.5 0.1 add_convert_fusion
  26.6 1.4 %collective-permute-start.11 = (bf16[1728,128]{1,0:T(8,128)(2,1)S(1)}, bf16[1728,128]{1,0:T(8,128)(2,1)S(1)}, u32[]{:S(2)}, u32[]{:S(2)}) collective-permute-start(bf16[1728,128]{1,0:T(8,128)(2,1)S(1)} %add_convert_fusion.1), channel_id=1, source_target_pairs={{0,2},{1,3},{2,0},{3,1},{4,6},{5,7},{6,4},{7,5},{8,10},{9,11},{10,... | collective-permute-start | bytes 1327112 | tf_op jit(solution)/shard_map/ppermute | solution.py:228
  28.0 0.7 collective-permute-start.15
  28.7 4.4 %shard_map.117 = (bf16[1728,128]{1,0:T(8,128)(2,1)S(1)}, bf16[1728,128]{1,0:T(8,128)(2,1)S(1)}, f32[1728,128]{1,0:T(8,128)S(1)}, f32[1728,128]{1,0:T(8,128)S(1)}) custom-call(s32[144]{0:T(256)} %source_hbm.7, s32[144]{0:T(256)} %target_hbm.7, s32[1,16]{1,0:T(1,128)} %counts_hbm.7, bf16[1,69,1536]{2,1,0:T(8,128)(2,1)} %x_hbm.5, bf16[144,128,128]{2,1,0:T(8,128)(2,1)} %w_hbm.7), custom_call_target="tpu_custom_call" | custom-call | flops 162791424 | bytes 7372800 | tf_op jit(solution)/shard_map/pallas_call | solution.py:200
  33.0 0.8 %collective-permute-done.5.refs_7_ = bf16[1728,128]{1,0:T(8,128)(2,1)S(1)} collective-permute-done((bf16[1728,128]{1,0:T(8,128)(2,1)S(1)}, bf16[1728,128]{1,0:T(8,128)(2,1)S(1)}, u32[]{:S(2)}, u32[]{:S(2)}) %collective-permute-start.5) | collective-permute-done | bytes 442400 | tf_op jit(solution)/shard_map/ppermute | solution.py:228
  33.9 0.0 collective-permute-start.13
  33.9 0.5 collective-permute-start.17
  34.4 0.1 add_convert_fusion.6
  34.5 2.0 %collective-permute-start.8 = (bf16[864,128]{1,0:T(8,128)(2,1)S(1)}, bf16[864,128]{1,0:T(8,128)(2,1)S(1)}, u32[]{:S(2)}, u32[]{:S(2)}) collective-permute-start(bf16[864,128]{1,0:T(8,128)(2,1)S(1)} %add_convert_fusion.6), channel_id=1, source_target_pairs={{0,4},{1,5},{2,6},{3,7},{4,0},{5,1},{6,2},{7,3},{8,12},{9,13},{10,... | collective-permute-start | bytes 663560 | tf_op jit(solution)/shard_map/ppermute | solution.py:228
  36.5 0.1 add_convert_fusion.11
  36.5 6.8 %collective-permute-done.11.refs_2_ = bf16[1728,128]{1,0:T(8,128)(2,1)S(1)} collective-permute-done((bf16[1728,128]{1,0:T(8,128)(2,1)S(1)}, bf16[1728,128]{1,0:T(8,128)(2,1)S(1)}, u32[]{:S(2)}, u32[]{:S(2)}) %collective-permute-start.11) | collective-permute-done | bytes 442400 | tf_op jit(solution)/shard_map/ppermute | solution.py:228
  43.4 3.5 %collective-permute-start.6 = (bf16[432,128]{1,0:T(8,128)(2,1)S(1)}, bf16[432,128]{1,0:T(8,128)(2,1)S(1)}, u32[]{:S(2)}, u32[]{:S(2)}) collective-permute-start(bf16[432,128]{1,0:T(8,128)(2,1)S(1)} %add_convert_fusion.11), channel_id=1, source_target_pairs={{0,8},{1,9},{2,10},{3,11},{4,12},{5,13},{6,14},{7,15},{8,0},{9,1},... | collective-permute-start | bytes 331784 | tf_op jit(solution)/shard_map/ppermute | solution.py:228
  46.8 0.1 add_convert_fusion.5
  46.9 1.4 %collective-permute-start.14 = (bf16[864,128]{1,0:T(8,128)(2,1)S(1)}, bf16[864,128]{1,0:T(8,128)(2,1)S(1)}, u32[]{:S(2)}, u32[]{:S(2)}) collective-permute-start(bf16[864,128]{1,0:T(8,128)(2,1)S(1)} %add_convert_fusion.5), channel_id=1, source_target_pairs={{0,4},{1,5},{2,6},{3,7},{4,0},{5,1},{6,2},{7,3},{8,12},{9,13},{10,... | collective-permute-start | bytes 663560 | tf_op jit(solution)/shard_map/ppermute | solution.py:228
  48.3 0.1 add_convert_fusion.10
  48.4 0.1 collective-permute-start.12
  48.5 4.1 %collective-permute-done.15.refs_7_ = bf16[1728,128]{1,0:T(8,128)(2,1)S(1)} collective-permute-done((bf16[1728,128]{1,0:T(8,128)(2,1)S(1)}, bf16[1728,128]{1,0:T(8,128)(2,1)S(1)}, u32[]{:S(2)}, u32[]{:S(2)}) %collective-permute-start.15) | collective-permute-done | bytes 442400 | tf_op jit(solution)/shard_map/ppermute | solution.py:228
  52.6 4.2 %collective-permute-done.14.refs_3_ = bf16[864,128]{1,0:T(8,128)(2,1)S(1)} collective-permute-done((bf16[864,128]{1,0:T(8,128)(2,1)S(1)}, bf16[864,128]{1,0:T(8,128)(2,1)S(1)}, u32[]{:S(2)}, u32[]{:S(2)}) %collective-permute-start.14) | collective-permute-done | bytes 221216 | tf_op jit(solution)/shard_map/ppermute | solution.py:228
  56.8 0.1 add_convert_fusion.4
  56.8 0.6 collective-permute-start.18
  57.5 0.1 add_convert_fusion.9
  57.5 2.7 %collective-permute-start.16 = (bf16[432,128]{1,0:T(8,128)(2,1)S(1)}, bf16[432,128]{1,0:T(8,128)(2,1)S(1)}, u32[]{:S(2)}, u32[]{:S(2)}) collective-permute-start(bf16[432,128]{1,0:T(8,128)(2,1)S(1)} %add_convert_fusion.9), channel_id=1, source_target_pairs={{0,8},{1,9},{2,10},{3,11},{4,12},{5,13},{6,14},{7,15},{8,0},{9,1},... | collective-permute-start | bytes 331784 | tf_op jit(solution)/shard_map/ppermute | solution.py:228
  60.3 5.0 %collective-permute-done.18.refs_8_ = bf16[864,128]{1,0:T(8,128)(2,1)S(1)} collective-permute-done((bf16[864,128]{1,0:T(8,128)(2,1)S(1)}, bf16[864,128]{1,0:T(8,128)(2,1)S(1)}, u32[]{:S(2)}, u32[]{:S(2)}) %collective-permute-start.18) | collective-permute-done | bytes 221216 | tf_op jit(solution)/shard_map/ppermute | solution.py:228
  65.2 0.1 add_convert_fusion.8
  65.3 1.3 %collective-permute-start.19 = (bf16[432,128]{1,0:T(8,128)(2,1)S(1)}, bf16[432,128]{1,0:T(8,128)(2,1)S(1)}, u32[]{:S(2)}, u32[]{:S(2)}) collective-permute-start(bf16[432,128]{1,0:T(8,128)(2,1)S(1)} %add_convert_fusion.8), channel_id=1, source_target_pairs={{0,8},{1,9},{2,10},{3,11},{4,12},{5,13},{6,14},{7,15},{8,0},{9,1},... | collective-permute-start | bytes 331784 | tf_op jit(solution)/shard_map/ppermute | solution.py:228
  66.6 0.8 %shard_map.116 = bf16[1,69,1536]{2,1,0:T(8,128)(2,1)} custom-call(f32[1728,128]{1,0:T(8,128)S(1)} %get-tuple-element.35.refs_0_, bf16[1728,128]{1,0:T(8,128)(2,1)S(1)} %collective-permute-done.2.refs_1_, bf16[1728,128]{1,0:T(8,128)(2,1)S(1)} %collective-permute-done.3.refs_2_, bf16[864,128]{1,0:T(8,128)(2,1)S(1)} %collective-permute-done.4.refs_3_, ...), custom_call_target="tpu_custom_call" | custom-call | tf_op jit(solution)/shard_map/pallas_call | solution.py:293
  67.4 4.8 %collective-permute-done.19.refs_9_ = bf16[432,128]{1,0:T(8,128)(2,1)S(1)} collective-permute-done((bf16[432,128]{1,0:T(8,128)(2,1)S(1)}, bf16[432,128]{1,0:T(8,128)(2,1)S(1)}, u32[]{:S(2)}, u32[]{:S(2)}) %collective-permute-start.19) | collective-permute-done | bytes 110624 | tf_op jit(solution)/shard_map/ppermute | solution.py:228
  72.2 0.8 %shard_map.118 = bf16[1,69,1536]{2,1,0:T(8,128)(2,1)} custom-call(f32[1728,128]{1,0:T(8,128)S(1)} %get-tuple-element.50.refs_0_, bf16[1728,128]{1,0:T(8,128)(2,1)S(1)} %collective-permute-done.13.refs_1_, bf16[1728,128]{1,0:T(8,128)(2,1)S(1)} %collective-permute-done.11.refs_2_, bf16[864,128]{1,0:T(8,128)(2,1)S(1)} %collective-permute-done.14.refs_3_, ...), custom_call_target="tpu_custom_call" | custom-call | tf_op jit(solution)/shard_map/pallas_call | solution.py:293
  (10 shorter events, 0.0 us)
Async XLA Ops:
  5.0 5.3 %collective-permute-start = (bf16[1728,128]{1,0:T(8,128)(2,1)S(1)}, bf16[1728,128]{1,0:T(8,128)(2,1)S(1)}, u32[]{:S(2)}, u32[]{:S(2)}) collective-permute-start(bf16[1728,128]{1,0:T(8,128)(2,1)S(1)} %get-tuple-element.31), channel_id=1, source_target_pairs={{0,1},{1,0},{2,3},{3,2},{4,5},{5,4},{6,7},{7,6},{8,9},{9,8},{10,11... | collective-permute-start | bytes 1327112 | tf_op jit(solution)/shard_map/ppermute | solution.py:228
  5.1 5.4 %collective-permute-start.1 = (bf16[1728,128]{1,0:T(8,128)(2,1)S(1)}, bf16[1728,128]{1,0:T(8,128)(2,1)S(1)}, u32[]{:S(2)}, u32[]{:S(2)}) collective-permute-start(bf16[1728,128]{1,0:T(8,128)(2,1)S(1)} %get-tuple-element.33), channel_id=1, source_target_pairs={{0,1},{1,0},{2,3},{3,2},{4,5},{5,4},{6,7},{7,6},{8,9},{9,8},{10,11... | collective-permute-start | bytes 1327112 | tf_op jit(solution)/shard_map/ppermute | solution.py:228
  9.6 9.1 %collective-permute-start.9 = (bf16[1728,128]{1,0:T(8,128)(2,1)S(1)}, bf16[1728,128]{1,0:T(8,128)(2,1)S(1)}, u32[]{:S(2)}, u32[]{:S(2)}) collective-permute-start(bf16[1728,128]{1,0:T(8,128)(2,1)S(1)} %get-tuple-element.44), channel_id=1, source_target_pairs={{0,1},{1,0},{2,3},{3,2},{4,5},{5,4},{6,7},{7,6},{8,9},{9,8},{10,11... | collective-permute-start | bytes 1327112 | tf_op jit(solution)/shard_map/ppermute | solution.py:228
  10.3 16.2 %collective-permute-start.10 = (bf16[1728,128]{1,0:T(8,128)(2,1)S(1)}, bf16[1728,128]{1,0:T(8,128)(2,1)S(1)}, u32[]{:S(2)}, u32[]{:S(2)}) collective-permute-start(bf16[1728,128]{1,0:T(8,128)(2,1)S(1)} %get-tuple-element.46), channel_id=1, source_target_pairs={{0,1},{1,0},{2,3},{3,2},{4,5},{5,4},{6,7},{7,6},{8,9},{9,8},{10,11... | collective-permute-start | bytes 1327112 | tf_op jit(solution)/shard_map/ppermute | solution.py:228
  10.6 13.8 %collective-permute-start.3 = (bf16[1728,128]{1,0:T(8,128)(2,1)S(1)}, bf16[1728,128]{1,0:T(8,128)(2,1)S(1)}, u32[]{:S(2)}, u32[]{:S(2)}) collective-permute-start(bf16[1728,128]{1,0:T(8,128)(2,1)S(1)} %add_convert_fusion.3), channel_id=1, source_target_pairs={{0,2},{1,3},{2,0},{3,1},{4,6},{5,7},{6,4},{7,5},{8,10},{9,11},{10,... | collective-permute-start | bytes 1327112 | tf_op jit(solution)/shard_map/ppermute | solution.py:228
  13.4 20.5 %collective-permute-start.5 = (bf16[1728,128]{1,0:T(8,128)(2,1)S(1)}, bf16[1728,128]{1,0:T(8,128)(2,1)S(1)}, u32[]{:S(2)}, u32[]{:S(2)}) collective-permute-start(bf16[1728,128]{1,0:T(8,128)(2,1)S(1)} %add_convert_fusion.2), channel_id=1, source_target_pairs={{0,2},{1,3},{2,0},{3,1},{4,6},{5,7},{6,4},{7,5},{8,10},{9,11},{10,... | collective-permute-start | bytes 1327112 | tf_op jit(solution)/shard_map/ppermute | solution.py:228
  17.2 7.2 %collective-permute-start.2 = (bf16[1728,128]{1,0:T(8,128)(2,1)S(1)}, bf16[1728,128]{1,0:T(8,128)(2,1)S(1)}, u32[]{:S(2)}, u32[]{:S(2)}) collective-permute-start(bf16[1728,128]{1,0:T(8,128)(2,1)S(1)} %get-tuple-element.36), channel_id=1, source_target_pairs={{0,1},{1,0},{2,3},{3,2},{4,5},{5,4},{6,7},{7,6},{8,9},{9,8},{10,11... | collective-permute-start | bytes 1327112 | tf_op jit(solution)/shard_map/ppermute | solution.py:228
  18.7 15.7 %collective-permute-start.7 = (bf16[1728,128]{1,0:T(8,128)(2,1)S(1)}, bf16[1728,128]{1,0:T(8,128)(2,1)S(1)}, u32[]{:S(2)}, u32[]{:S(2)}) collective-permute-start(bf16[1728,128]{1,0:T(8,128)(2,1)S(1)} %get-tuple-element.41), channel_id=1, source_target_pairs={{0,1},{1,0},{2,3},{3,2},{4,5},{5,4},{6,7},{7,6},{8,9},{9,8},{10,11... | collective-permute-start | bytes 1327112 | tf_op jit(solution)/shard_map/ppermute | solution.py:228
  24.5 9.4 %collective-permute-start.4 = (bf16[864,128]{1,0:T(8,128)(2,1)S(1)}, bf16[864,128]{1,0:T(8,128)(2,1)S(1)}, u32[]{:S(2)}, u32[]{:S(2)}) collective-permute-start(bf16[864,128]{1,0:T(8,128)(2,1)S(1)} %add_convert_fusion.7), channel_id=1, source_target_pairs={{0,4},{1,5},{2,6},{3,7},{4,0},{5,1},{6,2},{7,3},{8,12},{9,13},{10,... | collective-permute-start | bytes 663560 | tf_op jit(solution)/shard_map/ppermute | solution.py:228
  26.6 16.8 %collective-permute-start.11 = (bf16[1728,128]{1,0:T(8,128)(2,1)S(1)}, bf16[1728,128]{1,0:T(8,128)(2,1)S(1)}, u32[]{:S(2)}, u32[]{:S(2)}) collective-permute-start(bf16[1728,128]{1,0:T(8,128)(2,1)S(1)} %add_convert_fusion.1), channel_id=1, source_target_pairs={{0,2},{1,3},{2,0},{3,1},{4,6},{5,7},{6,4},{7,5},{8,10},{9,11},{10,... | collective-permute-start | bytes 1327112 | tf_op jit(solution)/shard_map/ppermute | solution.py:228
  28.0 24.6 %collective-permute-start.15 = (bf16[1728,128]{1,0:T(8,128)(2,1)S(1)}, bf16[1728,128]{1,0:T(8,128)(2,1)S(1)}, u32[]{:S(2)}, u32[]{:S(2)}) collective-permute-start(bf16[1728,128]{1,0:T(8,128)(2,1)S(1)} %add_convert_fusion), channel_id=1, source_target_pairs={{0,2},{1,3},{2,0},{3,1},{4,6},{5,7},{6,4},{7,5},{8,10},{9,11},{10,... | collective-permute-start | bytes 1327112 | tf_op jit(solution)/shard_map/ppermute | solution.py:228
  33.9 13.0 %collective-permute-start.13 = (bf16[1728,128]{1,0:T(8,128)(2,1)S(1)}, bf16[1728,128]{1,0:T(8,128)(2,1)S(1)}, u32[]{:S(2)}, u32[]{:S(2)}) collective-permute-start(bf16[1728,128]{1,0:T(8,128)(2,1)S(1)} %get-tuple-element.51), channel_id=1, source_target_pairs={{0,1},{1,0},{2,3},{3,2},{4,5},{5,4},{6,7},{7,6},{8,9},{9,8},{10,11... | collective-permute-start | bytes 1327112 | tf_op jit(solution)/shard_map/ppermute | solution.py:228
  33.9 22.9 %collective-permute-start.17 = (bf16[1728,128]{1,0:T(8,128)(2,1)S(1)}, bf16[1728,128]{1,0:T(8,128)(2,1)S(1)}, u32[]{:S(2)}, u32[]{:S(2)}) collective-permute-start(bf16[1728,128]{1,0:T(8,128)(2,1)S(1)} %get-tuple-element.56), channel_id=1, source_target_pairs={{0,1},{1,0},{2,3},{3,2},{4,5},{5,4},{6,7},{7,6},{8,9},{9,8},{10,11... | collective-permute-start | bytes 1327112 | tf_op jit(solution)/shard_map/ppermute | solution.py:228
  34.5 12.4 %collective-permute-start.8 = (bf16[864,128]{1,0:T(8,128)(2,1)S(1)}, bf16[864,128]{1,0:T(8,128)(2,1)S(1)}, u32[]{:S(2)}, u32[]{:S(2)}) collective-permute-start(bf16[864,128]{1,0:T(8,128)(2,1)S(1)} %add_convert_fusion.6), channel_id=1, source_target_pairs={{0,4},{1,5},{2,6},{3,7},{4,0},{5,1},{6,2},{7,3},{8,12},{9,13},{10,... | collective-permute-start | bytes 663560 | tf_op jit(solution)/shard_map/ppermute | solution.py:228
  43.4 23.2 %collective-permute-start.6 = (bf16[432,128]{1,0:T(8,128)(2,1)S(1)}, bf16[432,128]{1,0:T(8,128)(2,1)S(1)}, u32[]{:S(2)}, u32[]{:S(2)}) collective-permute-start(bf16[432,128]{1,0:T(8,128)(2,1)S(1)} %add_convert_fusion.11), channel_id=1, source_target_pairs={{0,8},{1,9},{2,10},{3,11},{4,12},{5,13},{6,14},{7,15},{8,0},{9,1},... | collective-permute-start | bytes 331784 | tf_op jit(solution)/shard_map/ppermute | solution.py:228
  46.9 9.8 %collective-permute-start.14 = (bf16[864,128]{1,0:T(8,128)(2,1)S(1)}, bf16[864,128]{1,0:T(8,128)(2,1)S(1)}, u32[]{:S(2)}, u32[]{:S(2)}) collective-permute-start(bf16[864,128]{1,0:T(8,128)(2,1)S(1)} %add_convert_fusion.5), channel_id=1, source_target_pairs={{0,4},{1,5},{2,6},{3,7},{4,0},{5,1},{6,2},{7,3},{8,12},{9,13},{10,... | collective-permute-start | bytes 663560 | tf_op jit(solution)/shard_map/ppermute | solution.py:228
  48.4 18.2 %collective-permute-start.12 = (bf16[432,128]{1,0:T(8,128)(2,1)S(1)}, bf16[432,128]{1,0:T(8,128)(2,1)S(1)}, u32[]{:S(2)}, u32[]{:S(2)}) collective-permute-start(bf16[432,128]{1,0:T(8,128)(2,1)S(1)} %add_convert_fusion.10), channel_id=1, source_target_pairs={{0,8},{1,9},{2,10},{3,11},{4,12},{5,13},{6,14},{7,15},{8,0},{9,1},... | collective-permute-start | bytes 331784 | tf_op jit(solution)/shard_map/ppermute | solution.py:228
  56.8 8.4 %collective-permute-start.18 = (bf16[864,128]{1,0:T(8,128)(2,1)S(1)}, bf16[864,128]{1,0:T(8,128)(2,1)S(1)}, u32[]{:S(2)}, u32[]{:S(2)}) collective-permute-start(bf16[864,128]{1,0:T(8,128)(2,1)S(1)} %add_convert_fusion.4), channel_id=1, source_target_pairs={{0,4},{1,5},{2,6},{3,7},{4,0},{5,1},{6,2},{7,3},{8,12},{9,13},{10,... | collective-permute-start | bytes 663560 | tf_op jit(solution)/shard_map/ppermute | solution.py:228
  57.5 9.9 %collective-permute-start.16 = (bf16[432,128]{1,0:T(8,128)(2,1)S(1)}, bf16[432,128]{1,0:T(8,128)(2,1)S(1)}, u32[]{:S(2)}, u32[]{:S(2)}) collective-permute-start(bf16[432,128]{1,0:T(8,128)(2,1)S(1)} %add_convert_fusion.9), channel_id=1, source_target_pairs={{0,8},{1,9},{2,10},{3,11},{4,12},{5,13},{6,14},{7,15},{8,0},{9,1},... | collective-permute-start | bytes 331784 | tf_op jit(solution)/shard_map/ppermute | solution.py:228
  65.3 6.9 %collective-permute-start.19 = (bf16[432,128]{1,0:T(8,128)(2,1)S(1)}, bf16[432,128]{1,0:T(8,128)(2,1)S(1)}, u32[]{:S(2)}, u32[]{:S(2)}) collective-permute-start(bf16[432,128]{1,0:T(8,128)(2,1)S(1)} %add_convert_fusion.8), channel_id=1, source_target_pairs={{0,8},{1,9},{2,10},{3,11},{4,12},{5,13},{6,14},{7,15},{8,0},{9,1},... | collective-permute-start | bytes 331784 | tf_op jit(solution)/shard_map/ppermute | solution.py:228

commit v3 on v0

v3 whole, which is shorter than its diff:
```python
import functools

import jax
import jax.numpy as jnp
from jax import lax
from jax.experimental import pallas as pl
from jax.experimental.pallas import tpu as pltpu
from jax.sharding import PartitionSpec as P

LANES = 128
ACC_LIMIT = 16 * 1024 * 1024


def round_up(value, unit):
    return -(-value // unit) * unit


def block_products(cotangent, weights, source):
    width = weights.shape[1]
    lead = cotangent.shape[0] * cotangent.shape[1]
    tiled = cotangent.reshape(lead, cotangent.shape[2] // width, width)
    picked = jnp.take(tiled, source, axis=1)
    products = jnp.einsum("kbi,bij->bkj", picked, weights, preferred_element_type=jnp.float32)
    return products.astype(jnp.bfloat16)


def pack_slots(products, target, count_row):
    blocks = products.shape[0]
    devices = count_row.shape[0]
    per_device = 2 * blocks // devices
    inclusive = jnp.cumsum(count_row)
    exclusive = inclusive - count_row
    positions = jnp.arange(blocks, dtype=jnp.int32)
    owner = jnp.sum((positions[:, None] >= inclusive[None, :]).astype(jnp.int32), axis=1)
    chosen = owner[:, None] == jnp.arange(devices, dtype=jnp.int32)[None, :]
    first = jnp.sum(jnp.where(chosen, exclusive[None, :], 0), axis=1)
    slot_index = owner * per_device + positions - first
    buffer = (
        jnp.zeros((devices * per_device,) + products.shape[1:], jnp.bfloat16)
        .at[slot_index]
        .set(products)
    )
    labels = jnp.full((devices * per_device,), -1, jnp.int32).at[slot_index].set(target)
    return (buffer, labels)


def sum_slots(received, labels, tiles_out, like_shape):
    selector = (labels[None, :] == jnp.arange(tiles_out, dtype=jnp.int32)[:, None]).astype(
        jnp.bfloat16
    )
    summed = jnp.einsum("ts,skc->ktc", selector, received, preferred_element_type=jnp.float32)
    return summed.reshape(like_shape[0], like_shape[1], -1).astype(jnp.bfloat16)


def slot_remap(cotangent, weights, source, target, counts, like_shape):
    products = block_products(cotangent, weights, source)
    buffer, labels = pack_slots(products, target, counts[0])
    arrived = lax.all_to_all(buffer, "curve", split_axis=0, concat_axis=0, tiled=True)
    arrived_labels = lax.all_to_all(labels, "curve", split_axis=0, concat_axis=0, tiled=True)
    return sum_slots(arrived, arrived_labels, like_shape[2] // weights.shape[1], like_shape)


def product_kernel(
    devices, channels, pitch, tiles, step_blocks,
    source_hbm, target_hbm, counts_hbm, x_hbm, w_hbm, out, acc, xs, x_in, w, source, target, counts, sems,
):
    steps = w.shape[0] // step_blocks
    scalars = [
        pltpu.make_async_copy(source_hbm, source, sems.at[0]),
        pltpu.make_async_copy(target_hbm, target, sems.at[1]),
        pltpu.make_async_copy(counts_hbm, counts, sems.at[2]),
    ]
    x_copy = pltpu.make_async_copy(x_hbm, x_in, sems.at[3])

    def w_copy(step):
        at = pl.ds(step * step_blocks, step_blocks)
        return pltpu.make_async_copy(w_hbm.at[at], w.at[at], sems.at[4 + step])

    for copy in scalars + [x_copy]:
        copy.start()
    for step in range(steps):
        w_copy(step).start()

    @pl.loop(0, acc.shape[0] // pitch)
    def clear(index):
        acc[pl.ds(pl.multiple_of(index * pitch, pitch), pitch), :] = jnp.zeros((pitch, LANES), jnp.float32)

    for tile in range(xs.shape[0]):
        xs[tile] = jnp.zeros(xs.shape[1:], xs.dtype)
    x_copy.wait()
    for tile in range(xs.shape[0]):
        xs[tile, :channels, :] = x_in[0, :, tile * LANES:(tile + 1) * LANES]
    for copy in scalars:
        copy.wait()

    def some(step, carry):
        owner, end = carry
        w_copy(step).wait()
        rows = []
        for index in range(step_blocks):
            block = step * step_blocks + index
            passed = (block >= end).astype(jnp.int32)
            owner = jnp.minimum(owner + passed, devices - 1)
            end = end + passed * counts[0, owner]
            rows.append(pl.multiple_of((owner * tiles + target[block]) * pitch, 8))
        for index, row in enumerate(rows):
            block = step * step_blocks + index
            product = jnp.dot(xs[source[block], :pitch, :], w[block], preferred_element_type=jnp.float32)
            acc[pl.ds(row, pitch), :] += product
        return owner, end

    lax.fori_loop(0, steps, some, (jnp.int32(0), counts[0, 0]))

    @pl.loop(0, devices)
    def finish(index):
        unit = tiles * pitch
        at = pl.multiple_of(index * unit, 8)
        out[pl.ds(at, unit), :] = acc[pl.ds(at, unit), :].astype(out.dtype)


def sums(cotangent, weights, source, target, counts, like_shape):
    devices = counts.shape[1]
    channels = cotangent.shape[1]
    pitch = round_up(channels, 8)
    tiles_in, tiles = cotangent.shape[2] // LANES, like_shape[2] // LANES
    blocks = weights.shape[0]
    step_blocks = max(size for size in range(1, 17) if blocks % size == 0)
    rows = devices * tiles * pitch
    return pl.pallas_call(
        functools.partial(product_kernel, devices, channels, pitch, tiles, step_blocks),
        out_shape=jax.ShapeDtypeStruct((rows, LANES), jnp.bfloat16),
        in_specs=[pl.BlockSpec(memory_space=pltpu.HBM)] * 5,
        out_specs=pl.BlockSpec(memory_space=pltpu.VMEM),
        scratch_shapes=[
            pltpu.VMEM((rows, LANES), jnp.float32),
            pltpu.VMEM((tiles_in, round_up(pitch, 16), LANES), jnp.bfloat16),
            pltpu.VMEM(cotangent.shape, jnp.bfloat16),
            pltpu.VMEM(weights.shape, jnp.bfloat16),
            pltpu.SMEM(source.shape, jnp.int32),
            pltpu.SMEM(target.shape, jnp.int32),
            pltpu.SMEM(counts.shape, jnp.int32),
            pltpu.SemaphoreType.DMA((4 + blocks // step_blocks,)),
        ],
        compiler_params=pltpu.CompilerParams(vmem_limit_bytes=28 * 1024 * 1024),
        cost_estimate=pl.CostEstimate(
            flops=2 * blocks * channels * LANES * LANES, bytes_accessed=2 * weights.size + 2 * rows * LANES,
            transcendentals=0,
        ),
    )(*[pltpu.with_memory_space_constraint(value, pltpu.HBM) for value in (source, target, counts, cotangent, weights)])


def final_kernel(channels, pitch, tiles, total, out):
    for tile in range(tiles):
        out[0, :, tile * LANES:(tile + 1) * LANES] = total[tile * pitch:tile * pitch + channels, :]


def sum_remap(cotangent, weights, source, target, counts, like_shape):
    made = sums(cotangent, weights, source, target, counts, like_shape)
    total = lax.psum_scatter(made, "curve", scatter_dimension=0, tiled=True)
    return pl.pallas_call(
        functools.partial(
            final_kernel, like_shape[1], round_up(like_shape[1], 8), like_shape[2] // LANES
        ),
        out_shape=jax.ShapeDtypeStruct(like_shape, jnp.bfloat16),
    )(total)


def on_device(devices, *args):
    latlon, healpix = args[:2]
    remaps = [
        (latlon, args[2], args[3], args[4], args[5], healpix.shape),
        (healpix, args[6], args[7], args[8], args[9], latlon.shape),
    ]
    bits = devices.bit_length() - 1
    tiles = max(latlon.shape[2], healpix.shape[2]) // LANES
    size = devices * tiles * round_up(latlon.shape[1], 8) * LANES * 4
    if devices == 1 << bits and bits > 2 and size <= ACC_LIMIT:
        return tuple(sum_remap(*remap) for remap in remaps)
    return tuple(slot_remap(*remap) for remap in remaps)


def solution(mesh):
    in_specs = (
        P("groups", None, "curve"),
        P("groups", None, "curve"),
        P("curve", None, None),
        P("curve"),
        P("curve"),
        P("curve", None),
        P("curve", None, None),
        P("curve"),
        P("curve"),
        P("curve", None),
    )
    out_specs = (P("groups", None, "curve"), P("groups", None, "curve"))
    return jax.shard_map(
        functools.partial(on_device, mesh.shape["curve"]),
        mesh=mesh, in_specs=in_specs, out_specs=out_specs, check_vma=False,
    )
```

time: 301 us -> 164 us (0.54)
  the two profiles are of different devices: /device:TPU:13 before, /device:TPU:0 now
where the time goes in v3:
time: 164 us
  waiting for transfers between devices  133 us (81%)
  Pallas kernels  16.3 us (10%)
  between operations  14.1 us (9%)
    reduce_scatter x2, waiting for transfers between devices, sum_remap(): total = lax.psum_scatter(made, 'curve', scatter_dimension=0, tiled=True)  133 us
    pallas_call x2, Pallas kernels, sums(): pl.pallas_call(functools.partial(product_kernel, devices, channels, pitch...  13 us
    pallas_call x2, Pallas kernels, sum_remap(): pl.pallas_call(functools.partial(final_kernel, like_shape[1], round_up(li...  3.32 us
  transfers between devices with their start and end apart: 2, of which 2 were waited for; matrix products, arithmetic and copies ran while one was open for 0% of the time, Pallas kernels for 5%

profile of v3, /device:TPU:0, one launch (start us, length us, event | category | flops | bytes accessed | tf_op | source)
XLA Modules:
  0.0 163.9 jit_solution(683482382381704946)
XLA Ops:
  7.2 0.0 reduce-scatter.3.cloned.1.call-start
  7.2 6.5 %shard_map.113 = bf16[13824,128]{1,0:T(8,128)(2,1)} custom-call(s32[144]{0:T(256)} %source_hbm.2, s32[144]{0:T(256)} %target_hbm.2, s32[1,16]{1,0:T(1,128)} %counts_hbm.2, bf16[1,69,1536]{2,1,0:T(8,128)(2,1)} %x_hbm.2, bf16[144,128,128]{2,1,0:T(8,128)(2,1)} %w_hbm.2), custom_call_target="tpu_custom_call" | custom-call | flops 325582848 | bytes 8257536 | tf_op jit(solution)/shard_map/pallas_call | solution.py:129
  13.7 0.0 reduce-scatter.3.cloned.1.call-update
  13.7 0.0 reduce-scatter.5.cloned.1.call-start
  13.8 6.5 %shard_map.115 = bf16[13824,128]{1,0:T(8,128)(2,1)} custom-call(s32[144]{0:T(256)} %source_hbm.3, s32[144]{0:T(256)} %target_hbm.3, s32[1,16]{1,0:T(1,128)} %counts_hbm.3, bf16[1,69,1536]{2,1,0:T(8,128)(2,1)} %x_hbm.3, bf16[144,128,128]{2,1,0:T(8,128)(2,1)} %w_hbm.3), custom_call_target="tpu_custom_call" | custom-call | flops 325582848 | bytes 8257536 | tf_op jit(solution)/shard_map/pallas_call | solution.py:129
  20.3 0.0 reduce-scatter.5.cloned.1.call-update
  20.3 64.3 %reduce-scatter.3.cloned.1.call-done.total = bf16[864,128]{1,0:T(8,128)(2,1)} async-done(((bf16[13824,128]{1,0:T(8,128)(2,1)}), bf16[864,128]{1,0:T(8,128)(2,1)}) %reduce-scatter.3.cloned.1.call-update) | async-done | bytes 221200 | tf_op jit(solution)/shard_map/reduce_scatter | solution.py:159
  84.6 1.7 %shard_map.114 = bf16[1,69,1536]{2,1,0:T(8,128)(2,1)} custom-call(bf16[864,128]{1,0:T(8,128)(2,1)} %reduce-scatter.3.cloned.1.call-done.total), custom_call_target="tpu_custom_call" | custom-call | tf_op jit(solution)/shard_map/pallas_call | solution.py:160
  86.3 69.2 %reduce-scatter.5.cloned.1.call-done.total = bf16[864,128]{1,0:T(8,128)(2,1)} async-done(((bf16[13824,128]{1,0:T(8,128)(2,1)}), bf16[864,128]{1,0:T(8,128)(2,1)}) %reduce-scatter.5.cloned.1.call-update) | async-done | bytes 221200 | tf_op jit(solution)/shard_map/reduce_scatter | solution.py:159
  155.4 1.7 %shard_map.116 = bf16[1,69,1536]{2,1,0:T(8,128)(2,1)} custom-call(bf16[864,128]{1,0:T(8,128)(2,1)} %reduce-scatter.5.cloned.1.call-done.total), custom_call_target="tpu_custom_call" | custom-call | tf_op jit(solution)/shard_map/pallas_call | solution.py:160
Async XLA Ops:
  7.2 77.4 %reduce-scatter.3.cloned.1.call-start = ((), (), s32[]{:S(2)}) async-start(), calls=%async_computation.2 | async-start | bytes 3760128 | tf_op jit(solution)/shard_map/reduce_scatter | solution.py:159
  13.7 141.7 %reduce-scatter.5.cloned.1.call-start = ((), (), s32[]{:S(2)}) async-start(), calls=%async_computation.3 | async-start | bytes 3760128 | tf_op jit(solution)/shard_map/reduce_scatter | solution.py:159
Sparse Core Ops, SparseCore 0:
  13.8 70.7 reduce-scatter.2
  88.5 66.9 reduce-scatter.4

commit v4 on v3

--- a/solution.py
+++ b/solution.py
@@ -60,11 +60,28 @@
     return sum_slots(arrived, arrived_labels, like_shape[2] // weights.shape[1], like_shape)
 
 
+def slots_of(stages):
+    return [[sum(((m >> i) & 1) << bit for i, bit in enumerate(stage)) for m in range(1 << len(stage))]
+            for stage in stages]
+
+
+def owners_in_order(stages):
+    masks = [0]
+    for stage in slots_of(stages):
+        masks = [left + right for left in masks for right in stage]
+    return masks
+
+
 def product_kernel(
-    devices, channels, pitch, tiles, step_blocks,
-    source_hbm, target_hbm, counts_hbm, x_hbm, w_hbm, out, acc, xs, x_in, w, source, target, counts, sems,
+    bits, channels, pitch, chunks, step_blocks,
+    source_hbm, target_hbm, counts_hbm, x_hbm, w_hbm, *rest,
 ):
+    number = len(chunks)
+    outs, (acc, xs, x_in, w, source, target, counts, places, sems) = rest[:4], rest[4:]
+    devices = 1 << bits
     steps = w.shape[0] // step_blocks
+    me = lax.axis_index("curve")
+
     scalars = [
         pltpu.make_async_copy(source_hbm, source, sems.at[0]),
         pltpu.make_async_copy(target_hbm, target, sems.at[1]),
@@ -87,6 +104,20 @@
 
     for tile in range(xs.shape[0]):
         xs[tile] = jnp.zeros(xs.shape[1:], xs.dtype)
+
+    bases, base = [], 0
+    for chunk, (low, high, stages) in enumerate(chunks):
+        bases.append(base)
+        order = [stages[1], stages[0]] + list(stages[2:])
+        for owner in range(devices):
+            differ = jnp.bitwise_xor(me, owner)
+            place = jnp.int32(0)
+            for stage in order:
+                for bit in reversed(stage):
+                    place = place * 2 + jnp.bitwise_and(jnp.right_shift(differ, bit), 1)
+            places[chunk, owner] = base + place * (high - low) - low
+        base += devices * (high - low)
+
     x_copy.wait()
     for tile in range(xs.shape[0]):
         xs[tile, :channels, :] = x_in[0, :, tile * LANES:(tile + 1) * LANES]
@@ -102,7 +133,11 @@
             passed = (block >= end).astype(jnp.int32)
             owner = jnp.minimum(owner + passed, devices - 1)
             end = end + passed * counts[0, owner]
-            rows.append(pl.multiple_of((owner * tiles + target[block]) * pitch, 8))
+            tile = target[block]
+            place = places[0, owner]
+            for chunk in range(1, number):
+                place = jnp.where(tile >= chunks[chunk][0], places[chunk, owner], place)
+            rows.append(pl.multiple_of((place + tile) * pitch, 8))
         for index, row in enumerate(rows):
             block = step * step_blocks + index
             product = jnp.dot(xs[source[block], :pitch, :], w[block], preferred_element_type=jnp.float32)
@@ -111,58 +146,215 @@
 
     lax.fori_loop(0, steps, some, (jnp.int32(0), counts[0, 0]))
 
-    @pl.loop(0, devices)
-    def finish(index):
-        unit = tiles * pitch
-        at = pl.multiple_of(index * unit, 8)
-        out[pl.ds(at, unit), :] = acc[pl.ds(at, unit), :].astype(out.dtype)
-
-
-def sums(cotangent, weights, source, target, counts, like_shape):
-    devices = counts.shape[1]
+    for base, (low, high, stages) in zip(bases, chunks):
+        unit = (high - low) * pitch
+        quarter = devices // 4
+
+        @pl.loop(0, quarter)
+        def finish(index):
+            at = pl.multiple_of(quarter * low * pitch + index * unit, 8)
+            for part, ref in enumerate(outs):
+                row = pl.multiple_of((base + part * quarter * (high - low)) * pitch + index * unit, 8)
+                ref[pl.ds(at, unit), :] = acc[pl.ds(row, unit), :].astype(ref.dtype)
+
+
+def products(remap, chunks, bits):
+    cotangent, weights, source, target, counts = remap[:5]
+    devices = 1 << bits
     channels = cotangent.shape[1]
     pitch = round_up(channels, 8)
-    tiles_in, tiles = cotangent.shape[2] // LANES, like_shape[2] // LANES
+    tiles_in = cotangent.shape[2] // LANES
     blocks = weights.shape[0]
     step_blocks = max(size for size in range(1, 17) if blocks % size == 0)
-    rows = devices * tiles * pitch
+    rows = devices // 4 * chunks[-1][1] * pitch
     return pl.pallas_call(
-        functools.partial(product_kernel, devices, channels, pitch, tiles, step_blocks),
-        out_shape=jax.ShapeDtypeStruct((rows, LANES), jnp.bfloat16),
+        functools.partial(product_kernel, bits, channels, pitch, chunks, step_blocks),
+        out_shape=[jax.ShapeDtypeStruct((rows, LANES), kind) for kind in (jnp.float32, jnp.bfloat16) * 2],
         in_specs=[pl.BlockSpec(memory_space=pltpu.HBM)] * 5,
-        out_specs=pl.BlockSpec(memory_space=pltpu.VMEM),
+        out_specs=[pl.BlockSpec(memory_space=pltpu.VMEM)] * 4,
         scratch_shapes=[
-            pltpu.VMEM((rows, LANES), jnp.float32),
+            pltpu.VMEM((rows * 4, LANES), jnp.float32),
             pltpu.VMEM((tiles_in, round_up(pitch, 16), LANES), jnp.bfloat16),
             pltpu.VMEM(cotangent.shape, jnp.bfloat16),
             pltpu.VMEM(weights.shape, jnp.bfloat16),
             pltpu.SMEM(source.shape, jnp.int32),
             pltpu.SMEM(target.shape, jnp.int32),
             pltpu.SMEM(counts.shape, jnp.int32),
+            pltpu.SMEM((len(chunks), devices), jnp.int32),
             pltpu.SemaphoreType.DMA((4 + blocks // step_blocks,)),
         ],
         compiler_params=pltpu.CompilerParams(vmem_limit_bytes=28 * 1024 * 1024),
         cost_estimate=pl.CostEstimate(
-            flops=2 * blocks * channels * LANES * LANES, bytes_accessed=2 * weights.size + 2 * rows * LANES,
+            flops=2 * blocks * channels * LANES * LANES,
+            bytes_accessed=2 * weights.size + 12 * rows * LANES,
             transcendentals=0,
         ),
     )(*[pltpu.with_memory_space_constraint(value, pltpu.HBM) for value in (source, target, counts, cotangent, weights)])
 
 
-def final_kernel(channels, pitch, tiles, total, out):
-    for tile in range(tiles):
-        out[0, :, tile * LANES:(tile + 1) * LANES] = total[tile * pitch:tile * pitch + channels, :]
-
-
-def sum_remap(cotangent, weights, source, target, counts, like_shape):
-    made = sums(cotangent, weights, source, target, counts, like_shape)
-    total = lax.psum_scatter(made, "curve", scatter_dimension=0, tiled=True)
+def exchange(value, mask, devices):
+    return lax.ppermute(value, "curve", [(at, at ^ mask) for at in range(devices)])
+
+
+def added(terms, low, high):
+    return sum(term[low:high].astype(jnp.float32) for term in terms)
+
+
+class Chain:
+    def __init__(self, chunk, bits, pitch):
+        self.chunk, self.devices = chunk, 1 << bits
+        self.slots = slots_of(chunk[2])
+        self.stage = 2
+        self.base = self.devices // 4 * chunk[0] * pitch
+        self.length = self.devices // 4 * (chunk[1] - chunk[0]) * pitch
+
+    def first(self, terms, at):
+        base = self.base - at
+        self.total = added(terms, base, base + self.length).astype(jnp.bfloat16)
+
+    def second(self):
+        self.got = [exchange(self.total, self.slots[1][1], self.devices)]
+
+    def rest(self, terms):
+        self.terms = [(term, self.base) for term in terms]
+
+    def part(self, place):
+        at = place * self.length
+        return sum(term[base + at:base + at + self.length].astype(jnp.float32) for term, base in self.terms)
+
+    def send_next(self):
+        self.terms = self.terms + [(got, 0) for got in self.got]
+        masks = self.slots[self.stage]
+        self.length //= len(masks)
+        self.sent = [self.part(place).astype(jnp.bfloat16) for place in range(1, len(masks))]
+        self.got = [exchange(sent, mask, self.devices) for sent, mask in zip(self.sent, masks[1:])]
+        self.stage += 1
+
+    def finish(self):
+        self.terms = self.terms + [(got, 0) for got in self.got]
+        self.sent = ()
+
+
+def final_kernel(channels, pitch, parts, *refs):
+    out = refs[-1]
+    at = 0
+    for low, high, count in parts:
+        terms = refs[at:at + count]
+        at += count
+        for tile in range(high - low):
+            total = sum(
+                term[tile * pitch:(tile + 1) * pitch, :].astype(jnp.float32) for term in terms
+            )
+            lane = (low + tile) * LANES
+            out[0, :, lane:lane + LANES] = total[:channels].astype(jnp.bfloat16)
+
+
+def final_sum(chains, like_shape, pitch):
+    parts = [(chain.chunk[0], chain.chunk[1], len(chain.terms)) for chain in chains]
+    flat, specs = [], []
+    for chain in chains:
+        rows = (chain.chunk[1] - chain.chunk[0]) * pitch
+        for term, base in chain.terms:
+            flat.append(term if base % rows == 0 else term[base:base + rows])
+            at = base // rows if base % rows == 0 else 0
+            specs.append(pl.BlockSpec((rows, LANES), lambda step, at=at: (at, 0)))
     return pl.pallas_call(
-        functools.partial(
-            final_kernel, like_shape[1], round_up(like_shape[1], 8), like_shape[2] // LANES
-        ),
+        functools.partial(final_kernel, like_shape[1], pitch, parts),
         out_shape=jax.ShapeDtypeStruct(like_shape, jnp.bfloat16),
-    )(total)
+        grid=(1,),
+        in_specs=specs,
+        out_specs=pl.BlockSpec(like_shape, lambda step: (0, 0, 0)),
+        compiler_params=pltpu.CompilerParams(vmem_limit_bytes=28 * 1024 * 1024),
+    )(*flat)
+
+
+def plan(tiles, bits):
+    later = tuple((bit,) for bit in range(3, bits))
+    straight = ((0,), (1,), (2,)) + later
+    turned = ((0,), (2,), (1,)) + later
+    half, more, most = tiles // 2, (tiles + 2) * 7 // 14, tiles * 5 // 6
+    return (
+        [(0, more, straight), (more, tiles, turned)],
+        [(0, half, straight), (half, most, straight), (most, tiles, straight)],
+    )
+
+
+class Order:
+    def __init__(self):
+        self.last = ()
+
+    def after(self, values):
+        values, unused = lax.optimization_barrier((values, self.last))
+        return values
+
+    def before(self, values):
+        self.last = values
+
+
+def bit_remaps(remaps, bits):
+    one, two = remaps
+    devices = 1 << bits
+    pitch = round_up(one[-1][1], 8)
+    plans = plan(one[-1][2] // LANES, bits)
+    ones, twos = [[Chain(chunk, bits, pitch) for chunk in chunks] for chunks in plans]
+    order = Order()
+
+    def step(*chains):
+        gots = order.after([chain.got for chain in chains])
+        for chain, got in zip(chains, gots):
+            chain.got = got
+            if chain.stage < len(chain.slots):
+                chain.send_next()
+            else:
+                chain.finish()
+        order.before([chain.sent for chain in chains])
+
+    def summed(line, terms, at):
+        terms = order.after(terms)
+        for chain in line:
+            chain.first(terms, at)
+        order.before([chain.total for chain in line])
+
+    def both_cores(keep, send):
+        return [keep, exchange(send, 1, devices)]
+
+    keep, send, keep_on, send_on = products(one, plans[0], bits)
+    on = both_cores(keep_on, send_on)
+    rest = both_cores(keep, send)
+    summed(ones, on, 0)
+    for chain in ones:
+        chain.second()
+    rest = order.after(rest)
+    order.before(rest)
+    for chain in ones:
+        chain.rest(rest)
+    keep, send, keep_on, send_on = products((order.after(two[0]),) + two[1:], plans[1], bits)
+    cut = devices // 4 * plans[1][0][1] * pitch
+    on = [both_cores(keep_on[:cut], send_on[:cut]), both_cores(keep_on[cut:], send_on[cut:])]
+    late = both_cores(keep, send)
+    step(ones[1])
+    step(ones[0])
+    summed(twos[:1], on[0], 0)
+    twos[0].second()
+    step(ones[1])
+    step(ones[0])
+    summed(twos[1:], on[1], cut)
+    twos[1].second()
+    late = order.after(late)
+    order.before(late)
+    for chain in twos:
+        chain.rest(late)
+    step(twos[0])
+    twos[2].total = order.after(twos[2].total)
+    twos[2].second()
+    step(twos[1])
+    step(twos[0])
+    step(*ones)
+    step(twos[2])
+    step(twos[1])
+    step(twos[2])
+    step(*twos)
+    return [final_sum(line, remap[-1], pitch) for line, remap in zip((ones, twos), remaps)]
 
 
 def on_device(devices, *args):
@@ -175,7 +367,7 @@
     tiles = max(latlon.shape[2], healpix.shape[2]) // LANES
     size = devices * tiles * round_up(latlon.shape[1], 8) * LANES * 4
     if devices == 1 << bits and bits > 2 and size <= ACC_LIMIT:
-        return tuple(sum_remap(*remap) for remap in remaps)
+        return tuple(bit_remaps(remaps, bits))
     return tuple(slot_remap(*remap) for remap in remaps)
 
 

time: 164 us -> 61.7 us (0.38)
  waiting for transfers between devices: 133 us -> 19.6 us
  starting transfers between devices: 0.08 us -> 28.5 us
  between operations: 14.1 us -> 0.77 us
  Pallas kernels: 16.3 us -> 11.5 us
    reduce_scatter x2 -> x0, waiting for transfers between devices: 133 us -> none  [sum_remap(): total = lax.psum_scatter(made, 'curve', scatter_dimension=0, tiled=True)]
    ppermute x0 -> x20, starting transfers between devices: none -> 28.5 us  [exchange(): lax.ppermute(value, 'curve', [(at, at ^ mask) for at in range(devices)])]
    ppermute x0 -> x20, waiting for transfers between devices: none -> 19.6 us  [exchange(): lax.ppermute(value, 'curve', [(at, at ^ mask) for at in range(devices)])]
    pallas_call x4, Pallas kernels: 16.3 us -> 11.5 us  [the longest x2 9.79 us: products(): pl.pallas_call(functools.partial(product_kernel, bits, channels, pitch, c...]
  transfers between devices with their start and end apart: 2 -> 20, of which waited for: 2 -> 10; matrix products, arithmetic and copies ran while one was open for 0% -> 2% of each run, Pallas kernels for 5% -> 9%
where the time goes in v4:
time: 61.7 us; the launch traced here: 61.6 us
  starting transfers between devices  28.5 us (46%)
  waiting for transfers between devices  19.6 us (32%)
  Pallas kernels  11.5 us (19%)
  other arithmetic  1.01 us (2%)
  between operations  0.77 us (1%)
    ppermute x20, starting transfers between devices, exchange(): lax.ppermute(value, 'curve', [(at, at ^ mask) for at in range(devices)])  28.5 us
    ppermute x20, waiting for transfers between devices, exchange(): lax.ppermute(value, 'curve', [(at, at ^ mask) for at in range(devices)])  19.6 us
    pallas_call x2, Pallas kernels, products(): pl.pallas_call(functools.partial(product_kernel, bits, channels, pitch, c...  9.79 us
    pallas_call x2, Pallas kernels, final_sum(): pl.pallas_call(functools.partial(final_kernel, like_shape[1], pitch, part...  1.67 us
  transfers between devices with their start and end apart: 20, of which 10 were waited for; matrix products, arithmetic and copies ran while one was open for 2% of the time, Pallas kernels for 9%

profile of v4, /device:TPU:0, one launch (start us, length us, event | category | flops | bytes accessed | tf_op | source)
XLA Modules:
  0.0 61.6 jit_solution(18296033914462281851)
XLA Ops:
  0.6 4.9 %shard_map.113 = (f32[3456,128]{1,0:T(8,128)S(1)}, bf16[3456,128]{1,0:T(8,128)(2,1)S(1)}, f32[3456,128]{1,0:T(8,128)S(1)}, bf16[3456,128]{1,0:T(8,128)(2,1)S(1)}) custom-call(s32[144]{0:T(256)} %source_hbm.2, s32[144]{0:T(256)} %target_hbm.2, s32[1,16]{1,0:T(1,128)} %counts_hbm.2, bf16[1,69,1536]{2,1,0:T(8,128)(2,1)} %x_hbm.1, bf16[144,128,128]{2,1,0:T(8,128)(2,1)} %w_hbm.2), custom_call_target="tpu_custom_call" | custom-call | flops 325582848 | bytes 10027008 | tf_op jit(solution)/shard_map/pallas_call | solution.py:170
  5.6 0.5 collective-permute-start.1
  6.1 0.1 collective-permute-start
  6.1 2.0 %collective-permute-done.1 = bf16[3456,128]{1,0:T(8,128)(2,1)S(1)} collective-permute-done((bf16[3456,128]{1,0:T(8,128)(2,1)S(1)}, bf16[3456,128]{1,0:T(8,128)(2,1)S(1)}, u32[]{:S(2)}, u32[]{:S(2)}) %collective-permute-start.1) | collective-permute-done | bytes 884768 | tf_op jit(solution)/shard_map/ppermute | solution.py:196
  8.1 0.1 add_convert_fusion.2
  8.2 3.0 %collective-permute-start.3 = (bf16[1440,128]{1,0:T(8,128)(2,1)S(1)}, bf16[1440,128]{1,0:T(8,128)(2,1)S(1)}, u32[]{:S(2)}, u32[]{:S(2)}) collective-permute-start(bf16[1440,128]{1,0:T(8,128)(2,1)S(1)} %add_convert_fusion.2), channel_id=1, source_target_pairs={{0,4},{1,5},{2,6},{3,7},{4,0},{5,1},{6,2},{7,3},{8,12},{9,13},{10,... | collective-permute-start | bytes 1105928 | tf_op jit(solution)/shard_map/ppermute | solution.py:196
  11.2 0.1 add_convert_fusion
  11.3 1.6 %collective-permute-start.2 = (bf16[2016,128]{1,0:T(8,128)(2,1)S(1)}, bf16[2016,128]{1,0:T(8,128)(2,1)S(1)}, u32[]{:S(2)}, u32[]{:S(2)}) collective-permute-start(bf16[2016,128]{1,0:T(8,128)(2,1)S(1)} %add_convert_fusion), channel_id=1, source_target_pairs={{0,2},{1,3},{2,0},{3,1},{4,6},{5,7},{6,4},{7,5},{8,10},{9,11},{10,... | collective-permute-start | bytes 1548296 | tf_op jit(solution)/shard_map/ppermute | solution.py:196
  12.9 0.0 collective-permute-done.refs_1_
  12.9 4.9 %shard_map.114 = (f32[3456,128]{1,0:T(8,128)S(1)}, bf16[3456,128]{1,0:T(8,128)(2,1)S(1)}, f32[3456,128]{1,0:T(8,128)S(1)}, bf16[3456,128]{1,0:T(8,128)(2,1)S(1)}) custom-call(s32[144]{0:T(256)} %source_hbm.3, s32[144]{0:T(256)} %target_hbm.3, s32[1,16]{1,0:T(1,128)} %counts_hbm.3, bf16[1,69,1536]{2,1,0:T(8,128)(2,1)} %x_hbm.2, bf16[144,128,128]{2,1,0:T(8,128)(2,1)} %w_hbm.3), custom_call_target="tpu_custom_call" | custom-call | flops 325582848 | bytes 10027008 | tf_op jit(solution)/shard_map/pallas_call | solution.py:170
  17.8 0.1 fusion.2
  17.9 0.1 collective-permute-start.6
  17.9 0.5 collective-permute-start.10
  18.4 0.1 collective-permute-start.9
  18.5 0.1 fusion.1
  18.6 1.5 %collective-permute-done.3.refs_7_ = bf16[1440,128]{1,0:T(8,128)(2,1)S(1)} collective-permute-done((bf16[1440,128]{1,0:T(8,128)(2,1)S(1)}, bf16[1440,128]{1,0:T(8,128)(2,1)S(1)}, u32[]{:S(2)}, u32[]{:S(2)}) %collective-permute-start.3) | collective-permute-done | bytes 368672 | tf_op jit(solution)/shard_map/ppermute | solution.py:196
  20.1 0.1 add_convert_fusion.6
  20.2 1.8 %collective-permute-start.5 = (bf16[720,128]{1,0:T(8,128)(2,1)S(1)}, bf16[720,128]{1,0:T(8,128)(2,1)S(1)}, u32[]{:S(2)}, u32[]{:S(2)}) collective-permute-start(bf16[720,128]{1,0:T(8,128)(2,1)S(1)} %add_convert_fusion.6), channel_id=1, source_target_pairs={{0,2},{1,3},{2,0},{3,1},{4,6},{5,7},{6,4},{7,5},{8,10},{9,11},{10,... | collective-permute-start | bytes 552968 | tf_op jit(solution)/shard_map/ppermute | solution.py:196
  21.9 4.1 %collective-permute-done.2.refs_2_ = bf16[2016,128]{1,0:T(8,128)(2,1)S(1)} collective-permute-done((bf16[2016,128]{1,0:T(8,128)(2,1)S(1)}, bf16[2016,128]{1,0:T(8,128)(2,1)S(1)}, u32[]{:S(2)}, u32[]{:S(2)}) %collective-permute-start.2) | collective-permute-done | bytes 516128 | tf_op jit(solution)/shard_map/ppermute | solution.py:196
  26.0 0.1 add_convert_fusion.4
  26.1 0.1 collective-permute-start.4
  26.2 0.1 add_convert_fusion.1
  26.3 2.0 %collective-permute-start.11 = (bf16[1728,128]{1,0:T(8,128)(2,1)S(1)}, bf16[1728,128]{1,0:T(8,128)(2,1)S(1)}, u32[]{:S(2)}, u32[]{:S(2)}) collective-permute-start(bf16[1728,128]{1,0:T(8,128)(2,1)S(1)} %add_convert_fusion.1), channel_id=1, source_target_pairs={{0,2},{1,3},{2,0},{3,1},{4,6},{5,7},{6,4},{7,5},{8,10},{9,11},{10,... | collective-permute-start | bytes 1327112 | tf_op jit(solution)/shard_map/ppermute | solution.py:196
  28.3 1.6 %collective-permute-done.5.refs_8_ = bf16[720,128]{1,0:T(8,128)(2,1)S(1)} collective-permute-done((bf16[720,128]{1,0:T(8,128)(2,1)S(1)}, bf16[720,128]{1,0:T(8,128)(2,1)S(1)}, u32[]{:S(2)}, u32[]{:S(2)}) %collective-permute-start.5) | collective-permute-done | bytes 184352 | tf_op jit(solution)/shard_map/ppermute | solution.py:196
  30.0 0.1 fusion
  30.0 2.7 %collective-permute-start.8 = (bf16[360,128]{1,0:T(8,128)(2,1)S(1)}, bf16[360,128]{1,0:T(8,128)(2,1)S(1)}, u32[]{:S(2)}, u32[]{:S(2)}) collective-permute-start(bf16[360,128]{1,0:T(8,128)(2,1)S(1)} %get-tuple-element.71), channel_id=1, source_target_pairs={{0,8},{1,9},{2,10},{3,11},{4,12},{5,13},{6,14},{7,15},{8,0},{9,1},... | collective-permute-start | bytes 276488 | tf_op jit(solution)/shard_map/ppermute | solution.py:196
  32.7 0.8 %collective-permute-done.4.refs_3_ = bf16[1008,128]{1,0:T(8,128)(2,1)S(1)} collective-permute-done((bf16[1008,128]{1,0:T(8,128)(2,1)S(1)}, bf16[1008,128]{1,0:T(8,128)(2,1)S(1)}, u32[]{:S(2)}, u32[]{:S(2)}) %collective-permute-start.4) | collective-permute-done | bytes 258080 | tf_op jit(solution)/shard_map/ppermute | solution.py:196
  33.5 0.1 add_convert_fusion.9
  33.6 0.1 add_convert_fusion.3
  33.6 1.6 %collective-permute-start.13 = (bf16[1152,128]{1,0:T(8,128)(2,1)S(1)}, bf16[1152,128]{1,0:T(8,128)(2,1)S(1)}, u32[]{:S(2)}, u32[]{:S(2)}) collective-permute-start(bf16[1152,128]{1,0:T(8,128)(2,1)S(1)} %add_convert_fusion.3), channel_id=1, source_target_pairs={{0,2},{1,3},{2,0},{3,1},{4,6},{5,7},{6,4},{7,5},{8,10},{9,11},{10,... | collective-permute-start | bytes 884744 | tf_op jit(solution)/shard_map/ppermute | solution.py:196
  35.3 3.2 %collective-permute-start.7 = (bf16[504,128]{1,0:T(8,128)(2,1)S(1)}, bf16[504,128]{1,0:T(8,128)(2,1)S(1)}, u32[]{:S(2)}, u32[]{:S(2)}) collective-permute-start(bf16[504,128]{1,0:T(8,128)(2,1)S(1)} %add_convert_fusion.9), channel_id=1, source_target_pairs={{0,8},{1,9},{2,10},{3,11},{4,12},{5,13},{6,14},{7,15},{8,0},{9,1},... | collective-permute-start | bytes 387080 | tf_op jit(solution)/shard_map/ppermute | solution.py:196
  38.5 1.0 %collective-permute-done.11.refs_2_ = bf16[1728,128]{1,0:T(8,128)(2,1)S(1)} collective-permute-done((bf16[1728,128]{1,0:T(8,128)(2,1)S(1)}, bf16[1728,128]{1,0:T(8,128)(2,1)S(1)}, u32[]{:S(2)}, u32[]{:S(2)}) %collective-permute-start.11) | collective-permute-done | bytes 442400 | tf_op jit(solution)/shard_map/ppermute | solution.py:196
  39.4 0.1 add_convert_fusion.5
  39.5 2.1 %collective-permute-start.12 = (bf16[864,128]{1,0:T(8,128)(2,1)S(1)}, bf16[864,128]{1,0:T(8,128)(2,1)S(1)}, u32[]{:S(2)}, u32[]{:S(2)}) collective-permute-start(bf16[864,128]{1,0:T(8,128)(2,1)S(1)} %add_convert_fusion.5), channel_id=1, source_target_pairs={{0,4},{1,5},{2,6},{3,7},{4,0},{5,1},{6,2},{7,3},{8,12},{9,13},{10,... | collective-permute-start | bytes 663560 | tf_op jit(solution)/shard_map/ppermute | solution.py:196
  41.7 1.5 %collective-permute-start.16 = (bf16[576,128]{1,0:T(8,128)(2,1)S(1)}, bf16[576,128]{1,0:T(8,128)(2,1)S(1)}, u32[]{:S(2)}, u32[]{:S(2)}) collective-permute-start(bf16[576,128]{1,0:T(8,128)(2,1)S(1)} %add_convert_fusion.8), channel_id=1, source_target_pairs={{0,2},{1,3},{2,0},{3,1},{4,6},{5,7},{6,4},{7,5},{8,10},{9,11},{10,... | collective-permute-start | bytes 442376 | tf_op jit(solution)/shard_map/ppermute | solution.py:196
  43.2 2.6 %collective-permute-done.13.refs_7_ = bf16[1152,128]{1,0:T(8,128)(2,1)S(1)} collective-permute-done((bf16[1152,128]{1,0:T(8,128)(2,1)S(1)}, bf16[1152,128]{1,0:T(8,128)(2,1)S(1)}, u32[]{:S(2)}, u32[]{:S(2)}) %collective-permute-start.13) | collective-permute-done | bytes 294944 | tf_op jit(solution)/shard_map/ppermute | solution.py:196
  45.8 0.1 add_convert_fusion.7
  45.8 0.8 %collective-permute-start.15 = (bf16[576,128]{1,0:T(8,128)(2,1)S(1)}, bf16[576,128]{1,0:T(8,128)(2,1)S(1)}, u32[]{:S(2)}, u32[]{:S(2)}) collective-permute-start(bf16[576,128]{1,0:T(8,128)(2,1)S(1)} %add_convert_fusion.7), channel_id=1, source_target_pairs={{0,4},{1,5},{2,6},{3,7},{4,0},{5,1},{6,2},{7,3},{8,12},{9,13},{10,... | collective-permute-start | bytes 442376 | tf_op jit(solution)/shard_map/ppermute | solution.py:196
  46.6 1.2 %collective-permute-done.16.refs_12_ = bf16[576,128]{1,0:T(8,128)(2,1)S(1)} collective-permute-done((bf16[576,128]{1,0:T(8,128)(2,1)S(1)}, bf16[576,128]{1,0:T(8,128)(2,1)S(1)}, u32[]{:S(2)}, u32[]{:S(2)}) %collective-permute-start.16) | collective-permute-done | bytes 147488 | tf_op jit(solution)/shard_map/ppermute | solution.py:196
  47.8 0.4 collective-permute-start.18
  48.2 0.1 add_convert_fusion.10
  48.3 2.9 %collective-permute-start.14 = (bf16[432,128]{1,0:T(8,128)(2,1)S(1)}, bf16[432,128]{1,0:T(8,128)(2,1)S(1)}, u32[]{:S(2)}, u32[]{:S(2)}) collective-permute-start(bf16[432,128]{1,0:T(8,128)(2,1)S(1)} %add_convert_fusion.10), channel_id=1, source_target_pairs={{0,8},{1,9},{2,10},{3,11},{4,12},{5,13},{6,14},{7,15},{8,0},{9,1},... | collective-permute-start | bytes 331784 | tf_op jit(solution)/shard_map/ppermute | solution.py:196
  51.2 2.3 %collective-permute-done.15.refs_8_ = bf16[576,128]{1,0:T(8,128)(2,1)S(1)} collective-permute-done((bf16[576,128]{1,0:T(8,128)(2,1)S(1)}, bf16[576,128]{1,0:T(8,128)(2,1)S(1)}, u32[]{:S(2)}, u32[]{:S(2)}) %collective-permute-start.15) | collective-permute-done | bytes 147488 | tf_op jit(solution)/shard_map/ppermute | solution.py:196
  53.6 2.2 %collective-permute-start.17 = (bf16[288,128]{1,0:T(8,128)(2,1)S(1)}, bf16[288,128]{1,0:T(8,128)(2,1)S(1)}, u32[]{:S(2)}, u32[]{:S(2)}) collective-permute-start(bf16[288,128]{1,0:T(8,128)(2,1)S(1)} %add_convert_fusion.12), channel_id=1, source_target_pairs={{0,8},{1,9},{2,10},{3,11},{4,12},{5,13},{6,14},{7,15},{8,0},{9,1},... | collective-permute-start | bytes 221192 | tf_op jit(solution)/shard_map/ppermute | solution.py:196
  55.8 1.4 %collective-permute-start.19 = (bf16[144,128]{1,0:T(8,128)(2,1)S(1)}, bf16[144,128]{1,0:T(8,128)(2,1)S(1)}, u32[]{:S(2)}, u32[]{:S(2)}) collective-permute-start(bf16[144,128]{1,0:T(8,128)(2,1)S(1)} %add_convert_fusion.14), channel_id=1, source_target_pairs={{0,8},{1,9},{2,10},{3,11},{4,12},{5,13},{6,14},{7,15},{8,0},{9,1},... | collective-permute-start | bytes 110600 | tf_op jit(solution)/shard_map/ppermute | solution.py:196
  57.2 0.8 %shard_map.115 = bf16[1,69,1536]{2,1,0:T(8,128)(2,1)} custom-call(f32[3456,128]{1,0:T(8,128)S(1)} %get-tuple-element.42.refs_0_, bf16[3456,128]{1,0:T(8,128)(2,1)S(1)} %collective-permute-done.refs_1_, bf16[2016,128]{1,0:T(8,128)(2,1)S(1)} %collective-permute-done.2.refs_2_, bf16[1008,128]{1,0:T(8,128)(2,1)S(1)} %collective-permute-done.4.refs_3_, ...), custom_call_target="tpu_custom_call" | custom-call | tf_op jit(solution)/shard_map/pallas_call | solution.py:261
  58.1 2.6 %collective-permute-done.19.refs_14_ = bf16[144,128]{1,0:T(8,128)(2,1)S(1)} collective-permute-done((bf16[144,128]{1,0:T(8,128)(2,1)S(1)}, bf16[144,128]{1,0:T(8,128)(2,1)S(1)}, u32[]{:S(2)}, u32[]{:S(2)}) %collective-permute-start.19) | collective-permute-done | bytes 36896 | tf_op jit(solution)/shard_map/ppermute | solution.py:196
  60.7 0.8 %shard_map.116 = bf16[1,69,1536]{2,1,0:T(8,128)(2,1)} custom-call(f32[3456,128]{1,0:T(8,128)S(1)} %get-tuple-element.57.refs_0_.refs_5_.refs_10_, bf16[3456,128]{1,0:T(8,128)(2,1)S(1)} %collective-permute-done.9.refs_1_.refs_6_.refs_11_, bf16[1728,128]{1,0:T(8,128)(2,1)S(1)} %collective-permute-done.11.refs_2_, ...), custom_call_target="tpu_custom_call" | custom-call | tf_op jit(solution)/shard_map/pallas_call | solution.py:261
  (14 shorter events, 0.2 us)
Async XLA Ops:
  5.6 2.6 %collective-permute-start.1 = (bf16[3456,128]{1,0:T(8,128)(2,1)S(1)}, bf16[3456,128]{1,0:T(8,128)(2,1)S(1)}, u32[]{:S(2)}, u32[]{:S(2)}) collective-permute-start(bf16[3456,128]{1,0:T(8,128)(2,1)S(1)} %get-tuple-element.39), channel_id=1, source_target_pairs={{0,1},{1,0},{2,3},{3,2},{4,5},{5,4},{6,7},{7,6},{8,9},{9,8},{10,11... | collective-permute-start | bytes 2654216 | tf_op jit(solution)/shard_map/ppermute | solution.py:196
  6.1 6.8 %collective-permute-start = (bf16[3456,128]{1,0:T(8,128)(2,1)S(1)}, bf16[3456,128]{1,0:T(8,128)(2,1)S(1)}, u32[]{:S(2)}, u32[]{:S(2)}) collective-permute-start(bf16[3456,128]{1,0:T(8,128)(2,1)S(1)} %get-tuple-element.37), channel_id=1, source_target_pairs={{0,1},{1,0},{2,3},{3,2},{4,5},{5,4},{6,7},{7,6},{8,9},{9,8},{10,11... | collective-permute-start | bytes 2654216 | tf_op jit(solution)/shard_map/ppermute | solution.py:196
  8.2 11.9 %collective-permute-start.3 = (bf16[1440,128]{1,0:T(8,128)(2,1)S(1)}, bf16[1440,128]{1,0:T(8,128)(2,1)S(1)}, u32[]{:S(2)}, u32[]{:S(2)}) collective-permute-start(bf16[1440,128]{1,0:T(8,128)(2,1)S(1)} %add_convert_fusion.2), channel_id=1, source_target_pairs={{0,4},{1,5},{2,6},{3,7},{4,0},{5,1},{6,2},{7,3},{8,12},{9,13},{10,... | collective-permute-start | bytes 1105928 | tf_op jit(solution)/shard_map/ppermute | solution.py:196
  11.3 14.7 %collective-permute-start.2 = (bf16[2016,128]{1,0:T(8,128)(2,1)S(1)}, bf16[2016,128]{1,0:T(8,128)(2,1)S(1)}, u32[]{:S(2)}, u32[]{:S(2)}) collective-permute-start(bf16[2016,128]{1,0:T(8,128)(2,1)S(1)} %add_convert_fusion), channel_id=1, source_target_pairs={{0,2},{1,3},{2,0},{3,1},{4,6},{5,7},{6,4},{7,5},{8,10},{9,11},{10,... | collective-permute-start | bytes 1548296 | tf_op jit(solution)/shard_map/ppermute | solution.py:196
  17.9 8.3 %collective-permute-start.6 = (bf16[1728,128]{1,0:T(8,128)(2,1)S(1)}, bf16[1728,128]{1,0:T(8,128)(2,1)S(1)}, u32[]{:S(2)}, u32[]{:S(2)}) collective-permute-start(bf16[1728,128]{1,0:T(8,128)(2,1)S(1)} %get-tuple-element.75), channel_id=1, source_target_pairs={{0,1},{1,0},{2,3},{3,2},{4,5},{5,4},{6,7},{7,6},{8,9},{9,8},{10,11... | collective-permute-start | bytes 1327112 | tf_op jit(solution)/shard_map/ppermute | solution.py:196
  17.9 15.6 %collective-permute-start.10 = (bf16[1728,128]{1,0:T(8,128)(2,1)S(1)}, bf16[1728,128]{1,0:T(8,128)(2,1)S(1)}, u32[]{:S(2)}, u32[]{:S(2)}) collective-permute-start(bf16[1728,128]{1,0:T(8,128)(2,1)S(1)} %get-tuple-element.74), channel_id=1, source_target_pairs={{0,1},{1,0},{2,3},{3,2},{4,5},{5,4},{6,7},{7,6},{8,9},{9,8},{10,11... | collective-permute-start | bytes 1327112 | tf_op jit(solution)/shard_map/ppermute | solution.py:196
  18.4 20.0 %collective-permute-start.9 = (bf16[3456,128]{1,0:T(8,128)(2,1)S(1)}, bf16[3456,128]{1,0:T(8,128)(2,1)S(1)}, u32[]{:S(2)}, u32[]{:S(2)}) collective-permute-start(bf16[3456,128]{1,0:T(8,128)(2,1)S(1)} %get-tuple-element.54), channel_id=1, source_target_pairs={{0,1},{1,0},{2,3},{3,2},{4,5},{5,4},{6,7},{7,6},{8,9},{9,8},{10,11... | collective-permute-start | bytes 2654216 | tf_op jit(solution)/shard_map/ppermute | solution.py:196
  20.2 9.8 %collective-permute-start.5 = (bf16[720,128]{1,0:T(8,128)(2,1)S(1)}, bf16[720,128]{1,0:T(8,128)(2,1)S(1)}, u32[]{:S(2)}, u32[]{:S(2)}) collective-permute-start(bf16[720,128]{1,0:T(8,128)(2,1)S(1)} %add_convert_fusion.6), channel_id=1, source_target_pairs={{0,2},{1,3},{2,0},{3,1},{4,6},{5,7},{6,4},{7,5},{8,10},{9,11},{10,... | collective-permute-start | bytes 552968 | tf_op jit(solution)/shard_map/ppermute | solution.py:196
  26.1 7.4 %collective-permute-start.4 = (bf16[1008,128]{1,0:T(8,128)(2,1)S(1)}, bf16[1008,128]{1,0:T(8,128)(2,1)S(1)}, u32[]{:S(2)}, u32[]{:S(2)}) collective-permute-start(bf16[1008,128]{1,0:T(8,128)(2,1)S(1)} %add_convert_fusion.4), channel_id=1, source_target_pairs={{0,4},{1,5},{2,6},{3,7},{4,0},{5,1},{6,2},{7,3},{8,12},{9,13},{10,... | collective-permute-start | bytes 774152 | tf_op jit(solution)/shard_map/ppermute | solution.py:196
  26.3 13.1 %collective-permute-start.11 = (bf16[1728,128]{1,0:T(8,128)(2,1)S(1)}, bf16[1728,128]{1,0:T(8,128)(2,1)S(1)}, u32[]{:S(2)}, u32[]{:S(2)}) collective-permute-start(bf16[1728,128]{1,0:T(8,128)(2,1)S(1)} %add_convert_fusion.1), channel_id=1, source_target_pairs={{0,2},{1,3},{2,0},{3,1},{4,6},{5,7},{6,4},{7,5},{8,10},{9,11},{10,... | collective-permute-start | bytes 1327112 | tf_op jit(solution)/shard_map/ppermute | solution.py:196
  30.0 27.2 %collective-permute-start.8 = (bf16[360,128]{1,0:T(8,128)(2,1)S(1)}, bf16[360,128]{1,0:T(8,128)(2,1)S(1)}, u32[]{:S(2)}, u32[]{:S(2)}) collective-permute-start(bf16[360,128]{1,0:T(8,128)(2,1)S(1)} %get-tuple-element.71), channel_id=1, source_target_pairs={{0,8},{1,9},{2,10},{3,11},{4,12},{5,13},{6,14},{7,15},{8,0},{9,1},... | collective-permute-start | bytes 276488 | tf_op jit(solution)/shard_map/ppermute | solution.py:196
  33.6 12.1 %collective-permute-start.13 = (bf16[1152,128]{1,0:T(8,128)(2,1)S(1)}, bf16[1152,128]{1,0:T(8,128)(2,1)S(1)}, u32[]{:S(2)}, u32[]{:S(2)}) collective-permute-start(bf16[1152,128]{1,0:T(8,128)(2,1)S(1)} %add_convert_fusion.3), channel_id=1, source_target_pairs={{0,2},{1,3},{2,0},{3,1},{4,6},{5,7},{6,4},{7,5},{8,10},{9,11},{10,... | collective-permute-start | bytes 884744 | tf_op jit(solution)/shard_map/ppermute | solution.py:196
  35.3 22.0 %collective-permute-start.7 = (bf16[504,128]{1,0:T(8,128)(2,1)S(1)}, bf16[504,128]{1,0:T(8,128)(2,1)S(1)}, u32[]{:S(2)}, u32[]{:S(2)}) collective-permute-start(bf16[504,128]{1,0:T(8,128)(2,1)S(1)} %add_convert_fusion.9), channel_id=1, source_target_pairs={{0,8},{1,9},{2,10},{3,11},{4,12},{5,13},{6,14},{7,15},{8,0},{9,1},... | collective-permute-start | bytes 387080 | tf_op jit(solution)/shard_map/ppermute | solution.py:196
  39.5 8.7 %collective-permute-start.12 = (bf16[864,128]{1,0:T(8,128)(2,1)S(1)}, bf16[864,128]{1,0:T(8,128)(2,1)S(1)}, u32[]{:S(2)}, u32[]{:S(2)}) collective-permute-start(bf16[864,128]{1,0:T(8,128)(2,1)S(1)} %add_convert_fusion.5), channel_id=1, source_target_pairs={{0,4},{1,5},{2,6},{3,7},{4,0},{5,1},{6,2},{7,3},{8,12},{9,13},{10,... | collective-permute-start | bytes 663560 | tf_op jit(solution)/shard_map/ppermute | solution.py:196
  41.7 6.1 %collective-permute-start.16 = (bf16[576,128]{1,0:T(8,128)(2,1)S(1)}, bf16[576,128]{1,0:T(8,128)(2,1)S(1)}, u32[]{:S(2)}, u32[]{:S(2)}) collective-permute-start(bf16[576,128]{1,0:T(8,128)(2,1)S(1)} %add_convert_fusion.8), channel_id=1, source_target_pairs={{0,2},{1,3},{2,0},{3,1},{4,6},{5,7},{6,4},{7,5},{8,10},{9,11},{10,... | collective-permute-start | bytes 442376 | tf_op jit(solution)/shard_map/ppermute | solution.py:196
  45.8 7.7 %collective-permute-start.15 = (bf16[576,128]{1,0:T(8,128)(2,1)S(1)}, bf16[576,128]{1,0:T(8,128)(2,1)S(1)}, u32[]{:S(2)}, u32[]{:S(2)}) collective-permute-start(bf16[576,128]{1,0:T(8,128)(2,1)S(1)} %add_convert_fusion.7), channel_id=1, source_target_pairs={{0,4},{1,5},{2,6},{3,7},{4,0},{5,1},{6,2},{7,3},{8,12},{9,13},{10,... | collective-permute-start | bytes 442376 | tf_op jit(solution)/shard_map/ppermute | solution.py:196
  47.8 7.9 %collective-permute-start.18 = (bf16[288,128]{1,0:T(8,128)(2,1)S(1)}, bf16[288,128]{1,0:T(8,128)(2,1)S(1)}, u32[]{:S(2)}, u32[]{:S(2)}) collective-permute-start(bf16[288,128]{1,0:T(8,128)(2,1)S(1)} %add_convert_fusion.13), channel_id=1, source_target_pairs={{0,4},{1,5},{2,6},{3,7},{4,0},{5,1},{6,2},{7,3},{8,12},{9,13},{10,... | collective-permute-start | bytes 221192 | tf_op jit(solution)/shard_map/ppermute | solution.py:196
  48.3 12.5 %collective-permute-start.14 = (bf16[432,128]{1,0:T(8,128)(2,1)S(1)}, bf16[432,128]{1,0:T(8,128)(2,1)S(1)}, u32[]{:S(2)}, u32[]{:S(2)}) collective-permute-start(bf16[432,128]{1,0:T(8,128)(2,1)S(1)} %add_convert_fusion.10), channel_id=1, source_target_pairs={{0,8},{1,9},{2,10},{3,11},{4,12},{5,13},{6,14},{7,15},{8,0},{9,1},... | collective-permute-start | bytes 331784 | tf_op jit(solution)/shard_map/ppermute | solution.py:196
  53.6 7.1 %collective-permute-start.17 = (bf16[288,128]{1,0:T(8,128)(2,1)S(1)}, bf16[288,128]{1,0:T(8,128)(2,1)S(1)}, u32[]{:S(2)}, u32[]{:S(2)}) collective-permute-start(bf16[288,128]{1,0:T(8,128)(2,1)S(1)} %add_convert_fusion.12), channel_id=1, source_target_pairs={{0,8},{1,9},{2,10},{3,11},{4,12},{5,13},{6,14},{7,15},{8,0},{9,1},... | collective-permute-start | bytes 221192 | tf_op jit(solution)/shard_map/ppermute | solution.py:196
  55.8 4.9 %collective-permute-start.19 = (bf16[144,128]{1,0:T(8,128)(2,1)S(1)}, bf16[144,128]{1,0:T(8,128)(2,1)S(1)}, u32[]{:S(2)}, u32[]{:S(2)}) collective-permute-start(bf16[144,128]{1,0:T(8,128)(2,1)S(1)} %add_convert_fusion.14), channel_id=1, source_target_pairs={{0,8},{1,9},{2,10},{3,11},{4,12},{5,13},{6,14},{7,15},{8,0},{9,1},... | collective-permute-start | bytes 110600 | tf_op jit(solution)/shard_map/ppermute | solution.py:196

commit v5 on v4

--- a/solution.py
+++ b/solution.py
@@ -208,9 +208,8 @@
         self.base = self.devices // 4 * chunk[0] * pitch
         self.length = self.devices // 4 * (chunk[1] - chunk[0]) * pitch
 
-    def first(self, terms, at):
-        base = self.base - at
-        self.total = added(terms, base, base + self.length).astype(jnp.bfloat16)
+    def first(self, terms):
+        self.total = added(terms, self.base, self.base + self.length).astype(jnp.bfloat16)
 
     def second(self):
         self.got = [exchange(self.total, self.slots[1][1], self.devices)]
@@ -268,14 +267,13 @@
     )(*flat)
 
 
-def plan(tiles, bits):
-    later = tuple((bit,) for bit in range(3, bits))
-    straight = ((0,), (1,), (2,)) + later
-    turned = ((0,), (2,), (1,)) + later
-    half, more, most = tiles // 2, (tiles + 2) * 7 // 14, tiles * 5 // 6
+def plan(tiles):
+    straight = ((0,), (1,), (2,), (3,))
+    turned = ((0,), (2,), (3,), (1,))
+    half, some, most = tiles // 2, tiles * 5 // 12, tiles * 3 // 4
     return (
-        [(0, more, straight), (more, tiles, turned)],
-        [(0, half, straight), (half, most, straight), (most, tiles, straight)],
+        [(0, half, straight), (half, tiles, turned)],
+        [(0, some, straight), (some, most, straight), (most, tiles, straight)],
     )
 
 
@@ -295,7 +293,7 @@
     one, two = remaps
     devices = 1 << bits
     pitch = round_up(one[-1][1], 8)
-    plans = plan(one[-1][2] // LANES, bits)
+    plans = plan(one[-1][2] // LANES)
     ones, twos = [[Chain(chunk, bits, pitch) for chunk in chunks] for chunks in plans]
     order = Order()
 
@@ -309,50 +307,59 @@
                 chain.finish()
         order.before([chain.sent for chain in chains])
 
-    def summed(line, terms, at):
+    def summed(line, terms):
         terms = order.after(terms)
         for chain in line:
-            chain.first(terms, at)
+            chain.first(terms)
         order.before([chain.total for chain in line])
 
     def both_cores(keep, send):
         return [keep, exchange(send, 1, devices)]
 
-    keep, send, keep_on, send_on = products(one, plans[0], bits)
+    def tied(first, second):
+        return lax.optimization_barrier((first, second))
+
+    made = products(one, plans[0], bits)
+    cotangent, made = tied(two[0], made)
+    keep, send, keep_on, send_on = made
     on = both_cores(keep_on, send_on)
     rest = both_cores(keep, send)
-    summed(ones, on, 0)
+    keep, send, keep_on, send_on = products((cotangent,) + two[1:], plans[1], bits)
+    order.before(keep)
+    late_on = both_cores(keep_on, send_on)
+    late = both_cores(keep, send)
+    across, turned = ones
+    early, middle, last = twos
+
+    summed(ones, on)
     for chain in ones:
         chain.second()
     rest = order.after(rest)
     order.before(rest)
     for chain in ones:
         chain.rest(rest)
-    keep, send, keep_on, send_on = products((order.after(two[0]),) + two[1:], plans[1], bits)
-    cut = devices // 4 * plans[1][0][1] * pitch
-    on = [both_cores(keep_on[:cut], send_on[:cut]), both_cores(keep_on[cut:], send_on[cut:])]
-    late = both_cores(keep, send)
-    step(ones[1])
-    step(ones[0])
-    summed(twos[:1], on[0], 0)
-    twos[0].second()
-    step(ones[1])
-    step(ones[0])
-    summed(twos[1:], on[1], cut)
-    twos[1].second()
+    summed(twos, late_on)
+    early.second()
     late = order.after(late)
     order.before(late)
     for chain in twos:
         chain.rest(late)
-    step(twos[0])
-    twos[2].total = order.after(twos[2].total)
-    twos[2].second()
-    step(twos[1])
-    step(twos[0])
-    step(*ones)
-    step(twos[2])
-    step(twos[1])
-    step(twos[2])
+    step(across)
+    step(turned)
+    middle.total = order.after(middle.total)
+    middle.second()
+    step(across)
+    step(early)
+    last.total = order.after(last.total)
+    last.second()
+    step(middle)
+    step(turned)
+    step(early)
+    step(across)
+    step(last)
+    step(middle)
+    step(last)
+    step(turned)
     step(*twos)
     return [final_sum(line, remap[-1], pitch) for line, remap in zip((ones, twos), remaps)]
 
@@ -366,7 +373,7 @@
     bits = devices.bit_length() - 1
     tiles = max(latlon.shape[2], healpix.shape[2]) // LANES
     size = devices * tiles * round_up(latlon.shape[1], 8) * LANES * 4
-    if devices == 1 << bits and bits > 2 and size <= ACC_LIMIT:
+    if devices == 1 << bits and bits == 4 and size <= ACC_LIMIT:
         return tuple(bit_remaps(remaps, bits))
     return tuple(slot_remap(*remap) for remap in remaps)
 

time: 61.7 us -> 61.5 us (level)
  starting transfers between devices: 28.5 us -> 21.7 us
  waiting for transfers between devices: 19.6 us -> 26.2 us
    ppermute x20 -> x19, starting transfers between devices: 28.5 us -> 21.7 us  [exchange(): lax.ppermute(value, 'curve', [(at, at ^ mask) for at in range(devices)])]
    ppermute x20 -> x19, waiting for transfers between devices: 19.6 us -> 26.2 us  [exchange(): lax.ppermute(value, 'curve', [(at, at ^ mask) for at in range(devices)])]
  transfers between devices with their start and end apart: 20 -> 19, of which waited for: 10 -> 7; matrix products, arithmetic and copies ran while one was open for 2% -> 2% of each run, Pallas kernels for 9% -> 9%
where the time goes in v5:
time: 61.5 us; the launch traced here: 61.1 us
  waiting for transfers between devices  26.2 us (43%)
  starting transfers between devices  21.7 us (35%)
  Pallas kernels  11.4 us (19%)
  other arithmetic  1.02 us (2%)
  between operations  0.74 us (1%)
    ppermute x19, waiting for transfers between devices, exchange(): lax.ppermute(value, 'curve', [(at, at ^ mask) for at in range(devices)])  26.2 us
    ppermute x19, starting transfers between devices, exchange(): lax.ppermute(value, 'curve', [(at, at ^ mask) for at in range(devices)])  21.7 us
    pallas_call x2, Pallas kernels, products(): pl.pallas_call(functools.partial(product_kernel, bits, channels, pitch, c...  9.78 us
    pallas_call x2, Pallas kernels, final_sum(): pl.pallas_call(functools.partial(final_kernel, like_shape[1], pitch, part...  1.66 us
  transfers between devices with their start and end apart: 19, of which 7 were waited for; matrix products, arithmetic and copies ran while one was open for 2% of the time, Pallas kernels for 9%

profile of v5, /device:TPU:0, one launch (start us, length us, event | category | flops | bytes accessed | tf_op | source)
XLA Modules:
  0.0 61.1 jit_solution(17235429278399121455)
XLA Ops:
  0.6 4.9 %shard_map.113 = (f32[3456,128]{1,0:T(8,128)S(1)}, bf16[3456,128]{1,0:T(8,128)(2,1)S(1)}, f32[3456,128]{1,0:T(8,128)S(1)}, bf16[3456,128]{1,0:T(8,128)(2,1)S(1)}) custom-call(s32[144]{0:T(256)} %source_hbm.2, s32[144]{0:T(256)} %target_hbm.2, s32[1,16]{1,0:T(1,128)} %counts_hbm.2, bf16[1,69,1536]{2,1,0:T(8,128)(2,1)} %x_hbm.1, bf16[144,128,128]{2,1,0:T(8,128)(2,1)} %w_hbm.2), custom_call_target="tpu_custom_call" | custom-call | flops 325582848 | bytes 10027008 | tf_op jit(solution)/shard_map/pallas_call | solution.py:170
  5.5 0.5 collective-permute-start.1
  6.1 0.1 collective-permute-start
  6.1 4.9 %shard_map.114 = (f32[3456,128]{1,0:T(8,128)S(1)}, bf16[3456,128]{1,0:T(8,128)(2,1)S(1)}, f32[3456,128]{1,0:T(8,128)S(1)}, bf16[3456,128]{1,0:T(8,128)(2,1)S(1)}) custom-call(s32[144]{0:T(256)} %source_hbm.3, s32[144]{0:T(256)} %target_hbm.3, s32[1,16]{1,0:T(1,128)} %counts_hbm.3, bf16[1,69,1536]{2,1,0:T(8,128)(2,1)} %x_hbm.2, bf16[144,128,128]{2,1,0:T(8,128)(2,1)} %w_hbm.3), custom_call_target="tpu_custom_call" | custom-call | flops 325582848 | bytes 10027008 | tf_op jit(solution)/shard_map/pallas_call | solution.py:170
  11.0 0.5 collective-permute-start.4
  11.5 0.1 collective-permute-start.3
  11.6 0.2 add_convert_fusion
  11.8 3.1 %collective-permute-start.6 = (bf16[1728,128]{1,0:T(8,128)(2,1)S(1)}, bf16[1728,128]{1,0:T(8,128)(2,1)S(1)}, u32[]{:S(2)}, u32[]{:S(2)}) collective-permute-start(bf16[1728,128]{1,0:T(8,128)(2,1)S(1)} %get-tuple-element.76), channel_id=1, source_target_pairs={{0,4},{1,5},{2,6},{3,7},{4,0},{5,1},{6,2},{7,3},{8,12},{9,13},{10,... | collective-permute-start | bytes 1327112 | tf_op jit(solution)/shard_map/ppermute | solution.py:196
  14.9 1.5 %collective-permute-start.2 = (bf16[1728,128]{1,0:T(8,128)(2,1)S(1)}, bf16[1728,128]{1,0:T(8,128)(2,1)S(1)}, u32[]{:S(2)}, u32[]{:S(2)}) collective-permute-start(bf16[1728,128]{1,0:T(8,128)(2,1)S(1)} %get-tuple-element.77), channel_id=1, source_target_pairs={{0,2},{1,3},{2,0},{3,1},{4,6},{5,7},{6,4},{7,5},{8,10},{9,11},{10,... | collective-permute-start | bytes 1327112 | tf_op jit(solution)/shard_map/ppermute | solution.py:196
  16.4 0.1 add_convert_fusion.3
  16.5 0.1 add_convert_fusion.2
  16.6 0.6 collective-permute-start.8
  17.1 0.1 add_convert_fusion.6
  17.2 0.0 collective-permute-done.3.refs_1_.refs_6_.refs_11_
  17.2 10.7 %collective-permute-done.2.refs_2_ = bf16[1728,128]{1,0:T(8,128)(2,1)S(1)} collective-permute-done((bf16[1728,128]{1,0:T(8,128)(2,1)S(1)}, bf16[1728,128]{1,0:T(8,128)(2,1)S(1)}, u32[]{:S(2)}, u32[]{:S(2)}) %collective-permute-start.2) | collective-permute-done | bytes 442400 | tf_op jit(solution)/shard_map/ppermute | solution.py:196
  27.9 0.1 add_convert_fusion.5
  28.0 0.1 collective-permute-start.5
  28.1 0.0 collective-permute-done.6.refs_7_
  28.1 0.1 add_convert_fusion.4
  28.2 3.1 %collective-permute-start.10 = (bf16[864,128]{1,0:T(8,128)(2,1)S(1)}, bf16[864,128]{1,0:T(8,128)(2,1)S(1)}, u32[]{:S(2)}, u32[]{:S(2)}) collective-permute-start(bf16[864,128]{1,0:T(8,128)(2,1)S(1)} %add_convert_fusion.4), channel_id=1, source_target_pairs={{0,8},{1,9},{2,10},{3,11},{4,12},{5,13},{6,14},{7,15},{8,0},{9,1},... | collective-permute-start | bytes 663560 | tf_op jit(solution)/shard_map/ppermute | solution.py:196
  31.3 1.5 %collective-permute-start.11 = (bf16[1152,128]{1,0:T(8,128)(2,1)S(1)}, bf16[1152,128]{1,0:T(8,128)(2,1)S(1)}, u32[]{:S(2)}, u32[]{:S(2)}) collective-permute-start(bf16[1152,128]{1,0:T(8,128)(2,1)S(1)} %add_convert_fusion.3), channel_id=1, source_target_pairs={{0,2},{1,3},{2,0},{3,1},{4,6},{5,7},{6,4},{7,5},{8,10},{9,11},{10,... | collective-permute-start | bytes 884744 | tf_op jit(solution)/shard_map/ppermute | solution.py:196
  32.8 4.6 %collective-permute-done.5.refs_3_ = bf16[864,128]{1,0:T(8,128)(2,1)S(1)} collective-permute-done((bf16[864,128]{1,0:T(8,128)(2,1)S(1)}, bf16[864,128]{1,0:T(8,128)(2,1)S(1)}, u32[]{:S(2)}, u32[]{:S(2)}) %collective-permute-start.5) | collective-permute-done | bytes 221216 | tf_op jit(solution)/shard_map/ppermute | solution.py:196
  37.4 0.1 add_convert_fusion.11
  37.5 1.7 %collective-permute-start.7 = (bf16[432,128]{1,0:T(8,128)(2,1)S(1)}, bf16[432,128]{1,0:T(8,128)(2,1)S(1)}, u32[]{:S(2)}, u32[]{:S(2)}) collective-permute-start(bf16[432,128]{1,0:T(8,128)(2,1)S(1)} %add_convert_fusion.11), channel_id=1, source_target_pairs={{0,8},{1,9},{2,10},{3,11},{4,12},{5,13},{6,14},{7,15},{8,0},{9,1},... | collective-permute-start | bytes 331784 | tf_op jit(solution)/shard_map/ppermute | solution.py:196
  39.2 0.0 collective-permute-done.8.refs_2_
  39.2 0.1 add_convert_fusion.7
  39.2 0.2 collective-permute-start.9
  39.4 1.8 %collective-permute-start.13 = (bf16[864,128]{1,0:T(8,128)(2,1)S(1)}, bf16[864,128]{1,0:T(8,128)(2,1)S(1)}, u32[]{:S(2)}, u32[]{:S(2)}) collective-permute-start(bf16[864,128]{1,0:T(8,128)(2,1)S(1)} %add_convert_fusion.6), channel_id=1, source_target_pairs={{0,2},{1,3},{2,0},{3,1},{4,6},{5,7},{6,4},{7,5},{8,10},{9,11},{10,... | collective-permute-start | bytes 663560 | tf_op jit(solution)/shard_map/ppermute | solution.py:196
  41.2 1.0 %collective-permute-done.11.refs_7_ = bf16[1152,128]{1,0:T(8,128)(2,1)S(1)} collective-permute-done((bf16[1152,128]{1,0:T(8,128)(2,1)S(1)}, bf16[1152,128]{1,0:T(8,128)(2,1)S(1)}, u32[]{:S(2)}, u32[]{:S(2)}) %collective-permute-start.11) | collective-permute-done | bytes 294944 | tf_op jit(solution)/shard_map/ppermute | solution.py:196
  42.1 0.1 add_convert_fusion.8
  42.2 0.7 %collective-permute-start.15 = (bf16[576,128]{1,0:T(8,128)(2,1)S(1)}, bf16[576,128]{1,0:T(8,128)(2,1)S(1)}, u32[]{:S(2)}, u32[]{:S(2)}) collective-permute-start(bf16[576,128]{1,0:T(8,128)(2,1)S(1)} %add_convert_fusion.8), channel_id=1, source_target_pairs={{0,4},{1,5},{2,6},{3,7},{4,0},{5,1},{6,2},{7,3},{8,12},{9,13},{10,... | collective-permute-start | bytes 442376 | tf_op jit(solution)/shard_map/ppermute | solution.py:196
  42.9 0.0 collective-permute-done.10.refs_8_
  42.9 0.1 add_convert_fusion.10
  43.0 1.6 %collective-permute-start.12 = (bf16[432,128]{1,0:T(8,128)(2,1)S(1)}, bf16[432,128]{1,0:T(8,128)(2,1)S(1)}, u32[]{:S(2)}, u32[]{:S(2)}) collective-permute-start(bf16[432,128]{1,0:T(8,128)(2,1)S(1)} %add_convert_fusion.10), channel_id=1, source_target_pairs={{0,2},{1,3},{2,0},{3,1},{4,6},{5,7},{6,4},{7,5},{8,10},{9,11},{10,... | collective-permute-start | bytes 331784 | tf_op jit(solution)/shard_map/ppermute | solution.py:196
  44.6 4.0 %collective-permute-done.9.refs_3_ = bf16[720,128]{1,0:T(8,128)(2,1)S(1)} collective-permute-done((bf16[720,128]{1,0:T(8,128)(2,1)S(1)}, bf16[720,128]{1,0:T(8,128)(2,1)S(1)}, u32[]{:S(2)}, u32[]{:S(2)}) %collective-permute-start.9) | collective-permute-done | bytes 184352 | tf_op jit(solution)/shard_map/ppermute | solution.py:196
  48.5 0.1 add_convert_fusion.12
  48.6 0.1 collective-permute-start.16
  48.7 0.1 add_convert_fusion.9
  48.7 2.8 %collective-permute-start.14 = (bf16[432,128]{1,0:T(8,128)(2,1)S(1)}, bf16[432,128]{1,0:T(8,128)(2,1)S(1)}, u32[]{:S(2)}, u32[]{:S(2)}) collective-permute-start(bf16[432,128]{1,0:T(8,128)(2,1)S(1)} %add_convert_fusion.9), channel_id=1, source_target_pairs={{0,4},{1,5},{2,6},{3,7},{4,0},{5,1},{6,2},{7,3},{8,12},{9,13},{10,... | collective-permute-start | bytes 331784 | tf_op jit(solution)/shard_map/ppermute | solution.py:196
  51.6 0.2 collective-permute-start.17
  51.9 3.3 %collective-permute-done.14.refs_13_ = bf16[432,128]{1,0:T(8,128)(2,1)S(1)} collective-permute-done((bf16[432,128]{1,0:T(8,128)(2,1)S(1)}, bf16[432,128]{1,0:T(8,128)(2,1)S(1)}, u32[]{:S(2)}, u32[]{:S(2)}) %collective-permute-start.14) | collective-permute-done | bytes 110624 | tf_op jit(solution)/shard_map/ppermute | solution.py:196
  55.2 1.6 %collective-permute-start.18 = (bf16[216,128]{1,0:T(8,128)(2,1)S(1)}, bf16[216,128]{1,0:T(8,128)(2,1)S(1)}, u32[]{:S(2)}, u32[]{:S(2)}) collective-permute-start(bf16[216,128]{1,0:T(8,128)(2,1)S(1)} %add_convert_fusion.14), channel_id=1, source_target_pairs={{0,8},{1,9},{2,10},{3,11},{4,12},{5,13},{6,14},{7,15},{8,0},{9,1},... | collective-permute-start | bytes 165896 | tf_op jit(solution)/shard_map/ppermute | solution.py:196
  56.8 0.0 collective-permute-done.7.refs_4_
  56.8 0.0 collective-permute-done.12.refs_9_
  56.8 0.8 %shard_map.115 = bf16[1,69,1536]{2,1,0:T(8,128)(2,1)} custom-call(f32[3456,128]{1,0:T(8,128)S(1)} %get-tuple-element.51.refs_0_.refs_5_, bf16[3456,128]{1,0:T(8,128)(2,1)S(1)} %collective-permute-done.refs_1_.refs_6_, bf16[1728,128]{1,0:T(8,128)(2,1)S(1)} %collective-permute-done.2.refs_2_, bf16[864,128]{1,0:T(8,128)(2,1)S(1)} %collective-permute-done.5.refs_3_, ...), custom_call_target="tpu_custom_call" | custom-call | tf_op jit(solution)/shard_map/pallas_call | solution.py:260
  57.6 0.1 collective-permute-done.17.refs_9_
  57.7 2.6 %collective-permute-done.18.refs_14_ = bf16[216,128]{1,0:T(8,128)(2,1)S(1)} collective-permute-done((bf16[216,128]{1,0:T(8,128)(2,1)S(1)}, bf16[216,128]{1,0:T(8,128)(2,1)S(1)}, u32[]{:S(2)}, u32[]{:S(2)}) %collective-permute-start.18) | collective-permute-done | bytes 55328 | tf_op jit(solution)/shard_map/ppermute | solution.py:196
  60.3 0.8 %shard_map.116 = bf16[1,69,1536]{2,1,0:T(8,128)(2,1)} custom-call(f32[3456,128]{1,0:T(8,128)S(1)} %get-tuple-element.58.refs_0_.refs_5_.refs_10_, bf16[3456,128]{1,0:T(8,128)(2,1)S(1)} %collective-permute-done.3.refs_1_.refs_6_.refs_11_, bf16[1440,128]{1,0:T(8,128)(2,1)S(1)} %collective-permute-done.8.refs_2_, ...), custom_call_target="tpu_custom_call" | custom-call | tf_op jit(solution)/shard_map/pallas_call | solution.py:260
  (8 shorter events, 0.1 us)
Async XLA Ops:
  5.5 6.1 %collective-permute-start.1 = (bf16[3456,128]{1,0:T(8,128)(2,1)S(1)}, bf16[3456,128]{1,0:T(8,128)(2,1)S(1)}, u32[]{:S(2)}, u32[]{:S(2)}) collective-permute-start(bf16[3456,128]{1,0:T(8,128)(2,1)S(1)} %get-tuple-element.46), channel_id=1, source_target_pairs={{0,1},{1,0},{2,3},{3,2},{4,5},{5,4},{6,7},{7,6},{8,9},{9,8},{10,11... | collective-permute-start | bytes 2654216 | tf_op jit(solution)/shard_map/ppermute | solution.py:196
  6.1 10.3 %collective-permute-start = (bf16[3456,128]{1,0:T(8,128)(2,1)S(1)}, bf16[3456,128]{1,0:T(8,128)(2,1)S(1)}, u32[]{:S(2)}, u32[]{:S(2)}) collective-permute-start(bf16[3456,128]{1,0:T(8,128)(2,1)S(1)} %get-tuple-element.44), channel_id=1, source_target_pairs={{0,1},{1,0},{2,3},{3,2},{4,5},{5,4},{6,7},{7,6},{8,9},{9,8},{10,11... | collective-permute-start | bytes 2654216 | tf_op jit(solution)/shard_map/ppermute | solution.py:196
  11.0 5.3 %collective-permute-start.4 = (bf16[3456,128]{1,0:T(8,128)(2,1)S(1)}, bf16[3456,128]{1,0:T(8,128)(2,1)S(1)}, u32[]{:S(2)}, u32[]{:S(2)}) collective-permute-start(bf16[3456,128]{1,0:T(8,128)(2,1)S(1)} %get-tuple-element.55), channel_id=1, source_target_pairs={{0,1},{1,0},{2,3},{3,2},{4,5},{5,4},{6,7},{7,6},{8,9},{9,8},{10,11... | collective-permute-start | bytes 2654216 | tf_op jit(solution)/shard_map/ppermute | solution.py:196
  11.5 5.7 %collective-permute-start.3 = (bf16[3456,128]{1,0:T(8,128)(2,1)S(1)}, bf16[3456,128]{1,0:T(8,128)(2,1)S(1)}, u32[]{:S(2)}, u32[]{:S(2)}) collective-permute-start(bf16[3456,128]{1,0:T(8,128)(2,1)S(1)} %get-tuple-element.53), channel_id=1, source_target_pairs={{0,1},{1,0},{2,3},{3,2},{4,5},{5,4},{6,7},{7,6},{8,9},{9,8},{10,11... | collective-permute-start | bytes 2654216 | tf_op jit(solution)/shard_map/ppermute | solution.py:196
  11.8 16.3 %collective-permute-start.6 = (bf16[1728,128]{1,0:T(8,128)(2,1)S(1)}, bf16[1728,128]{1,0:T(8,128)(2,1)S(1)}, u32[]{:S(2)}, u32[]{:S(2)}) collective-permute-start(bf16[1728,128]{1,0:T(8,128)(2,1)S(1)} %get-tuple-element.76), channel_id=1, source_target_pairs={{0,4},{1,5},{2,6},{3,7},{4,0},{5,1},{6,2},{7,3},{8,12},{9,13},{10,... | collective-permute-start | bytes 1327112 | tf_op jit(solution)/shard_map/ppermute | solution.py:196
  14.9 13.1 %collective-permute-start.2 = (bf16[1728,128]{1,0:T(8,128)(2,1)S(1)}, bf16[1728,128]{1,0:T(8,128)(2,1)S(1)}, u32[]{:S(2)}, u32[]{:S(2)}) collective-permute-start(bf16[1728,128]{1,0:T(8,128)(2,1)S(1)} %get-tuple-element.77), channel_id=1, source_target_pairs={{0,2},{1,3},{2,0},{3,1},{4,6},{5,7},{6,4},{7,5},{8,10},{9,11},{10,... | collective-permute-start | bytes 1327112 | tf_op jit(solution)/shard_map/ppermute | solution.py:196
  16.6 22.6 %collective-permute-start.8 = (bf16[1440,128]{1,0:T(8,128)(2,1)S(1)}, bf16[1440,128]{1,0:T(8,128)(2,1)S(1)}, u32[]{:S(2)}, u32[]{:S(2)}) collective-permute-start(bf16[1440,128]{1,0:T(8,128)(2,1)S(1)} %add_convert_fusion.2), channel_id=1, source_target_pairs={{0,2},{1,3},{2,0},{3,1},{4,6},{5,7},{6,4},{7,5},{8,10},{9,11},{10,... | collective-permute-start | bytes 1105928 | tf_op jit(solution)/shard_map/ppermute | solution.py:196
  28.0 9.4 %collective-permute-start.5 = (bf16[864,128]{1,0:T(8,128)(2,1)S(1)}, bf16[864,128]{1,0:T(8,128)(2,1)S(1)}, u32[]{:S(2)}, u32[]{:S(2)}) collective-permute-start(bf16[864,128]{1,0:T(8,128)(2,1)S(1)} %add_convert_fusion.5), channel_id=1, source_target_pairs={{0,4},{1,5},{2,6},{3,7},{4,0},{5,1},{6,2},{7,3},{8,12},{9,13},{10,... | collective-permute-start | bytes 663560 | tf_op jit(solution)/shard_map/ppermute | solution.py:196
  28.2 14.7 %collective-permute-start.10 = (bf16[864,128]{1,0:T(8,128)(2,1)S(1)}, bf16[864,128]{1,0:T(8,128)(2,1)S(1)}, u32[]{:S(2)}, u32[]{:S(2)}) collective-permute-start(bf16[864,128]{1,0:T(8,128)(2,1)S(1)} %add_convert_fusion.4), channel_id=1, source_target_pairs={{0,8},{1,9},{2,10},{3,11},{4,12},{5,13},{6,14},{7,15},{8,0},{9,1},... | collective-permute-start | bytes 663560 | tf_op jit(solution)/shard_map/ppermute | solution.py:196
  31.3 10.9 %collective-permute-start.11 = (bf16[1152,128]{1,0:T(8,128)(2,1)S(1)}, bf16[1152,128]{1,0:T(8,128)(2,1)S(1)}, u32[]{:S(2)}, u32[]{:S(2)}) collective-permute-start(bf16[1152,128]{1,0:T(8,128)(2,1)S(1)} %add_convert_fusion.3), channel_id=1, source_target_pairs={{0,2},{1,3},{2,0},{3,1},{4,6},{5,7},{6,4},{7,5},{8,10},{9,11},{10,... | collective-permute-start | bytes 884744 | tf_op jit(solution)/shard_map/ppermute | solution.py:196
  37.5 19.3 %collective-permute-start.7 = (bf16[432,128]{1,0:T(8,128)(2,1)S(1)}, bf16[432,128]{1,0:T(8,128)(2,1)S(1)}, u32[]{:S(2)}, u32[]{:S(2)}) collective-permute-start(bf16[432,128]{1,0:T(8,128)(2,1)S(1)} %add_convert_fusion.11), channel_id=1, source_target_pairs={{0,8},{1,9},{2,10},{3,11},{4,12},{5,13},{6,14},{7,15},{8,0},{9,1},... | collective-permute-start | bytes 331784 | tf_op jit(solution)/shard_map/ppermute | solution.py:196
  39.2 9.3 %collective-permute-start.9 = (bf16[720,128]{1,0:T(8,128)(2,1)S(1)}, bf16[720,128]{1,0:T(8,128)(2,1)S(1)}, u32[]{:S(2)}, u32[]{:S(2)}) collective-permute-start(bf16[720,128]{1,0:T(8,128)(2,1)S(1)} %add_convert_fusion.7), channel_id=1, source_target_pairs={{0,4},{1,5},{2,6},{3,7},{4,0},{5,1},{6,2},{7,3},{8,12},{9,13},{10,... | collective-permute-start | bytes 552968 | tf_op jit(solution)/shard_map/ppermute | solution.py:196
  39.4 9.3 %collective-permute-start.13 = (bf16[864,128]{1,0:T(8,128)(2,1)S(1)}, bf16[864,128]{1,0:T(8,128)(2,1)S(1)}, u32[]{:S(2)}, u32[]{:S(2)}) collective-permute-start(bf16[864,128]{1,0:T(8,128)(2,1)S(1)} %add_convert_fusion.6), channel_id=1, source_target_pairs={{0,2},{1,3},{2,0},{3,1},{4,6},{5,7},{6,4},{7,5},{8,10},{9,11},{10,... | collective-permute-start | bytes 663560 | tf_op jit(solution)/shard_map/ppermute | solution.py:196
  42.2 9.4 %collective-permute-start.15 = (bf16[576,128]{1,0:T(8,128)(2,1)S(1)}, bf16[576,128]{1,0:T(8,128)(2,1)S(1)}, u32[]{:S(2)}, u32[]{:S(2)}) collective-permute-start(bf16[576,128]{1,0:T(8,128)(2,1)S(1)} %add_convert_fusion.8), channel_id=1, source_target_pairs={{0,4},{1,5},{2,6},{3,7},{4,0},{5,1},{6,2},{7,3},{8,12},{9,13},{10,... | collective-permute-start | bytes 442376 | tf_op jit(solution)/shard_map/ppermute | solution.py:196
  43.0 13.8 %collective-permute-start.12 = (bf16[432,128]{1,0:T(8,128)(2,1)S(1)}, bf16[432,128]{1,0:T(8,128)(2,1)S(1)}, u32[]{:S(2)}, u32[]{:S(2)}) collective-permute-start(bf16[432,128]{1,0:T(8,128)(2,1)S(1)} %add_convert_fusion.10), channel_id=1, source_target_pairs={{0,2},{1,3},{2,0},{3,1},{4,6},{5,7},{6,4},{7,5},{8,10},{9,11},{10,... | collective-permute-start | bytes 331784 | tf_op jit(solution)/shard_map/ppermute | solution.py:196
  48.6 9.0 %collective-permute-start.16 = (bf16[360,128]{1,0:T(8,128)(2,1)S(1)}, bf16[360,128]{1,0:T(8,128)(2,1)S(1)}, u32[]{:S(2)}, u32[]{:S(2)}) collective-permute-start(bf16[360,128]{1,0:T(8,128)(2,1)S(1)} %add_convert_fusion.12), channel_id=1, source_target_pairs={{0,8},{1,9},{2,10},{3,11},{4,12},{5,13},{6,14},{7,15},{8,0},{9,1},... | collective-permute-start | bytes 276488 | tf_op jit(solution)/shard_map/ppermute | solution.py:196
  48.7 6.4 %collective-permute-start.14 = (bf16[432,128]{1,0:T(8,128)(2,1)S(1)}, bf16[432,128]{1,0:T(8,128)(2,1)S(1)}, u32[]{:S(2)}, u32[]{:S(2)}) collective-permute-start(bf16[432,128]{1,0:T(8,128)(2,1)S(1)} %add_convert_fusion.9), channel_id=1, source_target_pairs={{0,4},{1,5},{2,6},{3,7},{4,0},{5,1},{6,2},{7,3},{8,12},{9,13},{10,... | collective-permute-start | bytes 331784 | tf_op jit(solution)/shard_map/ppermute | solution.py:196
  51.6 6.1 %collective-permute-start.17 = (bf16[288,128]{1,0:T(8,128)(2,1)S(1)}, bf16[288,128]{1,0:T(8,128)(2,1)S(1)}, u32[]{:S(2)}, u32[]{:S(2)}) collective-permute-start(bf16[288,128]{1,0:T(8,128)(2,1)S(1)} %add_convert_fusion.13), channel_id=1, source_target_pairs={{0,8},{1,9},{2,10},{3,11},{4,12},{5,13},{6,14},{7,15},{8,0},{9,1},... | collective-permute-start | bytes 221192 | tf_op jit(solution)/shard_map/ppermute | solution.py:196
  55.2 5.1 %collective-permute-start.18 = (bf16[216,128]{1,0:T(8,128)(2,1)S(1)}, bf16[216,128]{1,0:T(8,128)(2,1)S(1)}, u32[]{:S(2)}, u32[]{:S(2)}) collective-permute-start(bf16[216,128]{1,0:T(8,128)(2,1)S(1)} %add_convert_fusion.14), channel_id=1, source_target_pairs={{0,8},{1,9},{2,10},{3,11},{4,12},{5,13},{6,14},{7,15},{8,0},{9,1},... | collective-permute-start | bytes 165896 | tf_op jit(solution)/shard_map/ppermute | solution.py:196

commit v6 on v5

--- a/solution.py
+++ b/solution.py
@@ -60,25 +60,17 @@
     return sum_slots(arrived, arrived_labels, like_shape[2] // weights.shape[1], like_shape)
 
 
-def slots_of(stages):
-    return [[sum(((m >> i) & 1) << bit for i, bit in enumerate(stage)) for m in range(1 << len(stage))]
-            for stage in stages]
-
-
-def owners_in_order(stages):
-    masks = [0]
-    for stage in slots_of(stages):
-        masks = [left + right for left in masks for right in stage]
-    return masks
+EVEN = (0, 1, 2, 3)
+ODD = (0, 2, 1, 3)
 
 
 def product_kernel(
-    bits, channels, pitch, chunks, step_blocks,
+    channels, pitch, chunks, step_blocks,
     source_hbm, target_hbm, counts_hbm, x_hbm, w_hbm, *rest,
 ):
     number = len(chunks)
     outs, (acc, xs, x_in, w, source, target, counts, places, sems) = rest[:4], rest[4:]
-    devices = 1 << bits
+    devices = counts.shape[1]
     steps = w.shape[0] // step_blocks
     me = lax.axis_index("curve")
 
@@ -105,18 +97,14 @@
     for tile in range(xs.shape[0]):
         xs[tile] = jnp.zeros(xs.shape[1:], xs.dtype)
 
-    bases, base = [], 0
-    for chunk, (low, high, stages) in enumerate(chunks):
-        bases.append(base)
-        order = [stages[1], stages[0]] + list(stages[2:])
-        for owner in range(devices):
-            differ = jnp.bitwise_xor(me, owner)
-            place = jnp.int32(0)
-            for stage in order:
-                for bit in reversed(stage):
-                    place = place * 2 + jnp.bitwise_and(jnp.right_shift(differ, bit), 1)
-            places[chunk, owner] = base + place * (high - low) - low
-        base += devices * (high - low)
+    for owner in range(devices):
+        differ = jnp.bitwise_xor(me, owner)
+        first, second, *others = ODD if owner % 2 else EVEN
+        place = jnp.int32(0)
+        for bit in [second, first] + others:
+            place = place * 2 + jnp.bitwise_and(jnp.right_shift(differ, bit), 1)
+        for chunk, (low, high) in enumerate(chunks):
+            places[chunk, owner] = devices * low + place * (high - low) - low
 
     x_copy.wait()
     for tile in range(xs.shape[0]):
@@ -146,21 +134,20 @@
 
     lax.fori_loop(0, steps, some, (jnp.int32(0), counts[0, 0]))
 
-    for base, (low, high, stages) in zip(bases, chunks):
+    quarter = devices // 4
+    for low, high in chunks:
         unit = (high - low) * pitch
-        quarter = devices // 4
 
         @pl.loop(0, quarter)
         def finish(index):
             at = pl.multiple_of(quarter * low * pitch + index * unit, 8)
             for part, ref in enumerate(outs):
-                row = pl.multiple_of((base + part * quarter * (high - low)) * pitch + index * unit, 8)
+                row = pl.multiple_of((devices * low + part * quarter * (high - low)) * pitch + index * unit, 8)
                 ref[pl.ds(at, unit), :] = acc[pl.ds(row, unit), :].astype(ref.dtype)
 
 
-def products(remap, chunks, bits):
+def products(remap, chunks, devices):
     cotangent, weights, source, target, counts = remap[:5]
-    devices = 1 << bits
     channels = cotangent.shape[1]
     pitch = round_up(channels, 8)
     tiles_in = cotangent.shape[2] // LANES
@@ -168,7 +155,7 @@
     step_blocks = max(size for size in range(1, 17) if blocks % size == 0)
     rows = devices // 4 * chunks[-1][1] * pitch
     return pl.pallas_call(
-        functools.partial(product_kernel, bits, channels, pitch, chunks, step_blocks),
+        functools.partial(product_kernel, channels, pitch, chunks, step_blocks),
         out_shape=[jax.ShapeDtypeStruct((rows, LANES), kind) for kind in (jnp.float32, jnp.bfloat16) * 2],
         in_specs=[pl.BlockSpec(memory_space=pltpu.HBM)] * 5,
         out_specs=[pl.BlockSpec(memory_space=pltpu.VMEM)] * 4,
@@ -192,8 +179,9 @@
     )(*[pltpu.with_memory_space_constraint(value, pltpu.HBM) for value in (source, target, counts, cotangent, weights)])
 
 
-def exchange(value, mask, devices):
-    return lax.ppermute(value, "curve", [(at, at ^ mask) for at in range(devices)])
+def exchange(value, stage, devices):
+    pairs = [(at, at ^ (1 << (ODD if at % 2 else EVEN)[stage])) for at in range(devices)]
+    return lax.ppermute(value, "curve", pairs)
 
 
 def added(terms, low, high):
@@ -201,37 +189,32 @@
 
 
 class Chain:
-    def __init__(self, chunk, bits, pitch):
-        self.chunk, self.devices = chunk, 1 << bits
-        self.slots = slots_of(chunk[2])
-        self.stage = 2
-        self.base = self.devices // 4 * chunk[0] * pitch
-        self.length = self.devices // 4 * (chunk[1] - chunk[0]) * pitch
+    def __init__(self, chunk, devices, pitch):
+        self.chunk, self.devices = chunk, devices
+        self.base = devices // 4 * chunk[0] * pitch
+        self.length = devices // 4 * (chunk[1] - chunk[0]) * pitch
 
     def first(self, terms):
         self.total = added(terms, self.base, self.base + self.length).astype(jnp.bfloat16)
 
     def second(self):
-        self.got = [exchange(self.total, self.slots[1][1], self.devices)]
+        self.stage = 1
+        self.got = exchange(self.total, self.stage, self.devices)
 
     def rest(self, terms):
         self.terms = [(term, self.base) for term in terms]
 
-    def part(self, place):
-        at = place * self.length
-        return sum(term[base + at:base + at + self.length].astype(jnp.float32) for term, base in self.terms)
-
     def send_next(self):
-        self.terms = self.terms + [(got, 0) for got in self.got]
-        masks = self.slots[self.stage]
-        self.length //= len(masks)
-        self.sent = [self.part(place).astype(jnp.bfloat16) for place in range(1, len(masks))]
-        self.got = [exchange(sent, mask, self.devices) for sent, mask in zip(self.sent, masks[1:])]
+        self.terms = self.terms + [(self.got, 0)]
         self.stage += 1
-
-    def finish(self):
-        self.terms = self.terms + [(got, 0) for got in self.got]
-        self.sent = ()
+        self.total = self.got
+        if self.stage < len(EVEN):
+            half = self.length // 2
+            self.total = sum(
+                term[base + half:base + self.length].astype(jnp.float32) for term, base in self.terms
+            ).astype(jnp.bfloat16)
+            self.length = half
+            self.got = exchange(self.total, self.stage, self.devices)
 
 
 def final_kernel(channels, pitch, parts, *refs):
@@ -267,16 +250,6 @@
     )(*flat)
 
 
-def plan(tiles):
-    straight = ((0,), (1,), (2,), (3,))
-    turned = ((0,), (2,), (3,), (1,))
-    half, some, most = tiles // 2, tiles * 5 // 12, tiles * 3 // 4
-    return (
-        [(0, half, straight), (half, tiles, turned)],
-        [(0, some, straight), (some, most, straight), (most, tiles, straight)],
-    )
-
-
 class Order:
     def __init__(self):
         self.last = ()
@@ -289,23 +262,23 @@
         self.last = values
 
 
-def bit_remaps(remaps, bits):
+def bit_remaps(remaps, devices):
     one, two = remaps
-    devices = 1 << bits
     pitch = round_up(one[-1][1], 8)
-    plans = plan(one[-1][2] // LANES)
-    ones, twos = [[Chain(chunk, bits, pitch) for chunk in chunks] for chunks in plans]
+    tiles = one[-1][2] // LANES
+    plans = (
+        [(0, tiles // 2), (tiles // 2, tiles)],
+        [(0, tiles // 2), (tiles // 2, tiles * 5 // 6), (tiles * 5 // 6, tiles)],
+    )
+    ones, twos = [[Chain(chunk, devices, pitch) for chunk in chunks] for chunks in plans]
     order = Order()
 
     def step(*chains):
         gots = order.after([chain.got for chain in chains])
         for chain, got in zip(chains, gots):
             chain.got = got
-            if chain.stage < len(chain.slots):
-                chain.send_next()
-            else:
-                chain.finish()
-        order.before([chain.sent for chain in chains])
+            chain.send_next()
+        order.before([chain.total for chain in chains])
 
     def summed(line, terms):
         terms = order.after(terms)
@@ -313,53 +286,52 @@
             chain.first(terms)
         order.before([chain.total for chain in line])
 
+    def rested(line, terms):
+        terms = order.after(terms)
+        order.before(terms)
+        for chain in line:
+            chain.rest(terms)
+
+    def begun(chain):
+        chain.total = order.after(chain.total)
+        chain.second()
+
     def both_cores(keep, send):
-        return [keep, exchange(send, 1, devices)]
-
-    def tied(first, second):
-        return lax.optimization_barrier((first, second))
-
-    made = products(one, plans[0], bits)
-    cotangent, made = tied(two[0], made)
+        return [keep, exchange(send, 0, devices)]
+
+    made = products(one, plans[0], devices)
+    cotangent, made = lax.optimization_barrier((two[0], made))
     keep, send, keep_on, send_on = made
     on = both_cores(keep_on, send_on)
     rest = both_cores(keep, send)
-    keep, send, keep_on, send_on = products((cotangent,) + two[1:], plans[1], bits)
+    keep, send, keep_on, send_on = products((cotangent,) + two[1:], plans[1], devices)
     order.before(keep)
     late_on = both_cores(keep_on, send_on)
     late = both_cores(keep, send)
-    across, turned = ones
-    early, middle, last = twos
+    a, b = ones
+    c, d, e = twos
 
     summed(ones, on)
-    for chain in ones:
-        chain.second()
-    rest = order.after(rest)
-    order.before(rest)
-    for chain in ones:
-        chain.rest(rest)
+    a.second()
+    b.second()
+    rested(ones, rest)
     summed(twos, late_on)
-    early.second()
-    late = order.after(late)
-    order.before(late)
-    for chain in twos:
-        chain.rest(late)
-    step(across)
-    step(turned)
-    middle.total = order.after(middle.total)
-    middle.second()
-    step(across)
-    step(early)
-    last.total = order.after(last.total)
-    last.second()
-    step(middle)
-    step(turned)
-    step(early)
-    step(across)
-    step(last)
-    step(middle)
-    step(last)
-    step(turned)
+    c.second()
+    rested(twos, late)
+    step(a)
+    step(b)
+    begun(d)
+    step(c)
+    step(a)
+    begun(e)
+    step(b)
+    step(d)
+    step(c)
+    step(a)
+    step(e)
+    step(d)
+    step(b)
+    step(e)
     step(*twos)
     return [final_sum(line, remap[-1], pitch) for line, remap in zip((ones, twos), remaps)]
 
@@ -370,11 +342,10 @@
         (latlon, args[2], args[3], args[4], args[5], healpix.shape),
         (healpix, args[6], args[7], args[8], args[9], latlon.shape),
     ]
-    bits = devices.bit_length() - 1
     tiles = max(latlon.shape[2], healpix.shape[2]) // LANES
     size = devices * tiles * round_up(latlon.shape[1], 8) * LANES * 4
-    if devices == 1 << bits and bits == 4 and size <= ACC_LIMIT:
-        return tuple(bit_remaps(remaps, bits))
+    if devices == 1 << len(EVEN) and size <= ACC_LIMIT:
+        return tuple(bit_remaps(remaps, devices))
     return tuple(slot_remap(*remap) for remap in remaps)
 
 

time: 61.5 us -> 61.8 us (level)
  starting transfers between devices: 21.7 us -> 25.4 us
  waiting for transfers between devices: 26.2 us -> 23.1 us
    ppermute x19, starting transfers between devices: 21.7 us -> 25.4 us  [exchange(): return lax.ppermute(value, 'curve', pairs)]
    ppermute x19, waiting for transfers between devices: 26.2 us -> 23.1 us  [exchange(): return lax.ppermute(value, 'curve', pairs)]
  transfers between devices with their start and end apart: 19 -> 19, of which waited for: 7 -> 9; matrix products, arithmetic and copies ran while one was open for 2% -> 2% of each run, Pallas kernels for 9% -> 9%
where the time goes in v6:
time: 61.8 us; the launch traced here: 61.6 us
  starting transfers between devices  25.4 us (41%)
  waiting for transfers between devices  23.1 us (37%)
  Pallas kernels  11.3 us (18%)
  other arithmetic  1 us (2%)
  between operations  0.75 us (1%)
    ppermute x19, starting transfers between devices, exchange(): return lax.ppermute(value, 'curve', pairs)  25.4 us
    ppermute x19, waiting for transfers between devices, exchange(): return lax.ppermute(value, 'curve', pairs)  23.1 us
    pallas_call x2, Pallas kernels, products(): pl.pallas_call(functools.partial(product_kernel, channels, pitch, chunks,...  9.68 us
    pallas_call x2, Pallas kernels, final_sum(): pl.pallas_call(functools.partial(final_kernel, like_shape[1], pitch, part...  1.66 us
  transfers between devices with their start and end apart: 19, of which 9 were waited for; matrix products, arithmetic and copies ran while one was open for 2% of the time, Pallas kernels for 9%

profile of v6, /device:TPU:0, one launch (start us, length us, event | category | flops | bytes accessed | tf_op | source)
XLA Modules:
  0.0 61.6 jit_solution(1816903580563980036)
XLA Ops:
  0.6 4.8 %shard_map.113 = (f32[3456,128]{1,0:T(8,128)S(1)}, bf16[3456,128]{1,0:T(8,128)(2,1)S(1)}, f32[3456,128]{1,0:T(8,128)S(1)}, bf16[3456,128]{1,0:T(8,128)(2,1)S(1)}) custom-call(s32[144]{0:T(256)} %source_hbm.2, s32[144]{0:T(256)} %target_hbm.2, s32[1,16]{1,0:T(1,128)} %counts_hbm.2, bf16[1,69,1536]{2,1,0:T(8,128)(2,1)} %x_hbm.1, bf16[144,128,128]{2,1,0:T(8,128)(2,1)} %w_hbm.2), custom_call_target="tpu_custom_call" | custom-call | flops 325582848 | bytes 10027008 | tf_op jit(solution)/shard_map/pallas_call | solution.py:157
  5.5 0.5 collective-permute-start.1
  6.0 0.1 collective-permute-start
  6.1 4.8 %shard_map.114 = (f32[3456,128]{1,0:T(8,128)S(1)}, bf16[3456,128]{1,0:T(8,128)(2,1)S(1)}, f32[3456,128]{1,0:T(8,128)S(1)}, bf16[3456,128]{1,0:T(8,128)(2,1)S(1)}) custom-call(s32[144]{0:T(256)} %source_hbm.3, s32[144]{0:T(256)} %target_hbm.3, s32[1,16]{1,0:T(1,128)} %counts_hbm.3, bf16[1,69,1536]{2,1,0:T(8,128)(2,1)} %x_hbm.2, bf16[144,128,128]{2,1,0:T(8,128)(2,1)} %w_hbm.3), custom_call_target="tpu_custom_call" | custom-call | flops 325582848 | bytes 10027008 | tf_op jit(solution)/shard_map/pallas_call | solution.py:157
  10.9 0.5 collective-permute-start.4
  11.5 0.1 collective-permute-start.3
  11.5 0.0 collective-permute-done.1
  11.5 0.2 add_convert_fusion.1
  11.7 3.0 %collective-permute-start.7 = (bf16[1728,128]{1,0:T(8,128)(2,1)S(1)}, bf16[1728,128]{1,0:T(8,128)(2,1)S(1)}, u32[]{:S(2)}, u32[]{:S(2)}) collective-permute-start(bf16[1728,128]{1,0:T(8,128)(2,1)S(1)} %get-tuple-element.78), channel_id=1, source_target_pairs={{0,2},{1,5},{2,0},{3,7},{4,6},{5,1},{6,4},{7,3},{8,10},{9,13},{10,... | collective-permute-start | bytes 1327112 | tf_op jit(solution)/shard_map/ppermute | solution.py:184
  14.7 0.1 collective-permute-start.2
  14.8 0.0 collective-permute-done.refs_1_.refs_6_
  14.8 0.1 add_convert_fusion.3
  14.9 0.1 add_convert_fusion
  15.0 2.0 %collective-permute-start.6 = (bf16[1728,128]{1,0:T(8,128)(2,1)S(1)}, bf16[1728,128]{1,0:T(8,128)(2,1)S(1)}, u32[]{:S(2)}, u32[]{:S(2)}) collective-permute-start(bf16[1728,128]{1,0:T(8,128)(2,1)S(1)} %add_convert_fusion), channel_id=1, source_target_pairs={{0,2},{1,5},{2,0},{3,7},{4,6},{5,1},{6,4},{7,3},{8,10},{9,13},{10,... | collective-permute-start | bytes 1327112 | tf_op jit(solution)/shard_map/ppermute | solution.py:184
  17.1 8.7 %collective-permute-done.2.refs_2_ = bf16[1728,128]{1,0:T(8,128)(2,1)S(1)} collective-permute-done((bf16[1728,128]{1,0:T(8,128)(2,1)S(1)}, bf16[1728,128]{1,0:T(8,128)(2,1)S(1)}, u32[]{:S(2)}, u32[]{:S(2)}) %collective-permute-start.2) | collective-permute-done | bytes 442400 | tf_op jit(solution)/shard_map/ppermute | solution.py:184
  25.7 0.1 add_convert_fusion.6
  25.8 0.0 collective-permute-done.7.refs_7_
  25.8 0.1 add_convert_fusion.5
  25.9 2.1 %collective-permute-start.11 = (bf16[864,128]{1,0:T(8,128)(2,1)S(1)}, bf16[864,128]{1,0:T(8,128)(2,1)S(1)}, u32[]{:S(2)}, u32[]{:S(2)}) collective-permute-start(bf16[864,128]{1,0:T(8,128)(2,1)S(1)} %add_convert_fusion.5), channel_id=1, source_target_pairs={{0,4},{1,3},{2,6},{3,1},{4,0},{5,7},{6,2},{7,5},{8,12},{9,11},{10,... | collective-permute-start | bytes 663560 | tf_op jit(solution)/shard_map/ppermute | solution.py:184
  28.1 0.1 collective-permute-start.5
  28.1 1.9 %collective-permute-start.10 = (bf16[1152,128]{1,0:T(8,128)(2,1)S(1)}, bf16[1152,128]{1,0:T(8,128)(2,1)S(1)}, u32[]{:S(2)}, u32[]{:S(2)}) collective-permute-start(bf16[1152,128]{1,0:T(8,128)(2,1)S(1)} %add_convert_fusion.3), channel_id=1, source_target_pairs={{0,2},{1,5},{2,0},{3,7},{4,6},{5,1},{6,4},{7,3},{8,10},{9,13},{10,... | collective-permute-start | bytes 884744 | tf_op jit(solution)/shard_map/ppermute | solution.py:184
  30.0 2.7 %collective-permute-done.6.refs_2_ = bf16[1728,128]{1,0:T(8,128)(2,1)S(1)} collective-permute-done((bf16[1728,128]{1,0:T(8,128)(2,1)S(1)}, bf16[1728,128]{1,0:T(8,128)(2,1)S(1)}, u32[]{:S(2)}, u32[]{:S(2)}) %collective-permute-start.6) | collective-permute-done | bytes 442400 | tf_op jit(solution)/shard_map/ppermute | solution.py:184
  32.7 0.1 add_convert_fusion.4
  32.8 2.5 %collective-permute-start.9 = (bf16[864,128]{1,0:T(8,128)(2,1)S(1)}, bf16[864,128]{1,0:T(8,128)(2,1)S(1)}, u32[]{:S(2)}, u32[]{:S(2)}) collective-permute-start(bf16[864,128]{1,0:T(8,128)(2,1)S(1)} %add_convert_fusion.4), channel_id=1, source_target_pairs={{0,4},{1,3},{2,6},{3,1},{4,0},{5,7},{6,2},{7,5},{8,12},{9,11},{10,... | collective-permute-start | bytes 663560 | tf_op jit(solution)/shard_map/ppermute | solution.py:184
  35.3 2.5 %collective-permute-done.5.refs_3_ = bf16[864,128]{1,0:T(8,128)(2,1)S(1)} collective-permute-done((bf16[864,128]{1,0:T(8,128)(2,1)S(1)}, bf16[864,128]{1,0:T(8,128)(2,1)S(1)}, u32[]{:S(2)}, u32[]{:S(2)}) %collective-permute-start.5) | collective-permute-done | bytes 221216 | tf_op jit(solution)/shard_map/ppermute | solution.py:184
  37.8 0.1 add_convert_fusion.11
  37.9 2.8 %collective-permute-start.8 = (bf16[432,128]{1,0:T(8,128)(2,1)S(1)}, bf16[432,128]{1,0:T(8,128)(2,1)S(1)}, u32[]{:S(2)}, u32[]{:S(2)}) collective-permute-start(bf16[432,128]{1,0:T(8,128)(2,1)S(1)} %add_convert_fusion.11), channel_id=1, source_target_pairs={{0,8},{1,9},{2,10},{3,11},{4,12},{5,13},{6,14},{7,15},{8,0},{9,1},... | collective-permute-start | bytes 331784 | tf_op jit(solution)/shard_map/ppermute | solution.py:184
  40.7 0.0 collective-permute-done.11.refs_8_
  40.7 0.1 add_convert_fusion.10
  40.8 0.2 collective-permute-start.12
  41.0 1.7 %collective-permute-start.14 = (bf16[576,128]{1,0:T(8,128)(2,1)S(1)}, bf16[576,128]{1,0:T(8,128)(2,1)S(1)}, u32[]{:S(2)}, u32[]{:S(2)}) collective-permute-start(bf16[576,128]{1,0:T(8,128)(2,1)S(1)} %add_convert_fusion.8), channel_id=1, source_target_pairs={{0,2},{1,5},{2,0},{3,7},{4,6},{5,1},{6,4},{7,3},{8,10},{9,13},{10,... | collective-permute-start | bytes 442376 | tf_op jit(solution)/shard_map/ppermute | solution.py:184
  42.7 0.0 collective-permute-done.10.refs_7_
  42.7 0.1 add_convert_fusion.7
  42.8 1.6 %collective-permute-start.13 = (bf16[576,128]{1,0:T(8,128)(2,1)S(1)}, bf16[576,128]{1,0:T(8,128)(2,1)S(1)}, u32[]{:S(2)}, u32[]{:S(2)}) collective-permute-start(bf16[576,128]{1,0:T(8,128)(2,1)S(1)} %add_convert_fusion.7), channel_id=1, source_target_pairs={{0,4},{1,3},{2,6},{3,1},{4,0},{5,7},{6,2},{7,5},{8,12},{9,11},{10,... | collective-permute-start | bytes 442376 | tf_op jit(solution)/shard_map/ppermute | solution.py:184
  44.4 0.1 add_convert_fusion.9
  44.5 2.7 %collective-permute-start.15 = (bf16[432,128]{1,0:T(8,128)(2,1)S(1)}, bf16[432,128]{1,0:T(8,128)(2,1)S(1)}, u32[]{:S(2)}, u32[]{:S(2)}) collective-permute-start(bf16[432,128]{1,0:T(8,128)(2,1)S(1)} %add_convert_fusion.9), channel_id=1, source_target_pairs={{0,8},{1,9},{2,10},{3,11},{4,12},{5,13},{6,14},{7,15},{8,0},{9,1},... | collective-permute-start | bytes 331784 | tf_op jit(solution)/shard_map/ppermute | solution.py:184
  47.1 2.6 %collective-permute-done.8.refs_4_ = bf16[432,128]{1,0:T(8,128)(2,1)S(1)} collective-permute-done((bf16[432,128]{1,0:T(8,128)(2,1)S(1)}, bf16[432,128]{1,0:T(8,128)(2,1)S(1)}, u32[]{:S(2)}, u32[]{:S(2)}) %collective-permute-start.8) | collective-permute-done | bytes 110624 | tf_op jit(solution)/shard_map/ppermute | solution.py:184
  49.8 0.1 collective-permute-start.17
  49.8 0.3 collective-permute-done.13.refs_8_
  50.2 3.2 %collective-permute-start.16 = (bf16[288,128]{1,0:T(8,128)(2,1)S(1)}, bf16[288,128]{1,0:T(8,128)(2,1)S(1)}, u32[]{:S(2)}, u32[]{:S(2)}) collective-permute-start(bf16[288,128]{1,0:T(8,128)(2,1)S(1)} %add_convert_fusion.12), channel_id=1, source_target_pairs={{0,8},{1,9},{2,10},{3,11},{4,12},{5,13},{6,14},{7,15},{8,0},{9,1},... | collective-permute-start | bytes 221192 | tf_op jit(solution)/shard_map/ppermute | solution.py:184
  53.4 0.9 %collective-permute-done.12.refs_9_ = bf16[432,128]{1,0:T(8,128)(2,1)S(1)} collective-permute-done((bf16[432,128]{1,0:T(8,128)(2,1)S(1)}, bf16[432,128]{1,0:T(8,128)(2,1)S(1)}, u32[]{:S(2)}, u32[]{:S(2)}) %collective-permute-start.12) | collective-permute-done | bytes 110624 | tf_op jit(solution)/shard_map/ppermute | solution.py:184
  54.3 1.5 %collective-permute-done.17.refs_13_ = bf16[288,128]{1,0:T(8,128)(2,1)S(1)} collective-permute-done((bf16[288,128]{1,0:T(8,128)(2,1)S(1)}, bf16[288,128]{1,0:T(8,128)(2,1)S(1)}, u32[]{:S(2)}, u32[]{:S(2)}) %collective-permute-start.17) | collective-permute-done | bytes 73760 | tf_op jit(solution)/shard_map/ppermute | solution.py:184
  55.9 0.2 collective-permute-start.18
  56.1 0.8 %shard_map.115 = bf16[1,69,1536]{2,1,0:T(8,128)(2,1)} custom-call(f32[3456,128]{1,0:T(8,128)S(1)} %get-tuple-element.52.refs_0_.refs_5_, bf16[3456,128]{1,0:T(8,128)(2,1)S(1)} %collective-permute-done.refs_1_.refs_6_, bf16[1728,128]{1,0:T(8,128)(2,1)S(1)} %collective-permute-done.2.refs_2_, bf16[864,128]{1,0:T(8,128)(2,1)S(1)} %collective-permute-done.5.refs_3_, ...), custom_call_target="tpu_custom_call" | custom-call | tf_op jit(solution)/shard_map/pallas_call | solution.py:243
  56.9 1.3 %collective-permute-done.15.refs_4_ = bf16[432,128]{1,0:T(8,128)(2,1)S(1)} collective-permute-done((bf16[432,128]{1,0:T(8,128)(2,1)S(1)}, bf16[432,128]{1,0:T(8,128)(2,1)S(1)}, u32[]{:S(2)}, u32[]{:S(2)}) %collective-permute-start.15) | collective-permute-done | bytes 110624 | tf_op jit(solution)/shard_map/ppermute | solution.py:184
  58.2 2.6 %collective-permute-done.18.refs_14_ = bf16[144,128]{1,0:T(8,128)(2,1)S(1)} collective-permute-done((bf16[144,128]{1,0:T(8,128)(2,1)S(1)}, bf16[144,128]{1,0:T(8,128)(2,1)S(1)}, u32[]{:S(2)}, u32[]{:S(2)}) %collective-permute-start.18) | collective-permute-done | bytes 36896 | tf_op jit(solution)/shard_map/ppermute | solution.py:184
  60.8 0.0 collective-permute-done.16.refs_9_
  60.8 0.8 %shard_map.116 = bf16[1,69,1536]{2,1,0:T(8,128)(2,1)} custom-call(f32[3456,128]{1,0:T(8,128)S(1)} %get-tuple-element.59.refs_0_.refs_5_.refs_10_, bf16[3456,128]{1,0:T(8,128)(2,1)S(1)} %collective-permute-done.3.refs_1_.refs_6_.refs_11_, bf16[1728,128]{1,0:T(8,128)(2,1)S(1)} %collective-permute-done.6.refs_2_, ...), custom_call_target="tpu_custom_call" | custom-call | tf_op jit(solution)/shard_map/pallas_call | solution.py:243
  (8 shorter events, 0.2 us)
Async XLA Ops:
  5.5 6.1 %collective-permute-start.1 = (bf16[3456,128]{1,0:T(8,128)(2,1)S(1)}, bf16[3456,128]{1,0:T(8,128)(2,1)S(1)}, u32[]{:S(2)}, u32[]{:S(2)}) collective-permute-start(bf16[3456,128]{1,0:T(8,128)(2,1)S(1)} %get-tuple-element.47), channel_id=1, source_target_pairs={{0,1},{1,0},{2,3},{3,2},{4,5},{5,4},{6,7},{7,6},{8,9},{9,8},{10,11... | collective-permute-start | bytes 2654216 | tf_op jit(solution)/shard_map/ppermute | solution.py:184
  6.0 8.8 %collective-permute-start = (bf16[3456,128]{1,0:T(8,128)(2,1)S(1)}, bf16[3456,128]{1,0:T(8,128)(2,1)S(1)}, u32[]{:S(2)}, u32[]{:S(2)}) collective-permute-start(bf16[3456,128]{1,0:T(8,128)(2,1)S(1)} %get-tuple-element.45), channel_id=1, source_target_pairs={{0,1},{1,0},{2,3},{3,2},{4,5},{5,4},{6,7},{7,6},{8,9},{9,8},{10,11... | collective-permute-start | bytes 2654216 | tf_op jit(solution)/shard_map/ppermute | solution.py:184
  10.9 3.9 %collective-permute-start.4 = (bf16[3456,128]{1,0:T(8,128)(2,1)S(1)}, bf16[3456,128]{1,0:T(8,128)(2,1)S(1)}, u32[]{:S(2)}, u32[]{:S(2)}) collective-permute-start(bf16[3456,128]{1,0:T(8,128)(2,1)S(1)} %get-tuple-element.56), channel_id=1, source_target_pairs={{0,1},{1,0},{2,3},{3,2},{4,5},{5,4},{6,7},{7,6},{8,9},{9,8},{10,11... | collective-permute-start | bytes 2654216 | tf_op jit(solution)/shard_map/ppermute | solution.py:184
  11.5 5.6 %collective-permute-start.3 = (bf16[3456,128]{1,0:T(8,128)(2,1)S(1)}, bf16[3456,128]{1,0:T(8,128)(2,1)S(1)}, u32[]{:S(2)}, u32[]{:S(2)}) collective-permute-start(bf16[3456,128]{1,0:T(8,128)(2,1)S(1)} %get-tuple-element.54), channel_id=1, source_target_pairs={{0,1},{1,0},{2,3},{3,2},{4,5},{5,4},{6,7},{7,6},{8,9},{9,8},{10,11... | collective-permute-start | bytes 2654216 | tf_op jit(solution)/shard_map/ppermute | solution.py:184
  11.7 14.1 %collective-permute-start.7 = (bf16[1728,128]{1,0:T(8,128)(2,1)S(1)}, bf16[1728,128]{1,0:T(8,128)(2,1)S(1)}, u32[]{:S(2)}, u32[]{:S(2)}) collective-permute-start(bf16[1728,128]{1,0:T(8,128)(2,1)S(1)} %get-tuple-element.78), channel_id=1, source_target_pairs={{0,2},{1,5},{2,0},{3,7},{4,6},{5,1},{6,4},{7,3},{8,10},{9,13},{10,... | collective-permute-start | bytes 1327112 | tf_op jit(solution)/shard_map/ppermute | solution.py:184
  14.7 11.0 %collective-permute-start.2 = (bf16[1728,128]{1,0:T(8,128)(2,1)S(1)}, bf16[1728,128]{1,0:T(8,128)(2,1)S(1)}, u32[]{:S(2)}, u32[]{:S(2)}) collective-permute-start(bf16[1728,128]{1,0:T(8,128)(2,1)S(1)} %get-tuple-element.79), channel_id=1, source_target_pairs={{0,2},{1,5},{2,0},{3,7},{4,6},{5,1},{6,4},{7,3},{8,10},{9,13},{10,... | collective-permute-start | bytes 1327112 | tf_op jit(solution)/shard_map/ppermute | solution.py:184
  15.0 17.7 %collective-permute-start.6 = (bf16[1728,128]{1,0:T(8,128)(2,1)S(1)}, bf16[1728,128]{1,0:T(8,128)(2,1)S(1)}, u32[]{:S(2)}, u32[]{:S(2)}) collective-permute-start(bf16[1728,128]{1,0:T(8,128)(2,1)S(1)} %add_convert_fusion), channel_id=1, source_target_pairs={{0,2},{1,5},{2,0},{3,7},{4,6},{5,1},{6,4},{7,3},{8,10},{9,13},{10,... | collective-permute-start | bytes 1327112 | tf_op jit(solution)/shard_map/ppermute | solution.py:184
  25.9 14.8 %collective-permute-start.11 = (bf16[864,128]{1,0:T(8,128)(2,1)S(1)}, bf16[864,128]{1,0:T(8,128)(2,1)S(1)}, u32[]{:S(2)}, u32[]{:S(2)}) collective-permute-start(bf16[864,128]{1,0:T(8,128)(2,1)S(1)} %add_convert_fusion.5), channel_id=1, source_target_pairs={{0,4},{1,3},{2,6},{3,1},{4,0},{5,7},{6,2},{7,5},{8,12},{9,11},{10,... | collective-permute-start | bytes 663560 | tf_op jit(solution)/shard_map/ppermute | solution.py:184
  28.1 9.8 %collective-permute-start.5 = (bf16[864,128]{1,0:T(8,128)(2,1)S(1)}, bf16[864,128]{1,0:T(8,128)(2,1)S(1)}, u32[]{:S(2)}, u32[]{:S(2)}) collective-permute-start(bf16[864,128]{1,0:T(8,128)(2,1)S(1)} %add_convert_fusion.6), channel_id=1, source_target_pairs={{0,4},{1,3},{2,6},{3,1},{4,0},{5,7},{6,2},{7,5},{8,12},{9,11},{10,... | collective-permute-start | bytes 663560 | tf_op jit(solution)/shard_map/ppermute | solution.py:184
  28.1 14.6 %collective-permute-start.10 = (bf16[1152,128]{1,0:T(8,128)(2,1)S(1)}, bf16[1152,128]{1,0:T(8,128)(2,1)S(1)}, u32[]{:S(2)}, u32[]{:S(2)}) collective-permute-start(bf16[1152,128]{1,0:T(8,128)(2,1)S(1)} %add_convert_fusion.3), channel_id=1, source_target_pairs={{0,2},{1,5},{2,0},{3,7},{4,6},{5,1},{6,4},{7,3},{8,10},{9,13},{10,... | collective-permute-start | bytes 884744 | tf_op jit(solution)/shard_map/ppermute | solution.py:184
  32.8 11.6 %collective-permute-start.9 = (bf16[864,128]{1,0:T(8,128)(2,1)S(1)}, bf16[864,128]{1,0:T(8,128)(2,1)S(1)}, u32[]{:S(2)}, u32[]{:S(2)}) collective-permute-start(bf16[864,128]{1,0:T(8,128)(2,1)S(1)} %add_convert_fusion.4), channel_id=1, source_target_pairs={{0,4},{1,3},{2,6},{3,1},{4,0},{5,7},{6,2},{7,5},{8,12},{9,11},{10,... | collective-permute-start | bytes 663560 | tf_op jit(solution)/shard_map/ppermute | solution.py:184
  37.9 11.8 %collective-permute-start.8 = (bf16[432,128]{1,0:T(8,128)(2,1)S(1)}, bf16[432,128]{1,0:T(8,128)(2,1)S(1)}, u32[]{:S(2)}, u32[]{:S(2)}) collective-permute-start(bf16[432,128]{1,0:T(8,128)(2,1)S(1)} %add_convert_fusion.11), channel_id=1, source_target_pairs={{0,8},{1,9},{2,10},{3,11},{4,12},{5,13},{6,14},{7,15},{8,0},{9,1},... | collective-permute-start | bytes 331784 | tf_op jit(solution)/shard_map/ppermute | solution.py:184
  40.8 13.6 %collective-permute-start.12 = (bf16[432,128]{1,0:T(8,128)(2,1)S(1)}, bf16[432,128]{1,0:T(8,128)(2,1)S(1)}, u32[]{:S(2)}, u32[]{:S(2)}) collective-permute-start(bf16[432,128]{1,0:T(8,128)(2,1)S(1)} %add_convert_fusion.10), channel_id=1, source_target_pairs={{0,8},{1,9},{2,10},{3,11},{4,12},{5,13},{6,14},{7,15},{8,0},{9,1},... | collective-permute-start | bytes 331784 | tf_op jit(solution)/shard_map/ppermute | solution.py:184
  41.0 8.7 %collective-permute-start.14 = (bf16[576,128]{1,0:T(8,128)(2,1)S(1)}, bf16[576,128]{1,0:T(8,128)(2,1)S(1)}, u32[]{:S(2)}, u32[]{:S(2)}) collective-permute-start(bf16[576,128]{1,0:T(8,128)(2,1)S(1)} %add_convert_fusion.8), channel_id=1, source_target_pairs={{0,2},{1,5},{2,0},{3,7},{4,6},{5,1},{6,4},{7,3},{8,10},{9,13},{10,... | collective-permute-start | bytes 442376 | tf_op jit(solution)/shard_map/ppermute | solution.py:184
  42.8 7.3 %collective-permute-start.13 = (bf16[576,128]{1,0:T(8,128)(2,1)S(1)}, bf16[576,128]{1,0:T(8,128)(2,1)S(1)}, u32[]{:S(2)}, u32[]{:S(2)}) collective-permute-start(bf16[576,128]{1,0:T(8,128)(2,1)S(1)} %add_convert_fusion.7), channel_id=1, source_target_pairs={{0,4},{1,3},{2,6},{3,1},{4,0},{5,7},{6,2},{7,5},{8,12},{9,11},{10,... | collective-permute-start | bytes 442376 | tf_op jit(solution)/shard_map/ppermute | solution.py:184
  44.5 13.7 %collective-permute-start.15 = (bf16[432,128]{1,0:T(8,128)(2,1)S(1)}, bf16[432,128]{1,0:T(8,128)(2,1)S(1)}, u32[]{:S(2)}, u32[]{:S(2)}) collective-permute-start(bf16[432,128]{1,0:T(8,128)(2,1)S(1)} %add_convert_fusion.9), channel_id=1, source_target_pairs={{0,8},{1,9},{2,10},{3,11},{4,12},{5,13},{6,14},{7,15},{8,0},{9,1},... | collective-permute-start | bytes 331784 | tf_op jit(solution)/shard_map/ppermute | solution.py:184
  49.8 6.1 %collective-permute-start.17 = (bf16[288,128]{1,0:T(8,128)(2,1)S(1)}, bf16[288,128]{1,0:T(8,128)(2,1)S(1)}, u32[]{:S(2)}, u32[]{:S(2)}) collective-permute-start(bf16[288,128]{1,0:T(8,128)(2,1)S(1)} %add_convert_fusion.13), channel_id=1, source_target_pairs={{0,4},{1,3},{2,6},{3,1},{4,0},{5,7},{6,2},{7,5},{8,12},{9,11},{10,... | collective-permute-start | bytes 221192 | tf_op jit(solution)/shard_map/ppermute | solution.py:184
  50.2 10.6 %collective-permute-start.16 = (bf16[288,128]{1,0:T(8,128)(2,1)S(1)}, bf16[288,128]{1,0:T(8,128)(2,1)S(1)}, u32[]{:S(2)}, u32[]{:S(2)}) collective-permute-start(bf16[288,128]{1,0:T(8,128)(2,1)S(1)} %add_convert_fusion.12), channel_id=1, source_target_pairs={{0,8},{1,9},{2,10},{3,11},{4,12},{5,13},{6,14},{7,15},{8,0},{9,1},... | collective-permute-start | bytes 221192 | tf_op jit(solution)/shard_map/ppermute | solution.py:184
  55.9 4.9 %collective-permute-start.18 = (bf16[144,128]{1,0:T(8,128)(2,1)S(1)}, bf16[144,128]{1,0:T(8,128)(2,1)S(1)}, u32[]{:S(2)}, u32[]{:S(2)}) collective-permute-start(bf16[144,128]{1,0:T(8,128)(2,1)S(1)} %add_convert_fusion.14), channel_id=1, source_target_pairs={{0,8},{1,9},{2,10},{3,11},{4,12},{5,13},{6,14},{7,15},{8,0},{9,1},... | collective-permute-start | bytes 110600 | tf_op jit(solution)/shard_map/ppermute | solution.py:184

commit v7 on v6

--- a/solution.py
+++ b/solution.py
@@ -60,8 +60,9 @@
     return sum_slots(arrived, arrived_labels, like_shape[2] // weights.shape[1], like_shape)
 
 
-EVEN = (0, 1, 2, 3)
-ODD = (0, 2, 1, 3)
+STRAIGHT = ((0, 1, 2, 3), (0, 1, 2, 3))
+MIXED = ((0, 1, 2, 3), (0, 2, 1, 3))
+BITS = 4
 
 
 def product_kernel(
@@ -99,12 +100,16 @@
 
     for owner in range(devices):
         differ = jnp.bitwise_xor(me, owner)
-        first, second, *others = ODD if owner % 2 else EVEN
-        place = jnp.int32(0)
-        for bit in [second, first] + others:
-            place = place * 2 + jnp.bitwise_and(jnp.right_shift(differ, bit), 1)
-        for chunk, (low, high) in enumerate(chunks):
-            places[chunk, owner] = devices * low + place * (high - low) - low
+        found = {}
+        for chunk, (low, high, way) in enumerate(chunks):
+            first, second, *others = way[owner % 2]
+            key = (second, first, *others)
+            if key not in found:
+                place = jnp.int32(0)
+                for bit in key:
+                    place = place * 2 + jnp.bitwise_and(jnp.right_shift(differ, bit), 1)
+                found[key] = place
+            places[chunk, owner] = devices * low + found[key] * (high - low) - low
 
     x_copy.wait()
     for tile in range(xs.shape[0]):
@@ -135,7 +140,7 @@
     lax.fori_loop(0, steps, some, (jnp.int32(0), counts[0, 0]))
 
     quarter = devices // 4
-    for low, high in chunks:
+    for low, high, way in chunks:
         unit = (high - low) * pitch
 
         @pl.loop(0, quarter)
@@ -179,8 +184,8 @@
     )(*[pltpu.with_memory_space_constraint(value, pltpu.HBM) for value in (source, target, counts, cotangent, weights)])
 
 
-def exchange(value, stage, devices):
-    pairs = [(at, at ^ (1 << (ODD if at % 2 else EVEN)[stage])) for at in range(devices)]
+def exchange(value, way, stage, devices):
+    pairs = [(at, at ^ (1 << way[at % 2][stage])) for at in range(devices)]
     return lax.ppermute(value, "curve", pairs)
 
 
@@ -191,6 +196,7 @@
 class Chain:
     def __init__(self, chunk, devices, pitch):
         self.chunk, self.devices = chunk, devices
+        self.way = chunk[2]
         self.base = devices // 4 * chunk[0] * pitch
         self.length = devices // 4 * (chunk[1] - chunk[0]) * pitch
 
@@ -199,7 +205,7 @@
 
     def second(self):
         self.stage = 1
-        self.got = exchange(self.total, self.stage, self.devices)
+        self.got = exchange(self.total, self.way, self.stage, self.devices)
 
     def rest(self, terms):
         self.terms = [(term, self.base) for term in terms]
@@ -208,13 +214,13 @@
         self.terms = self.terms + [(self.got, 0)]
         self.stage += 1
         self.total = self.got
-        if self.stage < len(EVEN):
+        if self.stage < BITS:
             half = self.length // 2
             self.total = sum(
                 term[base + half:base + self.length].astype(jnp.float32) for term, base in self.terms
             ).astype(jnp.bfloat16)
             self.length = half
-            self.got = exchange(self.total, self.stage, self.devices)
+            self.got = exchange(self.total, self.way, self.stage, self.devices)
 
 
 def final_kernel(channels, pitch, parts, *refs):
@@ -266,9 +272,10 @@
     one, two = remaps
     pitch = round_up(one[-1][1], 8)
     tiles = one[-1][2] // LANES
+    some, most = tiles * 5 // 12, tiles * 3 // 4
     plans = (
-        [(0, tiles // 2), (tiles // 2, tiles)],
-        [(0, tiles // 2), (tiles // 2, tiles * 5 // 6), (tiles * 5 // 6, tiles)],
+        [(0, most, MIXED), (most, tiles, MIXED)],
+        [(0, some, MIXED), (some, most, STRAIGHT), (most, tiles, STRAIGHT)],
     )
     ones, twos = [[Chain(chunk, devices, pitch) for chunk in chunks] for chunks in plans]
     order = Order()
@@ -297,40 +304,40 @@
         chain.second()
 
     def both_cores(keep, send):
-        return [keep, exchange(send, 0, devices)]
-
-    made = products(one, plans[0], devices)
-    cotangent, made = lax.optimization_barrier((two[0], made))
-    keep, send, keep_on, send_on = made
+        return [keep, exchange(send, STRAIGHT, 0, devices)]
+
+    a, b = ones
+    c, d, e = twos
+
+    keep, send, keep_on, send_on = products(one, plans[0], devices)
     on = both_cores(keep_on, send_on)
     rest = both_cores(keep, send)
-    keep, send, keep_on, send_on = products((cotangent,) + two[1:], plans[1], devices)
-    order.before(keep)
-    late_on = both_cores(keep_on, send_on)
-    late = both_cores(keep, send)
-    a, b = ones
-    c, d, e = twos
-
     summed(ones, on)
     a.second()
     b.second()
     rested(ones, rest)
-    summed(twos, late_on)
-    c.second()
-    rested(twos, late)
+    made = products((order.after(two[0]),) + two[1:], plans[1], devices)
+    order.before(made)
+    keep, send, keep_on, send_on = made
+    on = both_cores(keep_on, send_on)
+    rest = both_cores(keep, send)
+
     step(a)
     step(b)
+    summed(twos, on)
+    c.second()
     begun(d)
+    step(a)
+    step(b)
+    rested(twos, rest)
     step(c)
-    step(a)
     begun(e)
+    step(d)
+    step(c)
+    step(e)
     step(b)
     step(d)
-    step(c)
     step(a)
-    step(e)
-    step(d)
-    step(b)
     step(e)
     step(*twos)
     return [final_sum(line, remap[-1], pitch) for line, remap in zip((ones, twos), remaps)]
@@ -344,7 +351,7 @@
     ]
     tiles = max(latlon.shape[2], healpix.shape[2]) // LANES
     size = devices * tiles * round_up(latlon.shape[1], 8) * LANES * 4
-    if devices == 1 << len(EVEN) and size <= ACC_LIMIT:
+    if devices == 1 << BITS and size <= ACC_LIMIT:
         return tuple(bit_remaps(remaps, devices))
     return tuple(slot_remap(*remap) for remap in remaps)
 

time: 61.8 us -> 58.5 us (0.947)
  waiting for transfers between devices: 23.1 us -> 13.9 us
  starting transfers between devices: 25.4 us -> 31.4 us
    ppermute x19, waiting for transfers between devices: 23.1 us -> 13.9 us  [exchange(): return lax.ppermute(value, 'curve', pairs)]
    ppermute x19, starting transfers between devices: 25.4 us -> 31.4 us  [exchange(): return lax.ppermute(value, 'curve', pairs)]
  transfers between devices with their start and end apart: 19 -> 19, of which waited for: 9 -> 10; matrix products, arithmetic and copies ran while one was open for 2% -> 2% of each run, Pallas kernels for 9% -> 10%
where the time goes in v7:
time: 58.5 us; the launch traced here: 58.3 us
  starting transfers between devices  31.4 us (54%)
  waiting for transfers between devices  13.9 us (24%)
  Pallas kernels  11.4 us (19%)
  other arithmetic  0.95 us (2%)
  between operations  0.74 us (1%)
    ppermute x19, starting transfers between devices, exchange(): return lax.ppermute(value, 'curve', pairs)  31.4 us
    ppermute x19, waiting for transfers between devices, exchange(): return lax.ppermute(value, 'curve', pairs)  13.9 us
    pallas_call x2, Pallas kernels, products(): pl.pallas_call(functools.partial(product_kernel, channels, pitch, chunks,...  9.73 us
    pallas_call x2, Pallas kernels, final_sum(): pl.pallas_call(functools.partial(final_kernel, like_shape[1], pitch, part...  1.66 us
  transfers between devices with their start and end apart: 19, of which 10 were waited for; matrix products, arithmetic and copies ran while one was open for 2% of the time, Pallas kernels for 10%

profile of v7, /device:TPU:0, one launch (start us, length us, event | category | flops | bytes accessed | tf_op | source)
XLA Modules:
  0.0 58.3 jit_solution(15067658287888267006)
XLA Ops:
  0.6 4.8 %shard_map.113 = (f32[3456,128]{1,0:T(8,128)S(1)}, bf16[3456,128]{1,0:T(8,128)(2,1)S(1)}, f32[3456,128]{1,0:T(8,128)S(1)}, bf16[3456,128]{1,0:T(8,128)(2,1)S(1)}) custom-call(s32[144]{0:T(256)} %source_hbm.2, s32[144]{0:T(256)} %target_hbm.2, s32[1,16]{1,0:T(1,128)} %counts_hbm.2, bf16[1,69,1536]{2,1,0:T(8,128)(2,1)} %x_hbm.1, bf16[144,128,128]{2,1,0:T(8,128)(2,1)} %w_hbm.2), custom_call_target="tpu_custom_call" | custom-call | flops 325582848 | bytes 10027008 | tf_op jit(solution)/shard_map/pallas_call | solution.py:162
  5.5 0.5 collective-permute-start.1
  6.0 0.1 collective-permute-start
  6.1 2.0 %collective-permute-done.1 = bf16[3456,128]{1,0:T(8,128)(2,1)S(1)} collective-permute-done((bf16[3456,128]{1,0:T(8,128)(2,1)S(1)}, bf16[3456,128]{1,0:T(8,128)(2,1)S(1)}, u32[]{:S(2)}, u32[]{:S(2)}) %collective-permute-start.1) | collective-permute-done | bytes 884768 | tf_op jit(solution)/shard_map/ppermute | solution.py:189
  8.1 0.1 add_convert_fusion
  8.2 3.0 %collective-permute-start.2 = (bf16[2592,128]{1,0:T(8,128)(2,1)S(1)}, bf16[2592,128]{1,0:T(8,128)(2,1)S(1)}, u32[]{:S(2)}, u32[]{:S(2)}) collective-permute-start(bf16[2592,128]{1,0:T(8,128)(2,1)S(1)} %add_convert_fusion), channel_id=1, source_target_pairs={{0,2},{1,5},{2,0},{3,7},{4,6},{5,1},{6,4},{7,3},{8,10},{9,13},{10,... | collective-permute-start | bytes 1990664 | tf_op jit(solution)/shard_map/ppermute | solution.py:189
  11.2 0.0 collective-permute-done.refs_1_.refs_6_
  11.2 4.9 %shard_map.114 = (f32[3456,128]{1,0:T(8,128)S(1)}, bf16[3456,128]{1,0:T(8,128)(2,1)S(1)}, f32[3456,128]{1,0:T(8,128)S(1)}, bf16[3456,128]{1,0:T(8,128)(2,1)S(1)}) custom-call(s32[144]{0:T(256)} %source_hbm.3, s32[144]{0:T(256)} %target_hbm.3, s32[1,16]{1,0:T(1,128)} %counts_hbm.3, bf16[1,69,1536]{2,1,0:T(8,128)(2,1)} %x_hbm.2, bf16[144,128,128]{2,1,0:T(8,128)(2,1)} %w_hbm.3), custom_call_target="tpu_custom_call" | custom-call | flops 325582848 | bytes 10027008 | tf_op jit(solution)/shard_map/pallas_call | solution.py:162
  16.1 0.1 collective-permute-start.4
  16.2 1.4 %collective-permute-start.5 = (bf16[864,128]{1,0:T(8,128)(2,1)S(1)}, bf16[864,128]{1,0:T(8,128)(2,1)S(1)}, u32[]{:S(2)}, u32[]{:S(2)}) collective-permute-start(bf16[864,128]{1,0:T(8,128)(2,1)S(1)} %add_convert_fusion.5), channel_id=1, source_target_pairs={{0,2},{1,5},{2,0},{3,7},{4,6},{5,1},{6,4},{7,3},{8,10},{9,13},{10,... | collective-permute-start | bytes 663560 | tf_op jit(solution)/shard_map/ppermute | solution.py:189
  17.6 0.4 collective-permute-start.7
  18.0 1.8 %collective-permute-done.2.refs_2_ = bf16[2592,128]{1,0:T(8,128)(2,1)S(1)} collective-permute-done((bf16[2592,128]{1,0:T(8,128)(2,1)S(1)}, bf16[2592,128]{1,0:T(8,128)(2,1)S(1)}, u32[]{:S(2)}, u32[]{:S(2)}) %collective-permute-start.2) | collective-permute-done | bytes 663584 | tf_op jit(solution)/shard_map/ppermute | solution.py:189
  19.8 0.1 add_convert_fusion.2
  19.9 2.2 %collective-permute-start.3 = (bf16[1296,128]{1,0:T(8,128)(2,1)S(1)}, bf16[1296,128]{1,0:T(8,128)(2,1)S(1)}, u32[]{:S(2)}, u32[]{:S(2)}) collective-permute-start(bf16[1296,128]{1,0:T(8,128)(2,1)S(1)} %add_convert_fusion.2), channel_id=1, source_target_pairs={{0,4},{1,3},{2,6},{3,1},{4,0},{5,7},{6,2},{7,5},{8,12},{9,11},{10,... | collective-permute-start | bytes 995336 | tf_op jit(solution)/shard_map/ppermute | solution.py:189
  22.1 0.1 collective-permute-done.5.refs_7_
  22.2 2.4 %collective-permute-start.8 = (bf16[432,128]{1,0:T(8,128)(2,1)S(1)}, bf16[432,128]{1,0:T(8,128)(2,1)S(1)}, u32[]{:S(2)}, u32[]{:S(2)}) collective-permute-start(bf16[432,128]{1,0:T(8,128)(2,1)S(1)} %add_convert_fusion.10), channel_id=1, source_target_pairs={{0,4},{1,3},{2,6},{3,1},{4,0},{5,7},{6,2},{7,5},{8,12},{9,11},{10,... | collective-permute-start | bytes 331784 | tf_op jit(solution)/shard_map/ppermute | solution.py:189
  24.6 0.0 collective-permute-done.4
  24.6 0.1 add_convert_fusion.3
  24.7 0.1 add_convert_fusion.1
  24.8 1.6 %collective-permute-start.10 = (bf16[1440,128]{1,0:T(8,128)(2,1)S(1)}, bf16[1440,128]{1,0:T(8,128)(2,1)S(1)}, u32[]{:S(2)}, u32[]{:S(2)}) collective-permute-start(bf16[1440,128]{1,0:T(8,128)(2,1)S(1)} %add_convert_fusion.1), channel_id=1, source_target_pairs={{0,2},{1,5},{2,0},{3,7},{4,6},{5,1},{6,4},{7,3},{8,10},{9,13},{10,... | collective-permute-start | bytes 1105928 | tf_op jit(solution)/shard_map/ppermute | solution.py:189
  26.4 0.6 collective-permute-start.9
  27.0 1.2 %collective-permute-done.3.refs_3_ = bf16[1296,128]{1,0:T(8,128)(2,1)S(1)} collective-permute-done((bf16[1296,128]{1,0:T(8,128)(2,1)S(1)}, bf16[1296,128]{1,0:T(8,128)(2,1)S(1)}, u32[]{:S(2)}, u32[]{:S(2)}) %collective-permute-start.3) | collective-permute-done | bytes 331808 | tf_op jit(solution)/shard_map/ppermute | solution.py:189
  28.2 0.1 add_convert_fusion.7
  28.2 3.5 %collective-permute-start.6 = (bf16[648,128]{1,0:T(8,128)(2,1)S(1)}, bf16[648,128]{1,0:T(8,128)(2,1)S(1)}, u32[]{:S(2)}, u32[]{:S(2)}) collective-permute-start(bf16[648,128]{1,0:T(8,128)(2,1)S(1)} %add_convert_fusion.7), channel_id=1, source_target_pairs={{0,8},{1,9},{2,10},{3,11},{4,12},{5,13},{6,14},{7,15},{8,0},{9,1},... | collective-permute-start | bytes 497672 | tf_op jit(solution)/shard_map/ppermute | solution.py:189
  31.8 0.5 collective-permute-done.8.refs_8_
  32.3 3.3 %collective-permute-start.12 = (bf16[216,128]{1,0:T(8,128)(2,1)S(1)}, bf16[216,128]{1,0:T(8,128)(2,1)S(1)}, u32[]{:S(2)}, u32[]{:S(2)}) collective-permute-start(bf16[216,128]{1,0:T(8,128)(2,1)S(1)} %add_convert_fusion.14), channel_id=1, source_target_pairs={{0,8},{1,9},{2,10},{3,11},{4,12},{5,13},{6,14},{7,15},{8,0},{9,1},... | collective-permute-start | bytes 165896 | tf_op jit(solution)/shard_map/ppermute | solution.py:189
  35.7 0.0 collective-permute-done.7.refs_1_.refs_6_.refs_11_
  35.7 0.1 add_convert_fusion.6
  35.8 2.4 %collective-permute-start.14 = (bf16[720,128]{1,0:T(8,128)(2,1)S(1)}, bf16[720,128]{1,0:T(8,128)(2,1)S(1)}, u32[]{:S(2)}, u32[]{:S(2)}) collective-permute-start(bf16[720,128]{1,0:T(8,128)(2,1)S(1)} %add_convert_fusion.6), channel_id=1, source_target_pairs={{0,4},{1,3},{2,6},{3,1},{4,0},{5,7},{6,2},{7,5},{8,12},{9,11},{10,... | collective-permute-start | bytes 552968 | tf_op jit(solution)/shard_map/ppermute | solution.py:189
  38.2 0.0 collective-permute-done.9.refs_7_
  38.2 2.6 %collective-permute-start.13 = (bf16[864,128]{1,0:T(8,128)(2,1)S(1)}, bf16[864,128]{1,0:T(8,128)(2,1)S(1)}, u32[]{:S(2)}, u32[]{:S(2)}) collective-permute-start(bf16[864,128]{1,0:T(8,128)(2,1)S(1)} %add_convert_fusion.4), channel_id=1, source_target_pairs={{0,2},{1,3},{2,0},{3,1},{4,6},{5,7},{6,4},{7,5},{8,10},{9,11},{10,... | collective-permute-start | bytes 663560 | tf_op jit(solution)/shard_map/ppermute | solution.py:189
  40.8 0.1 add_convert_fusion.8
  40.9 1.7 %collective-permute-start.11 = (bf16[576,128]{1,0:T(8,128)(2,1)S(1)}, bf16[576,128]{1,0:T(8,128)(2,1)S(1)}, u32[]{:S(2)}, u32[]{:S(2)}) collective-permute-start(bf16[576,128]{1,0:T(8,128)(2,1)S(1)} %add_convert_fusion.8), channel_id=1, source_target_pairs={{0,4},{1,5},{2,6},{3,7},{4,0},{5,1},{6,2},{7,3},{8,12},{9,13},{10,... | collective-permute-start | bytes 442376 | tf_op jit(solution)/shard_map/ppermute | solution.py:189
  42.5 1.5 %collective-permute-done.14.refs_3_ = bf16[720,128]{1,0:T(8,128)(2,1)S(1)} collective-permute-done((bf16[720,128]{1,0:T(8,128)(2,1)S(1)}, bf16[720,128]{1,0:T(8,128)(2,1)S(1)}, u32[]{:S(2)}, u32[]{:S(2)}) %collective-permute-start.14) | collective-permute-done | bytes 184352 | tf_op jit(solution)/shard_map/ppermute | solution.py:189
  44.0 0.1 add_convert_fusion.11
  44.1 0.9 %collective-permute-start.15 = (bf16[360,128]{1,0:T(8,128)(2,1)S(1)}, bf16[360,128]{1,0:T(8,128)(2,1)S(1)}, u32[]{:S(2)}, u32[]{:S(2)}) collective-permute-start(bf16[360,128]{1,0:T(8,128)(2,1)S(1)} %add_convert_fusion.11), channel_id=1, source_target_pairs={{0,8},{1,9},{2,10},{3,11},{4,12},{5,13},{6,14},{7,15},{8,0},{9,1},... | collective-permute-start | bytes 276488 | tf_op jit(solution)/shard_map/ppermute | solution.py:189
  45.0 0.8 %collective-permute-done.13.refs_12_ = bf16[864,128]{1,0:T(8,128)(2,1)S(1)} collective-permute-done((bf16[864,128]{1,0:T(8,128)(2,1)S(1)}, bf16[864,128]{1,0:T(8,128)(2,1)S(1)}, u32[]{:S(2)}, u32[]{:S(2)}) %collective-permute-start.13) | collective-permute-done | bytes 221216 | tf_op jit(solution)/shard_map/ppermute | solution.py:189
  45.8 0.1 add_convert_fusion.9
  45.9 1.7 %collective-permute-start.17 = (bf16[432,128]{1,0:T(8,128)(2,1)S(1)}, bf16[432,128]{1,0:T(8,128)(2,1)S(1)}, u32[]{:S(2)}, u32[]{:S(2)}) collective-permute-start(bf16[432,128]{1,0:T(8,128)(2,1)S(1)} %add_convert_fusion.9), channel_id=1, source_target_pairs={{0,4},{1,5},{2,6},{3,7},{4,0},{5,1},{6,2},{7,3},{8,12},{9,13},{10,... | collective-permute-start | bytes 331784 | tf_op jit(solution)/shard_map/ppermute | solution.py:189
  47.6 0.0 collective-permute-done.12.refs_9_
  47.7 1.5 %collective-permute-start.16 = (bf16[288,128]{1,0:T(8,128)(2,1)S(1)}, bf16[288,128]{1,0:T(8,128)(2,1)S(1)}, u32[]{:S(2)}, u32[]{:S(2)}) collective-permute-start(bf16[288,128]{1,0:T(8,128)(2,1)S(1)} %add_convert_fusion.12), channel_id=1, source_target_pairs={{0,8},{1,9},{2,10},{3,11},{4,12},{5,13},{6,14},{7,15},{8,0},{9,1},... | collective-permute-start | bytes 221192 | tf_op jit(solution)/shard_map/ppermute | solution.py:189
  49.2 2.6 %collective-permute-done.17.refs_13_ = bf16[432,128]{1,0:T(8,128)(2,1)S(1)} collective-permute-done((bf16[432,128]{1,0:T(8,128)(2,1)S(1)}, bf16[432,128]{1,0:T(8,128)(2,1)S(1)}, u32[]{:S(2)}, u32[]{:S(2)}) %collective-permute-start.17) | collective-permute-done | bytes 110624 | tf_op jit(solution)/shard_map/ppermute | solution.py:189
  51.8 1.4 %collective-permute-start.18 = (bf16[216,128]{1,0:T(8,128)(2,1)S(1)}, bf16[216,128]{1,0:T(8,128)(2,1)S(1)}, u32[]{:S(2)}, u32[]{:S(2)}) collective-permute-start(bf16[216,128]{1,0:T(8,128)(2,1)S(1)} %add_convert_fusion.13), channel_id=1, source_target_pairs={{0,8},{1,9},{2,10},{3,11},{4,12},{5,13},{6,14},{7,15},{8,0},{9,1},... | collective-permute-start | bytes 165896 | tf_op jit(solution)/shard_map/ppermute | solution.py:189
  53.2 0.8 %shard_map.115 = bf16[1,69,1536]{2,1,0:T(8,128)(2,1)} custom-call(f32[3456,128]{1,0:T(8,128)S(1)} %get-tuple-element.42.refs_0_.refs_5_, bf16[3456,128]{1,0:T(8,128)(2,1)S(1)} %collective-permute-done.refs_1_.refs_6_, bf16[2592,128]{1,0:T(8,128)(2,1)S(1)} %collective-permute-done.2.refs_2_, bf16[1296,128]{1,0:T(8,128)(2,1)S(1)} %collective-permute-done.3.refs_3_, ...), custom_call_target="tpu_custom_call" | custom-call | tf_op jit(solution)/shard_map/pallas_call | solution.py:249
  54.0 0.0 collective-permute-done.15.refs_4_
  54.0 0.8 %collective-permute-done.16.refs_9_ = bf16[288,128]{1,0:T(8,128)(2,1)S(1)} collective-permute-done((bf16[288,128]{1,0:T(8,128)(2,1)S(1)}, bf16[288,128]{1,0:T(8,128)(2,1)S(1)}, u32[]{:S(2)}, u32[]{:S(2)}) %collective-permute-start.16) | collective-permute-done | bytes 73760 | tf_op jit(solution)/shard_map/ppermute | solution.py:189
  54.9 2.6 %collective-permute-done.18.refs_14_ = bf16[216,128]{1,0:T(8,128)(2,1)S(1)} collective-permute-done((bf16[216,128]{1,0:T(8,128)(2,1)S(1)}, bf16[216,128]{1,0:T(8,128)(2,1)S(1)}, u32[]{:S(2)}, u32[]{:S(2)}) %collective-permute-start.18) | collective-permute-done | bytes 55328 | tf_op jit(solution)/shard_map/ppermute | solution.py:189
  57.5 0.8 %shard_map.116 = bf16[1,69,1536]{2,1,0:T(8,128)(2,1)} custom-call(f32[3456,128]{1,0:T(8,128)S(1)} %get-tuple-element.55.refs_0_.refs_5_.refs_10_, bf16[3456,128]{1,0:T(8,128)(2,1)S(1)} %collective-permute-done.7.refs_1_.refs_6_.refs_11_, bf16[1440,128]{1,0:T(8,128)(2,1)S(1)} %collective-permute-done.10.refs_2_, ...), custom_call_target="tpu_custom_call" | custom-call | tf_op jit(solution)/shard_map/pallas_call | solution.py:249
  (9 shorter events, 0.3 us)
Async XLA Ops:
  5.5 2.6 %collective-permute-start.1 = (bf16[3456,128]{1,0:T(8,128)(2,1)S(1)}, bf16[3456,128]{1,0:T(8,128)(2,1)S(1)}, u32[]{:S(2)}, u32[]{:S(2)}) collective-permute-start(bf16[3456,128]{1,0:T(8,128)(2,1)S(1)} %get-tuple-element.39), channel_id=1, source_target_pairs={{0,1},{1,0},{2,3},{3,2},{4,5},{5,4},{6,7},{7,6},{8,9},{9,8},{10,11... | collective-permute-start | bytes 2654216 | tf_op jit(solution)/shard_map/ppermute | solution.py:189
  6.0 5.2 %collective-permute-start = (bf16[3456,128]{1,0:T(8,128)(2,1)S(1)}, bf16[3456,128]{1,0:T(8,128)(2,1)S(1)}, u32[]{:S(2)}, u32[]{:S(2)}) collective-permute-start(bf16[3456,128]{1,0:T(8,128)(2,1)S(1)} %get-tuple-element.37), channel_id=1, source_target_pairs={{0,1},{1,0},{2,3},{3,2},{4,5},{5,4},{6,7},{7,6},{8,9},{9,8},{10,11... | collective-permute-start | bytes 2654216 | tf_op jit(solution)/shard_map/ppermute | solution.py:189
  8.2 11.6 %collective-permute-start.2 = (bf16[2592,128]{1,0:T(8,128)(2,1)S(1)}, bf16[2592,128]{1,0:T(8,128)(2,1)S(1)}, u32[]{:S(2)}, u32[]{:S(2)}) collective-permute-start(bf16[2592,128]{1,0:T(8,128)(2,1)S(1)} %add_convert_fusion), channel_id=1, source_target_pairs={{0,2},{1,5},{2,0},{3,7},{4,6},{5,1},{6,4},{7,3},{8,10},{9,13},{10,... | collective-permute-start | bytes 1990664 | tf_op jit(solution)/shard_map/ppermute | solution.py:189
  16.1 8.5 %collective-permute-start.4 = (bf16[3456,128]{1,0:T(8,128)(2,1)S(1)}, bf16[3456,128]{1,0:T(8,128)(2,1)S(1)}, u32[]{:S(2)}, u32[]{:S(2)}) collective-permute-start(bf16[3456,128]{1,0:T(8,128)(2,1)S(1)} %get-tuple-element.48), channel_id=1, source_target_pairs={{0,1},{1,0},{2,3},{3,2},{4,5},{5,4},{6,7},{7,6},{8,9},{9,8},{10,11... | collective-permute-start | bytes 2654216 | tf_op jit(solution)/shard_map/ppermute | solution.py:189
  16.2 6.0 %collective-permute-start.5 = (bf16[864,128]{1,0:T(8,128)(2,1)S(1)}, bf16[864,128]{1,0:T(8,128)(2,1)S(1)}, u32[]{:S(2)}, u32[]{:S(2)}) collective-permute-start(bf16[864,128]{1,0:T(8,128)(2,1)S(1)} %add_convert_fusion.5), channel_id=1, source_target_pairs={{0,2},{1,5},{2,0},{3,7},{4,6},{5,1},{6,4},{7,3},{8,10},{9,13},{10,... | collective-permute-start | bytes 663560 | tf_op jit(solution)/shard_map/ppermute | solution.py:189
  17.6 18.0 %collective-permute-start.7 = (bf16[3456,128]{1,0:T(8,128)(2,1)S(1)}, bf16[3456,128]{1,0:T(8,128)(2,1)S(1)}, u32[]{:S(2)}, u32[]{:S(2)}) collective-permute-start(bf16[3456,128]{1,0:T(8,128)(2,1)S(1)} %get-tuple-element.46), channel_id=1, source_target_pairs={{0,1},{1,0},{2,3},{3,2},{4,5},{5,4},{6,7},{7,6},{8,9},{9,8},{10,11... | collective-permute-start | bytes 2654216 | tf_op jit(solution)/shard_map/ppermute | solution.py:189
  19.9 8.2 %collective-permute-start.3 = (bf16[1296,128]{1,0:T(8,128)(2,1)S(1)}, bf16[1296,128]{1,0:T(8,128)(2,1)S(1)}, u32[]{:S(2)}, u32[]{:S(2)}) collective-permute-start(bf16[1296,128]{1,0:T(8,128)(2,1)S(1)} %add_convert_fusion.2), channel_id=1, source_target_pairs={{0,4},{1,3},{2,6},{3,1},{4,0},{5,7},{6,2},{7,5},{8,12},{9,11},{10,... | collective-permute-start | bytes 995336 | tf_op jit(solution)/shard_map/ppermute | solution.py:189
  22.2 10.1 %collective-permute-start.8 = (bf16[432,128]{1,0:T(8,128)(2,1)S(1)}, bf16[432,128]{1,0:T(8,128)(2,1)S(1)}, u32[]{:S(2)}, u32[]{:S(2)}) collective-permute-start(bf16[432,128]{1,0:T(8,128)(2,1)S(1)} %add_convert_fusion.10), channel_id=1, source_target_pairs={{0,4},{1,3},{2,6},{3,1},{4,0},{5,7},{6,2},{7,5},{8,12},{9,11},{10,... | collective-permute-start | bytes 331784 | tf_op jit(solution)/shard_map/ppermute | solution.py:189
  24.8 10.9 %collective-permute-start.10 = (bf16[1440,128]{1,0:T(8,128)(2,1)S(1)}, bf16[1440,128]{1,0:T(8,128)(2,1)S(1)}, u32[]{:S(2)}, u32[]{:S(2)}) collective-permute-start(bf16[1440,128]{1,0:T(8,128)(2,1)S(1)} %add_convert_fusion.1), channel_id=1, source_target_pairs={{0,2},{1,5},{2,0},{3,7},{4,6},{5,1},{6,4},{7,3},{8,10},{9,13},{10,... | collective-permute-start | bytes 1105928 | tf_op jit(solution)/shard_map/ppermute | solution.py:189
  26.4 11.8 %collective-permute-start.9 = (bf16[1152,128]{1,0:T(8,128)(2,1)S(1)}, bf16[1152,128]{1,0:T(8,128)(2,1)S(1)}, u32[]{:S(2)}, u32[]{:S(2)}) collective-permute-start(bf16[1152,128]{1,0:T(8,128)(2,1)S(1)} %add_convert_fusion.3), channel_id=1, source_target_pairs={{0,2},{1,3},{2,0},{3,1},{4,6},{5,7},{6,4},{7,5},{8,10},{9,11},{10,... | collective-permute-start | bytes 884744 | tf_op jit(solution)/shard_map/ppermute | solution.py:189
  28.2 20.9 %collective-permute-start.6 = (bf16[648,128]{1,0:T(8,128)(2,1)S(1)}, bf16[648,128]{1,0:T(8,128)(2,1)S(1)}, u32[]{:S(2)}, u32[]{:S(2)}) collective-permute-start(bf16[648,128]{1,0:T(8,128)(2,1)S(1)} %add_convert_fusion.7), channel_id=1, source_target_pairs={{0,8},{1,9},{2,10},{3,11},{4,12},{5,13},{6,14},{7,15},{8,0},{9,1},... | collective-permute-start | bytes 497672 | tf_op jit(solution)/shard_map/ppermute | solution.py:189
  32.3 15.3 %collective-permute-start.12 = (bf16[216,128]{1,0:T(8,128)(2,1)S(1)}, bf16[216,128]{1,0:T(8,128)(2,1)S(1)}, u32[]{:S(2)}, u32[]{:S(2)}) collective-permute-start(bf16[216,128]{1,0:T(8,128)(2,1)S(1)} %add_convert_fusion.14), channel_id=1, source_target_pairs={{0,8},{1,9},{2,10},{3,11},{4,12},{5,13},{6,14},{7,15},{8,0},{9,1},... | collective-permute-start | bytes 165896 | tf_op jit(solution)/shard_map/ppermute | solution.py:189
  35.8 8.2 %collective-permute-start.14 = (bf16[720,128]{1,0:T(8,128)(2,1)S(1)}, bf16[720,128]{1,0:T(8,128)(2,1)S(1)}, u32[]{:S(2)}, u32[]{:S(2)}) collective-permute-start(bf16[720,128]{1,0:T(8,128)(2,1)S(1)} %add_convert_fusion.6), channel_id=1, source_target_pairs={{0,4},{1,3},{2,6},{3,1},{4,0},{5,7},{6,2},{7,5},{8,12},{9,11},{10,... | collective-permute-start | bytes 552968 | tf_op jit(solution)/shard_map/ppermute | solution.py:189
  38.2 7.6 %collective-permute-start.13 = (bf16[864,128]{1,0:T(8,128)(2,1)S(1)}, bf16[864,128]{1,0:T(8,128)(2,1)S(1)}, u32[]{:S(2)}, u32[]{:S(2)}) collective-permute-start(bf16[864,128]{1,0:T(8,128)(2,1)S(1)} %add_convert_fusion.4), channel_id=1, source_target_pairs={{0,2},{1,3},{2,0},{3,1},{4,6},{5,7},{6,4},{7,5},{8,10},{9,11},{10,... | collective-permute-start | bytes 663560 | tf_op jit(solution)/shard_map/ppermute | solution.py:189
  40.9 6.8 %collective-permute-start.11 = (bf16[576,128]{1,0:T(8,128)(2,1)S(1)}, bf16[576,128]{1,0:T(8,128)(2,1)S(1)}, u32[]{:S(2)}, u32[]{:S(2)}) collective-permute-start(bf16[576,128]{1,0:T(8,128)(2,1)S(1)} %add_convert_fusion.8), channel_id=1, source_target_pairs={{0,4},{1,5},{2,6},{3,7},{4,0},{5,1},{6,2},{7,3},{8,12},{9,13},{10,... | collective-permute-start | bytes 442376 | tf_op jit(solution)/shard_map/ppermute | solution.py:189
  44.1 10.0 %collective-permute-start.15 = (bf16[360,128]{1,0:T(8,128)(2,1)S(1)}, bf16[360,128]{1,0:T(8,128)(2,1)S(1)}, u32[]{:S(2)}, u32[]{:S(2)}) collective-permute-start(bf16[360,128]{1,0:T(8,128)(2,1)S(1)} %add_convert_fusion.11), channel_id=1, source_target_pairs={{0,8},{1,9},{2,10},{3,11},{4,12},{5,13},{6,14},{7,15},{8,0},{9,1},... | collective-permute-start | bytes 276488 | tf_op jit(solution)/shard_map/ppermute | solution.py:189
  45.9 5.9 %collective-permute-start.17 = (bf16[432,128]{1,0:T(8,128)(2,1)S(1)}, bf16[432,128]{1,0:T(8,128)(2,1)S(1)}, u32[]{:S(2)}, u32[]{:S(2)}) collective-permute-start(bf16[432,128]{1,0:T(8,128)(2,1)S(1)} %add_convert_fusion.9), channel_id=1, source_target_pairs={{0,4},{1,5},{2,6},{3,7},{4,0},{5,1},{6,2},{7,3},{8,12},{9,13},{10,... | collective-permute-start | bytes 331784 | tf_op jit(solution)/shard_map/ppermute | solution.py:189
  47.7 7.2 %collective-permute-start.16 = (bf16[288,128]{1,0:T(8,128)(2,1)S(1)}, bf16[288,128]{1,0:T(8,128)(2,1)S(1)}, u32[]{:S(2)}, u32[]{:S(2)}) collective-permute-start(bf16[288,128]{1,0:T(8,128)(2,1)S(1)} %add_convert_fusion.12), channel_id=1, source_target_pairs={{0,8},{1,9},{2,10},{3,11},{4,12},{5,13},{6,14},{7,15},{8,0},{9,1},... | collective-permute-start | bytes 221192 | tf_op jit(solution)/shard_map/ppermute | solution.py:189
  51.8 5.7 %collective-permute-start.18 = (bf16[216,128]{1,0:T(8,128)(2,1)S(1)}, bf16[216,128]{1,0:T(8,128)(2,1)S(1)}, u32[]{:S(2)}, u32[]{:S(2)}) collective-permute-start(bf16[216,128]{1,0:T(8,128)(2,1)S(1)} %add_convert_fusion.13), channel_id=1, source_target_pairs={{0,8},{1,9},{2,10},{3,11},{4,12},{5,13},{6,14},{7,15},{8,0},{9,1},... | collective-permute-start | bytes 165896 | tf_op jit(solution)/shard_map/ppermute | solution.py:189

commit v8 on v7

--- a/solution.py
+++ b/solution.py
@@ -274,8 +274,8 @@
     tiles = one[-1][2] // LANES
     some, most = tiles * 5 // 12, tiles * 3 // 4
     plans = (
-        [(0, most, MIXED), (most, tiles, MIXED)],
-        [(0, some, MIXED), (some, most, STRAIGHT), (most, tiles, STRAIGHT)],
+        [(0, tiles, MIXED)],
+        [(0, some, MIXED), (some, most, MIXED), (most, tiles, STRAIGHT)],
     )
     ones, twos = [[Chain(chunk, devices, pitch) for chunk in chunks] for chunks in plans]
     order = Order()
@@ -299,22 +299,17 @@
         for chain in line:
             chain.rest(terms)
 
-    def begun(chain):
-        chain.total = order.after(chain.total)
-        chain.second()
-
     def both_cores(keep, send):
         return [keep, exchange(send, STRAIGHT, 0, devices)]
 
-    a, b = ones
-    c, d, e = twos
+    (a,) = ones
+    b, c, d = twos
 
     keep, send, keep_on, send_on = products(one, plans[0], devices)
     on = both_cores(keep_on, send_on)
     rest = both_cores(keep, send)
     summed(ones, on)
     a.second()
-    b.second()
     rested(ones, rest)
     made = products((order.after(two[0]),) + two[1:], plans[1], devices)
     order.before(made)
@@ -323,23 +318,20 @@
     rest = both_cores(keep, send)
 
     step(a)
+    summed(twos, on)
+    for chain in twos:
+        chain.second()
+    step(a)
+    rested(twos, rest)
     step(b)
-    summed(twos, on)
-    c.second()
-    begun(d)
-    step(a)
-    step(b)
-    rested(twos, rest)
     step(c)
-    begun(e)
-    step(d)
-    step(c)
-    step(e)
     step(b)
     step(d)
     step(a)
-    step(e)
-    step(*twos)
+    step(c)
+    step(d)
+    step(c)
+    step(b, d)
     return [final_sum(line, remap[-1], pitch) for line, remap in zip((ones, twos), remaps)]
 
 

time: 58.5 us -> 62.2 us (1.063)
  waiting for transfers between devices: 13.9 us -> 27.7 us
  starting transfers between devices: 31.4 us -> 21.6 us
    ppermute x19 -> x16, waiting for transfers between devices: 13.9 us -> 27.7 us  [exchange(): return lax.ppermute(value, 'curve', pairs)]
    ppermute x19 -> x16, starting transfers between devices: 31.4 us -> 21.6 us  [exchange(): return lax.ppermute(value, 'curve', pairs)]
  transfers between devices with their start and end apart: 19 -> 16, of which waited for: 10 -> 7; matrix products, arithmetic and copies ran while one was open for 2% -> 1% of each run, Pallas kernels for 10% -> 9%
where the time goes in v8:
time: 62.2 us; the launch traced here: 62.3 us
  waiting for transfers between devices  27.7 us (45%)
  starting transfers between devices  21.6 us (35%)
  Pallas kernels  11.3 us (18%)
  other arithmetic  0.93 us (1%)
  between operations  0.72 us (1%)
    ppermute x16, waiting for transfers between devices, exchange(): return lax.ppermute(value, 'curve', pairs)  27.7 us
    ppermute x16, starting transfers between devices, exchange(): return lax.ppermute(value, 'curve', pairs)  21.6 us
    pallas_call x2, Pallas kernels, products(): pl.pallas_call(functools.partial(product_kernel, channels, pitch, chunks,...  9.66 us
    pallas_call x2, Pallas kernels, final_sum(): pl.pallas_call(functools.partial(final_kernel, like_shape[1], pitch, part...  1.66 us
  transfers between devices with their start and end apart: 16, of which 7 were waited for; matrix products, arithmetic and copies ran while one was open for 1% of the time, Pallas kernels for 9%

profile of v8, /device:TPU:0, one launch (start us, length us, event | category | flops | bytes accessed | tf_op | source)
XLA Modules:
  0.0 62.3 jit_solution(6887521196787465916)
XLA Ops:
  0.6 4.8 %shard_map.113 = (f32[3456,128]{1,0:T(8,128)S(1)}, bf16[3456,128]{1,0:T(8,128)(2,1)S(1)}, f32[3456,128]{1,0:T(8,128)S(1)}, bf16[3456,128]{1,0:T(8,128)(2,1)S(1)}) custom-call(s32[144]{0:T(256)} %source_hbm.2, s32[144]{0:T(256)} %target_hbm.2, s32[1,16]{1,0:T(1,128)} %counts_hbm.2, bf16[1,69,1536]{2,1,0:T(8,128)(2,1)} %x_hbm.1, bf16[144,128,128]{2,1,0:T(8,128)(2,1)} %w_hbm.2), custom_call_target="tpu_custom_call" | custom-call | flops 325582848 | bytes 10027008 | tf_op jit(solution)/shard_map/pallas_call | solution.py:162
  5.4 0.5 collective-permute-start.1
  6.0 0.1 collective-permute-start
  6.1 2.0 %collective-permute-done.1 = bf16[3456,128]{1,0:T(8,128)(2,1)S(1)} collective-permute-done((bf16[3456,128]{1,0:T(8,128)(2,1)S(1)}, bf16[3456,128]{1,0:T(8,128)(2,1)S(1)}, u32[]{:S(2)}, u32[]{:S(2)}) %collective-permute-start.1) | collective-permute-done | bytes 884768 | tf_op jit(solution)/shard_map/ppermute | solution.py:189
  8.0 0.2 add_convert_fusion
  8.2 3.0 %collective-permute-start.2 = (bf16[3456,128]{1,0:T(8,128)(2,1)S(1)}, bf16[3456,128]{1,0:T(8,128)(2,1)S(1)}, u32[]{:S(2)}, u32[]{:S(2)}) collective-permute-start(bf16[3456,128]{1,0:T(8,128)(2,1)S(1)} %add_convert_fusion), channel_id=1, source_target_pairs={{0,2},{1,5},{2,0},{3,7},{4,6},{5,1},{6,4},{7,3},{8,10},{9,13},{10,... | collective-permute-start | bytes 2654216 | tf_op jit(solution)/shard_map/ppermute | solution.py:189
  11.2 0.0 collective-permute-done.refs_1_
  11.2 4.8 %shard_map.114 = (f32[3456,128]{1,0:T(8,128)S(1)}, bf16[3456,128]{1,0:T(8,128)(2,1)S(1)}, f32[3456,128]{1,0:T(8,128)S(1)}, bf16[3456,128]{1,0:T(8,128)(2,1)S(1)}) custom-call(s32[144]{0:T(256)} %source_hbm.3, s32[144]{0:T(256)} %target_hbm.3, s32[1,16]{1,0:T(1,128)} %counts_hbm.3, bf16[1,69,1536]{2,1,0:T(8,128)(2,1)} %x_hbm.2, bf16[144,128,128]{2,1,0:T(8,128)(2,1)} %w_hbm.3), custom_call_target="tpu_custom_call" | custom-call | flops 325582848 | bytes 10027008 | tf_op jit(solution)/shard_map/pallas_call | solution.py:162
  16.0 0.1 collective-permute-start.4
  16.1 0.5 collective-permute-start.6
  16.6 5.6 %collective-permute-done.2.refs_2_ = bf16[3456,128]{1,0:T(8,128)(2,1)S(1)} collective-permute-done((bf16[3456,128]{1,0:T(8,128)(2,1)S(1)}, bf16[3456,128]{1,0:T(8,128)(2,1)S(1)}, u32[]{:S(2)}, u32[]{:S(2)}) %collective-permute-start.2) | collective-permute-done | bytes 884768 | tf_op jit(solution)/shard_map/ppermute | solution.py:189
  22.2 0.1 add_convert_fusion.1
  22.3 2.1 %collective-permute-start.3 = (bf16[1728,128]{1,0:T(8,128)(2,1)S(1)}, bf16[1728,128]{1,0:T(8,128)(2,1)S(1)}, u32[]{:S(2)}, u32[]{:S(2)}) collective-permute-start(bf16[1728,128]{1,0:T(8,128)(2,1)S(1)} %add_convert_fusion.1), channel_id=1, source_target_pairs={{0,4},{1,3},{2,6},{3,1},{4,0},{5,7},{6,2},{7,5},{8,12},{9,11},{10,... | collective-permute-start | bytes 1327112 | tf_op jit(solution)/shard_map/ppermute | solution.py:189
  24.5 0.0 collective-permute-done.4
  24.5 0.1 add_convert_fusion.3
  24.5 0.1 add_convert_fusion.2
  24.6 1.6 %collective-permute-start.8 = (bf16[1440,128]{1,0:T(8,128)(2,1)S(1)}, bf16[1440,128]{1,0:T(8,128)(2,1)S(1)}, u32[]{:S(2)}, u32[]{:S(2)}) collective-permute-start(bf16[1440,128]{1,0:T(8,128)(2,1)S(1)} %add_convert_fusion.2), channel_id=1, source_target_pairs={{0,2},{1,5},{2,0},{3,7},{4,6},{5,1},{6,4},{7,3},{8,10},{9,13},{10,... | collective-permute-start | bytes 1105928 | tf_op jit(solution)/shard_map/ppermute | solution.py:189
  26.2 0.6 collective-permute-start.10
  26.8 1.5 %collective-permute-start.7 = (bf16[864,128]{1,0:T(8,128)(2,1)S(1)}, bf16[864,128]{1,0:T(8,128)(2,1)S(1)}, u32[]{:S(2)}, u32[]{:S(2)}) collective-permute-start(bf16[864,128]{1,0:T(8,128)(2,1)S(1)} %add_convert_fusion.5), channel_id=1, source_target_pairs={{0,2},{1,3},{2,0},{3,1},{4,6},{5,7},{6,4},{7,5},{8,10},{9,11},{10,... | collective-permute-start | bytes 663560 | tf_op jit(solution)/shard_map/ppermute | solution.py:189
  28.3 9.3 %collective-permute-done.3.refs_3_ = bf16[1728,128]{1,0:T(8,128)(2,1)S(1)} collective-permute-done((bf16[1728,128]{1,0:T(8,128)(2,1)S(1)}, bf16[1728,128]{1,0:T(8,128)(2,1)S(1)}, u32[]{:S(2)}, u32[]{:S(2)}) %collective-permute-start.3) | collective-permute-done | bytes 442400 | tf_op jit(solution)/shard_map/ppermute | solution.py:189
  37.6 0.1 add_convert_fusion.4
  37.7 1.0 %collective-permute-start.5 = (bf16[864,128]{1,0:T(8,128)(2,1)S(1)}, bf16[864,128]{1,0:T(8,128)(2,1)S(1)}, u32[]{:S(2)}, u32[]{:S(2)}) collective-permute-start(bf16[864,128]{1,0:T(8,128)(2,1)S(1)} %add_convert_fusion.4), channel_id=1, source_target_pairs={{0,8},{1,9},{2,10},{3,11},{4,12},{5,13},{6,14},{7,15},{8,0},{9,1},... | collective-permute-start | bytes 663560 | tf_op jit(solution)/shard_map/ppermute | solution.py:189
  38.7 0.0 collective-permute-done.6.refs_1_.refs_6_.refs_11_
  38.7 0.0 collective-permute-done.8.refs_2_
  38.7 0.1 add_convert_fusion.6
  38.8 3.9 %collective-permute-start.9 = (bf16[720,128]{1,0:T(8,128)(2,1)S(1)}, bf16[720,128]{1,0:T(8,128)(2,1)S(1)}, u32[]{:S(2)}, u32[]{:S(2)}) collective-permute-start(bf16[720,128]{1,0:T(8,128)(2,1)S(1)} %add_convert_fusion.6), channel_id=1, source_target_pairs={{0,4},{1,3},{2,6},{3,1},{4,0},{5,7},{6,2},{7,5},{8,12},{9,11},{10,... | collective-permute-start | bytes 552968 | tf_op jit(solution)/shard_map/ppermute | solution.py:189
  42.7 0.0 collective-permute-done.10.refs_7_
  42.7 0.1 add_convert_fusion.7
  42.8 0.1 collective-permute-start.13
  42.9 4.9 %collective-permute-done.9.refs_3_ = bf16[720,128]{1,0:T(8,128)(2,1)S(1)} collective-permute-done((bf16[720,128]{1,0:T(8,128)(2,1)S(1)}, bf16[720,128]{1,0:T(8,128)(2,1)S(1)}, u32[]{:S(2)}, u32[]{:S(2)}) %collective-permute-start.9) | collective-permute-done | bytes 184352 | tf_op jit(solution)/shard_map/ppermute | solution.py:189
  47.7 0.1 add_convert_fusion.9
  47.8 2.8 %collective-permute-start.11 = (bf16[360,128]{1,0:T(8,128)(2,1)S(1)}, bf16[360,128]{1,0:T(8,128)(2,1)S(1)}, u32[]{:S(2)}, u32[]{:S(2)}) collective-permute-start(bf16[360,128]{1,0:T(8,128)(2,1)S(1)} %add_convert_fusion.9), channel_id=1, source_target_pairs={{0,8},{1,9},{2,10},{3,11},{4,12},{5,13},{6,14},{7,15},{8,0},{9,1},... | collective-permute-start | bytes 276488 | tf_op jit(solution)/shard_map/ppermute | solution.py:189
  50.6 0.0 collective-permute-done.7.refs_12_
  50.6 0.1 add_convert_fusion.8
  50.6 2.4 %collective-permute-start.12 = (bf16[432,128]{1,0:T(8,128)(2,1)S(1)}, bf16[432,128]{1,0:T(8,128)(2,1)S(1)}, u32[]{:S(2)}, u32[]{:S(2)}) collective-permute-start(bf16[432,128]{1,0:T(8,128)(2,1)S(1)} %add_convert_fusion.8), channel_id=1, source_target_pairs={{0,4},{1,5},{2,6},{3,7},{4,0},{5,1},{6,2},{7,3},{8,12},{9,13},{10,... | collective-permute-start | bytes 331784 | tf_op jit(solution)/shard_map/ppermute | solution.py:189
  53.0 0.0 collective-permute-done.5.refs_4_
  53.0 0.0 collective-permute-done.13.refs_8_
  53.1 0.5 collective-permute-start.15
  53.5 2.8 %collective-permute-done.12.refs_13_ = bf16[432,128]{1,0:T(8,128)(2,1)S(1)} collective-permute-done((bf16[432,128]{1,0:T(8,128)(2,1)S(1)}, bf16[432,128]{1,0:T(8,128)(2,1)S(1)}, u32[]{:S(2)}, u32[]{:S(2)}) %collective-permute-start.12) | collective-permute-done | bytes 110624 | tf_op jit(solution)/shard_map/ppermute | solution.py:189
  56.4 1.1 %collective-permute-start.14 = (bf16[216,128]{1,0:T(8,128)(2,1)S(1)}, bf16[216,128]{1,0:T(8,128)(2,1)S(1)}, u32[]{:S(2)}, u32[]{:S(2)}) collective-permute-start(bf16[216,128]{1,0:T(8,128)(2,1)S(1)} %add_convert_fusion.11), channel_id=1, source_target_pairs={{0,8},{1,9},{2,10},{3,11},{4,12},{5,13},{6,14},{7,15},{8,0},{9,1},... | collective-permute-start | bytes 165896 | tf_op jit(solution)/shard_map/ppermute | solution.py:189
  57.5 0.8 %shard_map.115 = bf16[1,69,1536]{2,1,0:T(8,128)(2,1)} custom-call(f32[3456,128]{1,0:T(8,128)S(1)} %get-tuple-element.37.refs_0_, bf16[3456,128]{1,0:T(8,128)(2,1)S(1)} %collective-permute-done.refs_1_, bf16[3456,128]{1,0:T(8,128)(2,1)S(1)} %collective-permute-done.2.refs_2_, bf16[1728,128]{1,0:T(8,128)(2,1)S(1)} %collective-permute-done.3.refs_3_, ...), custom_call_target="tpu_custom_call" | custom-call | tf_op jit(solution)/shard_map/pallas_call | solution.py:249
  58.3 0.3 collective-permute-done.15.refs_9_
  58.6 0.0 collective-permute-done.11.refs_4_
  58.6 2.8 %collective-permute-done.14.refs_14_ = bf16[216,128]{1,0:T(8,128)(2,1)S(1)} collective-permute-done((bf16[216,128]{1,0:T(8,128)(2,1)S(1)}, bf16[216,128]{1,0:T(8,128)(2,1)S(1)}, u32[]{:S(2)}, u32[]{:S(2)}) %collective-permute-start.14) | collective-permute-done | bytes 55328 | tf_op jit(solution)/shard_map/ppermute | solution.py:189
  61.5 0.8 %shard_map.116 = bf16[1,69,1536]{2,1,0:T(8,128)(2,1)} custom-call(f32[3456,128]{1,0:T(8,128)S(1)} %get-tuple-element.48.refs_0_.refs_5_.refs_10_, bf16[3456,128]{1,0:T(8,128)(2,1)S(1)} %collective-permute-done.6.refs_1_.refs_6_.refs_11_, bf16[1440,128]{1,0:T(8,128)(2,1)S(1)} %collective-permute-done.8.refs_2_, ...), custom_call_target="tpu_custom_call" | custom-call | tf_op jit(solution)/shard_map/pallas_call | solution.py:249
  (3 shorter events, 0.1 us)
Async XLA Ops:
  5.4 2.6 %collective-permute-start.1 = (bf16[3456,128]{1,0:T(8,128)(2,1)S(1)}, bf16[3456,128]{1,0:T(8,128)(2,1)S(1)}, u32[]{:S(2)}, u32[]{:S(2)}) collective-permute-start(bf16[3456,128]{1,0:T(8,128)(2,1)S(1)} %get-tuple-element.34), channel_id=1, source_target_pairs={{0,1},{1,0},{2,3},{3,2},{4,5},{5,4},{6,7},{7,6},{8,9},{9,8},{10,11... | collective-permute-start | bytes 2654216 | tf_op jit(solution)/shard_map/ppermute | solution.py:189
  6.0 5.2 %collective-permute-start = (bf16[3456,128]{1,0:T(8,128)(2,1)S(1)}, bf16[3456,128]{1,0:T(8,128)(2,1)S(1)}, u32[]{:S(2)}, u32[]{:S(2)}) collective-permute-start(bf16[3456,128]{1,0:T(8,128)(2,1)S(1)} %get-tuple-element.32), channel_id=1, source_target_pairs={{0,1},{1,0},{2,3},{3,2},{4,5},{5,4},{6,7},{7,6},{8,9},{9,8},{10,11... | collective-permute-start | bytes 2654216 | tf_op jit(solution)/shard_map/ppermute | solution.py:189
  8.2 14.0 %collective-permute-start.2 = (bf16[3456,128]{1,0:T(8,128)(2,1)S(1)}, bf16[3456,128]{1,0:T(8,128)(2,1)S(1)}, u32[]{:S(2)}, u32[]{:S(2)}) collective-permute-start(bf16[3456,128]{1,0:T(8,128)(2,1)S(1)} %add_convert_fusion), channel_id=1, source_target_pairs={{0,2},{1,5},{2,0},{3,7},{4,6},{5,1},{6,4},{7,3},{8,10},{9,13},{10,... | collective-permute-start | bytes 2654216 | tf_op jit(solution)/shard_map/ppermute | solution.py:189
  16.0 8.4 %collective-permute-start.4 = (bf16[3456,128]{1,0:T(8,128)(2,1)S(1)}, bf16[3456,128]{1,0:T(8,128)(2,1)S(1)}, u32[]{:S(2)}, u32[]{:S(2)}) collective-permute-start(bf16[3456,128]{1,0:T(8,128)(2,1)S(1)} %get-tuple-element.43), channel_id=1, source_target_pairs={{0,1},{1,0},{2,3},{3,2},{4,5},{5,4},{6,7},{7,6},{8,9},{9,8},{10,11... | collective-permute-start | bytes 2654216 | tf_op jit(solution)/shard_map/ppermute | solution.py:189
  16.1 22.6 %collective-permute-start.6 = (bf16[3456,128]{1,0:T(8,128)(2,1)S(1)}, bf16[3456,128]{1,0:T(8,128)(2,1)S(1)}, u32[]{:S(2)}, u32[]{:S(2)}) collective-permute-start(bf16[3456,128]{1,0:T(8,128)(2,1)S(1)} %get-tuple-element.41), channel_id=1, source_target_pairs={{0,1},{1,0},{2,3},{3,2},{4,5},{5,4},{6,7},{7,6},{8,9},{9,8},{10,11... | collective-permute-start | bytes 2654216 | tf_op jit(solution)/shard_map/ppermute | solution.py:189
  22.3 15.3 %collective-permute-start.3 = (bf16[1728,128]{1,0:T(8,128)(2,1)S(1)}, bf16[1728,128]{1,0:T(8,128)(2,1)S(1)}, u32[]{:S(2)}, u32[]{:S(2)}) collective-permute-start(bf16[1728,128]{1,0:T(8,128)(2,1)S(1)} %add_convert_fusion.1), channel_id=1, source_target_pairs={{0,4},{1,3},{2,6},{3,1},{4,0},{5,7},{6,2},{7,5},{8,12},{9,11},{10,... | collective-permute-start | bytes 1327112 | tf_op jit(solution)/shard_map/ppermute | solution.py:189
  24.6 14.1 %collective-permute-start.8 = (bf16[1440,128]{1,0:T(8,128)(2,1)S(1)}, bf16[1440,128]{1,0:T(8,128)(2,1)S(1)}, u32[]{:S(2)}, u32[]{:S(2)}) collective-permute-start(bf16[1440,128]{1,0:T(8,128)(2,1)S(1)} %add_convert_fusion.2), channel_id=1, source_target_pairs={{0,2},{1,5},{2,0},{3,7},{4,6},{5,1},{6,4},{7,3},{8,10},{9,13},{10,... | collective-permute-start | bytes 1105928 | tf_op jit(solution)/shard_map/ppermute | solution.py:189
  26.2 16.5 %collective-permute-start.10 = (bf16[1152,128]{1,0:T(8,128)(2,1)S(1)}, bf16[1152,128]{1,0:T(8,128)(2,1)S(1)}, u32[]{:S(2)}, u32[]{:S(2)}) collective-permute-start(bf16[1152,128]{1,0:T(8,128)(2,1)S(1)} %add_convert_fusion.3), channel_id=1, source_target_pairs={{0,2},{1,5},{2,0},{3,7},{4,6},{5,1},{6,4},{7,3},{8,10},{9,13},{10,... | collective-permute-start | bytes 884744 | tf_op jit(solution)/shard_map/ppermute | solution.py:189
  26.8 23.7 %collective-permute-start.7 = (bf16[864,128]{1,0:T(8,128)(2,1)S(1)}, bf16[864,128]{1,0:T(8,128)(2,1)S(1)}, u32[]{:S(2)}, u32[]{:S(2)}) collective-permute-start(bf16[864,128]{1,0:T(8,128)(2,1)S(1)} %add_convert_fusion.5), channel_id=1, source_target_pairs={{0,2},{1,3},{2,0},{3,1},{4,6},{5,7},{6,4},{7,5},{8,10},{9,11},{10,... | collective-permute-start | bytes 663560 | tf_op jit(solution)/shard_map/ppermute | solution.py:189
  37.7 15.3 %collective-permute-start.5 = (bf16[864,128]{1,0:T(8,128)(2,1)S(1)}, bf16[864,128]{1,0:T(8,128)(2,1)S(1)}, u32[]{:S(2)}, u32[]{:S(2)}) collective-permute-start(bf16[864,128]{1,0:T(8,128)(2,1)S(1)} %add_convert_fusion.4), channel_id=1, source_target_pairs={{0,8},{1,9},{2,10},{3,11},{4,12},{5,13},{6,14},{7,15},{8,0},{9,1},... | collective-permute-start | bytes 663560 | tf_op jit(solution)/shard_map/ppermute | solution.py:189
  38.8 9.0 %collective-permute-start.9 = (bf16[720,128]{1,0:T(8,128)(2,1)S(1)}, bf16[720,128]{1,0:T(8,128)(2,1)S(1)}, u32[]{:S(2)}, u32[]{:S(2)}) collective-permute-start(bf16[720,128]{1,0:T(8,128)(2,1)S(1)} %add_convert_fusion.6), channel_id=1, source_target_pairs={{0,4},{1,3},{2,6},{3,1},{4,0},{5,7},{6,2},{7,5},{8,12},{9,11},{10,... | collective-permute-start | bytes 552968 | tf_op jit(solution)/shard_map/ppermute | solution.py:189
  42.8 10.2 %collective-permute-start.13 = (bf16[576,128]{1,0:T(8,128)(2,1)S(1)}, bf16[576,128]{1,0:T(8,128)(2,1)S(1)}, u32[]{:S(2)}, u32[]{:S(2)}) collective-permute-start(bf16[576,128]{1,0:T(8,128)(2,1)S(1)} %add_convert_fusion.7), channel_id=1, source_target_pairs={{0,4},{1,3},{2,6},{3,1},{4,0},{5,7},{6,2},{7,5},{8,12},{9,11},{10,... | collective-permute-start | bytes 442376 | tf_op jit(solution)/shard_map/ppermute | solution.py:189
  47.8 10.8 %collective-permute-start.11 = (bf16[360,128]{1,0:T(8,128)(2,1)S(1)}, bf16[360,128]{1,0:T(8,128)(2,1)S(1)}, u32[]{:S(2)}, u32[]{:S(2)}) collective-permute-start(bf16[360,128]{1,0:T(8,128)(2,1)S(1)} %add_convert_fusion.9), channel_id=1, source_target_pairs={{0,8},{1,9},{2,10},{3,11},{4,12},{5,13},{6,14},{7,15},{8,0},{9,1},... | collective-permute-start | bytes 276488 | tf_op jit(solution)/shard_map/ppermute | solution.py:189
  50.6 5.7 %collective-permute-start.12 = (bf16[432,128]{1,0:T(8,128)(2,1)S(1)}, bf16[432,128]{1,0:T(8,128)(2,1)S(1)}, u32[]{:S(2)}, u32[]{:S(2)}) collective-permute-start(bf16[432,128]{1,0:T(8,128)(2,1)S(1)} %add_convert_fusion.8), channel_id=1, source_target_pairs={{0,4},{1,5},{2,6},{3,7},{4,0},{5,1},{6,2},{7,3},{8,12},{9,13},{10,... | collective-permute-start | bytes 331784 | tf_op jit(solution)/shard_map/ppermute | solution.py:189
  53.1 5.6 %collective-permute-start.15 = (bf16[288,128]{1,0:T(8,128)(2,1)S(1)}, bf16[288,128]{1,0:T(8,128)(2,1)S(1)}, u32[]{:S(2)}, u32[]{:S(2)}) collective-permute-start(bf16[288,128]{1,0:T(8,128)(2,1)S(1)} %add_convert_fusion.10), channel_id=1, source_target_pairs={{0,8},{1,9},{2,10},{3,11},{4,12},{5,13},{6,14},{7,15},{8,0},{9,1},... | collective-permute-start | bytes 221192 | tf_op jit(solution)/shard_map/ppermute | solution.py:189
  56.4 5.1 %collective-permute-start.14 = (bf16[216,128]{1,0:T(8,128)(2,1)S(1)}, bf16[216,128]{1,0:T(8,128)(2,1)S(1)}, u32[]{:S(2)}, u32[]{:S(2)}) collective-permute-start(bf16[216,128]{1,0:T(8,128)(2,1)S(1)} %add_convert_fusion.11), channel_id=1, source_target_pairs={{0,8},{1,9},{2,10},{3,11},{4,12},{5,13},{6,14},{7,15},{8,0},{9,1},... | collective-permute-start | bytes 165896 | tf_op jit(solution)/shard_map/ppermute | solution.py:189

commit v9 on v7

--- a/solution.py
+++ b/solution.py
@@ -70,7 +70,7 @@
     source_hbm, target_hbm, counts_hbm, x_hbm, w_hbm, *rest,
 ):
     number = len(chunks)
-    outs, (acc, xs, x_in, w, source, target, counts, places, sems) = rest[:4], rest[4:]
+    acc, send, send_on, xs, x_in, w, source, target, counts, places, sems = rest
     devices = counts.shape[1]
     steps = w.shape[0] // step_blocks
     me = lax.axis_index("curve")
@@ -146,9 +146,10 @@
         @pl.loop(0, quarter)
         def finish(index):
             at = pl.multiple_of(quarter * low * pitch + index * unit, 8)
-            for part, ref in enumerate(outs):
-                row = pl.multiple_of((devices * low + part * quarter * (high - low)) * pitch + index * unit, 8)
-                ref[pl.ds(at, unit), :] = acc[pl.ds(row, unit), :].astype(ref.dtype)
+            row = pl.multiple_of((devices * low + quarter * (high - low)) * pitch + index * unit, 8)
+            send[pl.ds(at, unit), :] = acc[pl.ds(row, unit), :].astype(send.dtype)
+            row = pl.multiple_of(row + 2 * quarter * unit, 8)
+            send_on[pl.ds(at, unit), :] = acc[pl.ds(row, unit), :].astype(send.dtype)
 
 
 def products(remap, chunks, devices):
@@ -161,11 +162,14 @@
     rows = devices // 4 * chunks[-1][1] * pitch
     return pl.pallas_call(
         functools.partial(product_kernel, channels, pitch, chunks, step_blocks),
-        out_shape=[jax.ShapeDtypeStruct((rows, LANES), kind) for kind in (jnp.float32, jnp.bfloat16) * 2],
+        out_shape=[
+            jax.ShapeDtypeStruct((4 * rows, LANES), jnp.float32),
+            jax.ShapeDtypeStruct((rows, LANES), jnp.bfloat16),
+            jax.ShapeDtypeStruct((rows, LANES), jnp.bfloat16),
+        ],
         in_specs=[pl.BlockSpec(memory_space=pltpu.HBM)] * 5,
-        out_specs=[pl.BlockSpec(memory_space=pltpu.VMEM)] * 4,
+        out_specs=[pl.BlockSpec(memory_space=pltpu.VMEM)] * 3,
         scratch_shapes=[
-            pltpu.VMEM((rows * 4, LANES), jnp.float32),
             pltpu.VMEM((tiles_in, round_up(pitch, 16), LANES), jnp.bfloat16),
             pltpu.VMEM(cotangent.shape, jnp.bfloat16),
             pltpu.VMEM(weights.shape, jnp.bfloat16),
@@ -175,10 +179,10 @@
             pltpu.SMEM((len(chunks), devices), jnp.int32),
             pltpu.SemaphoreType.DMA((4 + blocks // step_blocks,)),
         ],
-        compiler_params=pltpu.CompilerParams(vmem_limit_bytes=28 * 1024 * 1024),
+        compiler_params=pltpu.CompilerParams(vmem_limit_bytes=24 * 1024 * 1024),
         cost_estimate=pl.CostEstimate(
             flops=2 * blocks * channels * LANES * LANES,
-            bytes_accessed=2 * weights.size + 12 * rows * LANES,
+            bytes_accessed=2 * weights.size + 20 * rows * LANES,
             transcendentals=0,
         ),
     )(*[pltpu.with_memory_space_constraint(value, pltpu.HBM) for value in (source, target, counts, cotangent, weights)])
@@ -187,10 +191,6 @@
 def exchange(value, way, stage, devices):
     pairs = [(at, at ^ (1 << way[at % 2][stage])) for at in range(devices)]
     return lax.ppermute(value, "curve", pairs)
-
-
-def added(terms, low, high):
-    return sum(term[low:high].astype(jnp.float32) for term in terms)
 
 
 class Chain:
@@ -200,15 +200,19 @@
         self.base = devices // 4 * chunk[0] * pitch
         self.length = devices // 4 * (chunk[1] - chunk[0]) * pitch
 
-    def first(self, terms):
-        self.total = added(terms, self.base, self.base + self.length).astype(jnp.bfloat16)
+    def first(self, sums, got):
+        self.terms = [(sums, 4 * self.base + 2 * self.length), (got, self.base)]
+        self.total = self.part(0, self.length).astype(jnp.bfloat16)
+
+    def part(self, low, high):
+        return sum(term[base + low:base + high].astype(jnp.float32) for term, base in self.terms)
 
     def second(self):
         self.stage = 1
         self.got = exchange(self.total, self.way, self.stage, self.devices)
 
-    def rest(self, terms):
-        self.terms = [(term, self.base) for term in terms]
+    def rest(self, sums, got):
+        self.terms = [(sums, 4 * self.base), (got, self.base)]
 
     def send_next(self):
         self.terms = self.terms + [(self.got, 0)]
@@ -216,11 +220,11 @@
         self.total = self.got
         if self.stage < BITS:
             half = self.length // 2
-            self.total = sum(
-                term[base + half:base + self.length].astype(jnp.float32) for term, base in self.terms
-            ).astype(jnp.bfloat16)
+            self.total = self.part(half, self.length).astype(jnp.bfloat16)
             self.length = half
             self.got = exchange(self.total, self.way, self.stage, self.devices)
+            if self.stage == BITS - 1:
+                self.terms = [(self.part(0, half), 0)]
 
 
 def final_kernel(channels, pitch, parts, *refs):
@@ -252,7 +256,7 @@
         grid=(1,),
         in_specs=specs,
         out_specs=pl.BlockSpec(like_shape, lambda step: (0, 0, 0)),
-        compiler_params=pltpu.CompilerParams(vmem_limit_bytes=28 * 1024 * 1024),
+        compiler_params=pltpu.CompilerParams(vmem_limit_bytes=24 * 1024 * 1024),
     )(*flat)
 
 
@@ -287,49 +291,47 @@
             chain.send_next()
         order.before([chain.total for chain in chains])
 
-    def summed(line, terms):
-        terms = order.after(terms)
+    def summed(line, sums, got):
+        got = order.after(got)
         for chain in line:
-            chain.first(terms)
+            chain.first(sums, got)
         order.before([chain.total for chain in line])
 
-    def rested(line, terms):
-        terms = order.after(terms)
-        order.before(terms)
+    def rested(line, sums, got):
+        got = order.after(got)
+        order.before(got)
         for chain in line:
-            chain.rest(terms)
+            chain.rest(sums, got)
 
     def begun(chain):
         chain.total = order.after(chain.total)
         chain.second()
 
-    def both_cores(keep, send):
-        return [keep, exchange(send, STRAIGHT, 0, devices)]
+    def cores(send):
+        return exchange(send, STRAIGHT, 0, devices)
 
     a, b = ones
     c, d, e = twos
 
-    keep, send, keep_on, send_on = products(one, plans[0], devices)
-    on = both_cores(keep_on, send_on)
-    rest = both_cores(keep, send)
-    summed(ones, on)
+    sums, send, send_on = products(one, plans[0], devices)
+    on, rest = cores(send_on), cores(send)
+    summed(ones, sums, on)
     a.second()
     b.second()
-    rested(ones, rest)
+    rested(ones, sums, rest)
     made = products((order.after(two[0]),) + two[1:], plans[1], devices)
     order.before(made)
-    keep, send, keep_on, send_on = made
-    on = both_cores(keep_on, send_on)
-    rest = both_cores(keep, send)
+    sums, send, send_on = made
+    on, rest = cores(send_on), cores(send)
 
     step(a)
     step(b)
-    summed(twos, on)
+    summed(twos, sums, on)
     c.second()
     begun(d)
     step(a)
     step(b)
-    rested(twos, rest)
+    rested(twos, sums, rest)
     step(c)
     begun(e)
     step(d)

time: 58.5 us -> 58.1 us (level)
  Pallas kernels: 11.4 us -> 10.8 us
  transfers between devices with their start and end apart: 19 -> 19, of which waited for: 10 -> 10; matrix products, arithmetic and copies ran while one was open for 2% -> 2% of each run, Pallas kernels for 10% -> 9%
where the time goes in v9:
time: 58.1 us; the launch traced here: 58 us
  starting transfers between devices  31.4 us (54%)
  waiting for transfers between devices  13.9 us (24%)
  Pallas kernels  10.8 us (19%)
  other arithmetic  1.1 us (2%)
  between operations  0.74 us (1%)
    ppermute x19, starting transfers between devices, exchange(): return lax.ppermute(value, 'curve', pairs)  31.4 us
    ppermute x19, waiting for transfers between devices, exchange(): return lax.ppermute(value, 'curve', pairs)  13.9 us
    pallas_call x2, Pallas kernels, products(): pl.pallas_call(functools.partial(product_kernel, channels, pitch, chunks,...  9.3 us
    pallas_call x2, Pallas kernels, final_sum(): pl.pallas_call(functools.partial(final_kernel, like_shape[1], pitch, part...  1.48 us
  transfers between devices with their start and end apart: 19, of which 10 were waited for; matrix products, arithmetic and copies ran while one was open for 2% of the time, Pallas kernels for 9%

profile of v9, /device:TPU:0, one launch (start us, length us, event | category | flops | bytes accessed | tf_op | source)
XLA Modules:
  0.0 58.0 jit_solution(7449091801082195394)
XLA Ops:
  0.6 4.6 %shard_map.113 = (f32[13824,128]{1,0:T(8,128)S(1)}, bf16[3456,128]{1,0:T(8,128)(2,1)S(1)}, bf16[3456,128]{1,0:T(8,128)(2,1)S(1)}) custom-call(s32[144]{0:T(256)} %source_hbm.2, s32[144]{0:T(256)} %target_hbm.2, s32[1,16]{1,0:T(1,128)} %counts_hbm.2, bf16[1,69,1536]{2,1,0:T(8,128)(2,1)} %x_hbm.1, bf16[144,128,128]{2,1,0:T(8,128)(2,1)} %w_hbm.2), custom_call_target="tpu_custom_call" | custom-call | flops 325582848 | bytes 13565952 | tf_op jit(solution)/shard_map/pallas_call | solution.py:163
  5.3 0.5 collective-permute-start.1
  5.8 0.1 collective-permute-start
  5.8 2.0 %collective-permute-done.1 = bf16[3456,128]{1,0:T(8,128)(2,1)S(1)} collective-permute-done((bf16[3456,128]{1,0:T(8,128)(2,1)S(1)}, bf16[3456,128]{1,0:T(8,128)(2,1)S(1)}, u32[]{:S(2)}, u32[]{:S(2)}) %collective-permute-start.1) | collective-permute-done | bytes 884768 | tf_op jit(solution)/shard_map/ppermute | solution.py:193
  7.8 0.1 add_convert_fusion
  8.0 3.0 %collective-permute-start.2 = (bf16[2592,128]{1,0:T(8,128)(2,1)S(1)}, bf16[2592,128]{1,0:T(8,128)(2,1)S(1)}, u32[]{:S(2)}, u32[]{:S(2)}) collective-permute-start(bf16[2592,128]{1,0:T(8,128)(2,1)S(1)} %add_convert_fusion), channel_id=1, source_target_pairs={{0,2},{1,5},{2,0},{3,7},{4,6},{5,1},{6,4},{7,3},{8,10},{9,13},{10,... | collective-permute-start | bytes 1990664 | tf_op jit(solution)/shard_map/ppermute | solution.py:193
  11.0 4.7 %shard_map.114 = (f32[13824,128]{1,0:T(8,128)S(1)}, bf16[3456,128]{1,0:T(8,128)(2,1)S(1)}, bf16[3456,128]{1,0:T(8,128)(2,1)S(1)}) custom-call(s32[144]{0:T(256)} %source_hbm.3, s32[144]{0:T(256)} %target_hbm.3, s32[1,16]{1,0:T(1,128)} %counts_hbm.3, bf16[1,69,1536]{2,1,0:T(8,128)(2,1)} %x_hbm.2, bf16[144,128,128]{2,1,0:T(8,128)(2,1)} %w_hbm.3), custom_call_target="tpu_custom_call" | custom-call | flops 325582848 | bytes 13565952 | tf_op jit(solution)/shard_map/pallas_call | solution.py:163
  15.7 0.1 collective-permute-start.4
  15.7 1.4 %collective-permute-start.5 = (bf16[864,128]{1,0:T(8,128)(2,1)S(1)}, bf16[864,128]{1,0:T(8,128)(2,1)S(1)}, u32[]{:S(2)}, u32[]{:S(2)}) collective-permute-start(bf16[864,128]{1,0:T(8,128)(2,1)S(1)} %add_convert_fusion.5), channel_id=1, source_target_pairs={{0,2},{1,5},{2,0},{3,7},{4,6},{5,1},{6,4},{7,3},{8,10},{9,13},{10,... | collective-permute-start | bytes 663560 | tf_op jit(solution)/shard_map/ppermute | solution.py:193
  17.1 0.4 collective-permute-start.7
  17.5 2.0 %collective-permute-done.2 = bf16[2592,128]{1,0:T(8,128)(2,1)S(1)} collective-permute-done((bf16[2592,128]{1,0:T(8,128)(2,1)S(1)}, bf16[2592,128]{1,0:T(8,128)(2,1)S(1)}, u32[]{:S(2)}, u32[]{:S(2)}) %collective-permute-start.2) | collective-permute-done | bytes 663584 | tf_op jit(solution)/shard_map/ppermute | solution.py:193
  19.6 0.1 add_convert_fusion.2
  19.7 2.1 %collective-permute-start.3 = (bf16[1296,128]{1,0:T(8,128)(2,1)S(1)}, bf16[1296,128]{1,0:T(8,128)(2,1)S(1)}, u32[]{:S(2)}, u32[]{:S(2)}) collective-permute-start(bf16[1296,128]{1,0:T(8,128)(2,1)S(1)} %add_convert_fusion.2), channel_id=1, source_target_pairs={{0,4},{1,3},{2,6},{3,1},{4,0},{5,7},{6,2},{7,5},{8,12},{9,11},{10,... | collective-permute-start | bytes 995336 | tf_op jit(solution)/shard_map/ppermute | solution.py:193
  21.8 0.1 collective-permute-done.5
  22.0 2.4 %collective-permute-start.8 = (bf16[432,128]{1,0:T(8,128)(2,1)S(1)}, bf16[432,128]{1,0:T(8,128)(2,1)S(1)}, u32[]{:S(2)}, u32[]{:S(2)}) collective-permute-start(bf16[432,128]{1,0:T(8,128)(2,1)S(1)} %add_convert_fusion.10), channel_id=1, source_target_pairs={{0,4},{1,3},{2,6},{3,1},{4,0},{5,7},{6,2},{7,5},{8,12},{9,11},{10,... | collective-permute-start | bytes 331784 | tf_op jit(solution)/shard_map/ppermute | solution.py:193
  24.4 0.0 collective-permute-done.4
  24.4 0.1 add_convert_fusion.3
  24.4 0.1 add_convert_fusion.1
  24.5 1.6 %collective-permute-start.10 = (bf16[1440,128]{1,0:T(8,128)(2,1)S(1)}, bf16[1440,128]{1,0:T(8,128)(2,1)S(1)}, u32[]{:S(2)}, u32[]{:S(2)}) collective-permute-start(bf16[1440,128]{1,0:T(8,128)(2,1)S(1)} %add_convert_fusion.1), channel_id=1, source_target_pairs={{0,2},{1,5},{2,0},{3,7},{4,6},{5,1},{6,4},{7,3},{8,10},{9,13},{10,... | collective-permute-start | bytes 1105928 | tf_op jit(solution)/shard_map/ppermute | solution.py:193
  26.2 0.6 collective-permute-start.9
  26.7 1.2 %collective-permute-done.3 = bf16[1296,128]{1,0:T(8,128)(2,1)S(1)} collective-permute-done((bf16[1296,128]{1,0:T(8,128)(2,1)S(1)}, bf16[1296,128]{1,0:T(8,128)(2,1)S(1)}, u32[]{:S(2)}, u32[]{:S(2)}) %collective-permute-start.3) | collective-permute-done | bytes 331808 | tf_op jit(solution)/shard_map/ppermute | solution.py:193
  27.9 0.1 add_convert_fusion.7
  28.1 3.5 %collective-permute-start.6 = (bf16[648,128]{1,0:T(8,128)(2,1)S(1)}, bf16[648,128]{1,0:T(8,128)(2,1)S(1)}, u32[]{:S(2)}, u32[]{:S(2)}) collective-permute-start(bf16[648,128]{1,0:T(8,128)(2,1)S(1)} %get-tuple-element.56), channel_id=1, source_target_pairs={{0,8},{1,9},{2,10},{3,11},{4,12},{5,13},{6,14},{7,15},{8,0},{9,1},... | collective-permute-start | bytes 497672 | tf_op jit(solution)/shard_map/ppermute | solution.py:193
  31.6 0.5 collective-permute-done.8
  32.1 0.1 convert_add_fusion.4
  32.1 3.2 %collective-permute-start.12 = (bf16[216,128]{1,0:T(8,128)(2,1)S(1)}, bf16[216,128]{1,0:T(8,128)(2,1)S(1)}, u32[]{:S(2)}, u32[]{:S(2)}) collective-permute-start(bf16[216,128]{1,0:T(8,128)(2,1)S(1)} %get-tuple-element.65), channel_id=1, source_target_pairs={{0,8},{1,9},{2,10},{3,11},{4,12},{5,13},{6,14},{7,15},{8,0},{9,1},... | collective-permute-start | bytes 165896 | tf_op jit(solution)/shard_map/ppermute | solution.py:193
  35.3 0.0 collective-permute-done.7
  35.3 0.1 add_convert_fusion.6
  35.4 2.5 %collective-permute-start.14 = (bf16[720,128]{1,0:T(8,128)(2,1)S(1)}, bf16[720,128]{1,0:T(8,128)(2,1)S(1)}, u32[]{:S(2)}, u32[]{:S(2)}) collective-permute-start(bf16[720,128]{1,0:T(8,128)(2,1)S(1)} %add_convert_fusion.6), channel_id=1, source_target_pairs={{0,4},{1,3},{2,6},{3,1},{4,0},{5,7},{6,2},{7,5},{8,12},{9,11},{10,... | collective-permute-start | bytes 552968 | tf_op jit(solution)/shard_map/ppermute | solution.py:193
  38.0 2.6 %collective-permute-start.13 = (bf16[864,128]{1,0:T(8,128)(2,1)S(1)}, bf16[864,128]{1,0:T(8,128)(2,1)S(1)}, u32[]{:S(2)}, u32[]{:S(2)}) collective-permute-start(bf16[864,128]{1,0:T(8,128)(2,1)S(1)} %add_convert_fusion.4), channel_id=1, source_target_pairs={{0,2},{1,3},{2,0},{3,1},{4,6},{5,7},{6,4},{7,5},{8,10},{9,11},{10,... | collective-permute-start | bytes 663560 | tf_op jit(solution)/shard_map/ppermute | solution.py:193
  40.6 0.1 add_convert_fusion.8
  40.6 1.7 %collective-permute-start.11 = (bf16[576,128]{1,0:T(8,128)(2,1)S(1)}, bf16[576,128]{1,0:T(8,128)(2,1)S(1)}, u32[]{:S(2)}, u32[]{:S(2)}) collective-permute-start(bf16[576,128]{1,0:T(8,128)(2,1)S(1)} %add_convert_fusion.8), channel_id=1, source_target_pairs={{0,4},{1,5},{2,6},{3,7},{4,0},{5,1},{6,2},{7,3},{8,12},{9,13},{10,... | collective-permute-start | bytes 442376 | tf_op jit(solution)/shard_map/ppermute | solution.py:193
  42.3 1.5 %collective-permute-done.14 = bf16[720,128]{1,0:T(8,128)(2,1)S(1)} collective-permute-done((bf16[720,128]{1,0:T(8,128)(2,1)S(1)}, bf16[720,128]{1,0:T(8,128)(2,1)S(1)}, u32[]{:S(2)}, u32[]{:S(2)}) %collective-permute-start.14) | collective-permute-done | bytes 184352 | tf_op jit(solution)/shard_map/ppermute | solution.py:193
  43.8 0.1 convert_add_fusion.1
  43.9 0.9 %collective-permute-start.15 = (bf16[360,128]{1,0:T(8,128)(2,1)S(1)}, bf16[360,128]{1,0:T(8,128)(2,1)S(1)}, u32[]{:S(2)}, u32[]{:S(2)}) collective-permute-start(bf16[360,128]{1,0:T(8,128)(2,1)S(1)} %get-tuple-element.59), channel_id=1, source_target_pairs={{0,8},{1,9},{2,10},{3,11},{4,12},{5,13},{6,14},{7,15},{8,0},{9,1},... | collective-permute-start | bytes 276488 | tf_op jit(solution)/shard_map/ppermute | solution.py:193
  44.8 0.7 %collective-permute-done.13 = bf16[864,128]{1,0:T(8,128)(2,1)S(1)} collective-permute-done((bf16[864,128]{1,0:T(8,128)(2,1)S(1)}, bf16[864,128]{1,0:T(8,128)(2,1)S(1)}, u32[]{:S(2)}, u32[]{:S(2)}) %collective-permute-start.13) | collective-permute-done | bytes 221216 | tf_op jit(solution)/shard_map/ppermute | solution.py:193
  45.5 0.1 add_convert_fusion.9
  45.6 1.8 %collective-permute-start.17 = (bf16[432,128]{1,0:T(8,128)(2,1)S(1)}, bf16[432,128]{1,0:T(8,128)(2,1)S(1)}, u32[]{:S(2)}, u32[]{:S(2)}) collective-permute-start(bf16[432,128]{1,0:T(8,128)(2,1)S(1)} %add_convert_fusion.9), channel_id=1, source_target_pairs={{0,4},{1,5},{2,6},{3,7},{4,0},{5,1},{6,2},{7,3},{8,12},{9,13},{10,... | collective-permute-start | bytes 331784 | tf_op jit(solution)/shard_map/ppermute | solution.py:193
  47.4 0.0 collective-permute-done.12.refs_3_
  47.4 0.1 convert_add_fusion.2
  47.5 1.5 %collective-permute-start.16 = (bf16[288,128]{1,0:T(8,128)(2,1)S(1)}, bf16[288,128]{1,0:T(8,128)(2,1)S(1)}, u32[]{:S(2)}, u32[]{:S(2)}) collective-permute-start(bf16[288,128]{1,0:T(8,128)(2,1)S(1)} %get-tuple-element.61), channel_id=1, source_target_pairs={{0,8},{1,9},{2,10},{3,11},{4,12},{5,13},{6,14},{7,15},{8,0},{9,1},... | collective-permute-start | bytes 221192 | tf_op jit(solution)/shard_map/ppermute | solution.py:193
  49.0 2.5 %collective-permute-done.17 = bf16[432,128]{1,0:T(8,128)(2,1)S(1)} collective-permute-done((bf16[432,128]{1,0:T(8,128)(2,1)S(1)}, bf16[432,128]{1,0:T(8,128)(2,1)S(1)}, u32[]{:S(2)}, u32[]{:S(2)}) %collective-permute-start.17) | collective-permute-done | bytes 110624 | tf_op jit(solution)/shard_map/ppermute | solution.py:193
  51.4 0.1 convert_add_fusion.3
  51.5 1.5 %collective-permute-start.18 = (bf16[216,128]{1,0:T(8,128)(2,1)S(1)}, bf16[216,128]{1,0:T(8,128)(2,1)S(1)}, u32[]{:S(2)}, u32[]{:S(2)}) collective-permute-start(bf16[216,128]{1,0:T(8,128)(2,1)S(1)} %get-tuple-element.63), channel_id=1, source_target_pairs={{0,8},{1,9},{2,10},{3,11},{4,12},{5,13},{6,14},{7,15},{8,0},{9,1},... | collective-permute-start | bytes 165896 | tf_op jit(solution)/shard_map/ppermute | solution.py:193
  53.0 0.7 %shard_map.115 = bf16[1,69,1536]{2,1,0:T(8,128)(2,1)} custom-call(f32[648,128]{1,0:T(8,128)S(1)} %get-tuple-element.57.refs_0_, bf16[648,128]{1,0:T(8,128)(2,1)S(1)} %collective-permute-done.6.refs_1_, f32[216,128]{1,0:T(8,128)S(1)} %get-tuple-element.64.refs_2_, bf16[216,128]{1,0:T(8,128)(2,1)S(1)} %collective-permute-done.12.refs_3_), custom_call_target="tpu_custom_call" | custom-call | tf_op jit(solution)/shard_map/pallas_call | solution.py:253
  53.8 0.8 %collective-permute-done.16.refs_3_ = bf16[288,128]{1,0:T(8,128)(2,1)S(1)} collective-permute-done((bf16[288,128]{1,0:T(8,128)(2,1)S(1)}, bf16[288,128]{1,0:T(8,128)(2,1)S(1)}, u32[]{:S(2)}, u32[]{:S(2)}) %collective-permute-start.16) | collective-permute-done | bytes 73760 | tf_op jit(solution)/shard_map/ppermute | solution.py:193
  54.6 2.6 %collective-permute-done.18.refs_5_ = bf16[216,128]{1,0:T(8,128)(2,1)S(1)} collective-permute-done((bf16[216,128]{1,0:T(8,128)(2,1)S(1)}, bf16[216,128]{1,0:T(8,128)(2,1)S(1)}, u32[]{:S(2)}, u32[]{:S(2)}) %collective-permute-start.18) | collective-permute-done | bytes 55328 | tf_op jit(solution)/shard_map/ppermute | solution.py:193
  57.2 0.7 %shard_map.116 = bf16[1,69,1536]{2,1,0:T(8,128)(2,1)} custom-call(f32[360,128]{1,0:T(8,128)S(1)} %get-tuple-element.58.refs_0_, bf16[360,128]{1,0:T(8,128)(2,1)S(1)} %collective-permute-done.15.refs_1_, f32[288,128]{1,0:T(8,128)S(1)} %get-tuple-element.60.refs_2_, bf16[288,128]{1,0:T(8,128)(2,1)S(1)} %collective-permute-done.16.refs_3_, ...), custom_call_target="tpu_custom_call" | custom-call | tf_op jit(solution)/shard_map/pallas_call | solution.py:253
  (9 shorter events, 0.1 us)
Async XLA Ops:
  5.3 2.5 %collective-permute-start.1 = (bf16[3456,128]{1,0:T(8,128)(2,1)S(1)}, bf16[3456,128]{1,0:T(8,128)(2,1)S(1)}, u32[]{:S(2)}, u32[]{:S(2)}) collective-permute-start(bf16[3456,128]{1,0:T(8,128)(2,1)S(1)} %get-tuple-element.31), channel_id=1, source_target_pairs={{0,1},{1,0},{2,3},{3,2},{4,5},{5,4},{6,7},{7,6},{8,9},{9,8},{10,11... | collective-permute-start | bytes 2654216 | tf_op jit(solution)/shard_map/ppermute | solution.py:193
  5.8 5.2 %collective-permute-start = (bf16[3456,128]{1,0:T(8,128)(2,1)S(1)}, bf16[3456,128]{1,0:T(8,128)(2,1)S(1)}, u32[]{:S(2)}, u32[]{:S(2)}) collective-permute-start(bf16[3456,128]{1,0:T(8,128)(2,1)S(1)} %get-tuple-element.30), channel_id=1, source_target_pairs={{0,1},{1,0},{2,3},{3,2},{4,5},{5,4},{6,7},{7,6},{8,9},{9,8},{10,11... | collective-permute-start | bytes 2654216 | tf_op jit(solution)/shard_map/ppermute | solution.py:193
  8.0 11.6 %collective-permute-start.2 = (bf16[2592,128]{1,0:T(8,128)(2,1)S(1)}, bf16[2592,128]{1,0:T(8,128)(2,1)S(1)}, u32[]{:S(2)}, u32[]{:S(2)}) collective-permute-start(bf16[2592,128]{1,0:T(8,128)(2,1)S(1)} %add_convert_fusion), channel_id=1, source_target_pairs={{0,2},{1,5},{2,0},{3,7},{4,6},{5,1},{6,4},{7,3},{8,10},{9,13},{10,... | collective-permute-start | bytes 1990664 | tf_op jit(solution)/shard_map/ppermute | solution.py:193
  15.7 8.7 %collective-permute-start.4 = (bf16[3456,128]{1,0:T(8,128)(2,1)S(1)}, bf16[3456,128]{1,0:T(8,128)(2,1)S(1)}, u32[]{:S(2)}, u32[]{:S(2)}) collective-permute-start(bf16[3456,128]{1,0:T(8,128)(2,1)S(1)} %get-tuple-element.36), channel_id=1, source_target_pairs={{0,1},{1,0},{2,3},{3,2},{4,5},{5,4},{6,7},{7,6},{8,9},{9,8},{10,11... | collective-permute-start | bytes 2654216 | tf_op jit(solution)/shard_map/ppermute | solution.py:193
  15.7 6.2 %collective-permute-start.5 = (bf16[864,128]{1,0:T(8,128)(2,1)S(1)}, bf16[864,128]{1,0:T(8,128)(2,1)S(1)}, u32[]{:S(2)}, u32[]{:S(2)}) collective-permute-start(bf16[864,128]{1,0:T(8,128)(2,1)S(1)} %add_convert_fusion.5), channel_id=1, source_target_pairs={{0,2},{1,5},{2,0},{3,7},{4,6},{5,1},{6,4},{7,3},{8,10},{9,13},{10,... | collective-permute-start | bytes 663560 | tf_op jit(solution)/shard_map/ppermute | solution.py:193
  17.1 18.2 %collective-permute-start.7 = (bf16[3456,128]{1,0:T(8,128)(2,1)S(1)}, bf16[3456,128]{1,0:T(8,128)(2,1)S(1)}, u32[]{:S(2)}, u32[]{:S(2)}) collective-permute-start(bf16[3456,128]{1,0:T(8,128)(2,1)S(1)} %get-tuple-element.35), channel_id=1, source_target_pairs={{0,1},{1,0},{2,3},{3,2},{4,5},{5,4},{6,7},{7,6},{8,9},{9,8},{10,11... | collective-permute-start | bytes 2654216 | tf_op jit(solution)/shard_map/ppermute | solution.py:193
  19.7 8.2 %collective-permute-start.3 = (bf16[1296,128]{1,0:T(8,128)(2,1)S(1)}, bf16[1296,128]{1,0:T(8,128)(2,1)S(1)}, u32[]{:S(2)}, u32[]{:S(2)}) collective-permute-start(bf16[1296,128]{1,0:T(8,128)(2,1)S(1)} %add_convert_fusion.2), channel_id=1, source_target_pairs={{0,4},{1,3},{2,6},{3,1},{4,0},{5,7},{6,2},{7,5},{8,12},{9,11},{10,... | collective-permute-start | bytes 995336 | tf_op jit(solution)/shard_map/ppermute | solution.py:193
  22.0 10.1 %collective-permute-start.8 = (bf16[432,128]{1,0:T(8,128)(2,1)S(1)}, bf16[432,128]{1,0:T(8,128)(2,1)S(1)}, u32[]{:S(2)}, u32[]{:S(2)}) collective-permute-start(bf16[432,128]{1,0:T(8,128)(2,1)S(1)} %add_convert_fusion.10), channel_id=1, source_target_pairs={{0,4},{1,3},{2,6},{3,1},{4,0},{5,7},{6,2},{7,5},{8,12},{9,11},{10,... | collective-permute-start | bytes 331784 | tf_op jit(solution)/shard_map/ppermute | solution.py:193
  24.5 10.8 %collective-permute-start.10 = (bf16[1440,128]{1,0:T(8,128)(2,1)S(1)}, bf16[1440,128]{1,0:T(8,128)(2,1)S(1)}, u32[]{:S(2)}, u32[]{:S(2)}) collective-permute-start(bf16[1440,128]{1,0:T(8,128)(2,1)S(1)} %add_convert_fusion.1), channel_id=1, source_target_pairs={{0,2},{1,5},{2,0},{3,7},{4,6},{5,1},{6,4},{7,3},{8,10},{9,13},{10,... | collective-permute-start | bytes 1105928 | tf_op jit(solution)/shard_map/ppermute | solution.py:193
  26.2 11.8 %collective-permute-start.9 = (bf16[1152,128]{1,0:T(8,128)(2,1)S(1)}, bf16[1152,128]{1,0:T(8,128)(2,1)S(1)}, u32[]{:S(2)}, u32[]{:S(2)}) collective-permute-start(bf16[1152,128]{1,0:T(8,128)(2,1)S(1)} %add_convert_fusion.3), channel_id=1, source_target_pairs={{0,2},{1,3},{2,0},{3,1},{4,6},{5,7},{6,4},{7,5},{8,10},{9,11},{10,... | collective-permute-start | bytes 884744 | tf_op jit(solution)/shard_map/ppermute | solution.py:193
  28.1 20.9 %collective-permute-start.6 = (bf16[648,128]{1,0:T(8,128)(2,1)S(1)}, bf16[648,128]{1,0:T(8,128)(2,1)S(1)}, u32[]{:S(2)}, u32[]{:S(2)}) collective-permute-start(bf16[648,128]{1,0:T(8,128)(2,1)S(1)} %get-tuple-element.56), channel_id=1, source_target_pairs={{0,8},{1,9},{2,10},{3,11},{4,12},{5,13},{6,14},{7,15},{8,0},{9,1},... | collective-permute-start | bytes 497672 | tf_op jit(solution)/shard_map/ppermute | solution.py:193
  32.1 15.3 %collective-permute-start.12 = (bf16[216,128]{1,0:T(8,128)(2,1)S(1)}, bf16[216,128]{1,0:T(8,128)(2,1)S(1)}, u32[]{:S(2)}, u32[]{:S(2)}) collective-permute-start(bf16[216,128]{1,0:T(8,128)(2,1)S(1)} %get-tuple-element.65), channel_id=1, source_target_pairs={{0,8},{1,9},{2,10},{3,11},{4,12},{5,13},{6,14},{7,15},{8,0},{9,1},... | collective-permute-start | bytes 165896 | tf_op jit(solution)/shard_map/ppermute | solution.py:193
  35.4 8.4 %collective-permute-start.14 = (bf16[720,128]{1,0:T(8,128)(2,1)S(1)}, bf16[720,128]{1,0:T(8,128)(2,1)S(1)}, u32[]{:S(2)}, u32[]{:S(2)}) collective-permute-start(bf16[720,128]{1,0:T(8,128)(2,1)S(1)} %add_convert_fusion.6), channel_id=1, source_target_pairs={{0,4},{1,3},{2,6},{3,1},{4,0},{5,7},{6,2},{7,5},{8,12},{9,11},{10,... | collective-permute-start | bytes 552968 | tf_op jit(solution)/shard_map/ppermute | solution.py:193
  38.0 7.6 %collective-permute-start.13 = (bf16[864,128]{1,0:T(8,128)(2,1)S(1)}, bf16[864,128]{1,0:T(8,128)(2,1)S(1)}, u32[]{:S(2)}, u32[]{:S(2)}) collective-permute-start(bf16[864,128]{1,0:T(8,128)(2,1)S(1)} %add_convert_fusion.4), channel_id=1, source_target_pairs={{0,2},{1,3},{2,0},{3,1},{4,6},{5,7},{6,4},{7,5},{8,10},{9,11},{10,... | collective-permute-start | bytes 663560 | tf_op jit(solution)/shard_map/ppermute | solution.py:193
  40.6 6.8 %collective-permute-start.11 = (bf16[576,128]{1,0:T(8,128)(2,1)S(1)}, bf16[576,128]{1,0:T(8,128)(2,1)S(1)}, u32[]{:S(2)}, u32[]{:S(2)}) collective-permute-start(bf16[576,128]{1,0:T(8,128)(2,1)S(1)} %add_convert_fusion.8), channel_id=1, source_target_pairs={{0,4},{1,5},{2,6},{3,7},{4,0},{5,1},{6,2},{7,3},{8,12},{9,13},{10,... | collective-permute-start | bytes 442376 | tf_op jit(solution)/shard_map/ppermute | solution.py:193
  43.9 9.9 %collective-permute-start.15 = (bf16[360,128]{1,0:T(8,128)(2,1)S(1)}, bf16[360,128]{1,0:T(8,128)(2,1)S(1)}, u32[]{:S(2)}, u32[]{:S(2)}) collective-permute-start(bf16[360,128]{1,0:T(8,128)(2,1)S(1)} %get-tuple-element.59), channel_id=1, source_target_pairs={{0,8},{1,9},{2,10},{3,11},{4,12},{5,13},{6,14},{7,15},{8,0},{9,1},... | collective-permute-start | bytes 276488 | tf_op jit(solution)/shard_map/ppermute | solution.py:193
  45.6 5.9 %collective-permute-start.17 = (bf16[432,128]{1,0:T(8,128)(2,1)S(1)}, bf16[432,128]{1,0:T(8,128)(2,1)S(1)}, u32[]{:S(2)}, u32[]{:S(2)}) collective-permute-start(bf16[432,128]{1,0:T(8,128)(2,1)S(1)} %add_convert_fusion.9), channel_id=1, source_target_pairs={{0,4},{1,5},{2,6},{3,7},{4,0},{5,1},{6,2},{7,3},{8,12},{9,13},{10,... | collective-permute-start | bytes 331784 | tf_op jit(solution)/shard_map/ppermute | solution.py:193
  47.5 7.1 %collective-permute-start.16 = (bf16[288,128]{1,0:T(8,128)(2,1)S(1)}, bf16[288,128]{1,0:T(8,128)(2,1)S(1)}, u32[]{:S(2)}, u32[]{:S(2)}) collective-permute-start(bf16[288,128]{1,0:T(8,128)(2,1)S(1)} %get-tuple-element.61), channel_id=1, source_target_pairs={{0,8},{1,9},{2,10},{3,11},{4,12},{5,13},{6,14},{7,15},{8,0},{9,1},... | collective-permute-start | bytes 221192 | tf_op jit(solution)/shard_map/ppermute | solution.py:193
  51.5 5.7 %collective-permute-start.18 = (bf16[216,128]{1,0:T(8,128)(2,1)S(1)}, bf16[216,128]{1,0:T(8,128)(2,1)S(1)}, u32[]{:S(2)}, u32[]{:S(2)}) collective-permute-start(bf16[216,128]{1,0:T(8,128)(2,1)S(1)} %get-tuple-element.63), channel_id=1, source_target_pairs={{0,8},{1,9},{2,10},{3,11},{4,12},{5,13},{6,14},{7,15},{8,0},{9,1},... | collective-permute-start | bytes 165896 | tf_op jit(solution)/shard_map/ppermute | solution.py:193

commit v10 on v9

--- a/solution.py
+++ b/solution.py
@@ -276,10 +276,10 @@
     one, two = remaps
     pitch = round_up(one[-1][1], 8)
     tiles = one[-1][2] // LANES
-    some, most = tiles * 5 // 12, tiles * 3 // 4
+    half, most, more = tiles // 2, tiles * 3 // 4, tiles * 5 // 6
     plans = (
         [(0, most, MIXED), (most, tiles, MIXED)],
-        [(0, some, MIXED), (some, most, STRAIGHT), (most, tiles, STRAIGHT)],
+        [(0, half, MIXED), (half, more, MIXED), (more, tiles, MIXED)],
     )
     ones, twos = [[Chain(chunk, devices, pitch) for chunk in chunks] for chunks in plans]
     order = Order()
@@ -329,19 +329,21 @@
     summed(twos, sums, on)
     c.second()
     begun(d)
-    step(a)
     step(b)
     rested(twos, sums, rest)
     step(c)
+    step(a)
     begun(e)
     step(d)
     step(c)
     step(e)
     step(b)
     step(d)
+    step(c)
     step(a)
     step(e)
-    step(*twos)
+    step(d)
+    step(e)
     return [final_sum(line, remap[-1], pitch) for line, remap in zip((ones, twos), remaps)]
 
 

time: 58.1 us -> 61.8 us (1.064)
  waiting for transfers between devices: 13.9 us -> 22.5 us
  starting transfers between devices: 31.4 us -> 26.6 us
    ppermute x19, waiting for transfers between devices: 13.9 us -> 22.5 us  [exchange(): return lax.ppermute(value, 'curve', pairs)]
    ppermute x19, starting transfers between devices: 31.4 us -> 26.6 us  [exchange(): return lax.ppermute(value, 'curve', pairs)]
  transfers between devices with their start and end apart: 19 -> 19, of which waited for: 10 -> 9; matrix products, arithmetic and copies ran while one was open for 2% -> 2% of each run, Pallas kernels for 9% -> 9%
where the time goes in v10:
time: 61.8 us; the launch traced here: 61.7 us
  starting transfers between devices  26.6 us (43%)
  waiting for transfers between devices  22.5 us (36%)
  Pallas kernels  10.8 us (17%)
  other arithmetic  1.09 us (2%)
  between operations  0.75 us (1%)
    ppermute x19, starting transfers between devices, exchange(): return lax.ppermute(value, 'curve', pairs)  26.6 us
    ppermute x19, waiting for transfers between devices, exchange(): return lax.ppermute(value, 'curve', pairs)  22.5 us
    pallas_call x2, Pallas kernels, products(): pl.pallas_call(functools.partial(product_kernel, channels, pitch, chunks,...  9.28 us
    pallas_call x2, Pallas kernels, final_sum(): pl.pallas_call(functools.partial(final_kernel, like_shape[1], pitch, part...  1.48 us
  transfers between devices with their start and end apart: 19, of which 9 were waited for; matrix products, arithmetic and copies ran while one was open for 2% of the time, Pallas kernels for 9%

profile of v10, /device:TPU:0, one launch (start us, length us, event | category | flops | bytes accessed | tf_op | source)
XLA Modules:
  0.0 61.7 jit_solution(10670644738779600142)
XLA Ops:
  0.6 4.6 %shard_map.113 = (f32[13824,128]{1,0:T(8,128)S(1)}, bf16[3456,128]{1,0:T(8,128)(2,1)S(1)}, bf16[3456,128]{1,0:T(8,128)(2,1)S(1)}) custom-call(s32[144]{0:T(256)} %source_hbm.2, s32[144]{0:T(256)} %target_hbm.2, s32[1,16]{1,0:T(1,128)} %counts_hbm.2, bf16[1,69,1536]{2,1,0:T(8,128)(2,1)} %x_hbm.1, bf16[144,128,128]{2,1,0:T(8,128)(2,1)} %w_hbm.2), custom_call_target="tpu_custom_call" | custom-call | flops 325582848 | bytes 13565952 | tf_op jit(solution)/shard_map/pallas_call | solution.py:163
  5.3 0.5 collective-permute-start.1
  5.8 0.1 collective-permute-start
  5.9 2.0 %collective-permute-done.1 = bf16[3456,128]{1,0:T(8,128)(2,1)S(1)} collective-permute-done((bf16[3456,128]{1,0:T(8,128)(2,1)S(1)}, bf16[3456,128]{1,0:T(8,128)(2,1)S(1)}, u32[]{:S(2)}, u32[]{:S(2)}) %collective-permute-start.1) | collective-permute-done | bytes 884768 | tf_op jit(solution)/shard_map/ppermute | solution.py:193
  7.8 0.1 add_convert_fusion
  8.0 2.9 %collective-permute-start.2 = (bf16[2592,128]{1,0:T(8,128)(2,1)S(1)}, bf16[2592,128]{1,0:T(8,128)(2,1)S(1)}, u32[]{:S(2)}, u32[]{:S(2)}) collective-permute-start(bf16[2592,128]{1,0:T(8,128)(2,1)S(1)} %add_convert_fusion), channel_id=1, source_target_pairs={{0,2},{1,5},{2,0},{3,7},{4,6},{5,1},{6,4},{7,3},{8,10},{9,13},{10,... | collective-permute-start | bytes 1990664 | tf_op jit(solution)/shard_map/ppermute | solution.py:193
  11.0 4.7 %shard_map.114 = (f32[13824,128]{1,0:T(8,128)S(1)}, bf16[3456,128]{1,0:T(8,128)(2,1)S(1)}, bf16[3456,128]{1,0:T(8,128)(2,1)S(1)}) custom-call(s32[144]{0:T(256)} %source_hbm.3, s32[144]{0:T(256)} %target_hbm.3, s32[1,16]{1,0:T(1,128)} %counts_hbm.3, bf16[1,69,1536]{2,1,0:T(8,128)(2,1)} %x_hbm.2, bf16[144,128,128]{2,1,0:T(8,128)(2,1)} %w_hbm.3), custom_call_target="tpu_custom_call" | custom-call | flops 325582848 | bytes 13565952 | tf_op jit(solution)/shard_map/pallas_call | solution.py:163
  15.6 0.1 collective-permute-start.7
  15.7 1.4 %collective-permute-start.5 = (bf16[864,128]{1,0:T(8,128)(2,1)S(1)}, bf16[864,128]{1,0:T(8,128)(2,1)S(1)}, u32[]{:S(2)}, u32[]{:S(2)}) collective-permute-start(bf16[864,128]{1,0:T(8,128)(2,1)S(1)} %add_convert_fusion.5), channel_id=1, source_target_pairs={{0,2},{1,5},{2,0},{3,7},{4,6},{5,1},{6,4},{7,3},{8,10},{9,13},{10,... | collective-permute-start | bytes 663560 | tf_op jit(solution)/shard_map/ppermute | solution.py:193
  17.1 0.4 collective-permute-start.4
  17.5 2.1 %collective-permute-done.2 = bf16[2592,128]{1,0:T(8,128)(2,1)S(1)} collective-permute-done((bf16[2592,128]{1,0:T(8,128)(2,1)S(1)}, bf16[2592,128]{1,0:T(8,128)(2,1)S(1)}, u32[]{:S(2)}, u32[]{:S(2)}) %collective-permute-start.2) | collective-permute-done | bytes 663584 | tf_op jit(solution)/shard_map/ppermute | solution.py:193
  19.6 0.1 add_convert_fusion.2
  19.7 2.1 %collective-permute-start.3 = (bf16[1296,128]{1,0:T(8,128)(2,1)S(1)}, bf16[1296,128]{1,0:T(8,128)(2,1)S(1)}, u32[]{:S(2)}, u32[]{:S(2)}) collective-permute-start(bf16[1296,128]{1,0:T(8,128)(2,1)S(1)} %add_convert_fusion.2), channel_id=1, source_target_pairs={{0,4},{1,3},{2,6},{3,1},{4,0},{5,7},{6,2},{7,5},{8,12},{9,11},{10,... | collective-permute-start | bytes 995336 | tf_op jit(solution)/shard_map/ppermute | solution.py:193
  21.8 0.1 collective-permute-done.5
  21.9 0.1 add_convert_fusion.10
  22.0 2.4 %collective-permute-start.6 = (bf16[432,128]{1,0:T(8,128)(2,1)S(1)}, bf16[432,128]{1,0:T(8,128)(2,1)S(1)}, u32[]{:S(2)}, u32[]{:S(2)}) collective-permute-start(bf16[432,128]{1,0:T(8,128)(2,1)S(1)} %add_convert_fusion.10), channel_id=1, source_target_pairs={{0,4},{1,3},{2,6},{3,1},{4,0},{5,7},{6,2},{7,5},{8,12},{9,11},{10,... | collective-permute-start | bytes 331784 | tf_op jit(solution)/shard_map/ppermute | solution.py:193
  24.4 0.1 add_convert_fusion.1
  24.5 1.6 %collective-permute-start.8 = (bf16[1728,128]{1,0:T(8,128)(2,1)S(1)}, bf16[1728,128]{1,0:T(8,128)(2,1)S(1)}, u32[]{:S(2)}, u32[]{:S(2)}) collective-permute-start(bf16[1728,128]{1,0:T(8,128)(2,1)S(1)} %add_convert_fusion.1), channel_id=1, source_target_pairs={{0,2},{1,5},{2,0},{3,7},{4,6},{5,1},{6,4},{7,3},{8,10},{9,13},{10,... | collective-permute-start | bytes 1327112 | tf_op jit(solution)/shard_map/ppermute | solution.py:193
  26.1 0.1 add_convert_fusion.3
  26.2 4.1 %collective-permute-done.6 = bf16[432,128]{1,0:T(8,128)(2,1)S(1)} collective-permute-done((bf16[432,128]{1,0:T(8,128)(2,1)S(1)}, bf16[432,128]{1,0:T(8,128)(2,1)S(1)}, u32[]{:S(2)}, u32[]{:S(2)}) %collective-permute-start.6) | collective-permute-done | bytes 110624 | tf_op jit(solution)/shard_map/ppermute | solution.py:193
  30.3 0.1 convert_add_fusion.3
  30.4 3.5 %collective-permute-start.14 = (bf16[216,128]{1,0:T(8,128)(2,1)S(1)}, bf16[216,128]{1,0:T(8,128)(2,1)S(1)}, u32[]{:S(2)}, u32[]{:S(2)}) collective-permute-start(bf16[216,128]{1,0:T(8,128)(2,1)S(1)} %get-tuple-element.63), channel_id=1, source_target_pairs={{0,8},{1,9},{2,10},{3,11},{4,12},{5,13},{6,14},{7,15},{8,0},{9,1},... | collective-permute-start | bytes 165896 | tf_op jit(solution)/shard_map/ppermute | solution.py:193
  33.9 0.0 collective-permute-done.4
  33.9 2.6 %collective-permute-start.11 = (bf16[1152,128]{1,0:T(8,128)(2,1)S(1)}, bf16[1152,128]{1,0:T(8,128)(2,1)S(1)}, u32[]{:S(2)}, u32[]{:S(2)}) collective-permute-start(bf16[1152,128]{1,0:T(8,128)(2,1)S(1)} %add_convert_fusion.3), channel_id=1, source_target_pairs={{0,2},{1,5},{2,0},{3,7},{4,6},{5,1},{6,4},{7,3},{8,10},{9,13},{10,... | collective-permute-start | bytes 884744 | tf_op jit(solution)/shard_map/ppermute | solution.py:193
  36.5 0.0 collective-permute-done.8
  36.5 0.1 add_convert_fusion.4
  36.6 2.2 %collective-permute-start.10 = (bf16[864,128]{1,0:T(8,128)(2,1)S(1)}, bf16[864,128]{1,0:T(8,128)(2,1)S(1)}, u32[]{:S(2)}, u32[]{:S(2)}) collective-permute-start(bf16[864,128]{1,0:T(8,128)(2,1)S(1)} %add_convert_fusion.4), channel_id=1, source_target_pairs={{0,4},{1,3},{2,6},{3,1},{4,0},{5,7},{6,2},{7,5},{8,12},{9,11},{10,... | collective-permute-start | bytes 663560 | tf_op jit(solution)/shard_map/ppermute | solution.py:193
  38.8 0.0 collective-permute-done.3
  38.8 0.1 add_convert_fusion.6
  39.0 0.1 collective-permute-start.9
  39.1 0.1 collective-permute-start.15
  39.2 3.1 %collective-permute-done.11 = bf16[1152,128]{1,0:T(8,128)(2,1)S(1)} collective-permute-done((bf16[1152,128]{1,0:T(8,128)(2,1)S(1)}, bf16[1152,128]{1,0:T(8,128)(2,1)S(1)}, u32[]{:S(2)}, u32[]{:S(2)}) %collective-permute-start.11) | collective-permute-done | bytes 294944 | tf_op jit(solution)/shard_map/ppermute | solution.py:193
  42.3 0.1 add_convert_fusion.7
  42.3 2.6 %collective-permute-start.13 = (bf16[576,128]{1,0:T(8,128)(2,1)S(1)}, bf16[576,128]{1,0:T(8,128)(2,1)S(1)}, u32[]{:S(2)}, u32[]{:S(2)}) collective-permute-start(bf16[576,128]{1,0:T(8,128)(2,1)S(1)} %add_convert_fusion.7), channel_id=1, source_target_pairs={{0,4},{1,3},{2,6},{3,1},{4,0},{5,7},{6,2},{7,5},{8,12},{9,11},{10,... | collective-permute-start | bytes 442376 | tf_op jit(solution)/shard_map/ppermute | solution.py:193
  44.9 1.9 %collective-permute-done.10 = bf16[864,128]{1,0:T(8,128)(2,1)S(1)} collective-permute-done((bf16[864,128]{1,0:T(8,128)(2,1)S(1)}, bf16[864,128]{1,0:T(8,128)(2,1)S(1)}, u32[]{:S(2)}, u32[]{:S(2)}) %collective-permute-start.10) | collective-permute-done | bytes 221216 | tf_op jit(solution)/shard_map/ppermute | solution.py:193
  46.7 0.1 convert_add_fusion.1
  46.8 0.5 collective-permute-start.12
  47.4 2.5 %collective-permute-start.17 = (bf16[288,128]{1,0:T(8,128)(2,1)S(1)}, bf16[288,128]{1,0:T(8,128)(2,1)S(1)}, u32[]{:S(2)}, u32[]{:S(2)}) collective-permute-start(bf16[288,128]{1,0:T(8,128)(2,1)S(1)} %add_convert_fusion.12), channel_id=1, source_target_pairs={{0,4},{1,3},{2,6},{3,1},{4,0},{5,7},{6,2},{7,5},{8,12},{9,11},{10,... | collective-permute-start | bytes 221192 | tf_op jit(solution)/shard_map/ppermute | solution.py:193
  50.0 0.0 collective-permute-done.14.refs_3_
  50.0 0.0 collective-permute-done.13
  50.0 0.1 convert_add_fusion.2
  50.0 0.8 %collective-permute-start.16 = (bf16[288,128]{1,0:T(8,128)(2,1)S(1)}, bf16[288,128]{1,0:T(8,128)(2,1)S(1)}, u32[]{:S(2)}, u32[]{:S(2)}) collective-permute-start(bf16[288,128]{1,0:T(8,128)(2,1)S(1)} %get-tuple-element.61), channel_id=1, source_target_pairs={{0,8},{1,9},{2,10},{3,11},{4,12},{5,13},{6,14},{7,15},{8,0},{9,1},... | collective-permute-start | bytes 221192 | tf_op jit(solution)/shard_map/ppermute | solution.py:193
  50.8 5.1 %collective-permute-done.12.refs_1_ = bf16[432,128]{1,0:T(8,128)(2,1)S(1)} collective-permute-done((bf16[432,128]{1,0:T(8,128)(2,1)S(1)}, bf16[432,128]{1,0:T(8,128)(2,1)S(1)}, u32[]{:S(2)}, u32[]{:S(2)}) %collective-permute-start.12) | collective-permute-done | bytes 110624 | tf_op jit(solution)/shard_map/ppermute | solution.py:193
  56.0 0.1 collective-permute-start.18
  56.1 0.7 %collective-permute-done.16.refs_3_ = bf16[288,128]{1,0:T(8,128)(2,1)S(1)} collective-permute-done((bf16[288,128]{1,0:T(8,128)(2,1)S(1)}, bf16[288,128]{1,0:T(8,128)(2,1)S(1)}, u32[]{:S(2)}, u32[]{:S(2)}) %collective-permute-start.16) | collective-permute-done | bytes 73760 | tf_op jit(solution)/shard_map/ppermute | solution.py:193
  56.7 0.7 %shard_map.115 = bf16[1,69,1536]{2,1,0:T(8,128)(2,1)} custom-call(f32[648,128]{1,0:T(8,128)S(1)} %get-tuple-element.57.refs_0_, bf16[648,128]{1,0:T(8,128)(2,1)S(1)} %collective-permute-done.9.refs_1_, f32[216,128]{1,0:T(8,128)S(1)} %get-tuple-element.62.refs_2_, bf16[216,128]{1,0:T(8,128)(2,1)S(1)} %collective-permute-done.14.refs_3_), custom_call_target="tpu_custom_call" | custom-call | tf_op jit(solution)/shard_map/pallas_call | solution.py:253
  57.5 3.4 %collective-permute-done.18.refs_5_ = bf16[144,128]{1,0:T(8,128)(2,1)S(1)} collective-permute-done((bf16[144,128]{1,0:T(8,128)(2,1)S(1)}, bf16[144,128]{1,0:T(8,128)(2,1)S(1)}, u32[]{:S(2)}, u32[]{:S(2)}) %collective-permute-start.18) | collective-permute-done | bytes 36896 | tf_op jit(solution)/shard_map/ppermute | solution.py:193
  60.9 0.7 %shard_map.116 = bf16[1,69,1536]{2,1,0:T(8,128)(2,1)} custom-call(f32[432,128]{1,0:T(8,128)S(1)} %get-tuple-element.58.refs_0_, bf16[432,128]{1,0:T(8,128)(2,1)S(1)} %collective-permute-done.12.refs_1_, f32[288,128]{1,0:T(8,128)S(1)} %get-tuple-element.60.refs_2_, bf16[288,128]{1,0:T(8,128)(2,1)S(1)} %collective-permute-done.16.refs_3_, ...), custom_call_target="tpu_custom_call" | custom-call | tf_op jit(solution)/shard_map/pallas_call | solution.py:253
  (9 shorter events, 0.2 us)
Async XLA Ops:
  5.3 2.6 %collective-permute-start.1 = (bf16[3456,128]{1,0:T(8,128)(2,1)S(1)}, bf16[3456,128]{1,0:T(8,128)(2,1)S(1)}, u32[]{:S(2)}, u32[]{:S(2)}) collective-permute-start(bf16[3456,128]{1,0:T(8,128)(2,1)S(1)} %get-tuple-element.31), channel_id=1, source_target_pairs={{0,1},{1,0},{2,3},{3,2},{4,5},{5,4},{6,7},{7,6},{8,9},{9,8},{10,11... | collective-permute-start | bytes 2654216 | tf_op jit(solution)/shard_map/ppermute | solution.py:193
  5.8 5.2 %collective-permute-start = (bf16[3456,128]{1,0:T(8,128)(2,1)S(1)}, bf16[3456,128]{1,0:T(8,128)(2,1)S(1)}, u32[]{:S(2)}, u32[]{:S(2)}) collective-permute-start(bf16[3456,128]{1,0:T(8,128)(2,1)S(1)} %get-tuple-element.30), channel_id=1, source_target_pairs={{0,1},{1,0},{2,3},{3,2},{4,5},{5,4},{6,7},{7,6},{8,9},{9,8},{10,11... | collective-permute-start | bytes 2654216 | tf_op jit(solution)/shard_map/ppermute | solution.py:193
  8.0 11.6 %collective-permute-start.2 = (bf16[2592,128]{1,0:T(8,128)(2,1)S(1)}, bf16[2592,128]{1,0:T(8,128)(2,1)S(1)}, u32[]{:S(2)}, u32[]{:S(2)}) collective-permute-start(bf16[2592,128]{1,0:T(8,128)(2,1)S(1)} %add_convert_fusion), channel_id=1, source_target_pairs={{0,2},{1,5},{2,0},{3,7},{4,6},{5,1},{6,4},{7,3},{8,10},{9,13},{10,... | collective-permute-start | bytes 1990664 | tf_op jit(solution)/shard_map/ppermute | solution.py:193
  15.6 8.8 %collective-permute-start.7 = (bf16[3456,128]{1,0:T(8,128)(2,1)S(1)}, bf16[3456,128]{1,0:T(8,128)(2,1)S(1)}, u32[]{:S(2)}, u32[]{:S(2)}) collective-permute-start(bf16[3456,128]{1,0:T(8,128)(2,1)S(1)} %get-tuple-element.36), channel_id=1, source_target_pairs={{0,1},{1,0},{2,3},{3,2},{4,5},{5,4},{6,7},{7,6},{8,9},{9,8},{10,11... | collective-permute-start | bytes 2654216 | tf_op jit(solution)/shard_map/ppermute | solution.py:193
  15.7 6.2 %collective-permute-start.5 = (bf16[864,128]{1,0:T(8,128)(2,1)S(1)}, bf16[864,128]{1,0:T(8,128)(2,1)S(1)}, u32[]{:S(2)}, u32[]{:S(2)}) collective-permute-start(bf16[864,128]{1,0:T(8,128)(2,1)S(1)} %add_convert_fusion.5), channel_id=1, source_target_pairs={{0,2},{1,5},{2,0},{3,7},{4,6},{5,1},{6,4},{7,3},{8,10},{9,13},{10,... | collective-permute-start | bytes 663560 | tf_op jit(solution)/shard_map/ppermute | solution.py:193
  17.1 16.8 %collective-permute-start.4 = (bf16[3456,128]{1,0:T(8,128)(2,1)S(1)}, bf16[3456,128]{1,0:T(8,128)(2,1)S(1)}, u32[]{:S(2)}, u32[]{:S(2)}) collective-permute-start(bf16[3456,128]{1,0:T(8,128)(2,1)S(1)} %get-tuple-element.35), channel_id=1, source_target_pairs={{0,1},{1,0},{2,3},{3,2},{4,5},{5,4},{6,7},{7,6},{8,9},{9,8},{10,11... | collective-permute-start | bytes 2654216 | tf_op jit(solution)/shard_map/ppermute | solution.py:193
  19.7 19.2 %collective-permute-start.3 = (bf16[1296,128]{1,0:T(8,128)(2,1)S(1)}, bf16[1296,128]{1,0:T(8,128)(2,1)S(1)}, u32[]{:S(2)}, u32[]{:S(2)}) collective-permute-start(bf16[1296,128]{1,0:T(8,128)(2,1)S(1)} %add_convert_fusion.2), channel_id=1, source_target_pairs={{0,4},{1,3},{2,6},{3,1},{4,0},{5,7},{6,2},{7,5},{8,12},{9,11},{10,... | collective-permute-start | bytes 995336 | tf_op jit(solution)/shard_map/ppermute | solution.py:193
  22.0 8.3 %collective-permute-start.6 = (bf16[432,128]{1,0:T(8,128)(2,1)S(1)}, bf16[432,128]{1,0:T(8,128)(2,1)S(1)}, u32[]{:S(2)}, u32[]{:S(2)}) collective-permute-start(bf16[432,128]{1,0:T(8,128)(2,1)S(1)} %add_convert_fusion.10), channel_id=1, source_target_pairs={{0,4},{1,3},{2,6},{3,1},{4,0},{5,7},{6,2},{7,5},{8,12},{9,11},{10,... | collective-permute-start | bytes 331784 | tf_op jit(solution)/shard_map/ppermute | solution.py:193
  24.5 12.1 %collective-permute-start.8 = (bf16[1728,128]{1,0:T(8,128)(2,1)S(1)}, bf16[1728,128]{1,0:T(8,128)(2,1)S(1)}, u32[]{:S(2)}, u32[]{:S(2)}) collective-permute-start(bf16[1728,128]{1,0:T(8,128)(2,1)S(1)} %add_convert_fusion.1), channel_id=1, source_target_pairs={{0,2},{1,5},{2,0},{3,7},{4,6},{5,1},{6,4},{7,3},{8,10},{9,13},{10,... | collective-permute-start | bytes 1327112 | tf_op jit(solution)/shard_map/ppermute | solution.py:193
  30.4 19.6 %collective-permute-start.14 = (bf16[216,128]{1,0:T(8,128)(2,1)S(1)}, bf16[216,128]{1,0:T(8,128)(2,1)S(1)}, u32[]{:S(2)}, u32[]{:S(2)}) collective-permute-start(bf16[216,128]{1,0:T(8,128)(2,1)S(1)} %get-tuple-element.63), channel_id=1, source_target_pairs={{0,8},{1,9},{2,10},{3,11},{4,12},{5,13},{6,14},{7,15},{8,0},{9,1},... | collective-permute-start | bytes 165896 | tf_op jit(solution)/shard_map/ppermute | solution.py:193
  33.9 8.4 %collective-permute-start.11 = (bf16[1152,128]{1,0:T(8,128)(2,1)S(1)}, bf16[1152,128]{1,0:T(8,128)(2,1)S(1)}, u32[]{:S(2)}, u32[]{:S(2)}) collective-permute-start(bf16[1152,128]{1,0:T(8,128)(2,1)S(1)} %add_convert_fusion.3), channel_id=1, source_target_pairs={{0,2},{1,5},{2,0},{3,7},{4,6},{5,1},{6,4},{7,3},{8,10},{9,13},{10,... | collective-permute-start | bytes 884744 | tf_op jit(solution)/shard_map/ppermute | solution.py:193
  36.6 10.1 %collective-permute-start.10 = (bf16[864,128]{1,0:T(8,128)(2,1)S(1)}, bf16[864,128]{1,0:T(8,128)(2,1)S(1)}, u32[]{:S(2)}, u32[]{:S(2)}) collective-permute-start(bf16[864,128]{1,0:T(8,128)(2,1)S(1)} %add_convert_fusion.4), channel_id=1, source_target_pairs={{0,4},{1,3},{2,6},{3,1},{4,0},{5,7},{6,2},{7,5},{8,12},{9,11},{10,... | collective-permute-start | bytes 663560 | tf_op jit(solution)/shard_map/ppermute | solution.py:193
  39.0 17.0 %collective-permute-start.9 = (bf16[648,128]{1,0:T(8,128)(2,1)S(1)}, bf16[648,128]{1,0:T(8,128)(2,1)S(1)}, u32[]{:S(2)}, u32[]{:S(2)}) collective-permute-start(bf16[648,128]{1,0:T(8,128)(2,1)S(1)} %get-tuple-element.56), channel_id=1, source_target_pairs={{0,8},{1,9},{2,10},{3,11},{4,12},{5,13},{6,14},{7,15},{8,0},{9,1},... | collective-permute-start | bytes 497672 | tf_op jit(solution)/shard_map/ppermute | solution.py:193
  39.1 8.3 %collective-permute-start.15 = (bf16[576,128]{1,0:T(8,128)(2,1)S(1)}, bf16[576,128]{1,0:T(8,128)(2,1)S(1)}, u32[]{:S(2)}, u32[]{:S(2)}) collective-permute-start(bf16[576,128]{1,0:T(8,128)(2,1)S(1)} %add_convert_fusion.8), channel_id=1, source_target_pairs={{0,2},{1,5},{2,0},{3,7},{4,6},{5,1},{6,4},{7,3},{8,10},{9,13},{10,... | collective-permute-start | bytes 442376 | tf_op jit(solution)/shard_map/ppermute | solution.py:193
  42.3 7.6 %collective-permute-start.13 = (bf16[576,128]{1,0:T(8,128)(2,1)S(1)}, bf16[576,128]{1,0:T(8,128)(2,1)S(1)}, u32[]{:S(2)}, u32[]{:S(2)}) collective-permute-start(bf16[576,128]{1,0:T(8,128)(2,1)S(1)} %add_convert_fusion.7), channel_id=1, source_target_pairs={{0,4},{1,3},{2,6},{3,1},{4,0},{5,7},{6,2},{7,5},{8,12},{9,11},{10,... | collective-permute-start | bytes 442376 | tf_op jit(solution)/shard_map/ppermute | solution.py:193
  46.8 9.1 %collective-permute-start.12 = (bf16[432,128]{1,0:T(8,128)(2,1)S(1)}, bf16[432,128]{1,0:T(8,128)(2,1)S(1)}, u32[]{:S(2)}, u32[]{:S(2)}) collective-permute-start(bf16[432,128]{1,0:T(8,128)(2,1)S(1)} %get-tuple-element.59), channel_id=1, source_target_pairs={{0,8},{1,9},{2,10},{3,11},{4,12},{5,13},{6,14},{7,15},{8,0},{9,1},... | collective-permute-start | bytes 331784 | tf_op jit(solution)/shard_map/ppermute | solution.py:193
  47.4 8.5 %collective-permute-start.17 = (bf16[288,128]{1,0:T(8,128)(2,1)S(1)}, bf16[288,128]{1,0:T(8,128)(2,1)S(1)}, u32[]{:S(2)}, u32[]{:S(2)}) collective-permute-start(bf16[288,128]{1,0:T(8,128)(2,1)S(1)} %add_convert_fusion.12), channel_id=1, source_target_pairs={{0,4},{1,3},{2,6},{3,1},{4,0},{5,7},{6,2},{7,5},{8,12},{9,11},{10,... | collective-permute-start | bytes 221192 | tf_op jit(solution)/shard_map/ppermute | solution.py:193
  50.0 6.7 %collective-permute-start.16 = (bf16[288,128]{1,0:T(8,128)(2,1)S(1)}, bf16[288,128]{1,0:T(8,128)(2,1)S(1)}, u32[]{:S(2)}, u32[]{:S(2)}) collective-permute-start(bf16[288,128]{1,0:T(8,128)(2,1)S(1)} %get-tuple-element.61), channel_id=1, source_target_pairs={{0,8},{1,9},{2,10},{3,11},{4,12},{5,13},{6,14},{7,15},{8,0},{9,1},... | collective-permute-start | bytes 221192 | tf_op jit(solution)/shard_map/ppermute | solution.py:193
  56.0 4.9 %collective-permute-start.18 = (bf16[144,128]{1,0:T(8,128)(2,1)S(1)}, bf16[144,128]{1,0:T(8,128)(2,1)S(1)}, u32[]{:S(2)}, u32[]{:S(2)}) collective-permute-start(bf16[144,128]{1,0:T(8,128)(2,1)S(1)} %get-tuple-element.65), channel_id=1, source_target_pairs={{0,8},{1,9},{2,10},{3,11},{4,12},{5,13},{6,14},{7,15},{8,0},{9,1},... | collective-permute-start | bytes 110600 | tf_op jit(solution)/shard_map/ppermute | solution.py:193

commit v11 on v10

--- a/solution.py
+++ b/solution.py
@@ -276,10 +276,10 @@
     one, two = remaps
     pitch = round_up(one[-1][1], 8)
     tiles = one[-1][2] // LANES
-    half, most, more = tiles // 2, tiles * 3 // 4, tiles * 5 // 6
+    most = tiles * 7 // 12
     plans = (
+        [(0, tiles, MIXED)],
         [(0, most, MIXED), (most, tiles, MIXED)],
-        [(0, half, MIXED), (half, more, MIXED), (more, tiles, MIXED)],
     )
     ones, twos = [[Chain(chunk, devices, pitch) for chunk in chunks] for chunks in plans]
     order = Order()
@@ -310,14 +310,13 @@
     def cores(send):
         return exchange(send, STRAIGHT, 0, devices)
 
-    a, b = ones
-    c, d, e = twos
+    (a,) = ones
+    b, c = twos
 
     sums, send, send_on = products(one, plans[0], devices)
     on, rest = cores(send_on), cores(send)
     summed(ones, sums, on)
     a.second()
-    b.second()
     rested(ones, sums, rest)
     made = products((order.after(two[0]),) + two[1:], plans[1], devices)
     order.before(made)
@@ -325,25 +324,18 @@
     on, rest = cores(send_on), cores(send)
 
     step(a)
+    summed(twos, sums, on)
+    b.second()
+    begun(c)
+    step(a)
+    rested(twos, sums, rest)
     step(b)
-    summed(twos, sums, on)
-    c.second()
-    begun(d)
-    step(b)
-    rested(twos, sums, rest)
     step(c)
     step(a)
-    begun(e)
-    step(d)
+    step(b)
     step(c)
-    step(e)
     step(b)
-    step(d)
     step(c)
-    step(a)
-    step(e)
-    step(d)
-    step(e)
     return [final_sum(line, remap[-1], pitch) for line, remap in zip((ones, twos), remaps)]
 
 

time: 61.8 us -> 61.3 us (level); the launches traced: 61.7 us -> 60.1 us
  starting transfers between devices: 26.6 us -> 18.5 us
  waiting for transfers between devices: 22.5 us -> 29.1 us
    ppermute x19 -> x13, starting transfers between devices: 26.6 us -> 18.5 us  [exchange(): return lax.ppermute(value, 'curve', pairs)]
    ppermute x19 -> x13, waiting for transfers between devices: 22.5 us -> 29.1 us  [exchange(): return lax.ppermute(value, 'curve', pairs)]
  transfers between devices with their start and end apart: 19 -> 13, of which waited for: 9 -> 7; matrix products, arithmetic and copies ran while one was open for 2% -> 2% of each run, Pallas kernels for 9% -> 9%
where the time goes in v11:
time: 61.3 us; the launch traced here: 60.1 us
  waiting for transfers between devices  29.1 us (47%)
  starting transfers between devices  18.5 us (30%)
  Pallas kernels  10.6 us (17%)
  other arithmetic  1.13 us (2%)
  between operations  0.71 us (1%)
    ppermute x13, waiting for transfers between devices, exchange(): return lax.ppermute(value, 'curve', pairs)  29.1 us
    ppermute x13, starting transfers between devices, exchange(): return lax.ppermute(value, 'curve', pairs)  18.5 us
    pallas_call x2, Pallas kernels, products(): pl.pallas_call(functools.partial(product_kernel, channels, pitch, chunks,...  9.15 us
    pallas_call x2, Pallas kernels, final_sum(): pl.pallas_call(functools.partial(final_kernel, like_shape[1], pitch, part...  1.48 us
  transfers between devices with their start and end apart: 13, of which 7 were waited for; matrix products, arithmetic and copies ran while one was open for 2% of the time, Pallas kernels for 9%

profile of v11, /device:TPU:0, one launch (start us, length us, event | category | flops | bytes accessed | tf_op | source)
XLA Modules:
  0.0 60.1 jit_solution(13617093266968761626)
XLA Ops:
  0.6 4.5 %shard_map.113 = (f32[13824,128]{1,0:T(8,128)S(1)}, bf16[3456,128]{1,0:T(8,128)(2,1)S(1)}, bf16[3456,128]{1,0:T(8,128)(2,1)S(1)}) custom-call(s32[144]{0:T(256)} %source_hbm.2, s32[144]{0:T(256)} %target_hbm.2, s32[1,16]{1,0:T(1,128)} %counts_hbm.2, bf16[1,69,1536]{2,1,0:T(8,128)(2,1)} %x_hbm.1, bf16[144,128,128]{2,1,0:T(8,128)(2,1)} %w_hbm.2), custom_call_target="tpu_custom_call" | custom-call | flops 325582848 | bytes 13565952 | tf_op jit(solution)/shard_map/pallas_call | solution.py:163
  5.2 0.5 collective-permute-start.1
  5.7 0.1 collective-permute-start
  5.8 2.0 %collective-permute-done.1 = bf16[3456,128]{1,0:T(8,128)(2,1)S(1)} collective-permute-done((bf16[3456,128]{1,0:T(8,128)(2,1)S(1)}, bf16[3456,128]{1,0:T(8,128)(2,1)S(1)}, u32[]{:S(2)}, u32[]{:S(2)}) %collective-permute-start.1) | collective-permute-done | bytes 884768 | tf_op jit(solution)/shard_map/ppermute | solution.py:193
  7.8 0.2 add_convert_fusion
  8.0 3.0 %collective-permute-start.2 = (bf16[3456,128]{1,0:T(8,128)(2,1)S(1)}, bf16[3456,128]{1,0:T(8,128)(2,1)S(1)}, u32[]{:S(2)}, u32[]{:S(2)}) collective-permute-start(bf16[3456,128]{1,0:T(8,128)(2,1)S(1)} %add_convert_fusion), channel_id=1, source_target_pairs={{0,2},{1,5},{2,0},{3,7},{4,6},{5,1},{6,4},{7,3},{8,10},{9,13},{10,... | collective-permute-start | bytes 2654216 | tf_op jit(solution)/shard_map/ppermute | solution.py:193
  11.0 0.0 collective-permute-done
  11.0 4.6 %shard_map.114 = (f32[13824,128]{1,0:T(8,128)S(1)}, bf16[3456,128]{1,0:T(8,128)(2,1)S(1)}, bf16[3456,128]{1,0:T(8,128)(2,1)S(1)}) custom-call(s32[144]{0:T(256)} %source_hbm.3, s32[144]{0:T(256)} %target_hbm.3, s32[1,16]{1,0:T(1,128)} %counts_hbm.3, bf16[1,69,1536]{2,1,0:T(8,128)(2,1)} %x_hbm.2, bf16[144,128,128]{2,1,0:T(8,128)(2,1)} %w_hbm.3), custom_call_target="tpu_custom_call" | custom-call | flops 325582848 | bytes 13565952 | tf_op jit(solution)/shard_map/pallas_call | solution.py:163
  15.6 0.1 collective-permute-start.4
  15.7 0.5 collective-permute-start.6
  16.2 5.8 %collective-permute-done.2 = bf16[3456,128]{1,0:T(8,128)(2,1)S(1)} collective-permute-done((bf16[3456,128]{1,0:T(8,128)(2,1)S(1)}, bf16[3456,128]{1,0:T(8,128)(2,1)S(1)}, u32[]{:S(2)}, u32[]{:S(2)}) %collective-permute-start.2) | collective-permute-done | bytes 884768 | tf_op jit(solution)/shard_map/ppermute | solution.py:193
  22.0 0.1 add_convert_fusion.2
  22.2 2.1 %collective-permute-start.3 = (bf16[1728,128]{1,0:T(8,128)(2,1)S(1)}, bf16[1728,128]{1,0:T(8,128)(2,1)S(1)}, u32[]{:S(2)}, u32[]{:S(2)}) collective-permute-start(bf16[1728,128]{1,0:T(8,128)(2,1)S(1)} %add_convert_fusion.2), channel_id=1, source_target_pairs={{0,4},{1,3},{2,6},{3,1},{4,0},{5,7},{6,2},{7,5},{8,12},{9,11},{10,... | collective-permute-start | bytes 1327112 | tf_op jit(solution)/shard_map/ppermute | solution.py:193
  24.3 0.0 collective-permute-done.4
  24.3 0.1 add_convert_fusion.1
  24.4 1.6 %collective-permute-start.8 = (bf16[2016,128]{1,0:T(8,128)(2,1)S(1)}, bf16[2016,128]{1,0:T(8,128)(2,1)S(1)}, u32[]{:S(2)}, u32[]{:S(2)}) collective-permute-start(bf16[2016,128]{1,0:T(8,128)(2,1)S(1)} %add_convert_fusion.1), channel_id=1, source_target_pairs={{0,2},{1,5},{2,0},{3,7},{4,6},{5,1},{6,4},{7,3},{8,10},{9,13},{10,... | collective-permute-start | bytes 1548296 | tf_op jit(solution)/shard_map/ppermute | solution.py:193
  26.0 0.1 add_convert_fusion.3
  26.1 0.6 collective-permute-start.7
  26.6 8.5 %collective-permute-done.3 = bf16[1728,128]{1,0:T(8,128)(2,1)S(1)} collective-permute-done((bf16[1728,128]{1,0:T(8,128)(2,1)S(1)}, bf16[1728,128]{1,0:T(8,128)(2,1)S(1)}, u32[]{:S(2)}, u32[]{:S(2)}) %collective-permute-start.3) | collective-permute-done | bytes 442400 | tf_op jit(solution)/shard_map/ppermute | solution.py:193
  35.2 0.2 add_convert_fusion.5
  35.3 0.0 collective-permute-done.6
  35.4 0.0 collective-permute-done.8
  35.4 0.1 add_convert_fusion.4
  35.5 2.3 %collective-permute-start.9 = (bf16[1008,128]{1,0:T(8,128)(2,1)S(1)}, bf16[1008,128]{1,0:T(8,128)(2,1)S(1)}, u32[]{:S(2)}, u32[]{:S(2)}) collective-permute-start(bf16[1008,128]{1,0:T(8,128)(2,1)S(1)} %add_convert_fusion.4), channel_id=1, source_target_pairs={{0,4},{1,3},{2,6},{3,1},{4,0},{5,7},{6,2},{7,5},{8,12},{9,11},{10,... | collective-permute-start | bytes 774152 | tf_op jit(solution)/shard_map/ppermute | solution.py:193
  37.7 2.6 %collective-permute-start.5 = (bf16[864,128]{1,0:T(8,128)(2,1)S(1)}, bf16[864,128]{1,0:T(8,128)(2,1)S(1)}, u32[]{:S(2)}, u32[]{:S(2)}) collective-permute-start(bf16[864,128]{1,0:T(8,128)(2,1)S(1)} %get-tuple-element.42), channel_id=1, source_target_pairs={{0,8},{1,9},{2,10},{3,11},{4,12},{5,13},{6,14},{7,15},{8,0},{9,1},... | collective-permute-start | bytes 663560 | tf_op jit(solution)/shard_map/ppermute | solution.py:193
  40.3 0.0 collective-permute-done.7
  40.3 0.1 add_convert_fusion.6
  40.4 0.5 collective-permute-start.11
  40.9 6.1 %collective-permute-done.5.refs_1_ = bf16[864,128]{1,0:T(8,128)(2,1)S(1)} collective-permute-done((bf16[864,128]{1,0:T(8,128)(2,1)S(1)}, bf16[864,128]{1,0:T(8,128)(2,1)S(1)}, u32[]{:S(2)}, u32[]{:S(2)}) %collective-permute-start.5) | collective-permute-done | bytes 221216 | tf_op jit(solution)/shard_map/ppermute | solution.py:193
  47.1 0.5 collective-permute-done.9
  47.6 0.1 add_convert_fusion.7
  47.7 2.8 %collective-permute-start.10 = (bf16[504,128]{1,0:T(8,128)(2,1)S(1)}, bf16[504,128]{1,0:T(8,128)(2,1)S(1)}, u32[]{:S(2)}, u32[]{:S(2)}) collective-permute-start(bf16[504,128]{1,0:T(8,128)(2,1)S(1)} %get-tuple-element.44), channel_id=1, source_target_pairs={{0,8},{1,9},{2,10},{3,11},{4,12},{5,13},{6,14},{7,15},{8,0},{9,1},... | collective-permute-start | bytes 387080 | tf_op jit(solution)/shard_map/ppermute | solution.py:193
  50.5 0.0 collective-permute-done.11
  50.5 0.1 convert_add_fusion.2
  50.6 1.9 %collective-permute-start.12 = (bf16[360,128]{1,0:T(8,128)(2,1)S(1)}, bf16[360,128]{1,0:T(8,128)(2,1)S(1)}, u32[]{:S(2)}, u32[]{:S(2)}) collective-permute-start(bf16[360,128]{1,0:T(8,128)(2,1)S(1)} %get-tuple-element.47), channel_id=1, source_target_pairs={{0,8},{1,9},{2,10},{3,11},{4,12},{5,13},{6,14},{7,15},{8,0},{9,1},... | collective-permute-start | bytes 276488 | tf_op jit(solution)/shard_map/ppermute | solution.py:193
  52.4 0.7 %shard_map.115 = bf16[1,69,1536]{2,1,0:T(8,128)(2,1)} custom-call(f32[864,128]{1,0:T(8,128)S(1)} %get-tuple-element.43.refs_0_, bf16[864,128]{1,0:T(8,128)(2,1)S(1)} %collective-permute-done.5.refs_1_), custom_call_target="tpu_custom_call" | custom-call | tf_op jit(solution)/shard_map/pallas_call | solution.py:253
  53.2 2.8 %collective-permute-done.10.refs_1_ = bf16[504,128]{1,0:T(8,128)(2,1)S(1)} collective-permute-done((bf16[504,128]{1,0:T(8,128)(2,1)S(1)}, bf16[504,128]{1,0:T(8,128)(2,1)S(1)}, u32[]{:S(2)}, u32[]{:S(2)}) %collective-permute-start.10) | collective-permute-done | bytes 129056 | tf_op jit(solution)/shard_map/ppermute | solution.py:193
  56.0 3.4 %collective-permute-done.12.refs_3_ = bf16[360,128]{1,0:T(8,128)(2,1)S(1)} collective-permute-done((bf16[360,128]{1,0:T(8,128)(2,1)S(1)}, bf16[360,128]{1,0:T(8,128)(2,1)S(1)}, u32[]{:S(2)}, u32[]{:S(2)}) %collective-permute-start.12) | collective-permute-done | bytes 92192 | tf_op jit(solution)/shard_map/ppermute | solution.py:193
  59.3 0.7 %shard_map.116 = bf16[1,69,1536]{2,1,0:T(8,128)(2,1)} custom-call(f32[504,128]{1,0:T(8,128)S(1)} %get-tuple-element.45.refs_0_, bf16[504,128]{1,0:T(8,128)(2,1)S(1)} %collective-permute-done.10.refs_1_, f32[360,128]{1,0:T(8,128)S(1)} %get-tuple-element.46.refs_2_, bf16[360,128]{1,0:T(8,128)(2,1)S(1)} %collective-permute-done.12.refs_3_), custom_call_target="tpu_custom_call" | custom-call | tf_op jit(solution)/shard_map/pallas_call | solution.py:253
Async XLA Ops:
  5.2 2.6 %collective-permute-start.1 = (bf16[3456,128]{1,0:T(8,128)(2,1)S(1)}, bf16[3456,128]{1,0:T(8,128)(2,1)S(1)}, u32[]{:S(2)}, u32[]{:S(2)}) collective-permute-start(bf16[3456,128]{1,0:T(8,128)(2,1)S(1)} %get-tuple-element.24), channel_id=1, source_target_pairs={{0,1},{1,0},{2,3},{3,2},{4,5},{5,4},{6,7},{7,6},{8,9},{9,8},{10,11... | collective-permute-start | bytes 2654216 | tf_op jit(solution)/shard_map/ppermute | solution.py:193
  5.7 5.3 %collective-permute-start = (bf16[3456,128]{1,0:T(8,128)(2,1)S(1)}, bf16[3456,128]{1,0:T(8,128)(2,1)S(1)}, u32[]{:S(2)}, u32[]{:S(2)}) collective-permute-start(bf16[3456,128]{1,0:T(8,128)(2,1)S(1)} %get-tuple-element.23), channel_id=1, source_target_pairs={{0,1},{1,0},{2,3},{3,2},{4,5},{5,4},{6,7},{7,6},{8,9},{9,8},{10,11... | collective-permute-start | bytes 2654216 | tf_op jit(solution)/shard_map/ppermute | solution.py:193
  8.0 14.0 %collective-permute-start.2 = (bf16[3456,128]{1,0:T(8,128)(2,1)S(1)}, bf16[3456,128]{1,0:T(8,128)(2,1)S(1)}, u32[]{:S(2)}, u32[]{:S(2)}) collective-permute-start(bf16[3456,128]{1,0:T(8,128)(2,1)S(1)} %add_convert_fusion), channel_id=1, source_target_pairs={{0,2},{1,5},{2,0},{3,7},{4,6},{5,1},{6,4},{7,3},{8,10},{9,13},{10,... | collective-permute-start | bytes 2654216 | tf_op jit(solution)/shard_map/ppermute | solution.py:193
  15.6 8.7 %collective-permute-start.4 = (bf16[3456,128]{1,0:T(8,128)(2,1)S(1)}, bf16[3456,128]{1,0:T(8,128)(2,1)S(1)}, u32[]{:S(2)}, u32[]{:S(2)}) collective-permute-start(bf16[3456,128]{1,0:T(8,128)(2,1)S(1)} %get-tuple-element.29), channel_id=1, source_target_pairs={{0,1},{1,0},{2,3},{3,2},{4,5},{5,4},{6,7},{7,6},{8,9},{9,8},{10,11... | collective-permute-start | bytes 2654216 | tf_op jit(solution)/shard_map/ppermute | solution.py:193
  15.7 19.7 %collective-permute-start.6 = (bf16[3456,128]{1,0:T(8,128)(2,1)S(1)}, bf16[3456,128]{1,0:T(8,128)(2,1)S(1)}, u32[]{:S(2)}, u32[]{:S(2)}) collective-permute-start(bf16[3456,128]{1,0:T(8,128)(2,1)S(1)} %get-tuple-element.28), channel_id=1, source_target_pairs={{0,1},{1,0},{2,3},{3,2},{4,5},{5,4},{6,7},{7,6},{8,9},{9,8},{10,11... | collective-permute-start | bytes 2654216 | tf_op jit(solution)/shard_map/ppermute | solution.py:193
  22.2 13.0 %collective-permute-start.3 = (bf16[1728,128]{1,0:T(8,128)(2,1)S(1)}, bf16[1728,128]{1,0:T(8,128)(2,1)S(1)}, u32[]{:S(2)}, u32[]{:S(2)}) collective-permute-start(bf16[1728,128]{1,0:T(8,128)(2,1)S(1)} %add_convert_fusion.2), channel_id=1, source_target_pairs={{0,4},{1,3},{2,6},{3,1},{4,0},{5,7},{6,2},{7,5},{8,12},{9,11},{10,... | collective-permute-start | bytes 1327112 | tf_op jit(solution)/shard_map/ppermute | solution.py:193
  24.4 10.9 %collective-permute-start.8 = (bf16[2016,128]{1,0:T(8,128)(2,1)S(1)}, bf16[2016,128]{1,0:T(8,128)(2,1)S(1)}, u32[]{:S(2)}, u32[]{:S(2)}) collective-permute-start(bf16[2016,128]{1,0:T(8,128)(2,1)S(1)} %add_convert_fusion.1), channel_id=1, source_target_pairs={{0,2},{1,5},{2,0},{3,7},{4,6},{5,1},{6,4},{7,3},{8,10},{9,13},{10,... | collective-permute-start | bytes 1548296 | tf_op jit(solution)/shard_map/ppermute | solution.py:193
  26.1 14.2 %collective-permute-start.7 = (bf16[1440,128]{1,0:T(8,128)(2,1)S(1)}, bf16[1440,128]{1,0:T(8,128)(2,1)S(1)}, u32[]{:S(2)}, u32[]{:S(2)}) collective-permute-start(bf16[1440,128]{1,0:T(8,128)(2,1)S(1)} %add_convert_fusion.3), channel_id=1, source_target_pairs={{0,2},{1,5},{2,0},{3,7},{4,6},{5,1},{6,4},{7,3},{8,10},{9,13},{10,... | collective-permute-start | bytes 1105928 | tf_op jit(solution)/shard_map/ppermute | solution.py:193
  35.5 12.1 %collective-permute-start.9 = (bf16[1008,128]{1,0:T(8,128)(2,1)S(1)}, bf16[1008,128]{1,0:T(8,128)(2,1)S(1)}, u32[]{:S(2)}, u32[]{:S(2)}) collective-permute-start(bf16[1008,128]{1,0:T(8,128)(2,1)S(1)} %add_convert_fusion.4), channel_id=1, source_target_pairs={{0,4},{1,3},{2,6},{3,1},{4,0},{5,7},{6,2},{7,5},{8,12},{9,11},{10,... | collective-permute-start | bytes 774152 | tf_op jit(solution)/shard_map/ppermute | solution.py:193
  37.7 9.3 %collective-permute-start.5 = (bf16[864,128]{1,0:T(8,128)(2,1)S(1)}, bf16[864,128]{1,0:T(8,128)(2,1)S(1)}, u32[]{:S(2)}, u32[]{:S(2)}) collective-permute-start(bf16[864,128]{1,0:T(8,128)(2,1)S(1)} %get-tuple-element.42), channel_id=1, source_target_pairs={{0,8},{1,9},{2,10},{3,11},{4,12},{5,13},{6,14},{7,15},{8,0},{9,1},... | collective-permute-start | bytes 663560 | tf_op jit(solution)/shard_map/ppermute | solution.py:193
  40.4 10.1 %collective-permute-start.11 = (bf16[720,128]{1,0:T(8,128)(2,1)S(1)}, bf16[720,128]{1,0:T(8,128)(2,1)S(1)}, u32[]{:S(2)}, u32[]{:S(2)}) collective-permute-start(bf16[720,128]{1,0:T(8,128)(2,1)S(1)} %add_convert_fusion.6), channel_id=1, source_target_pairs={{0,4},{1,3},{2,6},{3,1},{4,0},{5,7},{6,2},{7,5},{8,12},{9,11},{10,... | collective-permute-start | bytes 552968 | tf_op jit(solution)/shard_map/ppermute | solution.py:193
  47.7 8.3 %collective-permute-start.10 = (bf16[504,128]{1,0:T(8,128)(2,1)S(1)}, bf16[504,128]{1,0:T(8,128)(2,1)S(1)}, u32[]{:S(2)}, u32[]{:S(2)}) collective-permute-start(bf16[504,128]{1,0:T(8,128)(2,1)S(1)} %get-tuple-element.44), channel_id=1, source_target_pairs={{0,8},{1,9},{2,10},{3,11},{4,12},{5,13},{6,14},{7,15},{8,0},{9,1},... | collective-permute-start | bytes 387080 | tf_op jit(solution)/shard_map/ppermute | solution.py:193
  50.6 8.8 %collective-permute-start.12 = (bf16[360,128]{1,0:T(8,128)(2,1)S(1)}, bf16[360,128]{1,0:T(8,128)(2,1)S(1)}, u32[]{:S(2)}, u32[]{:S(2)}) collective-permute-start(bf16[360,128]{1,0:T(8,128)(2,1)S(1)} %get-tuple-element.47), channel_id=1, source_target_pairs={{0,8},{1,9},{2,10},{3,11},{4,12},{5,13},{6,14},{7,15},{8,0},{9,1},... | collective-permute-start | bytes 276488 | tf_op jit(solution)/shard_map/ppermute | solution.py:193

commit v12 on v10

--- a/solution.py
+++ b/solution.py
@@ -279,7 +279,7 @@
     half, most, more = tiles // 2, tiles * 3 // 4, tiles * 5 // 6
     plans = (
         [(0, most, MIXED), (most, tiles, MIXED)],
-        [(0, half, MIXED), (half, more, MIXED), (more, tiles, MIXED)],
+        [(0, half, STRAIGHT), (half, more, STRAIGHT), (more, tiles, STRAIGHT)],
     )
     ones, twos = [[Chain(chunk, devices, pitch) for chunk in chunks] for chunks in plans]
     order = Order()
@@ -329,18 +329,18 @@
     summed(twos, sums, on)
     c.second()
     begun(d)
+    step(a)
     step(b)
     rested(twos, sums, rest)
     step(c)
-    step(a)
     begun(e)
     step(d)
+    step(a)
+    step(b)
     step(c)
     step(e)
-    step(b)
+    step(c)
     step(d)
-    step(c)
-    step(a)
     step(e)
     step(d)
     step(e)

time: 61.8 us -> 60.8 us (0.984)
  waiting for transfers between devices: 22.5 us -> 21.8 us
    ppermute x19, waiting for transfers between devices: 22.5 us -> 21.8 us  [exchange(): return lax.ppermute(value, 'curve', pairs)]
  transfers between devices with their start and end apart: 19 -> 19, of which waited for: 9 -> 10; matrix products, arithmetic and copies ran while one was open for 2% -> 2% of each run, Pallas kernels for 9% -> 9%
where the time goes in v12:
time: 60.8 us; the launch traced here: 60.7 us
  starting transfers between devices  26.3 us (43%)
  waiting for transfers between devices  21.8 us (36%)
  Pallas kernels  10.7 us (18%)
  other arithmetic  1.09 us (2%)
  between operations  0.74 us (1%)
    ppermute x19, starting transfers between devices, exchange(): return lax.ppermute(value, 'curve', pairs)  26.3 us
    ppermute x19, waiting for transfers between devices, exchange(): return lax.ppermute(value, 'curve', pairs)  21.8 us
    pallas_call x2, Pallas kernels, products(): pl.pallas_call(functools.partial(product_kernel, channels, pitch, chunks,...  9.26 us
    pallas_call x2, Pallas kernels, final_sum(): pl.pallas_call(functools.partial(final_kernel, like_shape[1], pitch, part...  1.48 us
  transfers between devices with their start and end apart: 19, of which 10 were waited for; matrix products, arithmetic and copies ran while one was open for 2% of the time, Pallas kernels for 9%

profile of v12, /device:TPU:0, one launch (start us, length us, event | category | flops | bytes accessed | tf_op | source)
XLA Modules:
  0.0 60.7 jit_solution(14860979641807918635)
XLA Ops:
  0.6 4.6 %shard_map.113 = (f32[13824,128]{1,0:T(8,128)S(1)}, bf16[3456,128]{1,0:T(8,128)(2,1)S(1)}, bf16[3456,128]{1,0:T(8,128)(2,1)S(1)}) custom-call(s32[144]{0:T(256)} %source_hbm.2, s32[144]{0:T(256)} %target_hbm.2, s32[1,16]{1,0:T(1,128)} %counts_hbm.2, bf16[1,69,1536]{2,1,0:T(8,128)(2,1)} %x_hbm.1, bf16[144,128,128]{2,1,0:T(8,128)(2,1)} %w_hbm.2), custom_call_target="tpu_custom_call" | custom-call | flops 325582848 | bytes 13565952 | tf_op jit(solution)/shard_map/pallas_call | solution.py:163
  5.3 0.5 collective-permute-start.1
  5.8 0.1 collective-permute-start
  5.9 2.0 %collective-permute-done.1 = bf16[3456,128]{1,0:T(8,128)(2,1)S(1)} collective-permute-done((bf16[3456,128]{1,0:T(8,128)(2,1)S(1)}, bf16[3456,128]{1,0:T(8,128)(2,1)S(1)}, u32[]{:S(2)}, u32[]{:S(2)}) %collective-permute-start.1) | collective-permute-done | bytes 884768 | tf_op jit(solution)/shard_map/ppermute | solution.py:193
  7.8 0.1 add_convert_fusion
  8.0 2.9 %collective-permute-start.2 = (bf16[2592,128]{1,0:T(8,128)(2,1)S(1)}, bf16[2592,128]{1,0:T(8,128)(2,1)S(1)}, u32[]{:S(2)}, u32[]{:S(2)}) collective-permute-start(bf16[2592,128]{1,0:T(8,128)(2,1)S(1)} %add_convert_fusion), channel_id=1, source_target_pairs={{0,2},{1,5},{2,0},{3,7},{4,6},{5,1},{6,4},{7,3},{8,10},{9,13},{10,... | collective-permute-start | bytes 1990664 | tf_op jit(solution)/shard_map/ppermute | solution.py:193
  11.0 4.6 %shard_map.114 = (f32[13824,128]{1,0:T(8,128)S(1)}, bf16[3456,128]{1,0:T(8,128)(2,1)S(1)}, bf16[3456,128]{1,0:T(8,128)(2,1)S(1)}) custom-call(s32[144]{0:T(256)} %source_hbm.3, s32[144]{0:T(256)} %target_hbm.3, s32[1,16]{1,0:T(1,128)} %counts_hbm.3, bf16[1,69,1536]{2,1,0:T(8,128)(2,1)} %x_hbm.2, bf16[144,128,128]{2,1,0:T(8,128)(2,1)} %w_hbm.3), custom_call_target="tpu_custom_call" | custom-call | flops 325582848 | bytes 13565952 | tf_op jit(solution)/shard_map/pallas_call | solution.py:163
  15.6 0.1 collective-permute-start.4
  15.7 1.4 %collective-permute-start.5 = (bf16[864,128]{1,0:T(8,128)(2,1)S(1)}, bf16[864,128]{1,0:T(8,128)(2,1)S(1)}, u32[]{:S(2)}, u32[]{:S(2)}) collective-permute-start(bf16[864,128]{1,0:T(8,128)(2,1)S(1)} %add_convert_fusion.5), channel_id=1, source_target_pairs={{0,2},{1,5},{2,0},{3,7},{4,6},{5,1},{6,4},{7,3},{8,10},{9,13},{10,... | collective-permute-start | bytes 663560 | tf_op jit(solution)/shard_map/ppermute | solution.py:193
  17.1 0.4 collective-permute-start.7
  17.5 2.0 %collective-permute-done.2 = bf16[2592,128]{1,0:T(8,128)(2,1)S(1)} collective-permute-done((bf16[2592,128]{1,0:T(8,128)(2,1)S(1)}, bf16[2592,128]{1,0:T(8,128)(2,1)S(1)}, u32[]{:S(2)}, u32[]{:S(2)}) %collective-permute-start.2) | collective-permute-done | bytes 663584 | tf_op jit(solution)/shard_map/ppermute | solution.py:193
  19.6 0.1 add_convert_fusion.2
  19.7 2.2 %collective-permute-start.3 = (bf16[1296,128]{1,0:T(8,128)(2,1)S(1)}, bf16[1296,128]{1,0:T(8,128)(2,1)S(1)}, u32[]{:S(2)}, u32[]{:S(2)}) collective-permute-start(bf16[1296,128]{1,0:T(8,128)(2,1)S(1)} %add_convert_fusion.2), channel_id=1, source_target_pairs={{0,4},{1,3},{2,6},{3,1},{4,0},{5,7},{6,2},{7,5},{8,12},{9,11},{10,... | collective-permute-start | bytes 995336 | tf_op jit(solution)/shard_map/ppermute | solution.py:193
  21.8 0.1 collective-permute-done.5
  21.9 0.1 add_convert_fusion.10
  22.0 2.4 %collective-permute-start.8 = (bf16[432,128]{1,0:T(8,128)(2,1)S(1)}, bf16[432,128]{1,0:T(8,128)(2,1)S(1)}, u32[]{:S(2)}, u32[]{:S(2)}) collective-permute-start(bf16[432,128]{1,0:T(8,128)(2,1)S(1)} %add_convert_fusion.10), channel_id=1, source_target_pairs={{0,4},{1,3},{2,6},{3,1},{4,0},{5,7},{6,2},{7,5},{8,12},{9,11},{10,... | collective-permute-start | bytes 331784 | tf_op jit(solution)/shard_map/ppermute | solution.py:193
  24.4 0.1 add_convert_fusion.3
  24.5 0.1 add_convert_fusion.1
  24.6 1.6 %collective-permute-start.10 = (bf16[1728,128]{1,0:T(8,128)(2,1)S(1)}, bf16[1728,128]{1,0:T(8,128)(2,1)S(1)}, u32[]{:S(2)}, u32[]{:S(2)}) collective-permute-start(bf16[1728,128]{1,0:T(8,128)(2,1)S(1)} %add_convert_fusion.1), channel_id=1, source_target_pairs={{0,2},{1,3},{2,0},{3,1},{4,6},{5,7},{6,4},{7,5},{8,10},{9,11},{10,... | collective-permute-start | bytes 1327112 | tf_op jit(solution)/shard_map/ppermute | solution.py:193
  26.2 0.6 collective-permute-start.9
  26.8 0.2 collective-permute-done.3
  26.9 0.1 add_convert_fusion.6
  27.1 3.1 %collective-permute-start.6 = (bf16[648,128]{1,0:T(8,128)(2,1)S(1)}, bf16[648,128]{1,0:T(8,128)(2,1)S(1)}, u32[]{:S(2)}, u32[]{:S(2)}) collective-permute-start(bf16[648,128]{1,0:T(8,128)(2,1)S(1)} %get-tuple-element.56), channel_id=1, source_target_pairs={{0,8},{1,9},{2,10},{3,11},{4,12},{5,13},{6,14},{7,15},{8,0},{9,1},... | collective-permute-start | bytes 497672 | tf_op jit(solution)/shard_map/ppermute | solution.py:193
  30.2 0.1 convert_add_fusion.3
  30.2 1.0 %collective-permute-start.11 = (bf16[216,128]{1,0:T(8,128)(2,1)S(1)}, bf16[216,128]{1,0:T(8,128)(2,1)S(1)}, u32[]{:S(2)}, u32[]{:S(2)}) collective-permute-start(bf16[216,128]{1,0:T(8,128)(2,1)S(1)} %get-tuple-element.63), channel_id=1, source_target_pairs={{0,8},{1,9},{2,10},{3,11},{4,12},{5,13},{6,14},{7,15},{8,0},{9,1},... | collective-permute-start | bytes 165896 | tf_op jit(solution)/shard_map/ppermute | solution.py:193
  31.3 6.5 %collective-permute-done.10 = bf16[1728,128]{1,0:T(8,128)(2,1)S(1)} collective-permute-done((bf16[1728,128]{1,0:T(8,128)(2,1)S(1)}, bf16[1728,128]{1,0:T(8,128)(2,1)S(1)}, u32[]{:S(2)}, u32[]{:S(2)}) %collective-permute-start.10) | collective-permute-done | bytes 442400 | tf_op jit(solution)/shard_map/ppermute | solution.py:193
  37.7 0.1 add_convert_fusion.4
  37.8 0.1 collective-permute-start.12
  37.9 1.9 %collective-permute-start.14 = (bf16[576,128]{1,0:T(8,128)(2,1)S(1)}, bf16[576,128]{1,0:T(8,128)(2,1)S(1)}, u32[]{:S(2)}, u32[]{:S(2)}) collective-permute-start(bf16[576,128]{1,0:T(8,128)(2,1)S(1)} %add_convert_fusion.8), channel_id=1, source_target_pairs={{0,2},{1,3},{2,0},{3,1},{4,6},{5,7},{6,4},{7,5},{8,10},{9,11},{10,... | collective-permute-start | bytes 442376 | tf_op jit(solution)/shard_map/ppermute | solution.py:193
  39.8 3.8 %collective-permute-done.9 = bf16[1152,128]{1,0:T(8,128)(2,1)S(1)} collective-permute-done((bf16[1152,128]{1,0:T(8,128)(2,1)S(1)}, bf16[1152,128]{1,0:T(8,128)(2,1)S(1)}, u32[]{:S(2)}, u32[]{:S(2)}) %collective-permute-start.9) | collective-permute-done | bytes 294944 | tf_op jit(solution)/shard_map/ppermute | solution.py:193
  43.6 0.1 add_convert_fusion.7
  43.7 0.5 collective-permute-start.15
  44.2 0.0 collective-permute-done.6.refs_1_
  44.2 0.0 collective-permute-done.11.refs_3_
  44.2 0.4 collective-permute-done.12
  44.6 0.1 add_convert_fusion.9
  44.7 2.7 %collective-permute-start.13 = (bf16[432,128]{1,0:T(8,128)(2,1)S(1)}, bf16[432,128]{1,0:T(8,128)(2,1)S(1)}, u32[]{:S(2)}, u32[]{:S(2)}) collective-permute-start(bf16[432,128]{1,0:T(8,128)(2,1)S(1)} %get-tuple-element.58), channel_id=1, source_target_pairs={{0,8},{1,9},{2,10},{3,11},{4,12},{5,13},{6,14},{7,15},{8,0},{9,1},... | collective-permute-start | bytes 331784 | tf_op jit(solution)/shard_map/ppermute | solution.py:193
  47.4 0.0 collective-permute-done.14
  47.4 1.6 %collective-permute-start.17 = (bf16[288,128]{1,0:T(8,128)(2,1)S(1)}, bf16[288,128]{1,0:T(8,128)(2,1)S(1)}, u32[]{:S(2)}, u32[]{:S(2)}) collective-permute-start(bf16[288,128]{1,0:T(8,128)(2,1)S(1)} %add_convert_fusion.12), channel_id=1, source_target_pairs={{0,4},{1,5},{2,6},{3,7},{4,0},{5,1},{6,2},{7,3},{8,12},{9,13},{10,... | collective-permute-start | bytes 221192 | tf_op jit(solution)/shard_map/ppermute | solution.py:193
  49.1 3.2 %collective-permute-done.13.refs_1_ = bf16[432,128]{1,0:T(8,128)(2,1)S(1)} collective-permute-done((bf16[432,128]{1,0:T(8,128)(2,1)S(1)}, bf16[432,128]{1,0:T(8,128)(2,1)S(1)}, u32[]{:S(2)}, u32[]{:S(2)}) %collective-permute-start.13) | collective-permute-done | bytes 110624 | tf_op jit(solution)/shard_map/ppermute | solution.py:193
  52.3 0.0 collective-permute-done.15
  52.3 0.1 add_convert_fusion.11
  52.4 2.1 %collective-permute-start.16 = (bf16[288,128]{1,0:T(8,128)(2,1)S(1)}, bf16[288,128]{1,0:T(8,128)(2,1)S(1)}, u32[]{:S(2)}, u32[]{:S(2)}) collective-permute-start(bf16[288,128]{1,0:T(8,128)(2,1)S(1)} %get-tuple-element.60), channel_id=1, source_target_pairs={{0,8},{1,9},{2,10},{3,11},{4,12},{5,13},{6,14},{7,15},{8,0},{9,1},... | collective-permute-start | bytes 221192 | tf_op jit(solution)/shard_map/ppermute | solution.py:193
  54.5 1.1 %collective-permute-start.18 = (bf16[144,128]{1,0:T(8,128)(2,1)S(1)}, bf16[144,128]{1,0:T(8,128)(2,1)S(1)}, u32[]{:S(2)}, u32[]{:S(2)}) collective-permute-start(bf16[144,128]{1,0:T(8,128)(2,1)S(1)} %get-tuple-element.65), channel_id=1, source_target_pairs={{0,8},{1,9},{2,10},{3,11},{4,12},{5,13},{6,14},{7,15},{8,0},{9,1},... | collective-permute-start | bytes 110600 | tf_op jit(solution)/shard_map/ppermute | solution.py:193
  55.6 0.7 %shard_map.115 = bf16[1,69,1536]{2,1,0:T(8,128)(2,1)} custom-call(f32[648,128]{1,0:T(8,128)S(1)} %get-tuple-element.57.refs_0_, bf16[648,128]{1,0:T(8,128)(2,1)S(1)} %collective-permute-done.6.refs_1_, f32[216,128]{1,0:T(8,128)S(1)} %get-tuple-element.62.refs_2_, bf16[216,128]{1,0:T(8,128)(2,1)S(1)} %collective-permute-done.11.refs_3_), custom_call_target="tpu_custom_call" | custom-call | tf_op jit(solution)/shard_map/pallas_call | solution.py:253
  56.3 1.3 %collective-permute-done.16.refs_3_ = bf16[288,128]{1,0:T(8,128)(2,1)S(1)} collective-permute-done((bf16[288,128]{1,0:T(8,128)(2,1)S(1)}, bf16[288,128]{1,0:T(8,128)(2,1)S(1)}, u32[]{:S(2)}, u32[]{:S(2)}) %collective-permute-start.16) | collective-permute-done | bytes 73760 | tf_op jit(solution)/shard_map/ppermute | solution.py:193
  57.7 2.3 %collective-permute-done.18.refs_5_ = bf16[144,128]{1,0:T(8,128)(2,1)S(1)} collective-permute-done((bf16[144,128]{1,0:T(8,128)(2,1)S(1)}, bf16[144,128]{1,0:T(8,128)(2,1)S(1)}, u32[]{:S(2)}, u32[]{:S(2)}) %collective-permute-start.18) | collective-permute-done | bytes 36896 | tf_op jit(solution)/shard_map/ppermute | solution.py:193
  59.9 0.7 %shard_map.116 = bf16[1,69,1536]{2,1,0:T(8,128)(2,1)} custom-call(f32[432,128]{1,0:T(8,128)S(1)} %get-tuple-element.59.refs_0_, bf16[432,128]{1,0:T(8,128)(2,1)S(1)} %collective-permute-done.13.refs_1_, f32[288,128]{1,0:T(8,128)S(1)} %get-tuple-element.61.refs_2_, bf16[288,128]{1,0:T(8,128)(2,1)S(1)} %collective-permute-done.16.refs_3_, ...), custom_call_target="tpu_custom_call" | custom-call | tf_op jit(solution)/shard_map/pallas_call | solution.py:253
  (9 shorter events, 0.2 us)
Async XLA Ops:
  5.3 2.6 %collective-permute-start.1 = (bf16[3456,128]{1,0:T(8,128)(2,1)S(1)}, bf16[3456,128]{1,0:T(8,128)(2,1)S(1)}, u32[]{:S(2)}, u32[]{:S(2)}) collective-permute-start(bf16[3456,128]{1,0:T(8,128)(2,1)S(1)} %get-tuple-element.31), channel_id=1, source_target_pairs={{0,1},{1,0},{2,3},{3,2},{4,5},{5,4},{6,7},{7,6},{8,9},{9,8},{10,11... | collective-permute-start | bytes 2654216 | tf_op jit(solution)/shard_map/ppermute | solution.py:193
  5.8 5.2 %collective-permute-start = (bf16[3456,128]{1,0:T(8,128)(2,1)S(1)}, bf16[3456,128]{1,0:T(8,128)(2,1)S(1)}, u32[]{:S(2)}, u32[]{:S(2)}) collective-permute-start(bf16[3456,128]{1,0:T(8,128)(2,1)S(1)} %get-tuple-element.30), channel_id=1, source_target_pairs={{0,1},{1,0},{2,3},{3,2},{4,5},{5,4},{6,7},{7,6},{8,9},{9,8},{10,11... | collective-permute-start | bytes 2654216 | tf_op jit(solution)/shard_map/ppermute | solution.py:193
  8.0 11.6 %collective-permute-start.2 = (bf16[2592,128]{1,0:T(8,128)(2,1)S(1)}, bf16[2592,128]{1,0:T(8,128)(2,1)S(1)}, u32[]{:S(2)}, u32[]{:S(2)}) collective-permute-start(bf16[2592,128]{1,0:T(8,128)(2,1)S(1)} %add_convert_fusion), channel_id=1, source_target_pairs={{0,2},{1,5},{2,0},{3,7},{4,6},{5,1},{6,4},{7,3},{8,10},{9,13},{10,... | collective-permute-start | bytes 1990664 | tf_op jit(solution)/shard_map/ppermute | solution.py:193
  15.6 8.8 %collective-permute-start.4 = (bf16[3456,128]{1,0:T(8,128)(2,1)S(1)}, bf16[3456,128]{1,0:T(8,128)(2,1)S(1)}, u32[]{:S(2)}, u32[]{:S(2)}) collective-permute-start(bf16[3456,128]{1,0:T(8,128)(2,1)S(1)} %get-tuple-element.36), channel_id=1, source_target_pairs={{0,1},{1,0},{2,3},{3,2},{4,5},{5,4},{6,7},{7,6},{8,9},{9,8},{10,11... | collective-permute-start | bytes 2654216 | tf_op jit(solution)/shard_map/ppermute | solution.py:193
  15.7 6.2 %collective-permute-start.5 = (bf16[864,128]{1,0:T(8,128)(2,1)S(1)}, bf16[864,128]{1,0:T(8,128)(2,1)S(1)}, u32[]{:S(2)}, u32[]{:S(2)}) collective-permute-start(bf16[864,128]{1,0:T(8,128)(2,1)S(1)} %add_convert_fusion.5), channel_id=1, source_target_pairs={{0,2},{1,5},{2,0},{3,7},{4,6},{5,1},{6,4},{7,3},{8,10},{9,13},{10,... | collective-permute-start | bytes 663560 | tf_op jit(solution)/shard_map/ppermute | solution.py:193
  17.1 14.1 %collective-permute-start.7 = (bf16[3456,128]{1,0:T(8,128)(2,1)S(1)}, bf16[3456,128]{1,0:T(8,128)(2,1)S(1)}, u32[]{:S(2)}, u32[]{:S(2)}) collective-permute-start(bf16[3456,128]{1,0:T(8,128)(2,1)S(1)} %get-tuple-element.35), channel_id=1, source_target_pairs={{0,1},{1,0},{2,3},{3,2},{4,5},{5,4},{6,7},{7,6},{8,9},{9,8},{10,11... | collective-permute-start | bytes 2654216 | tf_op jit(solution)/shard_map/ppermute | solution.py:193
  19.7 7.3 %collective-permute-start.3 = (bf16[1296,128]{1,0:T(8,128)(2,1)S(1)}, bf16[1296,128]{1,0:T(8,128)(2,1)S(1)}, u32[]{:S(2)}, u32[]{:S(2)}) collective-permute-start(bf16[1296,128]{1,0:T(8,128)(2,1)S(1)} %add_convert_fusion.2), channel_id=1, source_target_pairs={{0,4},{1,3},{2,6},{3,1},{4,0},{5,7},{6,2},{7,5},{8,12},{9,11},{10,... | collective-permute-start | bytes 995336 | tf_op jit(solution)/shard_map/ppermute | solution.py:193
  22.0 8.2 %collective-permute-start.8 = (bf16[432,128]{1,0:T(8,128)(2,1)S(1)}, bf16[432,128]{1,0:T(8,128)(2,1)S(1)}, u32[]{:S(2)}, u32[]{:S(2)}) collective-permute-start(bf16[432,128]{1,0:T(8,128)(2,1)S(1)} %add_convert_fusion.10), channel_id=1, source_target_pairs={{0,4},{1,3},{2,6},{3,1},{4,0},{5,7},{6,2},{7,5},{8,12},{9,11},{10,... | collective-permute-start | bytes 331784 | tf_op jit(solution)/shard_map/ppermute | solution.py:193
  24.6 13.2 %collective-permute-start.10 = (bf16[1728,128]{1,0:T(8,128)(2,1)S(1)}, bf16[1728,128]{1,0:T(8,128)(2,1)S(1)}, u32[]{:S(2)}, u32[]{:S(2)}) collective-permute-start(bf16[1728,128]{1,0:T(8,128)(2,1)S(1)} %add_convert_fusion.1), channel_id=1, source_target_pairs={{0,2},{1,3},{2,0},{3,1},{4,6},{5,7},{6,4},{7,5},{8,10},{9,11},{10,... | collective-permute-start | bytes 1327112 | tf_op jit(solution)/shard_map/ppermute | solution.py:193
  26.2 17.5 %collective-permute-start.9 = (bf16[1152,128]{1,0:T(8,128)(2,1)S(1)}, bf16[1152,128]{1,0:T(8,128)(2,1)S(1)}, u32[]{:S(2)}, u32[]{:S(2)}) collective-permute-start(bf16[1152,128]{1,0:T(8,128)(2,1)S(1)} %add_convert_fusion.3), channel_id=1, source_target_pairs={{0,2},{1,3},{2,0},{3,1},{4,6},{5,7},{6,4},{7,5},{8,10},{9,11},{10,... | collective-permute-start | bytes 884744 | tf_op jit(solution)/shard_map/ppermute | solution.py:193
  27.1 17.1 %collective-permute-start.6 = (bf16[648,128]{1,0:T(8,128)(2,1)S(1)}, bf16[648,128]{1,0:T(8,128)(2,1)S(1)}, u32[]{:S(2)}, u32[]{:S(2)}) collective-permute-start(bf16[648,128]{1,0:T(8,128)(2,1)S(1)} %get-tuple-element.56), channel_id=1, source_target_pairs={{0,8},{1,9},{2,10},{3,11},{4,12},{5,13},{6,14},{7,15},{8,0},{9,1},... | collective-permute-start | bytes 497672 | tf_op jit(solution)/shard_map/ppermute | solution.py:193
  30.2 14.0 %collective-permute-start.11 = (bf16[216,128]{1,0:T(8,128)(2,1)S(1)}, bf16[216,128]{1,0:T(8,128)(2,1)S(1)}, u32[]{:S(2)}, u32[]{:S(2)}) collective-permute-start(bf16[216,128]{1,0:T(8,128)(2,1)S(1)} %get-tuple-element.63), channel_id=1, source_target_pairs={{0,8},{1,9},{2,10},{3,11},{4,12},{5,13},{6,14},{7,15},{8,0},{9,1},... | collective-permute-start | bytes 165896 | tf_op jit(solution)/shard_map/ppermute | solution.py:193
  37.8 6.8 %collective-permute-start.12 = (bf16[864,128]{1,0:T(8,128)(2,1)S(1)}, bf16[864,128]{1,0:T(8,128)(2,1)S(1)}, u32[]{:S(2)}, u32[]{:S(2)}) collective-permute-start(bf16[864,128]{1,0:T(8,128)(2,1)S(1)} %add_convert_fusion.4), channel_id=1, source_target_pairs={{0,4},{1,5},{2,6},{3,7},{4,0},{5,1},{6,2},{7,3},{8,12},{9,13},{10,... | collective-permute-start | bytes 663560 | tf_op jit(solution)/shard_map/ppermute | solution.py:193
  37.9 9.5 %collective-permute-start.14 = (bf16[576,128]{1,0:T(8,128)(2,1)S(1)}, bf16[576,128]{1,0:T(8,128)(2,1)S(1)}, u32[]{:S(2)}, u32[]{:S(2)}) collective-permute-start(bf16[576,128]{1,0:T(8,128)(2,1)S(1)} %add_convert_fusion.8), channel_id=1, source_target_pairs={{0,2},{1,3},{2,0},{3,1},{4,6},{5,7},{6,4},{7,5},{8,10},{9,11},{10,... | collective-permute-start | bytes 442376 | tf_op jit(solution)/shard_map/ppermute | solution.py:193
  43.7 8.6 %collective-permute-start.15 = (bf16[576,128]{1,0:T(8,128)(2,1)S(1)}, bf16[576,128]{1,0:T(8,128)(2,1)S(1)}, u32[]{:S(2)}, u32[]{:S(2)}) collective-permute-start(bf16[576,128]{1,0:T(8,128)(2,1)S(1)} %add_convert_fusion.7), channel_id=1, source_target_pairs={{0,4},{1,5},{2,6},{3,7},{4,0},{5,1},{6,2},{7,3},{8,12},{9,13},{10,... | collective-permute-start | bytes 442376 | tf_op jit(solution)/shard_map/ppermute | solution.py:193
  44.7 7.6 %collective-permute-start.13 = (bf16[432,128]{1,0:T(8,128)(2,1)S(1)}, bf16[432,128]{1,0:T(8,128)(2,1)S(1)}, u32[]{:S(2)}, u32[]{:S(2)}) collective-permute-start(bf16[432,128]{1,0:T(8,128)(2,1)S(1)} %get-tuple-element.58), channel_id=1, source_target_pairs={{0,8},{1,9},{2,10},{3,11},{4,12},{5,13},{6,14},{7,15},{8,0},{9,1},... | collective-permute-start | bytes 331784 | tf_op jit(solution)/shard_map/ppermute | solution.py:193
  47.4 7.0 %collective-permute-start.17 = (bf16[288,128]{1,0:T(8,128)(2,1)S(1)}, bf16[288,128]{1,0:T(8,128)(2,1)S(1)}, u32[]{:S(2)}, u32[]{:S(2)}) collective-permute-start(bf16[288,128]{1,0:T(8,128)(2,1)S(1)} %add_convert_fusion.12), channel_id=1, source_target_pairs={{0,4},{1,5},{2,6},{3,7},{4,0},{5,1},{6,2},{7,3},{8,12},{9,13},{10,... | collective-permute-start | bytes 221192 | tf_op jit(solution)/shard_map/ppermute | solution.py:193
  52.4 5.3 %collective-permute-start.16 = (bf16[288,128]{1,0:T(8,128)(2,1)S(1)}, bf16[288,128]{1,0:T(8,128)(2,1)S(1)}, u32[]{:S(2)}, u32[]{:S(2)}) collective-permute-start(bf16[288,128]{1,0:T(8,128)(2,1)S(1)} %get-tuple-element.60), channel_id=1, source_target_pairs={{0,8},{1,9},{2,10},{3,11},{4,12},{5,13},{6,14},{7,15},{8,0},{9,1},... | collective-permute-start | bytes 221192 | tf_op jit(solution)/shard_map/ppermute | solution.py:193
  54.5 5.4 %collective-permute-start.18 = (bf16[144,128]{1,0:T(8,128)(2,1)S(1)}, bf16[144,128]{1,0:T(8,128)(2,1)S(1)}, u32[]{:S(2)}, u32[]{:S(2)}) collective-permute-start(bf16[144,128]{1,0:T(8,128)(2,1)S(1)} %get-tuple-element.65), channel_id=1, source_target_pairs={{0,8},{1,9},{2,10},{3,11},{4,12},{5,13},{6,14},{7,15},{8,0},{9,1},... | collective-permute-start | bytes 110600 | tf_op jit(solution)/shard_map/ppermute | solution.py:193

commit v13 on v12

--- a/solution.py
+++ b/solution.py
@@ -339,9 +339,9 @@
     step(b)
     step(c)
     step(e)
-    step(c)
     step(d)
     step(e)
+    step(c)
     step(d)
     step(e)
     return [final_sum(line, remap[-1], pitch) for line, remap in zip((ones, twos), remaps)]

time: 60.8 us -> 59.9 us (0.985)
  waiting for transfers between devices: 21.8 us -> 19.1 us
  starting transfers between devices: 26.3 us -> 28 us
    ppermute x19, waiting for transfers between devices: 21.8 us -> 19.1 us  [exchange(): return lax.ppermute(value, 'curve', pairs)]
    ppermute x19, starting transfers between devices: 26.3 us -> 28 us  [exchange(): return lax.ppermute(value, 'curve', pairs)]
  transfers between devices with their start and end apart: 19 -> 19, of which waited for: 10 -> 11; matrix products, arithmetic and copies ran while one was open for 2% -> 2% of each run, Pallas kernels for 9% -> 9%
where the time goes in v13:
time: 59.9 us; the launch traced here: 59.7 us
  starting transfers between devices  28 us (47%)
  waiting for transfers between devices  19.1 us (32%)
  Pallas kernels  10.7 us (18%)
  other arithmetic  1.09 us (2%)
  between operations  0.74 us (1%)
    ppermute x19, starting transfers between devices, exchange(): return lax.ppermute(value, 'curve', pairs)  28 us
    ppermute x19, waiting for transfers between devices, exchange(): return lax.ppermute(value, 'curve', pairs)  19.1 us
    pallas_call x2, Pallas kernels, products(): pl.pallas_call(functools.partial(product_kernel, channels, pitch, chunks,...  9.26 us
    pallas_call x2, Pallas kernels, final_sum(): pl.pallas_call(functools.partial(final_kernel, like_shape[1], pitch, part...  1.48 us
  transfers between devices with their start and end apart: 19, of which 11 were waited for; matrix products, arithmetic and copies ran while one was open for 2% of the time, Pallas kernels for 9%

profile of v13, /device:TPU:0, one launch (start us, length us, event | category | flops | bytes accessed | tf_op | source)
XLA Modules:
  0.0 59.7 jit_solution(8563974062326307699)
XLA Ops:
  0.6 4.6 %shard_map.113 = (f32[13824,128]{1,0:T(8,128)S(1)}, bf16[3456,128]{1,0:T(8,128)(2,1)S(1)}, bf16[3456,128]{1,0:T(8,128)(2,1)S(1)}) custom-call(s32[144]{0:T(256)} %source_hbm.2, s32[144]{0:T(256)} %target_hbm.2, s32[1,16]{1,0:T(1,128)} %counts_hbm.2, bf16[1,69,1536]{2,1,0:T(8,128)(2,1)} %x_hbm.1, bf16[144,128,128]{2,1,0:T(8,128)(2,1)} %w_hbm.2), custom_call_target="tpu_custom_call" | custom-call | flops 325582848 | bytes 13565952 | tf_op jit(solution)/shard_map/pallas_call | solution.py:163
  5.2 0.5 collective-permute-start.1
  5.8 0.1 collective-permute-start
  5.8 2.0 %collective-permute-done.1 = bf16[3456,128]{1,0:T(8,128)(2,1)S(1)} collective-permute-done((bf16[3456,128]{1,0:T(8,128)(2,1)S(1)}, bf16[3456,128]{1,0:T(8,128)(2,1)S(1)}, u32[]{:S(2)}, u32[]{:S(2)}) %collective-permute-start.1) | collective-permute-done | bytes 884768 | tf_op jit(solution)/shard_map/ppermute | solution.py:193
  7.8 0.1 add_convert_fusion
  8.0 3.0 %collective-permute-start.2 = (bf16[2592,128]{1,0:T(8,128)(2,1)S(1)}, bf16[2592,128]{1,0:T(8,128)(2,1)S(1)}, u32[]{:S(2)}, u32[]{:S(2)}) collective-permute-start(bf16[2592,128]{1,0:T(8,128)(2,1)S(1)} %add_convert_fusion), channel_id=1, source_target_pairs={{0,2},{1,5},{2,0},{3,7},{4,6},{5,1},{6,4},{7,3},{8,10},{9,13},{10,... | collective-permute-start | bytes 1990664 | tf_op jit(solution)/shard_map/ppermute | solution.py:193
  11.0 4.7 %shard_map.114 = (f32[13824,128]{1,0:T(8,128)S(1)}, bf16[3456,128]{1,0:T(8,128)(2,1)S(1)}, bf16[3456,128]{1,0:T(8,128)(2,1)S(1)}) custom-call(s32[144]{0:T(256)} %source_hbm.3, s32[144]{0:T(256)} %target_hbm.3, s32[1,16]{1,0:T(1,128)} %counts_hbm.3, bf16[1,69,1536]{2,1,0:T(8,128)(2,1)} %x_hbm.2, bf16[144,128,128]{2,1,0:T(8,128)(2,1)} %w_hbm.3), custom_call_target="tpu_custom_call" | custom-call | flops 325582848 | bytes 13565952 | tf_op jit(solution)/shard_map/pallas_call | solution.py:163
  15.7 0.1 collective-permute-start.4
  15.7 1.4 %collective-permute-start.5 = (bf16[864,128]{1,0:T(8,128)(2,1)S(1)}, bf16[864,128]{1,0:T(8,128)(2,1)S(1)}, u32[]{:S(2)}, u32[]{:S(2)}) collective-permute-start(bf16[864,128]{1,0:T(8,128)(2,1)S(1)} %add_convert_fusion.5), channel_id=1, source_target_pairs={{0,2},{1,5},{2,0},{3,7},{4,6},{5,1},{6,4},{7,3},{8,10},{9,13},{10,... | collective-permute-start | bytes 663560 | tf_op jit(solution)/shard_map/ppermute | solution.py:193
  17.1 0.4 collective-permute-start.7
  17.5 2.1 %collective-permute-done.2 = bf16[2592,128]{1,0:T(8,128)(2,1)S(1)} collective-permute-done((bf16[2592,128]{1,0:T(8,128)(2,1)S(1)}, bf16[2592,128]{1,0:T(8,128)(2,1)S(1)}, u32[]{:S(2)}, u32[]{:S(2)}) %collective-permute-start.2) | collective-permute-done | bytes 663584 | tf_op jit(solution)/shard_map/ppermute | solution.py:193
  19.6 0.1 add_convert_fusion.2
  19.7 2.2 %collective-permute-start.3 = (bf16[1296,128]{1,0:T(8,128)(2,1)S(1)}, bf16[1296,128]{1,0:T(8,128)(2,1)S(1)}, u32[]{:S(2)}, u32[]{:S(2)}) collective-permute-start(bf16[1296,128]{1,0:T(8,128)(2,1)S(1)} %add_convert_fusion.2), channel_id=1, source_target_pairs={{0,4},{1,3},{2,6},{3,1},{4,0},{5,7},{6,2},{7,5},{8,12},{9,11},{10,... | collective-permute-start | bytes 995336 | tf_op jit(solution)/shard_map/ppermute | solution.py:193
  21.9 0.1 collective-permute-done.5
  22.0 0.1 add_convert_fusion.10
  22.0 2.4 %collective-permute-start.8 = (bf16[432,128]{1,0:T(8,128)(2,1)S(1)}, bf16[432,128]{1,0:T(8,128)(2,1)S(1)}, u32[]{:S(2)}, u32[]{:S(2)}) collective-permute-start(bf16[432,128]{1,0:T(8,128)(2,1)S(1)} %add_convert_fusion.10), channel_id=1, source_target_pairs={{0,4},{1,3},{2,6},{3,1},{4,0},{5,7},{6,2},{7,5},{8,12},{9,11},{10,... | collective-permute-start | bytes 331784 | tf_op jit(solution)/shard_map/ppermute | solution.py:193
  24.4 0.0 collective-permute-done.4
  24.4 0.1 add_convert_fusion.3
  24.5 0.1 add_convert_fusion.1
  24.6 1.6 %collective-permute-start.10 = (bf16[1728,128]{1,0:T(8,128)(2,1)S(1)}, bf16[1728,128]{1,0:T(8,128)(2,1)S(1)}, u32[]{:S(2)}, u32[]{:S(2)}) collective-permute-start(bf16[1728,128]{1,0:T(8,128)(2,1)S(1)} %add_convert_fusion.1), channel_id=1, source_target_pairs={{0,2},{1,3},{2,0},{3,1},{4,6},{5,7},{6,4},{7,5},{8,10},{9,11},{10,... | collective-permute-start | bytes 1327112 | tf_op jit(solution)/shard_map/ppermute | solution.py:193
  26.2 0.6 collective-permute-start.9
  26.8 0.2 collective-permute-done.3
  27.0 0.1 add_convert_fusion.6
  27.1 3.1 %collective-permute-start.6 = (bf16[648,128]{1,0:T(8,128)(2,1)S(1)}, bf16[648,128]{1,0:T(8,128)(2,1)S(1)}, u32[]{:S(2)}, u32[]{:S(2)}) collective-permute-start(bf16[648,128]{1,0:T(8,128)(2,1)S(1)} %get-tuple-element.56), channel_id=1, source_target_pairs={{0,8},{1,9},{2,10},{3,11},{4,12},{5,13},{6,14},{7,15},{8,0},{9,1},... | collective-permute-start | bytes 497672 | tf_op jit(solution)/shard_map/ppermute | solution.py:193
  30.2 0.0 collective-permute-done.8
  30.2 0.1 convert_add_fusion.3
  30.2 1.0 %collective-permute-start.11 = (bf16[216,128]{1,0:T(8,128)(2,1)S(1)}, bf16[216,128]{1,0:T(8,128)(2,1)S(1)}, u32[]{:S(2)}, u32[]{:S(2)}) collective-permute-start(bf16[216,128]{1,0:T(8,128)(2,1)S(1)} %get-tuple-element.63), channel_id=1, source_target_pairs={{0,8},{1,9},{2,10},{3,11},{4,12},{5,13},{6,14},{7,15},{8,0},{9,1},... | collective-permute-start | bytes 165896 | tf_op jit(solution)/shard_map/ppermute | solution.py:193
  31.3 0.0 collective-permute-done.7
  31.3 6.5 %collective-permute-done.10 = bf16[1728,128]{1,0:T(8,128)(2,1)S(1)} collective-permute-done((bf16[1728,128]{1,0:T(8,128)(2,1)S(1)}, bf16[1728,128]{1,0:T(8,128)(2,1)S(1)}, u32[]{:S(2)}, u32[]{:S(2)}) %collective-permute-start.10) | collective-permute-done | bytes 442400 | tf_op jit(solution)/shard_map/ppermute | solution.py:193
  37.8 0.1 add_convert_fusion.4
  37.8 0.1 collective-permute-start.12
  37.9 1.9 %collective-permute-start.14 = (bf16[576,128]{1,0:T(8,128)(2,1)S(1)}, bf16[576,128]{1,0:T(8,128)(2,1)S(1)}, u32[]{:S(2)}, u32[]{:S(2)}) collective-permute-start(bf16[576,128]{1,0:T(8,128)(2,1)S(1)} %add_convert_fusion.8), channel_id=1, source_target_pairs={{0,2},{1,3},{2,0},{3,1},{4,6},{5,7},{6,4},{7,5},{8,10},{9,11},{10,... | collective-permute-start | bytes 442376 | tf_op jit(solution)/shard_map/ppermute | solution.py:193
  39.9 3.8 %collective-permute-done.9 = bf16[1152,128]{1,0:T(8,128)(2,1)S(1)} collective-permute-done((bf16[1152,128]{1,0:T(8,128)(2,1)S(1)}, bf16[1152,128]{1,0:T(8,128)(2,1)S(1)}, u32[]{:S(2)}, u32[]{:S(2)}) %collective-permute-start.9) | collective-permute-done | bytes 294944 | tf_op jit(solution)/shard_map/ppermute | solution.py:193
  43.7 0.1 add_convert_fusion.7
  43.7 0.5 collective-permute-start.16
  44.2 0.4 collective-permute-done.12
  44.6 0.1 add_convert_fusion.9
  44.7 2.7 %collective-permute-start.13 = (bf16[432,128]{1,0:T(8,128)(2,1)S(1)}, bf16[432,128]{1,0:T(8,128)(2,1)S(1)}, u32[]{:S(2)}, u32[]{:S(2)}) collective-permute-start(bf16[432,128]{1,0:T(8,128)(2,1)S(1)} %get-tuple-element.58), channel_id=1, source_target_pairs={{0,8},{1,9},{2,10},{3,11},{4,12},{5,13},{6,14},{7,15},{8,0},{9,1},... | collective-permute-start | bytes 331784 | tf_op jit(solution)/shard_map/ppermute | solution.py:193
  47.4 1.7 %collective-permute-start.15 = (bf16[288,128]{1,0:T(8,128)(2,1)S(1)}, bf16[288,128]{1,0:T(8,128)(2,1)S(1)}, u32[]{:S(2)}, u32[]{:S(2)}) collective-permute-start(bf16[288,128]{1,0:T(8,128)(2,1)S(1)} %add_convert_fusion.12), channel_id=1, source_target_pairs={{0,4},{1,5},{2,6},{3,7},{4,0},{5,1},{6,2},{7,3},{8,12},{9,13},{10,... | collective-permute-start | bytes 221192 | tf_op jit(solution)/shard_map/ppermute | solution.py:193
  49.1 1.8 %collective-permute-done.16 = bf16[576,128]{1,0:T(8,128)(2,1)S(1)} collective-permute-done((bf16[576,128]{1,0:T(8,128)(2,1)S(1)}, bf16[576,128]{1,0:T(8,128)(2,1)S(1)}, u32[]{:S(2)}, u32[]{:S(2)}) %collective-permute-start.16) | collective-permute-done | bytes 147488 | tf_op jit(solution)/shard_map/ppermute | solution.py:193
  50.9 0.1 convert_add_fusion.2
  50.9 2.7 %collective-permute-start.17 = (bf16[288,128]{1,0:T(8,128)(2,1)S(1)}, bf16[288,128]{1,0:T(8,128)(2,1)S(1)}, u32[]{:S(2)}, u32[]{:S(2)}) collective-permute-start(bf16[288,128]{1,0:T(8,128)(2,1)S(1)} %get-tuple-element.61), channel_id=1, source_target_pairs={{0,8},{1,9},{2,10},{3,11},{4,12},{5,13},{6,14},{7,15},{8,0},{9,1},... | collective-permute-start | bytes 221192 | tf_op jit(solution)/shard_map/ppermute | solution.py:193
  53.6 0.4 collective-permute-done.15
  54.1 2.2 %collective-permute-start.18 = (bf16[144,128]{1,0:T(8,128)(2,1)S(1)}, bf16[144,128]{1,0:T(8,128)(2,1)S(1)}, u32[]{:S(2)}, u32[]{:S(2)}) collective-permute-start(bf16[144,128]{1,0:T(8,128)(2,1)S(1)} %get-tuple-element.65), channel_id=1, source_target_pairs={{0,8},{1,9},{2,10},{3,11},{4,12},{5,13},{6,14},{7,15},{8,0},{9,1},... | collective-permute-start | bytes 110600 | tf_op jit(solution)/shard_map/ppermute | solution.py:193
  56.3 0.7 %shard_map.115 = bf16[1,69,1536]{2,1,0:T(8,128)(2,1)} custom-call(f32[648,128]{1,0:T(8,128)S(1)} %get-tuple-element.57.refs_0_, bf16[648,128]{1,0:T(8,128)(2,1)S(1)} %collective-permute-done.6.refs_1_, f32[216,128]{1,0:T(8,128)S(1)} %get-tuple-element.62.refs_2_, bf16[216,128]{1,0:T(8,128)(2,1)S(1)} %collective-permute-done.11.refs_3_), custom_call_target="tpu_custom_call" | custom-call | tf_op jit(solution)/shard_map/pallas_call | solution.py:253
  57.0 0.3 collective-permute-done.17.refs_3_
  57.3 1.7 %collective-permute-done.18.refs_5_ = bf16[144,128]{1,0:T(8,128)(2,1)S(1)} collective-permute-done((bf16[144,128]{1,0:T(8,128)(2,1)S(1)}, bf16[144,128]{1,0:T(8,128)(2,1)S(1)}, u32[]{:S(2)}, u32[]{:S(2)}) %collective-permute-start.18) | collective-permute-done | bytes 36896 | tf_op jit(solution)/shard_map/ppermute | solution.py:193
  59.0 0.7 %shard_map.116 = bf16[1,69,1536]{2,1,0:T(8,128)(2,1)} custom-call(f32[432,128]{1,0:T(8,128)S(1)} %get-tuple-element.59.refs_0_, bf16[432,128]{1,0:T(8,128)(2,1)S(1)} %collective-permute-done.13.refs_1_, f32[288,128]{1,0:T(8,128)S(1)} %get-tuple-element.60.refs_2_, bf16[288,128]{1,0:T(8,128)(2,1)S(1)} %collective-permute-done.17.refs_3_, ...), custom_call_target="tpu_custom_call" | custom-call | tf_op jit(solution)/shard_map/pallas_call | solution.py:253
  (9 shorter events, 0.2 us)
Async XLA Ops:
  5.2 2.6 %collective-permute-start.1 = (bf16[3456,128]{1,0:T(8,128)(2,1)S(1)}, bf16[3456,128]{1,0:T(8,128)(2,1)S(1)}, u32[]{:S(2)}, u32[]{:S(2)}) collective-permute-start(bf16[3456,128]{1,0:T(8,128)(2,1)S(1)} %get-tuple-element.31), channel_id=1, source_target_pairs={{0,1},{1,0},{2,3},{3,2},{4,5},{5,4},{6,7},{7,6},{8,9},{9,8},{10,11... | collective-permute-start | bytes 2654216 | tf_op jit(solution)/shard_map/ppermute | solution.py:193
  5.8 5.2 %collective-permute-start = (bf16[3456,128]{1,0:T(8,128)(2,1)S(1)}, bf16[3456,128]{1,0:T(8,128)(2,1)S(1)}, u32[]{:S(2)}, u32[]{:S(2)}) collective-permute-start(bf16[3456,128]{1,0:T(8,128)(2,1)S(1)} %get-tuple-element.30), channel_id=1, source_target_pairs={{0,1},{1,0},{2,3},{3,2},{4,5},{5,4},{6,7},{7,6},{8,9},{9,8},{10,11... | collective-permute-start | bytes 2654216 | tf_op jit(solution)/shard_map/ppermute | solution.py:193
  8.0 11.6 %collective-permute-start.2 = (bf16[2592,128]{1,0:T(8,128)(2,1)S(1)}, bf16[2592,128]{1,0:T(8,128)(2,1)S(1)}, u32[]{:S(2)}, u32[]{:S(2)}) collective-permute-start(bf16[2592,128]{1,0:T(8,128)(2,1)S(1)} %add_convert_fusion), channel_id=1, source_target_pairs={{0,2},{1,5},{2,0},{3,7},{4,6},{5,1},{6,4},{7,3},{8,10},{9,13},{10,... | collective-permute-start | bytes 1990664 | tf_op jit(solution)/shard_map/ppermute | solution.py:193
  15.7 8.8 %collective-permute-start.4 = (bf16[3456,128]{1,0:T(8,128)(2,1)S(1)}, bf16[3456,128]{1,0:T(8,128)(2,1)S(1)}, u32[]{:S(2)}, u32[]{:S(2)}) collective-permute-start(bf16[3456,128]{1,0:T(8,128)(2,1)S(1)} %get-tuple-element.36), channel_id=1, source_target_pairs={{0,1},{1,0},{2,3},{3,2},{4,5},{5,4},{6,7},{7,6},{8,9},{9,8},{10,11... | collective-permute-start | bytes 2654216 | tf_op jit(solution)/shard_map/ppermute | solution.py:193
  15.7 6.2 %collective-permute-start.5 = (bf16[864,128]{1,0:T(8,128)(2,1)S(1)}, bf16[864,128]{1,0:T(8,128)(2,1)S(1)}, u32[]{:S(2)}, u32[]{:S(2)}) collective-permute-start(bf16[864,128]{1,0:T(8,128)(2,1)S(1)} %add_convert_fusion.5), channel_id=1, source_target_pairs={{0,2},{1,5},{2,0},{3,7},{4,6},{5,1},{6,4},{7,3},{8,10},{9,13},{10,... | collective-permute-start | bytes 663560 | tf_op jit(solution)/shard_map/ppermute | solution.py:193
  17.1 14.1 %collective-permute-start.7 = (bf16[3456,128]{1,0:T(8,128)(2,1)S(1)}, bf16[3456,128]{1,0:T(8,128)(2,1)S(1)}, u32[]{:S(2)}, u32[]{:S(2)}) collective-permute-start(bf16[3456,128]{1,0:T(8,128)(2,1)S(1)} %get-tuple-element.35), channel_id=1, source_target_pairs={{0,1},{1,0},{2,3},{3,2},{4,5},{5,4},{6,7},{7,6},{8,9},{9,8},{10,11... | collective-permute-start | bytes 2654216 | tf_op jit(solution)/shard_map/ppermute | solution.py:193
  19.7 7.3 %collective-permute-start.3 = (bf16[1296,128]{1,0:T(8,128)(2,1)S(1)}, bf16[1296,128]{1,0:T(8,128)(2,1)S(1)}, u32[]{:S(2)}, u32[]{:S(2)}) collective-permute-start(bf16[1296,128]{1,0:T(8,128)(2,1)S(1)} %add_convert_fusion.2), channel_id=1, source_target_pairs={{0,4},{1,3},{2,6},{3,1},{4,0},{5,7},{6,2},{7,5},{8,12},{9,11},{10,... | collective-permute-start | bytes 995336 | tf_op jit(solution)/shard_map/ppermute | solution.py:193
  22.0 8.2 %collective-permute-start.8 = (bf16[432,128]{1,0:T(8,128)(2,1)S(1)}, bf16[432,128]{1,0:T(8,128)(2,1)S(1)}, u32[]{:S(2)}, u32[]{:S(2)}) collective-permute-start(bf16[432,128]{1,0:T(8,128)(2,1)S(1)} %add_convert_fusion.10), channel_id=1, source_target_pairs={{0,4},{1,3},{2,6},{3,1},{4,0},{5,7},{6,2},{7,5},{8,12},{9,11},{10,... | collective-permute-start | bytes 331784 | tf_op jit(solution)/shard_map/ppermute | solution.py:193
  24.6 13.2 %collective-permute-start.10 = (bf16[1728,128]{1,0:T(8,128)(2,1)S(1)}, bf16[1728,128]{1,0:T(8,128)(2,1)S(1)}, u32[]{:S(2)}, u32[]{:S(2)}) collective-permute-start(bf16[1728,128]{1,0:T(8,128)(2,1)S(1)} %add_convert_fusion.1), channel_id=1, source_target_pairs={{0,2},{1,3},{2,0},{3,1},{4,6},{5,7},{6,4},{7,5},{8,10},{9,11},{10,... | collective-permute-start | bytes 1327112 | tf_op jit(solution)/shard_map/ppermute | solution.py:193
  26.2 17.5 %collective-permute-start.9 = (bf16[1152,128]{1,0:T(8,128)(2,1)S(1)}, bf16[1152,128]{1,0:T(8,128)(2,1)S(1)}, u32[]{:S(2)}, u32[]{:S(2)}) collective-permute-start(bf16[1152,128]{1,0:T(8,128)(2,1)S(1)} %add_convert_fusion.3), channel_id=1, source_target_pairs={{0,2},{1,3},{2,0},{3,1},{4,6},{5,7},{6,4},{7,5},{8,10},{9,11},{10,... | collective-permute-start | bytes 884744 | tf_op jit(solution)/shard_map/ppermute | solution.py:193
  27.1 17.1 %collective-permute-start.6 = (bf16[648,128]{1,0:T(8,128)(2,1)S(1)}, bf16[648,128]{1,0:T(8,128)(2,1)S(1)}, u32[]{:S(2)}, u32[]{:S(2)}) collective-permute-start(bf16[648,128]{1,0:T(8,128)(2,1)S(1)} %get-tuple-element.56), channel_id=1, source_target_pairs={{0,8},{1,9},{2,10},{3,11},{4,12},{5,13},{6,14},{7,15},{8,0},{9,1},... | collective-permute-start | bytes 497672 | tf_op jit(solution)/shard_map/ppermute | solution.py:193
  30.2 14.0 %collective-permute-start.11 = (bf16[216,128]{1,0:T(8,128)(2,1)S(1)}, bf16[216,128]{1,0:T(8,128)(2,1)S(1)}, u32[]{:S(2)}, u32[]{:S(2)}) collective-permute-start(bf16[216,128]{1,0:T(8,128)(2,1)S(1)} %get-tuple-element.63), channel_id=1, source_target_pairs={{0,8},{1,9},{2,10},{3,11},{4,12},{5,13},{6,14},{7,15},{8,0},{9,1},... | collective-permute-start | bytes 165896 | tf_op jit(solution)/shard_map/ppermute | solution.py:193
  37.8 6.8 %collective-permute-start.12 = (bf16[864,128]{1,0:T(8,128)(2,1)S(1)}, bf16[864,128]{1,0:T(8,128)(2,1)S(1)}, u32[]{:S(2)}, u32[]{:S(2)}) collective-permute-start(bf16[864,128]{1,0:T(8,128)(2,1)S(1)} %add_convert_fusion.4), channel_id=1, source_target_pairs={{0,4},{1,5},{2,6},{3,7},{4,0},{5,1},{6,2},{7,3},{8,12},{9,13},{10,... | collective-permute-start | bytes 663560 | tf_op jit(solution)/shard_map/ppermute | solution.py:193
  37.9 9.5 %collective-permute-start.14 = (bf16[576,128]{1,0:T(8,128)(2,1)S(1)}, bf16[576,128]{1,0:T(8,128)(2,1)S(1)}, u32[]{:S(2)}, u32[]{:S(2)}) collective-permute-start(bf16[576,128]{1,0:T(8,128)(2,1)S(1)} %add_convert_fusion.8), channel_id=1, source_target_pairs={{0,2},{1,3},{2,0},{3,1},{4,6},{5,7},{6,4},{7,5},{8,10},{9,11},{10,... | collective-permute-start | bytes 442376 | tf_op jit(solution)/shard_map/ppermute | solution.py:193
  43.7 7.1 %collective-permute-start.16 = (bf16[576,128]{1,0:T(8,128)(2,1)S(1)}, bf16[576,128]{1,0:T(8,128)(2,1)S(1)}, u32[]{:S(2)}, u32[]{:S(2)}) collective-permute-start(bf16[576,128]{1,0:T(8,128)(2,1)S(1)} %add_convert_fusion.7), channel_id=1, source_target_pairs={{0,4},{1,5},{2,6},{3,7},{4,0},{5,1},{6,2},{7,3},{8,12},{9,13},{10,... | collective-permute-start | bytes 442376 | tf_op jit(solution)/shard_map/ppermute | solution.py:193
  44.7 12.3 %collective-permute-start.13 = (bf16[432,128]{1,0:T(8,128)(2,1)S(1)}, bf16[432,128]{1,0:T(8,128)(2,1)S(1)}, u32[]{:S(2)}, u32[]{:S(2)}) collective-permute-start(bf16[432,128]{1,0:T(8,128)(2,1)S(1)} %get-tuple-element.58), channel_id=1, source_target_pairs={{0,8},{1,9},{2,10},{3,11},{4,12},{5,13},{6,14},{7,15},{8,0},{9,1},... | collective-permute-start | bytes 331784 | tf_op jit(solution)/shard_map/ppermute | solution.py:193
  47.4 6.6 %collective-permute-start.15 = (bf16[288,128]{1,0:T(8,128)(2,1)S(1)}, bf16[288,128]{1,0:T(8,128)(2,1)S(1)}, u32[]{:S(2)}, u32[]{:S(2)}) collective-permute-start(bf16[288,128]{1,0:T(8,128)(2,1)S(1)} %add_convert_fusion.12), channel_id=1, source_target_pairs={{0,4},{1,5},{2,6},{3,7},{4,0},{5,1},{6,2},{7,3},{8,12},{9,13},{10,... | collective-permute-start | bytes 221192 | tf_op jit(solution)/shard_map/ppermute | solution.py:193
  50.9 6.4 %collective-permute-start.17 = (bf16[288,128]{1,0:T(8,128)(2,1)S(1)}, bf16[288,128]{1,0:T(8,128)(2,1)S(1)}, u32[]{:S(2)}, u32[]{:S(2)}) collective-permute-start(bf16[288,128]{1,0:T(8,128)(2,1)S(1)} %get-tuple-element.61), channel_id=1, source_target_pairs={{0,8},{1,9},{2,10},{3,11},{4,12},{5,13},{6,14},{7,15},{8,0},{9,1},... | collective-permute-start | bytes 221192 | tf_op jit(solution)/shard_map/ppermute | solution.py:193
  54.1 4.9 %collective-permute-start.18 = (bf16[144,128]{1,0:T(8,128)(2,1)S(1)}, bf16[144,128]{1,0:T(8,128)(2,1)S(1)}, u32[]{:S(2)}, u32[]{:S(2)}) collective-permute-start(bf16[144,128]{1,0:T(8,128)(2,1)S(1)} %get-tuple-element.65), channel_id=1, source_target_pairs={{0,8},{1,9},{2,10},{3,11},{4,12},{5,13},{6,14},{7,15},{8,0},{9,1},... | collective-permute-start | bytes 110600 | tf_op jit(solution)/shard_map/ppermute | solution.py:193

commit v14 on v13

--- a/solution.py
+++ b/solution.py
@@ -276,10 +276,10 @@
     one, two = remaps
     pitch = round_up(one[-1][1], 8)
     tiles = one[-1][2] // LANES
-    half, most, more = tiles // 2, tiles * 3 // 4, tiles * 5 // 6
+    some, most = tiles * 5 // 12, tiles * 3 // 4
     plans = (
         [(0, most, MIXED), (most, tiles, MIXED)],
-        [(0, half, STRAIGHT), (half, more, STRAIGHT), (more, tiles, STRAIGHT)],
+        [(0, some, MIXED), (some, most, STRAIGHT), (most, tiles, STRAIGHT)],
     )
     ones, twos = [[Chain(chunk, devices, pitch) for chunk in chunks] for chunks in plans]
     order = Order()
@@ -335,9 +335,9 @@
     step(c)
     begun(e)
     step(d)
-    step(a)
     step(b)
     step(c)
+    step(a)
     step(e)
     step(d)
     step(e)

time: 59.9 us -> 59.4 us (level)
  waiting for transfers between devices: 19.1 us -> 17.5 us
  starting transfers between devices: 28 us -> 29.2 us
    ppermute x19, waiting for transfers between devices: 19.1 us -> 17.5 us  [exchange(): return lax.ppermute(value, 'curve', pairs)]
    ppermute x19, starting transfers between devices: 28 us -> 29.2 us  [exchange(): return lax.ppermute(value, 'curve', pairs)]
  transfers between devices with their start and end apart: 19 -> 19, of which waited for: 11 -> 9; matrix products, arithmetic and copies ran while one was open for 2% -> 2% of each run, Pallas kernels for 9% -> 9%
where the time goes in v14:
time: 59.4 us; the launch traced here: 59.3 us
  starting transfers between devices  29.2 us (49%)
  waiting for transfers between devices  17.5 us (29%)
  Pallas kernels  10.8 us (18%)
  other arithmetic  1.1 us (2%)
  between operations  0.74 us (1%)
    ppermute x19, starting transfers between devices, exchange(): return lax.ppermute(value, 'curve', pairs)  29.2 us
    ppermute x19, waiting for transfers between devices, exchange(): return lax.ppermute(value, 'curve', pairs)  17.5 us
    pallas_call x2, Pallas kernels, products(): pl.pallas_call(functools.partial(product_kernel, channels, pitch, chunks,...  9.28 us
    pallas_call x2, Pallas kernels, final_sum(): pl.pallas_call(functools.partial(final_kernel, like_shape[1], pitch, part...  1.48 us
  transfers between devices with their start and end apart: 19, of which 9 were waited for; matrix products, arithmetic and copies ran while one was open for 2% of the time, Pallas kernels for 9%

profile of v14, /device:TPU:0, one launch (start us, length us, event | category | flops | bytes accessed | tf_op | source)
XLA Modules:
  0.0 59.3 jit_solution(11694195948787811496)
XLA Ops:
  0.6 4.6 %shard_map.113 = (f32[13824,128]{1,0:T(8,128)S(1)}, bf16[3456,128]{1,0:T(8,128)(2,1)S(1)}, bf16[3456,128]{1,0:T(8,128)(2,1)S(1)}) custom-call(s32[144]{0:T(256)} %source_hbm.2, s32[144]{0:T(256)} %target_hbm.2, s32[1,16]{1,0:T(1,128)} %counts_hbm.2, bf16[1,69,1536]{2,1,0:T(8,128)(2,1)} %x_hbm.1, bf16[144,128,128]{2,1,0:T(8,128)(2,1)} %w_hbm.2), custom_call_target="tpu_custom_call" | custom-call | flops 325582848 | bytes 13565952 | tf_op jit(solution)/shard_map/pallas_call | solution.py:163
  5.3 0.5 collective-permute-start.1
  5.8 0.1 collective-permute-start
  5.9 2.0 %collective-permute-done.1 = bf16[3456,128]{1,0:T(8,128)(2,1)S(1)} collective-permute-done((bf16[3456,128]{1,0:T(8,128)(2,1)S(1)}, bf16[3456,128]{1,0:T(8,128)(2,1)S(1)}, u32[]{:S(2)}, u32[]{:S(2)}) %collective-permute-start.1) | collective-permute-done | bytes 884768 | tf_op jit(solution)/shard_map/ppermute | solution.py:193
  7.8 0.1 add_convert_fusion
  8.0 3.0 %collective-permute-start.2 = (bf16[2592,128]{1,0:T(8,128)(2,1)S(1)}, bf16[2592,128]{1,0:T(8,128)(2,1)S(1)}, u32[]{:S(2)}, u32[]{:S(2)}) collective-permute-start(bf16[2592,128]{1,0:T(8,128)(2,1)S(1)} %add_convert_fusion), channel_id=1, source_target_pairs={{0,2},{1,5},{2,0},{3,7},{4,6},{5,1},{6,4},{7,3},{8,10},{9,13},{10,... | collective-permute-start | bytes 1990664 | tf_op jit(solution)/shard_map/ppermute | solution.py:193
  11.0 4.7 %shard_map.114 = (f32[13824,128]{1,0:T(8,128)S(1)}, bf16[3456,128]{1,0:T(8,128)(2,1)S(1)}, bf16[3456,128]{1,0:T(8,128)(2,1)S(1)}) custom-call(s32[144]{0:T(256)} %source_hbm.3, s32[144]{0:T(256)} %target_hbm.3, s32[1,16]{1,0:T(1,128)} %counts_hbm.3, bf16[1,69,1536]{2,1,0:T(8,128)(2,1)} %x_hbm.2, bf16[144,128,128]{2,1,0:T(8,128)(2,1)} %w_hbm.3), custom_call_target="tpu_custom_call" | custom-call | flops 325582848 | bytes 13565952 | tf_op jit(solution)/shard_map/pallas_call | solution.py:163
  15.7 0.1 collective-permute-start.4
  15.7 1.4 %collective-permute-start.5 = (bf16[864,128]{1,0:T(8,128)(2,1)S(1)}, bf16[864,128]{1,0:T(8,128)(2,1)S(1)}, u32[]{:S(2)}, u32[]{:S(2)}) collective-permute-start(bf16[864,128]{1,0:T(8,128)(2,1)S(1)} %add_convert_fusion.5), channel_id=1, source_target_pairs={{0,2},{1,5},{2,0},{3,7},{4,6},{5,1},{6,4},{7,3},{8,10},{9,13},{10,... | collective-permute-start | bytes 663560 | tf_op jit(solution)/shard_map/ppermute | solution.py:193
  17.2 0.4 collective-permute-start.7
  17.5 2.1 %collective-permute-done.2 = bf16[2592,128]{1,0:T(8,128)(2,1)S(1)} collective-permute-done((bf16[2592,128]{1,0:T(8,128)(2,1)S(1)}, bf16[2592,128]{1,0:T(8,128)(2,1)S(1)}, u32[]{:S(2)}, u32[]{:S(2)}) %collective-permute-start.2) | collective-permute-done | bytes 663584 | tf_op jit(solution)/shard_map/ppermute | solution.py:193
  19.6 0.1 add_convert_fusion.2
  19.7 2.1 %collective-permute-start.3 = (bf16[1296,128]{1,0:T(8,128)(2,1)S(1)}, bf16[1296,128]{1,0:T(8,128)(2,1)S(1)}, u32[]{:S(2)}, u32[]{:S(2)}) collective-permute-start(bf16[1296,128]{1,0:T(8,128)(2,1)S(1)} %add_convert_fusion.2), channel_id=1, source_target_pairs={{0,4},{1,3},{2,6},{3,1},{4,0},{5,7},{6,2},{7,5},{8,12},{9,11},{10,... | collective-permute-start | bytes 995336 | tf_op jit(solution)/shard_map/ppermute | solution.py:193
  21.8 0.1 collective-permute-done.5
  22.0 2.4 %collective-permute-start.8 = (bf16[432,128]{1,0:T(8,128)(2,1)S(1)}, bf16[432,128]{1,0:T(8,128)(2,1)S(1)}, u32[]{:S(2)}, u32[]{:S(2)}) collective-permute-start(bf16[432,128]{1,0:T(8,128)(2,1)S(1)} %add_convert_fusion.10), channel_id=1, source_target_pairs={{0,4},{1,3},{2,6},{3,1},{4,0},{5,7},{6,2},{7,5},{8,12},{9,11},{10,... | collective-permute-start | bytes 331784 | tf_op jit(solution)/shard_map/ppermute | solution.py:193
  24.4 0.0 collective-permute-done.4
  24.4 0.1 add_convert_fusion.3
  24.4 0.1 add_convert_fusion.1
  24.5 1.6 %collective-permute-start.9 = (bf16[1440,128]{1,0:T(8,128)(2,1)S(1)}, bf16[1440,128]{1,0:T(8,128)(2,1)S(1)}, u32[]{:S(2)}, u32[]{:S(2)}) collective-permute-start(bf16[1440,128]{1,0:T(8,128)(2,1)S(1)} %add_convert_fusion.1), channel_id=1, source_target_pairs={{0,2},{1,5},{2,0},{3,7},{4,6},{5,1},{6,4},{7,3},{8,10},{9,13},{10,... | collective-permute-start | bytes 1105928 | tf_op jit(solution)/shard_map/ppermute | solution.py:193
  26.2 0.6 collective-permute-start.12
  26.7 1.2 %collective-permute-done.3 = bf16[1296,128]{1,0:T(8,128)(2,1)S(1)} collective-permute-done((bf16[1296,128]{1,0:T(8,128)(2,1)S(1)}, bf16[1296,128]{1,0:T(8,128)(2,1)S(1)}, u32[]{:S(2)}, u32[]{:S(2)}) %collective-permute-start.3) | collective-permute-done | bytes 331808 | tf_op jit(solution)/shard_map/ppermute | solution.py:193
  27.9 0.1 add_convert_fusion.7
  28.0 3.5 %collective-permute-start.6 = (bf16[648,128]{1,0:T(8,128)(2,1)S(1)}, bf16[648,128]{1,0:T(8,128)(2,1)S(1)}, u32[]{:S(2)}, u32[]{:S(2)}) collective-permute-start(bf16[648,128]{1,0:T(8,128)(2,1)S(1)} %get-tuple-element.56), channel_id=1, source_target_pairs={{0,8},{1,9},{2,10},{3,11},{4,12},{5,13},{6,14},{7,15},{8,0},{9,1},... | collective-permute-start | bytes 497672 | tf_op jit(solution)/shard_map/ppermute | solution.py:193
  31.5 0.5 collective-permute-done.8
  32.0 0.1 convert_add_fusion.4
  32.1 3.3 %collective-permute-start.11 = (bf16[216,128]{1,0:T(8,128)(2,1)S(1)}, bf16[216,128]{1,0:T(8,128)(2,1)S(1)}, u32[]{:S(2)}, u32[]{:S(2)}) collective-permute-start(bf16[216,128]{1,0:T(8,128)(2,1)S(1)} %get-tuple-element.65), channel_id=1, source_target_pairs={{0,8},{1,9},{2,10},{3,11},{4,12},{5,13},{6,14},{7,15},{8,0},{9,1},... | collective-permute-start | bytes 165896 | tf_op jit(solution)/shard_map/ppermute | solution.py:193
  35.3 0.0 collective-permute-done.7
  35.3 0.0 collective-permute-done.9
  35.4 0.1 add_convert_fusion.6
  35.4 2.5 %collective-permute-start.10 = (bf16[720,128]{1,0:T(8,128)(2,1)S(1)}, bf16[720,128]{1,0:T(8,128)(2,1)S(1)}, u32[]{:S(2)}, u32[]{:S(2)}) collective-permute-start(bf16[720,128]{1,0:T(8,128)(2,1)S(1)} %add_convert_fusion.6), channel_id=1, source_target_pairs={{0,4},{1,3},{2,6},{3,1},{4,0},{5,7},{6,2},{7,5},{8,12},{9,11},{10,... | collective-permute-start | bytes 552968 | tf_op jit(solution)/shard_map/ppermute | solution.py:193
  38.0 2.6 %collective-permute-start.14 = (bf16[864,128]{1,0:T(8,128)(2,1)S(1)}, bf16[864,128]{1,0:T(8,128)(2,1)S(1)}, u32[]{:S(2)}, u32[]{:S(2)}) collective-permute-start(bf16[864,128]{1,0:T(8,128)(2,1)S(1)} %add_convert_fusion.4), channel_id=1, source_target_pairs={{0,2},{1,3},{2,0},{3,1},{4,6},{5,7},{6,4},{7,5},{8,10},{9,11},{10,... | collective-permute-start | bytes 663560 | tf_op jit(solution)/shard_map/ppermute | solution.py:193
  40.6 0.0 collective-permute-done.12
  40.6 0.1 add_convert_fusion.8
  40.6 0.1 collective-permute-start.16
  40.8 3.0 %collective-permute-done.10 = bf16[720,128]{1,0:T(8,128)(2,1)S(1)} collective-permute-done((bf16[720,128]{1,0:T(8,128)(2,1)S(1)}, bf16[720,128]{1,0:T(8,128)(2,1)S(1)}, u32[]{:S(2)}, u32[]{:S(2)}) %collective-permute-start.10) | collective-permute-done | bytes 184352 | tf_op jit(solution)/shard_map/ppermute | solution.py:193
  43.8 0.1 convert_add_fusion.1
  43.8 0.9 %collective-permute-start.13 = (bf16[360,128]{1,0:T(8,128)(2,1)S(1)}, bf16[360,128]{1,0:T(8,128)(2,1)S(1)}, u32[]{:S(2)}, u32[]{:S(2)}) collective-permute-start(bf16[360,128]{1,0:T(8,128)(2,1)S(1)} %get-tuple-element.59), channel_id=1, source_target_pairs={{0,8},{1,9},{2,10},{3,11},{4,12},{5,13},{6,14},{7,15},{8,0},{9,1},... | collective-permute-start | bytes 276488 | tf_op jit(solution)/shard_map/ppermute | solution.py:193
  44.8 0.7 %collective-permute-done.14 = bf16[864,128]{1,0:T(8,128)(2,1)S(1)} collective-permute-done((bf16[864,128]{1,0:T(8,128)(2,1)S(1)}, bf16[864,128]{1,0:T(8,128)(2,1)S(1)}, u32[]{:S(2)}, u32[]{:S(2)}) %collective-permute-start.14) | collective-permute-done | bytes 221216 | tf_op jit(solution)/shard_map/ppermute | solution.py:193
  45.5 0.1 add_convert_fusion.9
  45.6 1.8 %collective-permute-start.15 = (bf16[432,128]{1,0:T(8,128)(2,1)S(1)}, bf16[432,128]{1,0:T(8,128)(2,1)S(1)}, u32[]{:S(2)}, u32[]{:S(2)}) collective-permute-start(bf16[432,128]{1,0:T(8,128)(2,1)S(1)} %add_convert_fusion.9), channel_id=1, source_target_pairs={{0,4},{1,5},{2,6},{3,7},{4,0},{5,1},{6,2},{7,3},{8,12},{9,13},{10,... | collective-permute-start | bytes 331784 | tf_op jit(solution)/shard_map/ppermute | solution.py:193
  47.4 0.1 convert_add_fusion.2
  47.5 0.6 %collective-permute-start.17 = (bf16[288,128]{1,0:T(8,128)(2,1)S(1)}, bf16[288,128]{1,0:T(8,128)(2,1)S(1)}, u32[]{:S(2)}, u32[]{:S(2)}) collective-permute-start(bf16[288,128]{1,0:T(8,128)(2,1)S(1)} %get-tuple-element.61), channel_id=1, source_target_pairs={{0,8},{1,9},{2,10},{3,11},{4,12},{5,13},{6,14},{7,15},{8,0},{9,1},... | collective-permute-start | bytes 221192 | tf_op jit(solution)/shard_map/ppermute | solution.py:193
  48.1 4.1 %collective-permute-done.15 = bf16[432,128]{1,0:T(8,128)(2,1)S(1)} collective-permute-done((bf16[432,128]{1,0:T(8,128)(2,1)S(1)}, bf16[432,128]{1,0:T(8,128)(2,1)S(1)}, u32[]{:S(2)}, u32[]{:S(2)}) %collective-permute-start.15) | collective-permute-done | bytes 110624 | tf_op jit(solution)/shard_map/ppermute | solution.py:193
  52.2 0.1 convert_add_fusion.3
  52.3 1.7 %collective-permute-start.18 = (bf16[216,128]{1,0:T(8,128)(2,1)S(1)}, bf16[216,128]{1,0:T(8,128)(2,1)S(1)}, u32[]{:S(2)}, u32[]{:S(2)}) collective-permute-start(bf16[216,128]{1,0:T(8,128)(2,1)S(1)} %get-tuple-element.63), channel_id=1, source_target_pairs={{0,8},{1,9},{2,10},{3,11},{4,12},{5,13},{6,14},{7,15},{8,0},{9,1},... | collective-permute-start | bytes 165896 | tf_op jit(solution)/shard_map/ppermute | solution.py:193
  53.9 0.7 %shard_map.115 = bf16[1,69,1536]{2,1,0:T(8,128)(2,1)} custom-call(f32[648,128]{1,0:T(8,128)S(1)} %get-tuple-element.57.refs_0_, bf16[648,128]{1,0:T(8,128)(2,1)S(1)} %collective-permute-done.6.refs_1_, f32[216,128]{1,0:T(8,128)S(1)} %get-tuple-element.64.refs_2_, bf16[216,128]{1,0:T(8,128)(2,1)S(1)} %collective-permute-done.11.refs_3_), custom_call_target="tpu_custom_call" | custom-call | tf_op jit(solution)/shard_map/pallas_call | solution.py:253
  54.7 3.9 %collective-permute-done.18.refs_5_ = bf16[216,128]{1,0:T(8,128)(2,1)S(1)} collective-permute-done((bf16[216,128]{1,0:T(8,128)(2,1)S(1)}, bf16[216,128]{1,0:T(8,128)(2,1)S(1)}, u32[]{:S(2)}, u32[]{:S(2)}) %collective-permute-start.18) | collective-permute-done | bytes 55328 | tf_op jit(solution)/shard_map/ppermute | solution.py:193
  58.6 0.7 %shard_map.116 = bf16[1,69,1536]{2,1,0:T(8,128)(2,1)} custom-call(f32[360,128]{1,0:T(8,128)S(1)} %get-tuple-element.58.refs_0_, bf16[360,128]{1,0:T(8,128)(2,1)S(1)} %collective-permute-done.13.refs_1_, f32[288,128]{1,0:T(8,128)S(1)} %get-tuple-element.60.refs_2_, bf16[288,128]{1,0:T(8,128)(2,1)S(1)} %collective-permute-done.17.refs_3_, ...), custom_call_target="tpu_custom_call" | custom-call | tf_op jit(solution)/shard_map/pallas_call | solution.py:253
  (9 shorter events, 0.1 us)
Async XLA Ops:
  5.3 2.6 %collective-permute-start.1 = (bf16[3456,128]{1,0:T(8,128)(2,1)S(1)}, bf16[3456,128]{1,0:T(8,128)(2,1)S(1)}, u32[]{:S(2)}, u32[]{:S(2)}) collective-permute-start(bf16[3456,128]{1,0:T(8,128)(2,1)S(1)} %get-tuple-element.31), channel_id=1, source_target_pairs={{0,1},{1,0},{2,3},{3,2},{4,5},{5,4},{6,7},{7,6},{8,9},{9,8},{10,11... | collective-permute-start | bytes 2654216 | tf_op jit(solution)/shard_map/ppermute | solution.py:193
  5.8 5.2 %collective-permute-start = (bf16[3456,128]{1,0:T(8,128)(2,1)S(1)}, bf16[3456,128]{1,0:T(8,128)(2,1)S(1)}, u32[]{:S(2)}, u32[]{:S(2)}) collective-permute-start(bf16[3456,128]{1,0:T(8,128)(2,1)S(1)} %get-tuple-element.30), channel_id=1, source_target_pairs={{0,1},{1,0},{2,3},{3,2},{4,5},{5,4},{6,7},{7,6},{8,9},{9,8},{10,11... | collective-permute-start | bytes 2654216 | tf_op jit(solution)/shard_map/ppermute | solution.py:193
  8.0 11.6 %collective-permute-start.2 = (bf16[2592,128]{1,0:T(8,128)(2,1)S(1)}, bf16[2592,128]{1,0:T(8,128)(2,1)S(1)}, u32[]{:S(2)}, u32[]{:S(2)}) collective-permute-start(bf16[2592,128]{1,0:T(8,128)(2,1)S(1)} %add_convert_fusion), channel_id=1, source_target_pairs={{0,2},{1,5},{2,0},{3,7},{4,6},{5,1},{6,4},{7,3},{8,10},{9,13},{10,... | collective-permute-start | bytes 1990664 | tf_op jit(solution)/shard_map/ppermute | solution.py:193
  15.7 8.7 %collective-permute-start.4 = (bf16[3456,128]{1,0:T(8,128)(2,1)S(1)}, bf16[3456,128]{1,0:T(8,128)(2,1)S(1)}, u32[]{:S(2)}, u32[]{:S(2)}) collective-permute-start(bf16[3456,128]{1,0:T(8,128)(2,1)S(1)} %get-tuple-element.36), channel_id=1, source_target_pairs={{0,1},{1,0},{2,3},{3,2},{4,5},{5,4},{6,7},{7,6},{8,9},{9,8},{10,11... | collective-permute-start | bytes 2654216 | tf_op jit(solution)/shard_map/ppermute | solution.py:193
  15.7 6.2 %collective-permute-start.5 = (bf16[864,128]{1,0:T(8,128)(2,1)S(1)}, bf16[864,128]{1,0:T(8,128)(2,1)S(1)}, u32[]{:S(2)}, u32[]{:S(2)}) collective-permute-start(bf16[864,128]{1,0:T(8,128)(2,1)S(1)} %add_convert_fusion.5), channel_id=1, source_target_pairs={{0,2},{1,5},{2,0},{3,7},{4,6},{5,1},{6,4},{7,3},{8,10},{9,13},{10,... | collective-permute-start | bytes 663560 | tf_op jit(solution)/shard_map/ppermute | solution.py:193
  17.2 18.2 %collective-permute-start.7 = (bf16[3456,128]{1,0:T(8,128)(2,1)S(1)}, bf16[3456,128]{1,0:T(8,128)(2,1)S(1)}, u32[]{:S(2)}, u32[]{:S(2)}) collective-permute-start(bf16[3456,128]{1,0:T(8,128)(2,1)S(1)} %get-tuple-element.35), channel_id=1, source_target_pairs={{0,1},{1,0},{2,3},{3,2},{4,5},{5,4},{6,7},{7,6},{8,9},{9,8},{10,11... | collective-permute-start | bytes 2654216 | tf_op jit(solution)/shard_map/ppermute | solution.py:193
  19.7 8.2 %collective-permute-start.3 = (bf16[1296,128]{1,0:T(8,128)(2,1)S(1)}, bf16[1296,128]{1,0:T(8,128)(2,1)S(1)}, u32[]{:S(2)}, u32[]{:S(2)}) collective-permute-start(bf16[1296,128]{1,0:T(8,128)(2,1)S(1)} %add_convert_fusion.2), channel_id=1, source_target_pairs={{0,4},{1,3},{2,6},{3,1},{4,0},{5,7},{6,2},{7,5},{8,12},{9,11},{10,... | collective-permute-start | bytes 995336 | tf_op jit(solution)/shard_map/ppermute | solution.py:193
  22.0 10.0 %collective-permute-start.8 = (bf16[432,128]{1,0:T(8,128)(2,1)S(1)}, bf16[432,128]{1,0:T(8,128)(2,1)S(1)}, u32[]{:S(2)}, u32[]{:S(2)}) collective-permute-start(bf16[432,128]{1,0:T(8,128)(2,1)S(1)} %add_convert_fusion.10), channel_id=1, source_target_pairs={{0,4},{1,3},{2,6},{3,1},{4,0},{5,7},{6,2},{7,5},{8,12},{9,11},{10,... | collective-permute-start | bytes 331784 | tf_op jit(solution)/shard_map/ppermute | solution.py:193
  24.5 10.8 %collective-permute-start.9 = (bf16[1440,128]{1,0:T(8,128)(2,1)S(1)}, bf16[1440,128]{1,0:T(8,128)(2,1)S(1)}, u32[]{:S(2)}, u32[]{:S(2)}) collective-permute-start(bf16[1440,128]{1,0:T(8,128)(2,1)S(1)} %add_convert_fusion.1), channel_id=1, source_target_pairs={{0,2},{1,5},{2,0},{3,7},{4,6},{5,1},{6,4},{7,3},{8,10},{9,13},{10,... | collective-permute-start | bytes 1105928 | tf_op jit(solution)/shard_map/ppermute | solution.py:193
  26.2 14.4 %collective-permute-start.12 = (bf16[1152,128]{1,0:T(8,128)(2,1)S(1)}, bf16[1152,128]{1,0:T(8,128)(2,1)S(1)}, u32[]{:S(2)}, u32[]{:S(2)}) collective-permute-start(bf16[1152,128]{1,0:T(8,128)(2,1)S(1)} %add_convert_fusion.3), channel_id=1, source_target_pairs={{0,2},{1,3},{2,0},{3,1},{4,6},{5,7},{6,4},{7,5},{8,10},{9,11},{10,... | collective-permute-start | bytes 884744 | tf_op jit(solution)/shard_map/ppermute | solution.py:193
  28.0 16.7 %collective-permute-start.6 = (bf16[648,128]{1,0:T(8,128)(2,1)S(1)}, bf16[648,128]{1,0:T(8,128)(2,1)S(1)}, u32[]{:S(2)}, u32[]{:S(2)}) collective-permute-start(bf16[648,128]{1,0:T(8,128)(2,1)S(1)} %get-tuple-element.56), channel_id=1, source_target_pairs={{0,8},{1,9},{2,10},{3,11},{4,12},{5,13},{6,14},{7,15},{8,0},{9,1},... | collective-permute-start | bytes 497672 | tf_op jit(solution)/shard_map/ppermute | solution.py:193
  32.1 8.7 %collective-permute-start.11 = (bf16[216,128]{1,0:T(8,128)(2,1)S(1)}, bf16[216,128]{1,0:T(8,128)(2,1)S(1)}, u32[]{:S(2)}, u32[]{:S(2)}) collective-permute-start(bf16[216,128]{1,0:T(8,128)(2,1)S(1)} %get-tuple-element.65), channel_id=1, source_target_pairs={{0,8},{1,9},{2,10},{3,11},{4,12},{5,13},{6,14},{7,15},{8,0},{9,1},... | collective-permute-start | bytes 165896 | tf_op jit(solution)/shard_map/ppermute | solution.py:193
  35.4 8.3 %collective-permute-start.10 = (bf16[720,128]{1,0:T(8,128)(2,1)S(1)}, bf16[720,128]{1,0:T(8,128)(2,1)S(1)}, u32[]{:S(2)}, u32[]{:S(2)}) collective-permute-start(bf16[720,128]{1,0:T(8,128)(2,1)S(1)} %add_convert_fusion.6), channel_id=1, source_target_pairs={{0,4},{1,3},{2,6},{3,1},{4,0},{5,7},{6,2},{7,5},{8,12},{9,11},{10,... | collective-permute-start | bytes 552968 | tf_op jit(solution)/shard_map/ppermute | solution.py:193
  38.0 7.6 %collective-permute-start.14 = (bf16[864,128]{1,0:T(8,128)(2,1)S(1)}, bf16[864,128]{1,0:T(8,128)(2,1)S(1)}, u32[]{:S(2)}, u32[]{:S(2)}) collective-permute-start(bf16[864,128]{1,0:T(8,128)(2,1)S(1)} %add_convert_fusion.4), channel_id=1, source_target_pairs={{0,2},{1,3},{2,0},{3,1},{4,6},{5,7},{6,4},{7,5},{8,10},{9,11},{10,... | collective-permute-start | bytes 663560 | tf_op jit(solution)/shard_map/ppermute | solution.py:193
  40.6 6.8 %collective-permute-start.16 = (bf16[576,128]{1,0:T(8,128)(2,1)S(1)}, bf16[576,128]{1,0:T(8,128)(2,1)S(1)}, u32[]{:S(2)}, u32[]{:S(2)}) collective-permute-start(bf16[576,128]{1,0:T(8,128)(2,1)S(1)} %add_convert_fusion.8), channel_id=1, source_target_pairs={{0,4},{1,5},{2,6},{3,7},{4,0},{5,1},{6,2},{7,3},{8,12},{9,13},{10,... | collective-permute-start | bytes 442376 | tf_op jit(solution)/shard_map/ppermute | solution.py:193
  43.8 10.8 %collective-permute-start.13 = (bf16[360,128]{1,0:T(8,128)(2,1)S(1)}, bf16[360,128]{1,0:T(8,128)(2,1)S(1)}, u32[]{:S(2)}, u32[]{:S(2)}) collective-permute-start(bf16[360,128]{1,0:T(8,128)(2,1)S(1)} %get-tuple-element.59), channel_id=1, source_target_pairs={{0,8},{1,9},{2,10},{3,11},{4,12},{5,13},{6,14},{7,15},{8,0},{9,1},... | collective-permute-start | bytes 276488 | tf_op jit(solution)/shard_map/ppermute | solution.py:193
  45.6 6.6 %collective-permute-start.15 = (bf16[432,128]{1,0:T(8,128)(2,1)S(1)}, bf16[432,128]{1,0:T(8,128)(2,1)S(1)}, u32[]{:S(2)}, u32[]{:S(2)}) collective-permute-start(bf16[432,128]{1,0:T(8,128)(2,1)S(1)} %add_convert_fusion.9), channel_id=1, source_target_pairs={{0,4},{1,5},{2,6},{3,7},{4,0},{5,1},{6,2},{7,3},{8,12},{9,13},{10,... | collective-permute-start | bytes 331784 | tf_op jit(solution)/shard_map/ppermute | solution.py:193
  47.5 7.2 %collective-permute-start.17 = (bf16[288,128]{1,0:T(8,128)(2,1)S(1)}, bf16[288,128]{1,0:T(8,128)(2,1)S(1)}, u32[]{:S(2)}, u32[]{:S(2)}) collective-permute-start(bf16[288,128]{1,0:T(8,128)(2,1)S(1)} %get-tuple-element.61), channel_id=1, source_target_pairs={{0,8},{1,9},{2,10},{3,11},{4,12},{5,13},{6,14},{7,15},{8,0},{9,1},... | collective-permute-start | bytes 221192 | tf_op jit(solution)/shard_map/ppermute | solution.py:193
  52.3 6.3 %collective-permute-start.18 = (bf16[216,128]{1,0:T(8,128)(2,1)S(1)}, bf16[216,128]{1,0:T(8,128)(2,1)S(1)}, u32[]{:S(2)}, u32[]{:S(2)}) collective-permute-start(bf16[216,128]{1,0:T(8,128)(2,1)S(1)} %get-tuple-element.63), channel_id=1, source_target_pairs={{0,8},{1,9},{2,10},{3,11},{4,12},{5,13},{6,14},{7,15},{8,0},{9,1},... | collective-permute-start | bytes 165896 | tf_op jit(solution)/shard_map/ppermute | solution.py:193

commit v15 on v9

--- a/solution.py
+++ b/solution.py
@@ -61,7 +61,7 @@
 
 
 STRAIGHT = ((0, 1, 2, 3), (0, 1, 2, 3))
-MIXED = ((0, 1, 2, 3), (0, 2, 1, 3))
+MIXED = ((0, 2, 1, 3), (0, 1, 2, 3))
 BITS = 4
 
 
@@ -243,19 +243,12 @@
 
 def final_sum(chains, like_shape, pitch):
     parts = [(chain.chunk[0], chain.chunk[1], len(chain.terms)) for chain in chains]
-    flat, specs = [], []
-    for chain in chains:
-        rows = (chain.chunk[1] - chain.chunk[0]) * pitch
-        for term, base in chain.terms:
-            flat.append(term if base % rows == 0 else term[base:base + rows])
-            at = base // rows if base % rows == 0 else 0
-            specs.append(pl.BlockSpec((rows, LANES), lambda step, at=at: (at, 0)))
+    flat = [term for chain in chains for term, base in chain.terms]
     return pl.pallas_call(
         functools.partial(final_kernel, like_shape[1], pitch, parts),
         out_shape=jax.ShapeDtypeStruct(like_shape, jnp.bfloat16),
-        grid=(1,),
-        in_specs=specs,
-        out_specs=pl.BlockSpec(like_shape, lambda step: (0, 0, 0)),
+        in_specs=[pl.BlockSpec(memory_space=pltpu.VMEM)] * len(flat),
+        out_specs=pl.BlockSpec(memory_space=pltpu.VMEM),
         compiler_params=pltpu.CompilerParams(vmem_limit_bytes=24 * 1024 * 1024),
     )(*flat)
 

time: 58.1 us -> 58.5 us (level)
  starting transfers between devices: 31.4 us -> 36 us
  waiting for transfers between devices: 13.9 us -> 9.66 us
    ppermute x19, starting transfers between devices: 31.4 us -> 36 us  [exchange(): return lax.ppermute(value, 'curve', pairs)]
    ppermute x19, waiting for transfers between devices: 13.9 us -> 9.66 us  [exchange(): return lax.ppermute(value, 'curve', pairs)]
  transfers between devices with their start and end apart: 19 -> 19, of which waited for: 10 -> 7; matrix products, arithmetic and copies ran while one was open for 2% -> 2% of each run, Pallas kernels for 9% -> 9%
where the time goes in v15:
time: 58.5 us; the launch traced here: 58.3 us
  starting transfers between devices  36 us (62%)
  Pallas kernels  10.8 us (18%)
  waiting for transfers between devices  9.66 us (17%)
  other arithmetic  1.1 us (2%)
  between operations  0.74 us (1%)
    ppermute x19, starting transfers between devices, exchange(): return lax.ppermute(value, 'curve', pairs)  36 us
    ppermute x19, waiting for transfers between devices, exchange(): return lax.ppermute(value, 'curve', pairs)  9.66 us
    pallas_call x2, Pallas kernels, products(): pl.pallas_call(functools.partial(product_kernel, channels, pitch, chunks,...  9.28 us
    pallas_call x2, Pallas kernels, final_sum(): pl.pallas_call(functools.partial(final_kernel, like_shape[1], pitch, part...  1.48 us
  transfers between devices with their start and end apart: 19, of which 7 were waited for; matrix products, arithmetic and copies ran while one was open for 2% of the time, Pallas kernels for 9%

profile of v15, /device:TPU:0, one launch (start us, length us, event | category | flops | bytes accessed | tf_op | source)
XLA Modules:
  0.0 58.3 jit_solution(4905029258810056581)
XLA Ops:
  0.6 4.6 %shard_map.113 = (f32[13824,128]{1,0:T(8,128)S(1)}, bf16[3456,128]{1,0:T(8,128)(2,1)S(1)}, bf16[3456,128]{1,0:T(8,128)(2,1)S(1)}) custom-call(s32[144]{0:T(256)} %source_hbm.2, s32[144]{0:T(256)} %target_hbm.2, s32[1,16]{1,0:T(1,128)} %counts_hbm.2, bf16[1,69,1536]{2,1,0:T(8,128)(2,1)} %x_hbm.1, bf16[144,128,128]{2,1,0:T(8,128)(2,1)} %w_hbm.2), custom_call_target="tpu_custom_call" | custom-call | flops 325582848 | bytes 13565952 | tf_op jit(solution)/shard_map/pallas_call | solution.py:163
  5.3 0.5 collective-permute-start.1
  5.7 0.1 collective-permute-start
  5.8 1.9 %collective-permute-done.1 = bf16[3456,128]{1,0:T(8,128)(2,1)S(1)} collective-permute-done((bf16[3456,128]{1,0:T(8,128)(2,1)S(1)}, bf16[3456,128]{1,0:T(8,128)(2,1)S(1)}, u32[]{:S(2)}, u32[]{:S(2)}) %collective-permute-start.1) | collective-permute-done | bytes 884768 | tf_op jit(solution)/shard_map/ppermute | solution.py:193
  7.8 0.1 add_convert_fusion
  7.9 3.1 %collective-permute-start.2 = (bf16[2592,128]{1,0:T(8,128)(2,1)S(1)}, bf16[2592,128]{1,0:T(8,128)(2,1)S(1)}, u32[]{:S(2)}, u32[]{:S(2)}) collective-permute-start(bf16[2592,128]{1,0:T(8,128)(2,1)S(1)} %add_convert_fusion), channel_id=1, source_target_pairs={{0,4},{1,3},{2,6},{3,1},{4,0},{5,7},{6,2},{7,5},{8,12},{9,11},{10,... | collective-permute-start | bytes 1990664 | tf_op jit(solution)/shard_map/ppermute | solution.py:193
  11.0 4.7 %shard_map.114 = (f32[13824,128]{1,0:T(8,128)S(1)}, bf16[3456,128]{1,0:T(8,128)(2,1)S(1)}, bf16[3456,128]{1,0:T(8,128)(2,1)S(1)}) custom-call(s32[144]{0:T(256)} %source_hbm.3, s32[144]{0:T(256)} %target_hbm.3, s32[1,16]{1,0:T(1,128)} %counts_hbm.3, bf16[1,69,1536]{2,1,0:T(8,128)(2,1)} %x_hbm.2, bf16[144,128,128]{2,1,0:T(8,128)(2,1)} %w_hbm.3), custom_call_target="tpu_custom_call" | custom-call | flops 325582848 | bytes 13565952 | tf_op jit(solution)/shard_map/pallas_call | solution.py:163
  15.7 0.1 collective-permute-start.4
  15.8 1.4 %collective-permute-start.5 = (bf16[864,128]{1,0:T(8,128)(2,1)S(1)}, bf16[864,128]{1,0:T(8,128)(2,1)S(1)}, u32[]{:S(2)}, u32[]{:S(2)}) collective-permute-start(bf16[864,128]{1,0:T(8,128)(2,1)S(1)} %add_convert_fusion.5), channel_id=1, source_target_pairs={{0,4},{1,3},{2,6},{3,1},{4,0},{5,7},{6,2},{7,5},{8,12},{9,11},{10,... | collective-permute-start | bytes 663560 | tf_op jit(solution)/shard_map/ppermute | solution.py:193
  17.1 0.3 collective-permute-start.7
  17.5 2.2 %collective-permute-done.2 = bf16[2592,128]{1,0:T(8,128)(2,1)S(1)} collective-permute-done((bf16[2592,128]{1,0:T(8,128)(2,1)S(1)}, bf16[2592,128]{1,0:T(8,128)(2,1)S(1)}, u32[]{:S(2)}, u32[]{:S(2)}) %collective-permute-start.2) | collective-permute-done | bytes 663584 | tf_op jit(solution)/shard_map/ppermute | solution.py:193
  19.6 0.1 add_convert_fusion.2
  19.8 2.0 %collective-permute-start.3 = (bf16[1296,128]{1,0:T(8,128)(2,1)S(1)}, bf16[1296,128]{1,0:T(8,128)(2,1)S(1)}, u32[]{:S(2)}, u32[]{:S(2)}) collective-permute-start(bf16[1296,128]{1,0:T(8,128)(2,1)S(1)} %add_convert_fusion.2), channel_id=1, source_target_pairs={{0,2},{1,5},{2,0},{3,7},{4,6},{5,1},{6,4},{7,3},{8,10},{9,13},{10,... | collective-permute-start | bytes 995336 | tf_op jit(solution)/shard_map/ppermute | solution.py:193
  21.8 0.2 collective-permute-done.5
  22.1 2.3 %collective-permute-start.8 = (bf16[432,128]{1,0:T(8,128)(2,1)S(1)}, bf16[432,128]{1,0:T(8,128)(2,1)S(1)}, u32[]{:S(2)}, u32[]{:S(2)}) collective-permute-start(bf16[432,128]{1,0:T(8,128)(2,1)S(1)} %add_convert_fusion.10), channel_id=1, source_target_pairs={{0,2},{1,5},{2,0},{3,7},{4,6},{5,1},{6,4},{7,3},{8,10},{9,13},{10,... | collective-permute-start | bytes 331784 | tf_op jit(solution)/shard_map/ppermute | solution.py:193
  24.3 0.0 collective-permute-done.4
  24.3 0.1 add_convert_fusion.3
  24.4 0.1 add_convert_fusion.1
  24.5 1.6 %collective-permute-start.10 = (bf16[1440,128]{1,0:T(8,128)(2,1)S(1)}, bf16[1440,128]{1,0:T(8,128)(2,1)S(1)}, u32[]{:S(2)}, u32[]{:S(2)}) collective-permute-start(bf16[1440,128]{1,0:T(8,128)(2,1)S(1)} %add_convert_fusion.1), channel_id=1, source_target_pairs={{0,4},{1,3},{2,6},{3,1},{4,0},{5,7},{6,2},{7,5},{8,12},{9,11},{10,... | collective-permute-start | bytes 1105928 | tf_op jit(solution)/shard_map/ppermute | solution.py:193
  26.2 0.6 collective-permute-start.9
  26.7 1.1 %collective-permute-done.3 = bf16[1296,128]{1,0:T(8,128)(2,1)S(1)} collective-permute-done((bf16[1296,128]{1,0:T(8,128)(2,1)S(1)}, bf16[1296,128]{1,0:T(8,128)(2,1)S(1)}, u32[]{:S(2)}, u32[]{:S(2)}) %collective-permute-start.3) | collective-permute-done | bytes 331808 | tf_op jit(solution)/shard_map/ppermute | solution.py:193
  27.9 0.1 add_convert_fusion.7
  28.0 3.6 %collective-permute-start.6 = (bf16[648,128]{1,0:T(8,128)(2,1)S(1)}, bf16[648,128]{1,0:T(8,128)(2,1)S(1)}, u32[]{:S(2)}, u32[]{:S(2)}) collective-permute-start(bf16[648,128]{1,0:T(8,128)(2,1)S(1)} %get-tuple-element.56), channel_id=1, source_target_pairs={{0,8},{1,9},{2,10},{3,11},{4,12},{5,13},{6,14},{7,15},{8,0},{9,1},... | collective-permute-start | bytes 497672 | tf_op jit(solution)/shard_map/ppermute | solution.py:193
  31.6 0.0 collective-permute-done.8
  31.6 0.1 convert_add_fusion.4
  31.6 2.2 %collective-permute-start.12 = (bf16[216,128]{1,0:T(8,128)(2,1)S(1)}, bf16[216,128]{1,0:T(8,128)(2,1)S(1)}, u32[]{:S(2)}, u32[]{:S(2)}) collective-permute-start(bf16[216,128]{1,0:T(8,128)(2,1)S(1)} %get-tuple-element.65), channel_id=1, source_target_pairs={{0,8},{1,9},{2,10},{3,11},{4,12},{5,13},{6,14},{7,15},{8,0},{9,1},... | collective-permute-start | bytes 165896 | tf_op jit(solution)/shard_map/ppermute | solution.py:193
  33.9 1.4 %collective-permute-done.10 = bf16[1440,128]{1,0:T(8,128)(2,1)S(1)} collective-permute-done((bf16[1440,128]{1,0:T(8,128)(2,1)S(1)}, bf16[1440,128]{1,0:T(8,128)(2,1)S(1)}, u32[]{:S(2)}, u32[]{:S(2)}) %collective-permute-start.10) | collective-permute-done | bytes 368672 | tf_op jit(solution)/shard_map/ppermute | solution.py:193
  35.3 0.1 add_convert_fusion.6
  35.3 0.1 collective-permute-start.14
  35.5 1.1 %collective-permute-done.9 = bf16[1152,128]{1,0:T(8,128)(2,1)S(1)} collective-permute-done((bf16[1152,128]{1,0:T(8,128)(2,1)S(1)}, bf16[1152,128]{1,0:T(8,128)(2,1)S(1)}, u32[]{:S(2)}, u32[]{:S(2)}) %collective-permute-start.9) | collective-permute-done | bytes 294944 | tf_op jit(solution)/shard_map/ppermute | solution.py:193
  36.5 2.4 %collective-permute-start.13 = (bf16[864,128]{1,0:T(8,128)(2,1)S(1)}, bf16[864,128]{1,0:T(8,128)(2,1)S(1)}, u32[]{:S(2)}, u32[]{:S(2)}) collective-permute-start(bf16[864,128]{1,0:T(8,128)(2,1)S(1)} %add_convert_fusion.4), channel_id=1, source_target_pairs={{0,2},{1,3},{2,0},{3,1},{4,6},{5,7},{6,4},{7,5},{8,10},{9,11},{10,... | collective-permute-start | bytes 663560 | tf_op jit(solution)/shard_map/ppermute | solution.py:193
  39.0 0.1 add_convert_fusion.8
  39.0 2.8 %collective-permute-start.11 = (bf16[576,128]{1,0:T(8,128)(2,1)S(1)}, bf16[576,128]{1,0:T(8,128)(2,1)S(1)}, u32[]{:S(2)}, u32[]{:S(2)}) collective-permute-start(bf16[576,128]{1,0:T(8,128)(2,1)S(1)} %add_convert_fusion.8), channel_id=1, source_target_pairs={{0,4},{1,5},{2,6},{3,7},{4,0},{5,1},{6,2},{7,3},{8,12},{9,13},{10,... | collective-permute-start | bytes 442376 | tf_op jit(solution)/shard_map/ppermute | solution.py:193
  41.8 0.0 collective-permute-done.14
  41.8 0.1 convert_add_fusion.1
  41.9 2.7 %collective-permute-start.15 = (bf16[360,128]{1,0:T(8,128)(2,1)S(1)}, bf16[360,128]{1,0:T(8,128)(2,1)S(1)}, u32[]{:S(2)}, u32[]{:S(2)}) collective-permute-start(bf16[360,128]{1,0:T(8,128)(2,1)S(1)} %get-tuple-element.59), channel_id=1, source_target_pairs={{0,8},{1,9},{2,10},{3,11},{4,12},{5,13},{6,14},{7,15},{8,0},{9,1},... | collective-permute-start | bytes 276488 | tf_op jit(solution)/shard_map/ppermute | solution.py:193
  44.6 0.0 collective-permute-done.13
  44.6 0.1 add_convert_fusion.9
  44.7 3.4 %collective-permute-start.17 = (bf16[432,128]{1,0:T(8,128)(2,1)S(1)}, bf16[432,128]{1,0:T(8,128)(2,1)S(1)}, u32[]{:S(2)}, u32[]{:S(2)}) collective-permute-start(bf16[432,128]{1,0:T(8,128)(2,1)S(1)} %add_convert_fusion.9), channel_id=1, source_target_pairs={{0,4},{1,5},{2,6},{3,7},{4,0},{5,1},{6,2},{7,3},{8,12},{9,13},{10,... | collective-permute-start | bytes 331784 | tf_op jit(solution)/shard_map/ppermute | solution.py:193
  48.0 0.0 collective-permute-done.12.refs_3_
  48.0 0.0 collective-permute-done.11
  48.0 0.1 convert_add_fusion.2
  48.1 2.8 %collective-permute-start.16 = (bf16[288,128]{1,0:T(8,128)(2,1)S(1)}, bf16[288,128]{1,0:T(8,128)(2,1)S(1)}, u32[]{:S(2)}, u32[]{:S(2)}) collective-permute-start(bf16[288,128]{1,0:T(8,128)(2,1)S(1)} %get-tuple-element.61), channel_id=1, source_target_pairs={{0,8},{1,9},{2,10},{3,11},{4,12},{5,13},{6,14},{7,15},{8,0},{9,1},... | collective-permute-start | bytes 221192 | tf_op jit(solution)/shard_map/ppermute | solution.py:193
  50.9 0.1 convert_add_fusion.3
  51.0 4.1 %collective-permute-start.18 = (bf16[216,128]{1,0:T(8,128)(2,1)S(1)}, bf16[216,128]{1,0:T(8,128)(2,1)S(1)}, u32[]{:S(2)}, u32[]{:S(2)}) collective-permute-start(bf16[216,128]{1,0:T(8,128)(2,1)S(1)} %get-tuple-element.63), channel_id=1, source_target_pairs={{0,8},{1,9},{2,10},{3,11},{4,12},{5,13},{6,14},{7,15},{8,0},{9,1},... | collective-permute-start | bytes 165896 | tf_op jit(solution)/shard_map/ppermute | solution.py:193
  55.1 0.7 %shard_map.115 = bf16[1,69,1536]{2,1,0:T(8,128)(2,1)} custom-call(f32[648,128]{1,0:T(8,128)S(1)} %get-tuple-element.57.refs_0_, bf16[648,128]{1,0:T(8,128)(2,1)S(1)} %collective-permute-done.6.refs_1_, f32[216,128]{1,0:T(8,128)S(1)} %get-tuple-element.64.refs_2_, bf16[216,128]{1,0:T(8,128)(2,1)S(1)} %collective-permute-done.12.refs_3_), custom_call_target="tpu_custom_call" | custom-call | tf_op jit(solution)/shard_map/pallas_call | solution.py:247
  55.8 1.7 %collective-permute-done.18.refs_5_ = bf16[216,128]{1,0:T(8,128)(2,1)S(1)} collective-permute-done((bf16[216,128]{1,0:T(8,128)(2,1)S(1)}, bf16[216,128]{1,0:T(8,128)(2,1)S(1)}, u32[]{:S(2)}, u32[]{:S(2)}) %collective-permute-start.18) | collective-permute-done | bytes 55328 | tf_op jit(solution)/shard_map/ppermute | solution.py:193
  57.6 0.7 %shard_map.116 = bf16[1,69,1536]{2,1,0:T(8,128)(2,1)} custom-call(f32[360,128]{1,0:T(8,128)S(1)} %get-tuple-element.58.refs_0_, bf16[360,128]{1,0:T(8,128)(2,1)S(1)} %collective-permute-done.15.refs_1_, f32[288,128]{1,0:T(8,128)S(1)} %get-tuple-element.60.refs_2_, bf16[288,128]{1,0:T(8,128)(2,1)S(1)} %collective-permute-done.16.refs_3_, ...), custom_call_target="tpu_custom_call" | custom-call | tf_op jit(solution)/shard_map/pallas_call | solution.py:247
  (9 shorter events, 0.1 us)
Async XLA Ops:
  5.3 2.5 %collective-permute-start.1 = (bf16[3456,128]{1,0:T(8,128)(2,1)S(1)}, bf16[3456,128]{1,0:T(8,128)(2,1)S(1)}, u32[]{:S(2)}, u32[]{:S(2)}) collective-permute-start(bf16[3456,128]{1,0:T(8,128)(2,1)S(1)} %get-tuple-element.31), channel_id=1, source_target_pairs={{0,1},{1,0},{2,3},{3,2},{4,5},{5,4},{6,7},{7,6},{8,9},{9,8},{10,11... | collective-permute-start | bytes 2654216 | tf_op jit(solution)/shard_map/ppermute | solution.py:193
  5.7 5.3 %collective-permute-start = (bf16[3456,128]{1,0:T(8,128)(2,1)S(1)}, bf16[3456,128]{1,0:T(8,128)(2,1)S(1)}, u32[]{:S(2)}, u32[]{:S(2)}) collective-permute-start(bf16[3456,128]{1,0:T(8,128)(2,1)S(1)} %get-tuple-element.30), channel_id=1, source_target_pairs={{0,1},{1,0},{2,3},{3,2},{4,5},{5,4},{6,7},{7,6},{8,9},{9,8},{10,11... | collective-permute-start | bytes 2654216 | tf_op jit(solution)/shard_map/ppermute | solution.py:193
  7.9 11.7 %collective-permute-start.2 = (bf16[2592,128]{1,0:T(8,128)(2,1)S(1)}, bf16[2592,128]{1,0:T(8,128)(2,1)S(1)}, u32[]{:S(2)}, u32[]{:S(2)}) collective-permute-start(bf16[2592,128]{1,0:T(8,128)(2,1)S(1)} %add_convert_fusion), channel_id=1, source_target_pairs={{0,4},{1,3},{2,6},{3,1},{4,0},{5,7},{6,2},{7,5},{8,12},{9,11},{10,... | collective-permute-start | bytes 1990664 | tf_op jit(solution)/shard_map/ppermute | solution.py:193
  15.7 8.6 %collective-permute-start.4 = (bf16[3456,128]{1,0:T(8,128)(2,1)S(1)}, bf16[3456,128]{1,0:T(8,128)(2,1)S(1)}, u32[]{:S(2)}, u32[]{:S(2)}) collective-permute-start(bf16[3456,128]{1,0:T(8,128)(2,1)S(1)} %get-tuple-element.36), channel_id=1, source_target_pairs={{0,1},{1,0},{2,3},{3,2},{4,5},{5,4},{6,7},{7,6},{8,9},{9,8},{10,11... | collective-permute-start | bytes 2654216 | tf_op jit(solution)/shard_map/ppermute | solution.py:193
  15.8 6.2 %collective-permute-start.5 = (bf16[864,128]{1,0:T(8,128)(2,1)S(1)}, bf16[864,128]{1,0:T(8,128)(2,1)S(1)}, u32[]{:S(2)}, u32[]{:S(2)}) collective-permute-start(bf16[864,128]{1,0:T(8,128)(2,1)S(1)} %add_convert_fusion.5), channel_id=1, source_target_pairs={{0,4},{1,3},{2,6},{3,1},{4,0},{5,7},{6,2},{7,5},{8,12},{9,11},{10,... | collective-permute-start | bytes 663560 | tf_op jit(solution)/shard_map/ppermute | solution.py:193
  17.1 16.7 %collective-permute-start.7 = (bf16[3456,128]{1,0:T(8,128)(2,1)S(1)}, bf16[3456,128]{1,0:T(8,128)(2,1)S(1)}, u32[]{:S(2)}, u32[]{:S(2)}) collective-permute-start(bf16[3456,128]{1,0:T(8,128)(2,1)S(1)} %get-tuple-element.35), channel_id=1, source_target_pairs={{0,1},{1,0},{2,3},{3,2},{4,5},{5,4},{6,7},{7,6},{8,9},{9,8},{10,11... | collective-permute-start | bytes 2654216 | tf_op jit(solution)/shard_map/ppermute | solution.py:193
  19.8 8.1 %collective-permute-start.3 = (bf16[1296,128]{1,0:T(8,128)(2,1)S(1)}, bf16[1296,128]{1,0:T(8,128)(2,1)S(1)}, u32[]{:S(2)}, u32[]{:S(2)}) collective-permute-start(bf16[1296,128]{1,0:T(8,128)(2,1)S(1)} %add_convert_fusion.2), channel_id=1, source_target_pairs={{0,2},{1,5},{2,0},{3,7},{4,6},{5,1},{6,4},{7,3},{8,10},{9,13},{10,... | collective-permute-start | bytes 995336 | tf_op jit(solution)/shard_map/ppermute | solution.py:193
  22.1 9.5 %collective-permute-start.8 = (bf16[432,128]{1,0:T(8,128)(2,1)S(1)}, bf16[432,128]{1,0:T(8,128)(2,1)S(1)}, u32[]{:S(2)}, u32[]{:S(2)}) collective-permute-start(bf16[432,128]{1,0:T(8,128)(2,1)S(1)} %add_convert_fusion.10), channel_id=1, source_target_pairs={{0,2},{1,5},{2,0},{3,7},{4,6},{5,1},{6,4},{7,3},{8,10},{9,13},{10,... | collective-permute-start | bytes 331784 | tf_op jit(solution)/shard_map/ppermute | solution.py:193
  24.5 10.8 %collective-permute-start.10 = (bf16[1440,128]{1,0:T(8,128)(2,1)S(1)}, bf16[1440,128]{1,0:T(8,128)(2,1)S(1)}, u32[]{:S(2)}, u32[]{:S(2)}) collective-permute-start(bf16[1440,128]{1,0:T(8,128)(2,1)S(1)} %add_convert_fusion.1), channel_id=1, source_target_pairs={{0,4},{1,3},{2,6},{3,1},{4,0},{5,7},{6,2},{7,5},{8,12},{9,11},{10,... | collective-permute-start | bytes 1105928 | tf_op jit(solution)/shard_map/ppermute | solution.py:193
  26.2 10.4 %collective-permute-start.9 = (bf16[1152,128]{1,0:T(8,128)(2,1)S(1)}, bf16[1152,128]{1,0:T(8,128)(2,1)S(1)}, u32[]{:S(2)}, u32[]{:S(2)}) collective-permute-start(bf16[1152,128]{1,0:T(8,128)(2,1)S(1)} %add_convert_fusion.3), channel_id=1, source_target_pairs={{0,2},{1,3},{2,0},{3,1},{4,6},{5,7},{6,4},{7,5},{8,10},{9,11},{10,... | collective-permute-start | bytes 884744 | tf_op jit(solution)/shard_map/ppermute | solution.py:193
  28.0 22.9 %collective-permute-start.6 = (bf16[648,128]{1,0:T(8,128)(2,1)S(1)}, bf16[648,128]{1,0:T(8,128)(2,1)S(1)}, u32[]{:S(2)}, u32[]{:S(2)}) collective-permute-start(bf16[648,128]{1,0:T(8,128)(2,1)S(1)} %get-tuple-element.56), channel_id=1, source_target_pairs={{0,8},{1,9},{2,10},{3,11},{4,12},{5,13},{6,14},{7,15},{8,0},{9,1},... | collective-permute-start | bytes 497672 | tf_op jit(solution)/shard_map/ppermute | solution.py:193
  31.6 16.4 %collective-permute-start.12 = (bf16[216,128]{1,0:T(8,128)(2,1)S(1)}, bf16[216,128]{1,0:T(8,128)(2,1)S(1)}, u32[]{:S(2)}, u32[]{:S(2)}) collective-permute-start(bf16[216,128]{1,0:T(8,128)(2,1)S(1)} %get-tuple-element.65), channel_id=1, source_target_pairs={{0,8},{1,9},{2,10},{3,11},{4,12},{5,13},{6,14},{7,15},{8,0},{9,1},... | collective-permute-start | bytes 165896 | tf_op jit(solution)/shard_map/ppermute | solution.py:193
  35.3 6.5 %collective-permute-start.14 = (bf16[720,128]{1,0:T(8,128)(2,1)S(1)}, bf16[720,128]{1,0:T(8,128)(2,1)S(1)}, u32[]{:S(2)}, u32[]{:S(2)}) collective-permute-start(bf16[720,128]{1,0:T(8,128)(2,1)S(1)} %add_convert_fusion.6), channel_id=1, source_target_pairs={{0,2},{1,5},{2,0},{3,7},{4,6},{5,1},{6,4},{7,3},{8,10},{9,13},{10,... | collective-permute-start | bytes 552968 | tf_op jit(solution)/shard_map/ppermute | solution.py:193
  36.5 8.1 %collective-permute-start.13 = (bf16[864,128]{1,0:T(8,128)(2,1)S(1)}, bf16[864,128]{1,0:T(8,128)(2,1)S(1)}, u32[]{:S(2)}, u32[]{:S(2)}) collective-permute-start(bf16[864,128]{1,0:T(8,128)(2,1)S(1)} %add_convert_fusion.4), channel_id=1, source_target_pairs={{0,2},{1,3},{2,0},{3,1},{4,6},{5,7},{6,4},{7,5},{8,10},{9,11},{10,... | collective-permute-start | bytes 663560 | tf_op jit(solution)/shard_map/ppermute | solution.py:193
  39.0 9.0 %collective-permute-start.11 = (bf16[576,128]{1,0:T(8,128)(2,1)S(1)}, bf16[576,128]{1,0:T(8,128)(2,1)S(1)}, u32[]{:S(2)}, u32[]{:S(2)}) collective-permute-start(bf16[576,128]{1,0:T(8,128)(2,1)S(1)} %add_convert_fusion.8), channel_id=1, source_target_pairs={{0,4},{1,5},{2,6},{3,7},{4,0},{5,1},{6,2},{7,3},{8,12},{9,13},{10,... | collective-permute-start | bytes 442376 | tf_op jit(solution)/shard_map/ppermute | solution.py:193
  41.9 13.9 %collective-permute-start.15 = (bf16[360,128]{1,0:T(8,128)(2,1)S(1)}, bf16[360,128]{1,0:T(8,128)(2,1)S(1)}, u32[]{:S(2)}, u32[]{:S(2)}) collective-permute-start(bf16[360,128]{1,0:T(8,128)(2,1)S(1)} %get-tuple-element.59), channel_id=1, source_target_pairs={{0,8},{1,9},{2,10},{3,11},{4,12},{5,13},{6,14},{7,15},{8,0},{9,1},... | collective-permute-start | bytes 276488 | tf_op jit(solution)/shard_map/ppermute | solution.py:193
  44.7 6.3 %collective-permute-start.17 = (bf16[432,128]{1,0:T(8,128)(2,1)S(1)}, bf16[432,128]{1,0:T(8,128)(2,1)S(1)}, u32[]{:S(2)}, u32[]{:S(2)}) collective-permute-start(bf16[432,128]{1,0:T(8,128)(2,1)S(1)} %add_convert_fusion.9), channel_id=1, source_target_pairs={{0,4},{1,5},{2,6},{3,7},{4,0},{5,1},{6,2},{7,3},{8,12},{9,13},{10,... | collective-permute-start | bytes 331784 | tf_op jit(solution)/shard_map/ppermute | solution.py:193
  48.1 7.7 %collective-permute-start.16 = (bf16[288,128]{1,0:T(8,128)(2,1)S(1)}, bf16[288,128]{1,0:T(8,128)(2,1)S(1)}, u32[]{:S(2)}, u32[]{:S(2)}) collective-permute-start(bf16[288,128]{1,0:T(8,128)(2,1)S(1)} %get-tuple-element.61), channel_id=1, source_target_pairs={{0,8},{1,9},{2,10},{3,11},{4,12},{5,13},{6,14},{7,15},{8,0},{9,1},... | collective-permute-start | bytes 221192 | tf_op jit(solution)/shard_map/ppermute | solution.py:193
  51.0 6.6 %collective-permute-start.18 = (bf16[216,128]{1,0:T(8,128)(2,1)S(1)}, bf16[216,128]{1,0:T(8,128)(2,1)S(1)}, u32[]{:S(2)}, u32[]{:S(2)}) collective-permute-start(bf16[216,128]{1,0:T(8,128)(2,1)S(1)} %get-tuple-element.63), channel_id=1, source_target_pairs={{0,8},{1,9},{2,10},{3,11},{4,12},{5,13},{6,14},{7,15},{8,0},{9,1},... | collective-permute-start | bytes 165896 | tf_op jit(solution)/shard_map/ppermute | solution.py:193

commit v16 on v15

--- a/solution.py
+++ b/solution.py
@@ -269,10 +269,10 @@
     one, two = remaps
     pitch = round_up(one[-1][1], 8)
     tiles = one[-1][2] // LANES
-    some, most = tiles * 5 // 12, tiles * 3 // 4
+    half, most, more = tiles // 2, tiles * 3 // 4, tiles * 5 // 6
     plans = (
         [(0, most, MIXED), (most, tiles, MIXED)],
-        [(0, some, MIXED), (some, most, STRAIGHT), (most, tiles, STRAIGHT)],
+        [(0, half, MIXED), (half, more, STRAIGHT), (more, tiles, STRAIGHT)],
     )
     ones, twos = [[Chain(chunk, devices, pitch) for chunk in chunks] for chunks in plans]
     order = Order()
@@ -330,11 +330,13 @@
     step(d)
     step(c)
     step(e)
+    step(d)
+    step(e)
     step(b)
+    step(a)
+    step(c)
     step(d)
-    step(a)
     step(e)
-    step(*twos)
     return [final_sum(line, remap[-1], pitch) for line, remap in zip((ones, twos), remaps)]
 
 

time: 58.5 us -> 57.5 us (0.983)
  starting transfers between devices: 36 us -> 25.9 us
  waiting for transfers between devices: 9.66 us -> 18.9 us
    ppermute x19, starting transfers between devices: 36 us -> 25.9 us  [exchange(): return lax.ppermute(value, 'curve', pairs)]
    ppermute x19, waiting for transfers between devices: 9.66 us -> 18.9 us  [exchange(): return lax.ppermute(value, 'curve', pairs)]
  transfers between devices with their start and end apart: 19 -> 19, of which waited for: 7 -> 10; matrix products, arithmetic and copies ran while one was open for 2% -> 2% of each run, Pallas kernels for 9% -> 9%
where the time goes in v16:
time: 57.5 us; the launch traced here: 57.4 us
  starting transfers between devices  25.9 us (45%)
  waiting for transfers between devices  18.9 us (33%)
  Pallas kernels  10.8 us (19%)
  other arithmetic  1.09 us (2%)
  between operations  0.78 us (1%)
    ppermute x19, starting transfers between devices, exchange(): return lax.ppermute(value, 'curve', pairs)  25.9 us
    ppermute x19, waiting for transfers between devices, exchange(): return lax.ppermute(value, 'curve', pairs)  18.9 us
    pallas_call x2, Pallas kernels, products(): pl.pallas_call(functools.partial(product_kernel, channels, pitch, chunks,...  9.28 us
    pallas_call x2, Pallas kernels, final_sum(): pl.pallas_call(functools.partial(final_kernel, like_shape[1], pitch, part...  1.48 us
  transfers between devices with their start and end apart: 19, of which 10 were waited for; matrix products, arithmetic and copies ran while one was open for 2% of the time, Pallas kernels for 9%

profile of v16, /device:TPU:0, one launch (start us, length us, event | category | flops | bytes accessed | tf_op | source)
XLA Modules:
  0.0 57.4 jit_solution(6567695237851641833)
XLA Ops:
  0.6 4.6 %shard_map.113 = (f32[13824,128]{1,0:T(8,128)S(1)}, bf16[3456,128]{1,0:T(8,128)(2,1)S(1)}, bf16[3456,128]{1,0:T(8,128)(2,1)S(1)}) custom-call(s32[144]{0:T(256)} %source_hbm.2, s32[144]{0:T(256)} %target_hbm.2, s32[1,16]{1,0:T(1,128)} %counts_hbm.2, bf16[1,69,1536]{2,1,0:T(8,128)(2,1)} %x_hbm.1, bf16[144,128,128]{2,1,0:T(8,128)(2,1)} %w_hbm.2), custom_call_target="tpu_custom_call" | custom-call | flops 325582848 | bytes 13565952 | tf_op jit(solution)/shard_map/pallas_call | solution.py:163
  5.3 0.5 collective-permute-start.1
  5.8 0.1 collective-permute-start
  5.9 2.0 %collective-permute-done.1 = bf16[3456,128]{1,0:T(8,128)(2,1)S(1)} collective-permute-done((bf16[3456,128]{1,0:T(8,128)(2,1)S(1)}, bf16[3456,128]{1,0:T(8,128)(2,1)S(1)}, u32[]{:S(2)}, u32[]{:S(2)}) %collective-permute-start.1) | collective-permute-done | bytes 884768 | tf_op jit(solution)/shard_map/ppermute | solution.py:193
  7.8 0.1 add_convert_fusion
  8.0 3.0 %collective-permute-start.2 = (bf16[2592,128]{1,0:T(8,128)(2,1)S(1)}, bf16[2592,128]{1,0:T(8,128)(2,1)S(1)}, u32[]{:S(2)}, u32[]{:S(2)}) collective-permute-start(bf16[2592,128]{1,0:T(8,128)(2,1)S(1)} %add_convert_fusion), channel_id=1, source_target_pairs={{0,4},{1,3},{2,6},{3,1},{4,0},{5,7},{6,2},{7,5},{8,12},{9,11},{10,... | collective-permute-start | bytes 1990664 | tf_op jit(solution)/shard_map/ppermute | solution.py:193
  11.1 4.7 %shard_map.114 = (f32[13824,128]{1,0:T(8,128)S(1)}, bf16[3456,128]{1,0:T(8,128)(2,1)S(1)}, bf16[3456,128]{1,0:T(8,128)(2,1)S(1)}) custom-call(s32[144]{0:T(256)} %source_hbm.3, s32[144]{0:T(256)} %target_hbm.3, s32[1,16]{1,0:T(1,128)} %counts_hbm.3, bf16[1,69,1536]{2,1,0:T(8,128)(2,1)} %x_hbm.2, bf16[144,128,128]{2,1,0:T(8,128)(2,1)} %w_hbm.3), custom_call_target="tpu_custom_call" | custom-call | flops 325582848 | bytes 13565952 | tf_op jit(solution)/shard_map/pallas_call | solution.py:163
  15.7 0.1 collective-permute-start.4
  15.8 1.3 %collective-permute-start.5 = (bf16[864,128]{1,0:T(8,128)(2,1)S(1)}, bf16[864,128]{1,0:T(8,128)(2,1)S(1)}, u32[]{:S(2)}, u32[]{:S(2)}) collective-permute-start(bf16[864,128]{1,0:T(8,128)(2,1)S(1)} %add_convert_fusion.5), channel_id=1, source_target_pairs={{0,4},{1,3},{2,6},{3,1},{4,0},{5,7},{6,2},{7,5},{8,12},{9,11},{10,... | collective-permute-start | bytes 663560 | tf_op jit(solution)/shard_map/ppermute | solution.py:193
  17.1 0.4 collective-permute-start.9
  17.5 2.1 %collective-permute-done.2 = bf16[2592,128]{1,0:T(8,128)(2,1)S(1)} collective-permute-done((bf16[2592,128]{1,0:T(8,128)(2,1)S(1)}, bf16[2592,128]{1,0:T(8,128)(2,1)S(1)}, u32[]{:S(2)}, u32[]{:S(2)}) %collective-permute-start.2) | collective-permute-done | bytes 663584 | tf_op jit(solution)/shard_map/ppermute | solution.py:193
  19.6 0.1 add_convert_fusion.2
  19.8 2.0 %collective-permute-start.3 = (bf16[1296,128]{1,0:T(8,128)(2,1)S(1)}, bf16[1296,128]{1,0:T(8,128)(2,1)S(1)}, u32[]{:S(2)}, u32[]{:S(2)}) collective-permute-start(bf16[1296,128]{1,0:T(8,128)(2,1)S(1)} %add_convert_fusion.2), channel_id=1, source_target_pairs={{0,2},{1,5},{2,0},{3,7},{4,6},{5,1},{6,4},{7,3},{8,10},{9,13},{10,... | collective-permute-start | bytes 995336 | tf_op jit(solution)/shard_map/ppermute | solution.py:193
  21.8 0.2 collective-permute-done.5
  22.0 0.1 add_convert_fusion.10
  22.1 2.3 %collective-permute-start.7 = (bf16[432,128]{1,0:T(8,128)(2,1)S(1)}, bf16[432,128]{1,0:T(8,128)(2,1)S(1)}, u32[]{:S(2)}, u32[]{:S(2)}) collective-permute-start(bf16[432,128]{1,0:T(8,128)(2,1)S(1)} %add_convert_fusion.10), channel_id=1, source_target_pairs={{0,2},{1,5},{2,0},{3,7},{4,6},{5,1},{6,4},{7,3},{8,10},{9,13},{10,... | collective-permute-start | bytes 331784 | tf_op jit(solution)/shard_map/ppermute | solution.py:193
  24.3 0.0 collective-permute-done.4
  24.3 0.1 add_convert_fusion.3
  24.4 0.1 add_convert_fusion.1
  24.5 1.6 %collective-permute-start.10 = (bf16[1728,128]{1,0:T(8,128)(2,1)S(1)}, bf16[1728,128]{1,0:T(8,128)(2,1)S(1)}, u32[]{:S(2)}, u32[]{:S(2)}) collective-permute-start(bf16[1728,128]{1,0:T(8,128)(2,1)S(1)} %add_convert_fusion.1), channel_id=1, source_target_pairs={{0,4},{1,3},{2,6},{3,1},{4,0},{5,7},{6,2},{7,5},{8,12},{9,11},{10,... | collective-permute-start | bytes 1327112 | tf_op jit(solution)/shard_map/ppermute | solution.py:193
  26.2 0.6 %collective-permute-start.13 = (bf16[1152,128]{1,0:T(8,128)(2,1)S(1)}, bf16[1152,128]{1,0:T(8,128)(2,1)S(1)}, u32[]{:S(2)}, u32[]{:S(2)}) collective-permute-start(bf16[1152,128]{1,0:T(8,128)(2,1)S(1)} %add_convert_fusion.3), channel_id=1, source_target_pairs={{0,2},{1,3},{2,0},{3,1},{4,6},{5,7},{6,4},{7,5},{8,10},{9,11},{10,... | collective-permute-start | bytes 884744 | tf_op jit(solution)/shard_map/ppermute | solution.py:193
  26.8 1.1 %collective-permute-done.3 = bf16[1296,128]{1,0:T(8,128)(2,1)S(1)} collective-permute-done((bf16[1296,128]{1,0:T(8,128)(2,1)S(1)}, bf16[1296,128]{1,0:T(8,128)(2,1)S(1)}, u32[]{:S(2)}, u32[]{:S(2)}) %collective-permute-start.3) | collective-permute-done | bytes 331808 | tf_op jit(solution)/shard_map/ppermute | solution.py:193
  27.8 0.1 add_convert_fusion.6
  28.0 3.5 %collective-permute-start.6 = (bf16[648,128]{1,0:T(8,128)(2,1)S(1)}, bf16[648,128]{1,0:T(8,128)(2,1)S(1)}, u32[]{:S(2)}, u32[]{:S(2)}) collective-permute-start(bf16[648,128]{1,0:T(8,128)(2,1)S(1)} %get-tuple-element.56), channel_id=1, source_target_pairs={{0,8},{1,9},{2,10},{3,11},{4,12},{5,13},{6,14},{7,15},{8,0},{9,1},... | collective-permute-start | bytes 497672 | tf_op jit(solution)/shard_map/ppermute | solution.py:193
  31.5 0.0 collective-permute-done.7
  31.5 0.1 convert_add_fusion.3
  31.6 2.2 %collective-permute-start.8 = (bf16[216,128]{1,0:T(8,128)(2,1)S(1)}, bf16[216,128]{1,0:T(8,128)(2,1)S(1)}, u32[]{:S(2)}, u32[]{:S(2)}) collective-permute-start(bf16[216,128]{1,0:T(8,128)(2,1)S(1)} %get-tuple-element.63), channel_id=1, source_target_pairs={{0,8},{1,9},{2,10},{3,11},{4,12},{5,13},{6,14},{7,15},{8,0},{9,1},... | collective-permute-start | bytes 165896 | tf_op jit(solution)/shard_map/ppermute | solution.py:193
  33.8 3.8 %collective-permute-done.10 = bf16[1728,128]{1,0:T(8,128)(2,1)S(1)} collective-permute-done((bf16[1728,128]{1,0:T(8,128)(2,1)S(1)}, bf16[1728,128]{1,0:T(8,128)(2,1)S(1)}, u32[]{:S(2)}, u32[]{:S(2)}) %collective-permute-start.10) | collective-permute-done | bytes 442400 | tf_op jit(solution)/shard_map/ppermute | solution.py:193
  37.6 0.1 add_convert_fusion.4
  37.7 0.1 collective-permute-start.12
  37.8 0.0 collective-permute-done.13
  37.8 2.0 %collective-permute-start.11 = (bf16[576,128]{1,0:T(8,128)(2,1)S(1)}, bf16[576,128]{1,0:T(8,128)(2,1)S(1)}, u32[]{:S(2)}, u32[]{:S(2)}) collective-permute-start(bf16[576,128]{1,0:T(8,128)(2,1)S(1)} %add_convert_fusion.8), channel_id=1, source_target_pairs={{0,2},{1,3},{2,0},{3,1},{4,6},{5,7},{6,4},{7,5},{8,10},{9,11},{10,... | collective-permute-start | bytes 442376 | tf_op jit(solution)/shard_map/ppermute | solution.py:193
  39.8 0.1 add_convert_fusion.7
  39.8 1.9 %collective-permute-start.15 = (bf16[576,128]{1,0:T(8,128)(2,1)S(1)}, bf16[576,128]{1,0:T(8,128)(2,1)S(1)}, u32[]{:S(2)}, u32[]{:S(2)}) collective-permute-start(bf16[576,128]{1,0:T(8,128)(2,1)S(1)} %add_convert_fusion.7), channel_id=1, source_target_pairs={{0,4},{1,5},{2,6},{3,7},{4,0},{5,1},{6,2},{7,3},{8,12},{9,13},{10,... | collective-permute-start | bytes 442376 | tf_op jit(solution)/shard_map/ppermute | solution.py:193
  41.8 3.5 %collective-permute-done.12 = bf16[864,128]{1,0:T(8,128)(2,1)S(1)} collective-permute-done((bf16[864,128]{1,0:T(8,128)(2,1)S(1)}, bf16[864,128]{1,0:T(8,128)(2,1)S(1)}, u32[]{:S(2)}, u32[]{:S(2)}) %collective-permute-start.12) | collective-permute-done | bytes 221216 | tf_op jit(solution)/shard_map/ppermute | solution.py:193
  45.3 0.1 convert_add_fusion.1
  45.4 0.1 collective-permute-start.16
  45.5 1.4 %collective-permute-done.11 = bf16[576,128]{1,0:T(8,128)(2,1)S(1)} collective-permute-done((bf16[576,128]{1,0:T(8,128)(2,1)S(1)}, bf16[576,128]{1,0:T(8,128)(2,1)S(1)}, u32[]{:S(2)}, u32[]{:S(2)}) %collective-permute-start.11) | collective-permute-done | bytes 147488 | tf_op jit(solution)/shard_map/ppermute | solution.py:193
  46.9 0.1 collective-permute-start.14
  47.0 0.1 convert_add_fusion.2
  47.1 1.6 %collective-permute-start.17 = (bf16[288,128]{1,0:T(8,128)(2,1)S(1)}, bf16[288,128]{1,0:T(8,128)(2,1)S(1)}, u32[]{:S(2)}, u32[]{:S(2)}) collective-permute-start(bf16[288,128]{1,0:T(8,128)(2,1)S(1)} %get-tuple-element.61), channel_id=1, source_target_pairs={{0,8},{1,9},{2,10},{3,11},{4,12},{5,13},{6,14},{7,15},{8,0},{9,1},... | collective-permute-start | bytes 221192 | tf_op jit(solution)/shard_map/ppermute | solution.py:193
  48.7 2.7 %collective-permute-done.14 = bf16[288,128]{1,0:T(8,128)(2,1)S(1)} collective-permute-done((bf16[288,128]{1,0:T(8,128)(2,1)S(1)}, bf16[288,128]{1,0:T(8,128)(2,1)S(1)}, u32[]{:S(2)}, u32[]{:S(2)}) %collective-permute-start.14) | collective-permute-done | bytes 73760 | tf_op jit(solution)/shard_map/ppermute | solution.py:193
  51.4 2.4 %collective-permute-start.18 = (bf16[144,128]{1,0:T(8,128)(2,1)S(1)}, bf16[144,128]{1,0:T(8,128)(2,1)S(1)}, u32[]{:S(2)}, u32[]{:S(2)}) collective-permute-start(bf16[144,128]{1,0:T(8,128)(2,1)S(1)} %get-tuple-element.65), channel_id=1, source_target_pairs={{0,8},{1,9},{2,10},{3,11},{4,12},{5,13},{6,14},{7,15},{8,0},{9,1},... | collective-permute-start | bytes 110600 | tf_op jit(solution)/shard_map/ppermute | solution.py:193
  53.8 0.0 collective-permute-done.8.refs_3_
  53.8 0.7 %shard_map.115 = bf16[1,69,1536]{2,1,0:T(8,128)(2,1)} custom-call(f32[648,128]{1,0:T(8,128)S(1)} %get-tuple-element.57.refs_0_, bf16[648,128]{1,0:T(8,128)(2,1)S(1)} %collective-permute-done.6.refs_1_, f32[216,128]{1,0:T(8,128)S(1)} %get-tuple-element.62.refs_2_, bf16[216,128]{1,0:T(8,128)(2,1)S(1)} %collective-permute-done.8.refs_3_), custom_call_target="tpu_custom_call" | custom-call | tf_op jit(solution)/shard_map/pallas_call | solution.py:247
  54.5 1.7 %collective-permute-done.17.refs_3_ = bf16[288,128]{1,0:T(8,128)(2,1)S(1)} collective-permute-done((bf16[288,128]{1,0:T(8,128)(2,1)S(1)}, bf16[288,128]{1,0:T(8,128)(2,1)S(1)}, u32[]{:S(2)}, u32[]{:S(2)}) %collective-permute-start.17) | collective-permute-done | bytes 73760 | tf_op jit(solution)/shard_map/ppermute | solution.py:193
  56.3 0.4 collective-permute-done.18.refs_5_
  56.7 0.7 %shard_map.116 = bf16[1,69,1536]{2,1,0:T(8,128)(2,1)} custom-call(f32[432,128]{1,0:T(8,128)S(1)} %get-tuple-element.58.refs_0_, bf16[432,128]{1,0:T(8,128)(2,1)S(1)} %collective-permute-done.16.refs_1_, f32[288,128]{1,0:T(8,128)S(1)} %get-tuple-element.60.refs_2_, bf16[288,128]{1,0:T(8,128)(2,1)S(1)} %collective-permute-done.17.refs_3_, ...), custom_call_target="tpu_custom_call" | custom-call | tf_op jit(solution)/shard_map/pallas_call | solution.py:247
  (9 shorter events, 0.2 us)
Async XLA Ops:
  5.3 2.6 %collective-permute-start.1 = (bf16[3456,128]{1,0:T(8,128)(2,1)S(1)}, bf16[3456,128]{1,0:T(8,128)(2,1)S(1)}, u32[]{:S(2)}, u32[]{:S(2)}) collective-permute-start(bf16[3456,128]{1,0:T(8,128)(2,1)S(1)} %get-tuple-element.31), channel_id=1, source_target_pairs={{0,1},{1,0},{2,3},{3,2},{4,5},{5,4},{6,7},{7,6},{8,9},{9,8},{10,11... | collective-permute-start | bytes 2654216 | tf_op jit(solution)/shard_map/ppermute | solution.py:193
  5.8 5.3 %collective-permute-start = (bf16[3456,128]{1,0:T(8,128)(2,1)S(1)}, bf16[3456,128]{1,0:T(8,128)(2,1)S(1)}, u32[]{:S(2)}, u32[]{:S(2)}) collective-permute-start(bf16[3456,128]{1,0:T(8,128)(2,1)S(1)} %get-tuple-element.30), channel_id=1, source_target_pairs={{0,1},{1,0},{2,3},{3,2},{4,5},{5,4},{6,7},{7,6},{8,9},{9,8},{10,11... | collective-permute-start | bytes 2654216 | tf_op jit(solution)/shard_map/ppermute | solution.py:193
  8.0 11.7 %collective-permute-start.2 = (bf16[2592,128]{1,0:T(8,128)(2,1)S(1)}, bf16[2592,128]{1,0:T(8,128)(2,1)S(1)}, u32[]{:S(2)}, u32[]{:S(2)}) collective-permute-start(bf16[2592,128]{1,0:T(8,128)(2,1)S(1)} %add_convert_fusion), channel_id=1, source_target_pairs={{0,4},{1,3},{2,6},{3,1},{4,0},{5,7},{6,2},{7,5},{8,12},{9,11},{10,... | collective-permute-start | bytes 1990664 | tf_op jit(solution)/shard_map/ppermute | solution.py:193
  15.7 8.6 %collective-permute-start.4 = (bf16[3456,128]{1,0:T(8,128)(2,1)S(1)}, bf16[3456,128]{1,0:T(8,128)(2,1)S(1)}, u32[]{:S(2)}, u32[]{:S(2)}) collective-permute-start(bf16[3456,128]{1,0:T(8,128)(2,1)S(1)} %get-tuple-element.36), channel_id=1, source_target_pairs={{0,1},{1,0},{2,3},{3,2},{4,5},{5,4},{6,7},{7,6},{8,9},{9,8},{10,11... | collective-permute-start | bytes 2654216 | tf_op jit(solution)/shard_map/ppermute | solution.py:193
  15.8 6.2 %collective-permute-start.5 = (bf16[864,128]{1,0:T(8,128)(2,1)S(1)}, bf16[864,128]{1,0:T(8,128)(2,1)S(1)}, u32[]{:S(2)}, u32[]{:S(2)}) collective-permute-start(bf16[864,128]{1,0:T(8,128)(2,1)S(1)} %add_convert_fusion.5), channel_id=1, source_target_pairs={{0,4},{1,3},{2,6},{3,1},{4,0},{5,7},{6,2},{7,5},{8,12},{9,11},{10,... | collective-permute-start | bytes 663560 | tf_op jit(solution)/shard_map/ppermute | solution.py:193
  17.1 16.7 %collective-permute-start.9 = (bf16[3456,128]{1,0:T(8,128)(2,1)S(1)}, bf16[3456,128]{1,0:T(8,128)(2,1)S(1)}, u32[]{:S(2)}, u32[]{:S(2)}) collective-permute-start(bf16[3456,128]{1,0:T(8,128)(2,1)S(1)} %get-tuple-element.35), channel_id=1, source_target_pairs={{0,1},{1,0},{2,3},{3,2},{4,5},{5,4},{6,7},{7,6},{8,9},{9,8},{10,11... | collective-permute-start | bytes 2654216 | tf_op jit(solution)/shard_map/ppermute | solution.py:193
  19.8 8.1 %collective-permute-start.3 = (bf16[1296,128]{1,0:T(8,128)(2,1)S(1)}, bf16[1296,128]{1,0:T(8,128)(2,1)S(1)}, u32[]{:S(2)}, u32[]{:S(2)}) collective-permute-start(bf16[1296,128]{1,0:T(8,128)(2,1)S(1)} %add_convert_fusion.2), channel_id=1, source_target_pairs={{0,2},{1,5},{2,0},{3,7},{4,6},{5,1},{6,4},{7,3},{8,10},{9,13},{10,... | collective-permute-start | bytes 995336 | tf_op jit(solution)/shard_map/ppermute | solution.py:193
  22.1 9.5 %collective-permute-start.7 = (bf16[432,128]{1,0:T(8,128)(2,1)S(1)}, bf16[432,128]{1,0:T(8,128)(2,1)S(1)}, u32[]{:S(2)}, u32[]{:S(2)}) collective-permute-start(bf16[432,128]{1,0:T(8,128)(2,1)S(1)} %add_convert_fusion.10), channel_id=1, source_target_pairs={{0,2},{1,5},{2,0},{3,7},{4,6},{5,1},{6,4},{7,3},{8,10},{9,13},{10,... | collective-permute-start | bytes 331784 | tf_op jit(solution)/shard_map/ppermute | solution.py:193
  24.5 13.1 %collective-permute-start.10 = (bf16[1728,128]{1,0:T(8,128)(2,1)S(1)}, bf16[1728,128]{1,0:T(8,128)(2,1)S(1)}, u32[]{:S(2)}, u32[]{:S(2)}) collective-permute-start(bf16[1728,128]{1,0:T(8,128)(2,1)S(1)} %add_convert_fusion.1), channel_id=1, source_target_pairs={{0,4},{1,3},{2,6},{3,1},{4,0},{5,7},{6,2},{7,5},{8,12},{9,11},{10,... | collective-permute-start | bytes 1327112 | tf_op jit(solution)/shard_map/ppermute | solution.py:193
  26.2 11.6 %collective-permute-start.13 = (bf16[1152,128]{1,0:T(8,128)(2,1)S(1)}, bf16[1152,128]{1,0:T(8,128)(2,1)S(1)}, u32[]{:S(2)}, u32[]{:S(2)}) collective-permute-start(bf16[1152,128]{1,0:T(8,128)(2,1)S(1)} %add_convert_fusion.3), channel_id=1, source_target_pairs={{0,2},{1,3},{2,0},{3,1},{4,6},{5,7},{6,4},{7,5},{8,10},{9,11},{10,... | collective-permute-start | bytes 884744 | tf_op jit(solution)/shard_map/ppermute | solution.py:193
  28.0 25.8 %collective-permute-start.6 = (bf16[648,128]{1,0:T(8,128)(2,1)S(1)}, bf16[648,128]{1,0:T(8,128)(2,1)S(1)}, u32[]{:S(2)}, u32[]{:S(2)}) collective-permute-start(bf16[648,128]{1,0:T(8,128)(2,1)S(1)} %get-tuple-element.56), channel_id=1, source_target_pairs={{0,8},{1,9},{2,10},{3,11},{4,12},{5,13},{6,14},{7,15},{8,0},{9,1},... | collective-permute-start | bytes 497672 | tf_op jit(solution)/shard_map/ppermute | solution.py:193
  31.6 22.2 %collective-permute-start.8 = (bf16[216,128]{1,0:T(8,128)(2,1)S(1)}, bf16[216,128]{1,0:T(8,128)(2,1)S(1)}, u32[]{:S(2)}, u32[]{:S(2)}) collective-permute-start(bf16[216,128]{1,0:T(8,128)(2,1)S(1)} %get-tuple-element.63), channel_id=1, source_target_pairs={{0,8},{1,9},{2,10},{3,11},{4,12},{5,13},{6,14},{7,15},{8,0},{9,1},... | collective-permute-start | bytes 165896 | tf_op jit(solution)/shard_map/ppermute | solution.py:193
  37.7 7.6 %collective-permute-start.12 = (bf16[864,128]{1,0:T(8,128)(2,1)S(1)}, bf16[864,128]{1,0:T(8,128)(2,1)S(1)}, u32[]{:S(2)}, u32[]{:S(2)}) collective-permute-start(bf16[864,128]{1,0:T(8,128)(2,1)S(1)} %add_convert_fusion.4), channel_id=1, source_target_pairs={{0,2},{1,5},{2,0},{3,7},{4,6},{5,1},{6,4},{7,3},{8,10},{9,13},{10,... | collective-permute-start | bytes 663560 | tf_op jit(solution)/shard_map/ppermute | solution.py:193
  37.8 9.1 %collective-permute-start.11 = (bf16[576,128]{1,0:T(8,128)(2,1)S(1)}, bf16[576,128]{1,0:T(8,128)(2,1)S(1)}, u32[]{:S(2)}, u32[]{:S(2)}) collective-permute-start(bf16[576,128]{1,0:T(8,128)(2,1)S(1)} %add_convert_fusion.8), channel_id=1, source_target_pairs={{0,2},{1,3},{2,0},{3,1},{4,6},{5,7},{6,4},{7,5},{8,10},{9,11},{10,... | collective-permute-start | bytes 442376 | tf_op jit(solution)/shard_map/ppermute | solution.py:193
  39.8 7.1 %collective-permute-start.15 = (bf16[576,128]{1,0:T(8,128)(2,1)S(1)}, bf16[576,128]{1,0:T(8,128)(2,1)S(1)}, u32[]{:S(2)}, u32[]{:S(2)}) collective-permute-start(bf16[576,128]{1,0:T(8,128)(2,1)S(1)} %add_convert_fusion.7), channel_id=1, source_target_pairs={{0,4},{1,5},{2,6},{3,7},{4,0},{5,1},{6,2},{7,3},{8,12},{9,13},{10,... | collective-permute-start | bytes 442376 | tf_op jit(solution)/shard_map/ppermute | solution.py:193
  45.4 9.2 %collective-permute-start.16 = (bf16[432,128]{1,0:T(8,128)(2,1)S(1)}, bf16[432,128]{1,0:T(8,128)(2,1)S(1)}, u32[]{:S(2)}, u32[]{:S(2)}) collective-permute-start(bf16[432,128]{1,0:T(8,128)(2,1)S(1)} %get-tuple-element.59), channel_id=1, source_target_pairs={{0,8},{1,9},{2,10},{3,11},{4,12},{5,13},{6,14},{7,15},{8,0},{9,1},... | collective-permute-start | bytes 331784 | tf_op jit(solution)/shard_map/ppermute | solution.py:193
  46.9 4.4 %collective-permute-start.14 = (bf16[288,128]{1,0:T(8,128)(2,1)S(1)}, bf16[288,128]{1,0:T(8,128)(2,1)S(1)}, u32[]{:S(2)}, u32[]{:S(2)}) collective-permute-start(bf16[288,128]{1,0:T(8,128)(2,1)S(1)} %add_convert_fusion.12), channel_id=1, source_target_pairs={{0,4},{1,5},{2,6},{3,7},{4,0},{5,1},{6,2},{7,3},{8,12},{9,13},{10,... | collective-permute-start | bytes 221192 | tf_op jit(solution)/shard_map/ppermute | solution.py:193
  47.1 9.2 %collective-permute-start.17 = (bf16[288,128]{1,0:T(8,128)(2,1)S(1)}, bf16[288,128]{1,0:T(8,128)(2,1)S(1)}, u32[]{:S(2)}, u32[]{:S(2)}) collective-permute-start(bf16[288,128]{1,0:T(8,128)(2,1)S(1)} %get-tuple-element.61), channel_id=1, source_target_pairs={{0,8},{1,9},{2,10},{3,11},{4,12},{5,13},{6,14},{7,15},{8,0},{9,1},... | collective-permute-start | bytes 221192 | tf_op jit(solution)/shard_map/ppermute | solution.py:193
  51.4 5.3 %collective-permute-start.18 = (bf16[144,128]{1,0:T(8,128)(2,1)S(1)}, bf16[144,128]{1,0:T(8,128)(2,1)S(1)}, u32[]{:S(2)}, u32[]{:S(2)}) collective-permute-start(bf16[144,128]{1,0:T(8,128)(2,1)S(1)} %get-tuple-element.65), channel_id=1, source_target_pairs={{0,8},{1,9},{2,10},{3,11},{4,12},{5,13},{6,14},{7,15},{8,0},{9,1},... | collective-permute-start | bytes 110600 | tf_op jit(solution)/shard_map/ppermute | solution.py:193

commit v17 on v16

--- a/solution.py
+++ b/solution.py
@@ -269,10 +269,10 @@
     one, two = remaps
     pitch = round_up(one[-1][1], 8)
     tiles = one[-1][2] // LANES
-    half, most, more = tiles // 2, tiles * 3 // 4, tiles * 5 // 6
+    some, most, more = tiles * 5 // 12, tiles * 3 // 4, tiles * 5 // 6
     plans = (
         [(0, most, MIXED), (most, tiles, MIXED)],
-        [(0, half, MIXED), (half, more, STRAIGHT), (more, tiles, STRAIGHT)],
+        [(0, some, MIXED), (some, more, STRAIGHT), (more, tiles, STRAIGHT)],
     )
     ones, twos = [[Chain(chunk, devices, pitch) for chunk in chunks] for chunks in plans]
     order = Order()

time: 57.5 us -> 60.5 us (1.052)
  starting transfers between devices: 25.9 us -> 31.7 us
  waiting for transfers between devices: 18.9 us -> 16 us
    ppermute x19, starting transfers between devices: 25.9 us -> 31.7 us  [exchange(): return lax.ppermute(value, 'curve', pairs)]
    ppermute x19, waiting for transfers between devices: 18.9 us -> 16 us  [exchange(): return lax.ppermute(value, 'curve', pairs)]
  transfers between devices with their start and end apart: 19 -> 19, of which waited for: 10 -> 9; matrix products, arithmetic and copies ran while one was open for 2% -> 2% of each run, Pallas kernels for 9% -> 9%
where the time goes in v17:
time: 60.5 us; the launch traced here: 60.3 us
  starting transfers between devices  31.7 us (52%)
  waiting for transfers between devices  16 us (26%)
  Pallas kernels  10.7 us (18%)
  other arithmetic  1.16 us (2%)
  between operations  0.73 us (1%)
    ppermute x19, starting transfers between devices, exchange(): return lax.ppermute(value, 'curve', pairs)  31.7 us
    ppermute x19, waiting for transfers between devices, exchange(): return lax.ppermute(value, 'curve', pairs)  16 us
    pallas_call x2, Pallas kernels, products(): pl.pallas_call(functools.partial(product_kernel, channels, pitch, chunks,...  9.24 us
    pallas_call x2, Pallas kernels, final_sum(): pl.pallas_call(functools.partial(final_kernel, like_shape[1], pitch, part...  1.48 us
  transfers between devices with their start and end apart: 19, of which 9 were waited for; matrix products, arithmetic and copies ran while one was open for 2% of the time, Pallas kernels for 9%

profile of v17, /device:TPU:0, one launch (start us, length us, event | category | flops | bytes accessed | tf_op | source)
XLA Modules:
  0.0 60.3 jit_solution(7926548770590314830)
XLA Ops:
  0.6 4.6 %shard_map.113 = (f32[13824,128]{1,0:T(8,128)S(1)}, bf16[3456,128]{1,0:T(8,128)(2,1)S(1)}, bf16[3456,128]{1,0:T(8,128)(2,1)S(1)}) custom-call(s32[144]{0:T(256)} %source_hbm.2, s32[144]{0:T(256)} %target_hbm.2, s32[1,16]{1,0:T(1,128)} %counts_hbm.2, bf16[1,69,1536]{2,1,0:T(8,128)(2,1)} %x_hbm.1, bf16[144,128,128]{2,1,0:T(8,128)(2,1)} %w_hbm.2), custom_call_target="tpu_custom_call" | custom-call | flops 325582848 | bytes 13565952 | tf_op jit(solution)/shard_map/pallas_call | solution.py:163
  5.3 0.5 collective-permute-start.1
  5.8 0.1 collective-permute-start
  5.8 2.0 %collective-permute-done.1 = bf16[3456,128]{1,0:T(8,128)(2,1)S(1)} collective-permute-done((bf16[3456,128]{1,0:T(8,128)(2,1)S(1)}, bf16[3456,128]{1,0:T(8,128)(2,1)S(1)}, u32[]{:S(2)}, u32[]{:S(2)}) %collective-permute-start.1) | collective-permute-done | bytes 884768 | tf_op jit(solution)/shard_map/ppermute | solution.py:193
  7.8 0.1 add_convert_fusion
  8.0 3.0 %collective-permute-start.2 = (bf16[2592,128]{1,0:T(8,128)(2,1)S(1)}, bf16[2592,128]{1,0:T(8,128)(2,1)S(1)}, u32[]{:S(2)}, u32[]{:S(2)}) collective-permute-start(bf16[2592,128]{1,0:T(8,128)(2,1)S(1)} %add_convert_fusion), channel_id=1, source_target_pairs={{0,4},{1,3},{2,6},{3,1},{4,0},{5,7},{6,2},{7,5},{8,12},{9,11},{10,... | collective-permute-start | bytes 1990664 | tf_op jit(solution)/shard_map/ppermute | solution.py:193
  11.0 0.0 collective-permute-done
  11.0 4.6 %shard_map.114 = (f32[13824,128]{1,0:T(8,128)S(1)}, bf16[3456,128]{1,0:T(8,128)(2,1)S(1)}, bf16[3456,128]{1,0:T(8,128)(2,1)S(1)}) custom-call(s32[144]{0:T(256)} %source_hbm.3, s32[144]{0:T(256)} %target_hbm.3, s32[1,16]{1,0:T(1,128)} %counts_hbm.3, bf16[1,69,1536]{2,1,0:T(8,128)(2,1)} %x_hbm.2, bf16[144,128,128]{2,1,0:T(8,128)(2,1)} %w_hbm.3), custom_call_target="tpu_custom_call" | custom-call | flops 325582848 | bytes 13565952 | tf_op jit(solution)/shard_map/pallas_call | solution.py:163
  15.7 0.1 collective-permute-start.4
  15.7 1.4 %collective-permute-start.5 = (bf16[864,128]{1,0:T(8,128)(2,1)S(1)}, bf16[864,128]{1,0:T(8,128)(2,1)S(1)}, u32[]{:S(2)}, u32[]{:S(2)}) collective-permute-start(bf16[864,128]{1,0:T(8,128)(2,1)S(1)} %add_convert_fusion.4), channel_id=1, source_target_pairs={{0,4},{1,3},{2,6},{3,1},{4,0},{5,7},{6,2},{7,5},{8,12},{9,11},{10,... | collective-permute-start | bytes 663560 | tf_op jit(solution)/shard_map/ppermute | solution.py:193
  17.1 0.4 collective-permute-start.9
  17.5 2.1 %collective-permute-done.2 = bf16[2592,128]{1,0:T(8,128)(2,1)S(1)} collective-permute-done((bf16[2592,128]{1,0:T(8,128)(2,1)S(1)}, bf16[2592,128]{1,0:T(8,128)(2,1)S(1)}, u32[]{:S(2)}, u32[]{:S(2)}) %collective-permute-start.2) | collective-permute-done | bytes 663584 | tf_op jit(solution)/shard_map/ppermute | solution.py:193
  19.6 0.1 add_convert_fusion.3
  19.7 2.0 %collective-permute-start.3 = (bf16[1296,128]{1,0:T(8,128)(2,1)S(1)}, bf16[1296,128]{1,0:T(8,128)(2,1)S(1)}, u32[]{:S(2)}, u32[]{:S(2)}) collective-permute-start(bf16[1296,128]{1,0:T(8,128)(2,1)S(1)} %add_convert_fusion.3), channel_id=1, source_target_pairs={{0,2},{1,5},{2,0},{3,7},{4,6},{5,1},{6,4},{7,3},{8,10},{9,13},{10,... | collective-permute-start | bytes 995336 | tf_op jit(solution)/shard_map/ppermute | solution.py:193
  21.8 0.2 collective-permute-done.5
  22.0 2.3 %collective-permute-start.7 = (bf16[432,128]{1,0:T(8,128)(2,1)S(1)}, bf16[432,128]{1,0:T(8,128)(2,1)S(1)}, u32[]{:S(2)}, u32[]{:S(2)}) collective-permute-start(bf16[432,128]{1,0:T(8,128)(2,1)S(1)} %add_convert_fusion.9), channel_id=1, source_target_pairs={{0,2},{1,5},{2,0},{3,7},{4,6},{5,1},{6,4},{7,3},{8,10},{9,13},{10,... | collective-permute-start | bytes 331784 | tf_op jit(solution)/shard_map/ppermute | solution.py:193
  24.3 0.0 collective-permute-done.4
  24.3 0.1 add_convert_fusion.1
  24.5 1.6 %collective-permute-start.10 = (bf16[1440,128]{1,0:T(8,128)(2,1)S(1)}, bf16[1440,128]{1,0:T(8,128)(2,1)S(1)}, u32[]{:S(2)}, u32[]{:S(2)}) collective-permute-start(bf16[1440,128]{1,0:T(8,128)(2,1)S(1)} %get-tuple-element.67), channel_id=1, source_target_pairs={{0,4},{1,3},{2,6},{3,1},{4,0},{5,7},{6,2},{7,5},{8,12},{9,11},{10,... | collective-permute-start | bytes 1105928 | tf_op jit(solution)/shard_map/ppermute | solution.py:193
  26.2 0.6 collective-permute-start.13
  26.7 1.1 %collective-permute-done.3 = bf16[1296,128]{1,0:T(8,128)(2,1)S(1)} collective-permute-done((bf16[1296,128]{1,0:T(8,128)(2,1)S(1)}, bf16[1296,128]{1,0:T(8,128)(2,1)S(1)}, u32[]{:S(2)}, u32[]{:S(2)}) %collective-permute-start.3) | collective-permute-done | bytes 331808 | tf_op jit(solution)/shard_map/ppermute | solution.py:193
  27.8 0.2 add_convert_fusion.7
  28.0 3.6 %collective-permute-start.6 = (bf16[648,128]{1,0:T(8,128)(2,1)S(1)}, bf16[648,128]{1,0:T(8,128)(2,1)S(1)}, u32[]{:S(2)}, u32[]{:S(2)}) collective-permute-start(bf16[648,128]{1,0:T(8,128)(2,1)S(1)} %get-tuple-element.56), channel_id=1, source_target_pairs={{0,8},{1,9},{2,10},{3,11},{4,12},{5,13},{6,14},{7,15},{8,0},{9,1},... | collective-permute-start | bytes 497672 | tf_op jit(solution)/shard_map/ppermute | solution.py:193
  31.6 0.0 collective-permute-done.7
  31.6 0.1 convert_add_fusion.3
  31.6 2.2 %collective-permute-start.8 = (bf16[216,128]{1,0:T(8,128)(2,1)S(1)}, bf16[216,128]{1,0:T(8,128)(2,1)S(1)}, u32[]{:S(2)}, u32[]{:S(2)}) collective-permute-start(bf16[216,128]{1,0:T(8,128)(2,1)S(1)} %get-tuple-element.63), channel_id=1, source_target_pairs={{0,8},{1,9},{2,10},{3,11},{4,12},{5,13},{6,14},{7,15},{8,0},{9,1},... | collective-permute-start | bytes 165896 | tf_op jit(solution)/shard_map/ppermute | solution.py:193
  33.8 0.0 collective-permute-done.9
  33.8 1.4 %collective-permute-done.10 = bf16[1440,128]{1,0:T(8,128)(2,1)S(1)} collective-permute-done((bf16[1440,128]{1,0:T(8,128)(2,1)S(1)}, bf16[1440,128]{1,0:T(8,128)(2,1)S(1)}, u32[]{:S(2)}, u32[]{:S(2)}) %collective-permute-start.10) | collective-permute-done | bytes 368672 | tf_op jit(solution)/shard_map/ppermute | solution.py:193
  35.2 0.1 add_convert_fusion.6
  35.3 0.2 collective-permute-start.12
  35.5 2.6 %collective-permute-done.13 = bf16[1440,128]{1,0:T(8,128)(2,1)S(1)} collective-permute-done((bf16[1440,128]{1,0:T(8,128)(2,1)S(1)}, bf16[1440,128]{1,0:T(8,128)(2,1)S(1)}, u32[]{:S(2)}, u32[]{:S(2)}) %collective-permute-start.13) | collective-permute-done | bytes 368672 | tf_op jit(solution)/shard_map/ppermute | solution.py:193
  38.1 2.4 %collective-permute-start.11 = (bf16[576,128]{1,0:T(8,128)(2,1)S(1)}, bf16[576,128]{1,0:T(8,128)(2,1)S(1)}, u32[]{:S(2)}, u32[]{:S(2)}) collective-permute-start(bf16[576,128]{1,0:T(8,128)(2,1)S(1)} %add_convert_fusion.8), channel_id=1, source_target_pairs={{0,2},{1,3},{2,0},{3,1},{4,6},{5,7},{6,4},{7,5},{8,10},{9,11},{10,... | collective-permute-start | bytes 442376 | tf_op jit(solution)/shard_map/ppermute | solution.py:193
  40.5 0.1 add_convert_fusion.5
  40.6 2.8 %collective-permute-start.15 = (bf16[720,128]{1,0:T(8,128)(2,1)S(1)}, bf16[720,128]{1,0:T(8,128)(2,1)S(1)}, u32[]{:S(2)}, u32[]{:S(2)}) collective-permute-start(bf16[720,128]{1,0:T(8,128)(2,1)S(1)} %add_convert_fusion.5), channel_id=1, source_target_pairs={{0,4},{1,5},{2,6},{3,7},{4,0},{5,1},{6,2},{7,3},{8,12},{9,13},{10,... | collective-permute-start | bytes 552968 | tf_op jit(solution)/shard_map/ppermute | solution.py:193
  43.4 0.0 collective-permute-done.12
  43.4 0.1 convert_add_fusion.2
  43.5 2.6 %collective-permute-start.16 = (bf16[360,128]{1,0:T(8,128)(2,1)S(1)}, bf16[360,128]{1,0:T(8,128)(2,1)S(1)}, u32[]{:S(2)}, u32[]{:S(2)}) collective-permute-start(bf16[360,128]{1,0:T(8,128)(2,1)S(1)} %get-tuple-element.61), channel_id=1, source_target_pairs={{0,8},{1,9},{2,10},{3,11},{4,12},{5,13},{6,14},{7,15},{8,0},{9,1},... | collective-permute-start | bytes 276488 | tf_op jit(solution)/shard_map/ppermute | solution.py:193
  46.2 1.8 %collective-permute-start.14 = (bf16[288,128]{1,0:T(8,128)(2,1)S(1)}, bf16[288,128]{1,0:T(8,128)(2,1)S(1)}, u32[]{:S(2)}, u32[]{:S(2)}) collective-permute-start(bf16[288,128]{1,0:T(8,128)(2,1)S(1)} %add_convert_fusion.12), channel_id=1, source_target_pairs={{0,4},{1,5},{2,6},{3,7},{4,0},{5,1},{6,2},{7,3},{8,12},{9,13},{10,... | collective-permute-start | bytes 221192 | tf_op jit(solution)/shard_map/ppermute | solution.py:193
  48.0 2.0 %collective-permute-done.15 = bf16[720,128]{1,0:T(8,128)(2,1)S(1)} collective-permute-done((bf16[720,128]{1,0:T(8,128)(2,1)S(1)}, bf16[720,128]{1,0:T(8,128)(2,1)S(1)}, u32[]{:S(2)}, u32[]{:S(2)}) %collective-permute-start.15) | collective-permute-done | bytes 184352 | tf_op jit(solution)/shard_map/ppermute | solution.py:193
  50.0 0.1 convert_add_fusion.1
  50.1 2.9 %collective-permute-start.17 = (bf16[360,128]{1,0:T(8,128)(2,1)S(1)}, bf16[360,128]{1,0:T(8,128)(2,1)S(1)}, u32[]{:S(2)}, u32[]{:S(2)}) collective-permute-start(bf16[360,128]{1,0:T(8,128)(2,1)S(1)} %get-tuple-element.59), channel_id=1, source_target_pairs={{0,8},{1,9},{2,10},{3,11},{4,12},{5,13},{6,14},{7,15},{8,0},{9,1},... | collective-permute-start | bytes 276488 | tf_op jit(solution)/shard_map/ppermute | solution.py:193
  53.0 0.0 collective-permute-done.14
  53.0 1.2 %collective-permute-start.18 = (bf16[144,128]{1,0:T(8,128)(2,1)S(1)}, bf16[144,128]{1,0:T(8,128)(2,1)S(1)}, u32[]{:S(2)}, u32[]{:S(2)}) collective-permute-start(bf16[144,128]{1,0:T(8,128)(2,1)S(1)} %get-tuple-element.65), channel_id=1, source_target_pairs={{0,8},{1,9},{2,10},{3,11},{4,12},{5,13},{6,14},{7,15},{8,0},{9,1},... | collective-permute-start | bytes 110600 | tf_op jit(solution)/shard_map/ppermute | solution.py:193
  54.2 0.0 collective-permute-done.6.refs_1_
  54.2 0.7 %shard_map.115 = bf16[1,69,1536]{2,1,0:T(8,128)(2,1)} custom-call(f32[648,128]{1,0:T(8,128)S(1)} %get-tuple-element.57.refs_0_, bf16[648,128]{1,0:T(8,128)(2,1)S(1)} %collective-permute-done.6.refs_1_, f32[216,128]{1,0:T(8,128)S(1)} %get-tuple-element.62.refs_2_, bf16[216,128]{1,0:T(8,128)(2,1)S(1)} %collective-permute-done.8.refs_3_), custom_call_target="tpu_custom_call" | custom-call | tf_op jit(solution)/shard_map/pallas_call | solution.py:247
  55.0 3.8 %collective-permute-done.17.refs_3_ = bf16[360,128]{1,0:T(8,128)(2,1)S(1)} collective-permute-done((bf16[360,128]{1,0:T(8,128)(2,1)S(1)}, bf16[360,128]{1,0:T(8,128)(2,1)S(1)}, u32[]{:S(2)}, u32[]{:S(2)}) %collective-permute-start.17) | collective-permute-done | bytes 92192 | tf_op jit(solution)/shard_map/ppermute | solution.py:193
  58.8 0.8 %collective-permute-done.18.refs_5_ = bf16[144,128]{1,0:T(8,128)(2,1)S(1)} collective-permute-done((bf16[144,128]{1,0:T(8,128)(2,1)S(1)}, bf16[144,128]{1,0:T(8,128)(2,1)S(1)}, u32[]{:S(2)}, u32[]{:S(2)}) %collective-permute-start.18) | collective-permute-done | bytes 36896 | tf_op jit(solution)/shard_map/ppermute | solution.py:193
  59.6 0.7 %shard_map.116 = bf16[1,69,1536]{2,1,0:T(8,128)(2,1)} custom-call(f32[360,128]{1,0:T(8,128)S(1)} %get-tuple-element.60.refs_0_, bf16[360,128]{1,0:T(8,128)(2,1)S(1)} %collective-permute-done.16.refs_1_, f32[360,128]{1,0:T(8,128)S(1)} %get-tuple-element.58.refs_2_, bf16[360,128]{1,0:T(8,128)(2,1)S(1)} %collective-permute-done.17.refs_3_, ...), custom_call_target="tpu_custom_call" | custom-call | tf_op jit(solution)/shard_map/pallas_call | solution.py:247
  (8 shorter events, 0.2 us)
Async XLA Ops:
  5.3 2.6 %collective-permute-start.1 = (bf16[3456,128]{1,0:T(8,128)(2,1)S(1)}, bf16[3456,128]{1,0:T(8,128)(2,1)S(1)}, u32[]{:S(2)}, u32[]{:S(2)}) collective-permute-start(bf16[3456,128]{1,0:T(8,128)(2,1)S(1)} %get-tuple-element.31), channel_id=1, source_target_pairs={{0,1},{1,0},{2,3},{3,2},{4,5},{5,4},{6,7},{7,6},{8,9},{9,8},{10,11... | collective-permute-start | bytes 2654216 | tf_op jit(solution)/shard_map/ppermute | solution.py:193
  5.8 5.2 %collective-permute-start = (bf16[3456,128]{1,0:T(8,128)(2,1)S(1)}, bf16[3456,128]{1,0:T(8,128)(2,1)S(1)}, u32[]{:S(2)}, u32[]{:S(2)}) collective-permute-start(bf16[3456,128]{1,0:T(8,128)(2,1)S(1)} %get-tuple-element.30), channel_id=1, source_target_pairs={{0,1},{1,0},{2,3},{3,2},{4,5},{5,4},{6,7},{7,6},{8,9},{9,8},{10,11... | collective-permute-start | bytes 2654216 | tf_op jit(solution)/shard_map/ppermute | solution.py:193
  8.0 11.7 %collective-permute-start.2 = (bf16[2592,128]{1,0:T(8,128)(2,1)S(1)}, bf16[2592,128]{1,0:T(8,128)(2,1)S(1)}, u32[]{:S(2)}, u32[]{:S(2)}) collective-permute-start(bf16[2592,128]{1,0:T(8,128)(2,1)S(1)} %add_convert_fusion), channel_id=1, source_target_pairs={{0,4},{1,3},{2,6},{3,1},{4,0},{5,7},{6,2},{7,5},{8,12},{9,11},{10,... | collective-permute-start | bytes 1990664 | tf_op jit(solution)/shard_map/ppermute | solution.py:193
  15.7 8.7 %collective-permute-start.4 = (bf16[3456,128]{1,0:T(8,128)(2,1)S(1)}, bf16[3456,128]{1,0:T(8,128)(2,1)S(1)}, u32[]{:S(2)}, u32[]{:S(2)}) collective-permute-start(bf16[3456,128]{1,0:T(8,128)(2,1)S(1)} %get-tuple-element.36), channel_id=1, source_target_pairs={{0,1},{1,0},{2,3},{3,2},{4,5},{5,4},{6,7},{7,6},{8,9},{9,8},{10,11... | collective-permute-start | bytes 2654216 | tf_op jit(solution)/shard_map/ppermute | solution.py:193
  15.7 6.2 %collective-permute-start.5 = (bf16[864,128]{1,0:T(8,128)(2,1)S(1)}, bf16[864,128]{1,0:T(8,128)(2,1)S(1)}, u32[]{:S(2)}, u32[]{:S(2)}) collective-permute-start(bf16[864,128]{1,0:T(8,128)(2,1)S(1)} %add_convert_fusion.4), channel_id=1, source_target_pairs={{0,4},{1,3},{2,6},{3,1},{4,0},{5,7},{6,2},{7,5},{8,12},{9,11},{10,... | collective-permute-start | bytes 663560 | tf_op jit(solution)/shard_map/ppermute | solution.py:193
  17.1 16.7 %collective-permute-start.9 = (bf16[3456,128]{1,0:T(8,128)(2,1)S(1)}, bf16[3456,128]{1,0:T(8,128)(2,1)S(1)}, u32[]{:S(2)}, u32[]{:S(2)}) collective-permute-start(bf16[3456,128]{1,0:T(8,128)(2,1)S(1)} %get-tuple-element.35), channel_id=1, source_target_pairs={{0,1},{1,0},{2,3},{3,2},{4,5},{5,4},{6,7},{7,6},{8,9},{9,8},{10,11... | collective-permute-start | bytes 2654216 | tf_op jit(solution)/shard_map/ppermute | solution.py:193
  19.7 8.1 %collective-permute-start.3 = (bf16[1296,128]{1,0:T(8,128)(2,1)S(1)}, bf16[1296,128]{1,0:T(8,128)(2,1)S(1)}, u32[]{:S(2)}, u32[]{:S(2)}) collective-permute-start(bf16[1296,128]{1,0:T(8,128)(2,1)S(1)} %add_convert_fusion.3), channel_id=1, source_target_pairs={{0,2},{1,5},{2,0},{3,7},{4,6},{5,1},{6,4},{7,3},{8,10},{9,13},{10,... | collective-permute-start | bytes 995336 | tf_op jit(solution)/shard_map/ppermute | solution.py:193
  22.0 9.5 %collective-permute-start.7 = (bf16[432,128]{1,0:T(8,128)(2,1)S(1)}, bf16[432,128]{1,0:T(8,128)(2,1)S(1)}, u32[]{:S(2)}, u32[]{:S(2)}) collective-permute-start(bf16[432,128]{1,0:T(8,128)(2,1)S(1)} %add_convert_fusion.9), channel_id=1, source_target_pairs={{0,2},{1,5},{2,0},{3,7},{4,6},{5,1},{6,4},{7,3},{8,10},{9,13},{10,... | collective-permute-start | bytes 331784 | tf_op jit(solution)/shard_map/ppermute | solution.py:193
  24.5 10.7 %collective-permute-start.10 = (bf16[1440,128]{1,0:T(8,128)(2,1)S(1)}, bf16[1440,128]{1,0:T(8,128)(2,1)S(1)}, u32[]{:S(2)}, u32[]{:S(2)}) collective-permute-start(bf16[1440,128]{1,0:T(8,128)(2,1)S(1)} %get-tuple-element.67), channel_id=1, source_target_pairs={{0,4},{1,3},{2,6},{3,1},{4,0},{5,7},{6,2},{7,5},{8,12},{9,11},{10,... | collective-permute-start | bytes 1105928 | tf_op jit(solution)/shard_map/ppermute | solution.py:193
  26.2 11.9 %collective-permute-start.13 = (bf16[1440,128]{1,0:T(8,128)(2,1)S(1)}, bf16[1440,128]{1,0:T(8,128)(2,1)S(1)}, u32[]{:S(2)}, u32[]{:S(2)}) collective-permute-start(bf16[1440,128]{1,0:T(8,128)(2,1)S(1)} %get-tuple-element.45), channel_id=1, source_target_pairs={{0,2},{1,3},{2,0},{3,1},{4,6},{5,7},{6,4},{7,5},{8,10},{9,11},{10,... | collective-permute-start | bytes 1105928 | tf_op jit(solution)/shard_map/ppermute | solution.py:193
  28.0 26.2 %collective-permute-start.6 = (bf16[648,128]{1,0:T(8,128)(2,1)S(1)}, bf16[648,128]{1,0:T(8,128)(2,1)S(1)}, u32[]{:S(2)}, u32[]{:S(2)}) collective-permute-start(bf16[648,128]{1,0:T(8,128)(2,1)S(1)} %get-tuple-element.56), channel_id=1, source_target_pairs={{0,8},{1,9},{2,10},{3,11},{4,12},{5,13},{6,14},{7,15},{8,0},{9,1},... | collective-permute-start | bytes 497672 | tf_op jit(solution)/shard_map/ppermute | solution.py:193
  31.6 22.6 %collective-permute-start.8 = (bf16[216,128]{1,0:T(8,128)(2,1)S(1)}, bf16[216,128]{1,0:T(8,128)(2,1)S(1)}, u32[]{:S(2)}, u32[]{:S(2)}) collective-permute-start(bf16[216,128]{1,0:T(8,128)(2,1)S(1)} %get-tuple-element.63), channel_id=1, source_target_pairs={{0,8},{1,9},{2,10},{3,11},{4,12},{5,13},{6,14},{7,15},{8,0},{9,1},... | collective-permute-start | bytes 165896 | tf_op jit(solution)/shard_map/ppermute | solution.py:193
  35.3 8.2 %collective-permute-start.12 = (bf16[720,128]{1,0:T(8,128)(2,1)S(1)}, bf16[720,128]{1,0:T(8,128)(2,1)S(1)}, u32[]{:S(2)}, u32[]{:S(2)}) collective-permute-start(bf16[720,128]{1,0:T(8,128)(2,1)S(1)} %add_convert_fusion.6), channel_id=1, source_target_pairs={{0,2},{1,5},{2,0},{3,7},{4,6},{5,1},{6,4},{7,3},{8,10},{9,13},{10,... | collective-permute-start | bytes 552968 | tf_op jit(solution)/shard_map/ppermute | solution.py:193
  38.1 8.1 %collective-permute-start.11 = (bf16[576,128]{1,0:T(8,128)(2,1)S(1)}, bf16[576,128]{1,0:T(8,128)(2,1)S(1)}, u32[]{:S(2)}, u32[]{:S(2)}) collective-permute-start(bf16[576,128]{1,0:T(8,128)(2,1)S(1)} %add_convert_fusion.8), channel_id=1, source_target_pairs={{0,2},{1,3},{2,0},{3,1},{4,6},{5,7},{6,4},{7,5},{8,10},{9,11},{10,... | collective-permute-start | bytes 442376 | tf_op jit(solution)/shard_map/ppermute | solution.py:193
  40.6 9.4 %collective-permute-start.15 = (bf16[720,128]{1,0:T(8,128)(2,1)S(1)}, bf16[720,128]{1,0:T(8,128)(2,1)S(1)}, u32[]{:S(2)}, u32[]{:S(2)}) collective-permute-start(bf16[720,128]{1,0:T(8,128)(2,1)S(1)} %add_convert_fusion.5), channel_id=1, source_target_pairs={{0,4},{1,5},{2,6},{3,7},{4,0},{5,1},{6,2},{7,3},{8,12},{9,13},{10,... | collective-permute-start | bytes 552968 | tf_op jit(solution)/shard_map/ppermute | solution.py:193
  43.5 11.4 %collective-permute-start.16 = (bf16[360,128]{1,0:T(8,128)(2,1)S(1)}, bf16[360,128]{1,0:T(8,128)(2,1)S(1)}, u32[]{:S(2)}, u32[]{:S(2)}) collective-permute-start(bf16[360,128]{1,0:T(8,128)(2,1)S(1)} %get-tuple-element.61), channel_id=1, source_target_pairs={{0,8},{1,9},{2,10},{3,11},{4,12},{5,13},{6,14},{7,15},{8,0},{9,1},... | collective-permute-start | bytes 276488 | tf_op jit(solution)/shard_map/ppermute | solution.py:193
  46.2 6.8 %collective-permute-start.14 = (bf16[288,128]{1,0:T(8,128)(2,1)S(1)}, bf16[288,128]{1,0:T(8,128)(2,1)S(1)}, u32[]{:S(2)}, u32[]{:S(2)}) collective-permute-start(bf16[288,128]{1,0:T(8,128)(2,1)S(1)} %add_convert_fusion.12), channel_id=1, source_target_pairs={{0,4},{1,5},{2,6},{3,7},{4,0},{5,1},{6,2},{7,3},{8,12},{9,13},{10,... | collective-permute-start | bytes 221192 | tf_op jit(solution)/shard_map/ppermute | solution.py:193
  50.1 8.7 %collective-permute-start.17 = (bf16[360,128]{1,0:T(8,128)(2,1)S(1)}, bf16[360,128]{1,0:T(8,128)(2,1)S(1)}, u32[]{:S(2)}, u32[]{:S(2)}) collective-permute-start(bf16[360,128]{1,0:T(8,128)(2,1)S(1)} %get-tuple-element.59), channel_id=1, source_target_pairs={{0,8},{1,9},{2,10},{3,11},{4,12},{5,13},{6,14},{7,15},{8,0},{9,1},... | collective-permute-start | bytes 276488 | tf_op jit(solution)/shard_map/ppermute | solution.py:193
  53.0 6.5 %collective-permute-start.18 = (bf16[144,128]{1,0:T(8,128)(2,1)S(1)}, bf16[144,128]{1,0:T(8,128)(2,1)S(1)}, u32[]{:S(2)}, u32[]{:S(2)}) collective-permute-start(bf16[144,128]{1,0:T(8,128)(2,1)S(1)} %get-tuple-element.65), channel_id=1, source_target_pairs={{0,8},{1,9},{2,10},{3,11},{4,12},{5,13},{6,14},{7,15},{8,0},{9,1},... | collective-permute-start | bytes 110600 | tf_op jit(solution)/shard_map/ppermute | solution.py:193

commit v18 on v16

--- a/solution.py
+++ b/solution.py
@@ -271,7 +271,7 @@
     tiles = one[-1][2] // LANES
     half, most, more = tiles // 2, tiles * 3 // 4, tiles * 5 // 6
     plans = (
-        [(0, most, MIXED), (most, tiles, MIXED)],
+        [(0, more, MIXED), (more, tiles, MIXED)],
         [(0, half, MIXED), (half, more, STRAIGHT), (more, tiles, STRAIGHT)],
     )
     ones, twos = [[Chain(chunk, devices, pitch) for chunk in chunks] for chunks in plans]

time: 57.5 us -> 59.3 us (1.031)
  starting transfers between devices: 25.9 us -> 32 us
  waiting for transfers between devices: 18.9 us -> 14.6 us
    ppermute x19, starting transfers between devices: 25.9 us -> 32 us  [exchange(): return lax.ppermute(value, 'curve', pairs)]
    ppermute x19, waiting for transfers between devices: 18.9 us -> 14.6 us  [exchange(): return lax.ppermute(value, 'curve', pairs)]
  transfers between devices with their start and end apart: 19 -> 19, of which waited for: 10 -> 8; matrix products, arithmetic and copies ran while one was open for 2% -> 2% of each run, Pallas kernels for 9% -> 9%
where the time goes in v18:
time: 59.3 us; the launch traced here: 59.1 us
  starting transfers between devices  32 us (54%)
  waiting for transfers between devices  14.6 us (25%)
  Pallas kernels  10.8 us (18%)
  other arithmetic  1.08 us (2%)
  between operations  0.74 us (1%)
    ppermute x19, starting transfers between devices, exchange(): return lax.ppermute(value, 'curve', pairs)  32 us
    ppermute x19, waiting for transfers between devices, exchange(): return lax.ppermute(value, 'curve', pairs)  14.6 us
    pallas_call x2, Pallas kernels, products(): pl.pallas_call(functools.partial(product_kernel, channels, pitch, chunks,...  9.29 us
    pallas_call x2, Pallas kernels, final_sum(): pl.pallas_call(functools.partial(final_kernel, like_shape[1], pitch, part...  1.48 us
  transfers between devices with their start and end apart: 19, of which 8 were waited for; matrix products, arithmetic and copies ran while one was open for 2% of the time, Pallas kernels for 9%

profile of v18, /device:TPU:0, one launch (start us, length us, event | category | flops | bytes accessed | tf_op | source)
XLA Modules:
  0.0 59.1 jit_solution(18329884028237183487)
XLA Ops:
  0.6 4.6 %shard_map.113 = (f32[13824,128]{1,0:T(8,128)S(1)}, bf16[3456,128]{1,0:T(8,128)(2,1)S(1)}, bf16[3456,128]{1,0:T(8,128)(2,1)S(1)}) custom-call(s32[144]{0:T(256)} %source_hbm.2, s32[144]{0:T(256)} %target_hbm.2, s32[1,16]{1,0:T(1,128)} %counts_hbm.2, bf16[1,69,1536]{2,1,0:T(8,128)(2,1)} %x_hbm.1, bf16[144,128,128]{2,1,0:T(8,128)(2,1)} %w_hbm.2), custom_call_target="tpu_custom_call" | custom-call | flops 325582848 | bytes 13565952 | tf_op jit(solution)/shard_map/pallas_call | solution.py:163
  5.3 0.5 collective-permute-start.1
  5.8 0.1 collective-permute-start
  5.9 2.0 %collective-permute-done.1 = bf16[3456,128]{1,0:T(8,128)(2,1)S(1)} collective-permute-done((bf16[3456,128]{1,0:T(8,128)(2,1)S(1)}, bf16[3456,128]{1,0:T(8,128)(2,1)S(1)}, u32[]{:S(2)}, u32[]{:S(2)}) %collective-permute-start.1) | collective-permute-done | bytes 884768 | tf_op jit(solution)/shard_map/ppermute | solution.py:193
  7.8 0.1 add_convert_fusion
  8.0 3.0 %collective-permute-start.2 = (bf16[2880,128]{1,0:T(8,128)(2,1)S(1)}, bf16[2880,128]{1,0:T(8,128)(2,1)S(1)}, u32[]{:S(2)}, u32[]{:S(2)}) collective-permute-start(bf16[2880,128]{1,0:T(8,128)(2,1)S(1)} %add_convert_fusion), channel_id=1, source_target_pairs={{0,4},{1,3},{2,6},{3,1},{4,0},{5,7},{6,2},{7,5},{8,12},{9,11},{10,... | collective-permute-start | bytes 2211848 | tf_op jit(solution)/shard_map/ppermute | solution.py:193
  11.0 0.0 collective-permute-done
  11.0 4.7 %shard_map.114 = (f32[13824,128]{1,0:T(8,128)S(1)}, bf16[3456,128]{1,0:T(8,128)(2,1)S(1)}, bf16[3456,128]{1,0:T(8,128)(2,1)S(1)}) custom-call(s32[144]{0:T(256)} %source_hbm.3, s32[144]{0:T(256)} %target_hbm.3, s32[1,16]{1,0:T(1,128)} %counts_hbm.3, bf16[1,69,1536]{2,1,0:T(8,128)(2,1)} %x_hbm.2, bf16[144,128,128]{2,1,0:T(8,128)(2,1)} %w_hbm.3), custom_call_target="tpu_custom_call" | custom-call | flops 325582848 | bytes 13565952 | tf_op jit(solution)/shard_map/pallas_call | solution.py:163
  15.7 0.1 collective-permute-start.4
  15.8 1.3 %collective-permute-start.5 = (bf16[576,128]{1,0:T(8,128)(2,1)S(1)}, bf16[576,128]{1,0:T(8,128)(2,1)S(1)}, u32[]{:S(2)}, u32[]{:S(2)}) collective-permute-start(bf16[576,128]{1,0:T(8,128)(2,1)S(1)} %add_convert_fusion.8), channel_id=1, source_target_pairs={{0,4},{1,3},{2,6},{3,1},{4,0},{5,7},{6,2},{7,5},{8,12},{9,11},{10,... | collective-permute-start | bytes 442376 | tf_op jit(solution)/shard_map/ppermute | solution.py:193
  17.1 0.4 collective-permute-start.9
  17.5 3.0 %collective-permute-done.2 = bf16[2880,128]{1,0:T(8,128)(2,1)S(1)} collective-permute-done((bf16[2880,128]{1,0:T(8,128)(2,1)S(1)}, bf16[2880,128]{1,0:T(8,128)(2,1)S(1)}, u32[]{:S(2)}, u32[]{:S(2)}) %collective-permute-start.2) | collective-permute-done | bytes 737312 | tf_op jit(solution)/shard_map/ppermute | solution.py:193
  20.4 0.1 add_convert_fusion.2
  20.6 2.0 %collective-permute-start.3 = (bf16[1440,128]{1,0:T(8,128)(2,1)S(1)}, bf16[1440,128]{1,0:T(8,128)(2,1)S(1)}, u32[]{:S(2)}, u32[]{:S(2)}) collective-permute-start(bf16[1440,128]{1,0:T(8,128)(2,1)S(1)} %add_convert_fusion.2), channel_id=1, source_target_pairs={{0,2},{1,5},{2,0},{3,7},{4,6},{5,1},{6,4},{7,3},{8,10},{9,13},{10,... | collective-permute-start | bytes 1105928 | tf_op jit(solution)/shard_map/ppermute | solution.py:193
  22.6 0.0 collective-permute-done.5
  22.6 1.4 %collective-permute-start.7 = (bf16[288,128]{1,0:T(8,128)(2,1)S(1)}, bf16[288,128]{1,0:T(8,128)(2,1)S(1)}, u32[]{:S(2)}, u32[]{:S(2)}) collective-permute-start(bf16[288,128]{1,0:T(8,128)(2,1)S(1)} %add_convert_fusion.12), channel_id=1, source_target_pairs={{0,2},{1,5},{2,0},{3,7},{4,6},{5,1},{6,4},{7,3},{8,10},{9,13},{10,... | collective-permute-start | bytes 221192 | tf_op jit(solution)/shard_map/ppermute | solution.py:193
  24.1 0.0 collective-permute-done.4
  24.1 0.1 add_convert_fusion.3
  24.1 0.1 add_convert_fusion.1
  24.2 1.6 %collective-permute-start.10 = (bf16[1728,128]{1,0:T(8,128)(2,1)S(1)}, bf16[1728,128]{1,0:T(8,128)(2,1)S(1)}, u32[]{:S(2)}, u32[]{:S(2)}) collective-permute-start(bf16[1728,128]{1,0:T(8,128)(2,1)S(1)} %add_convert_fusion.1), channel_id=1, source_target_pairs={{0,4},{1,3},{2,6},{3,1},{4,0},{5,7},{6,2},{7,5},{8,12},{9,11},{10,... | collective-permute-start | bytes 1327112 | tf_op jit(solution)/shard_map/ppermute | solution.py:193
  25.9 0.7 %collective-permute-start.13 = (bf16[1152,128]{1,0:T(8,128)(2,1)S(1)}, bf16[1152,128]{1,0:T(8,128)(2,1)S(1)}, u32[]{:S(2)}, u32[]{:S(2)}) collective-permute-start(bf16[1152,128]{1,0:T(8,128)(2,1)S(1)} %add_convert_fusion.3), channel_id=1, source_target_pairs={{0,2},{1,3},{2,0},{3,1},{4,6},{5,7},{6,4},{7,5},{8,10},{9,11},{10,... | collective-permute-start | bytes 884744 | tf_op jit(solution)/shard_map/ppermute | solution.py:193
  26.6 3.7 %collective-permute-done.3 = bf16[1440,128]{1,0:T(8,128)(2,1)S(1)} collective-permute-done((bf16[1440,128]{1,0:T(8,128)(2,1)S(1)}, bf16[1440,128]{1,0:T(8,128)(2,1)S(1)}, u32[]{:S(2)}, u32[]{:S(2)}) %collective-permute-start.3) | collective-permute-done | bytes 368672 | tf_op jit(solution)/shard_map/ppermute | solution.py:193
  30.3 0.2 add_convert_fusion.5
  30.4 3.6 %collective-permute-start.6 = (bf16[720,128]{1,0:T(8,128)(2,1)S(1)}, bf16[720,128]{1,0:T(8,128)(2,1)S(1)}, u32[]{:S(2)}, u32[]{:S(2)}) collective-permute-start(bf16[720,128]{1,0:T(8,128)(2,1)S(1)} %get-tuple-element.56), channel_id=1, source_target_pairs={{0,8},{1,9},{2,10},{3,11},{4,12},{5,13},{6,14},{7,15},{8,0},{9,1},... | collective-permute-start | bytes 552968 | tf_op jit(solution)/shard_map/ppermute | solution.py:193
  34.0 1.4 %collective-permute-start.8 = (bf16[144,128]{1,0:T(8,128)(2,1)S(1)}, bf16[144,128]{1,0:T(8,128)(2,1)S(1)}, u32[]{:S(2)}, u32[]{:S(2)}) collective-permute-start(bf16[144,128]{1,0:T(8,128)(2,1)S(1)} %get-tuple-element.65), channel_id=1, source_target_pairs={{0,8},{1,9},{2,10},{3,11},{4,12},{5,13},{6,14},{7,15},{8,0},{9,1},... | collective-permute-start | bytes 110600 | tf_op jit(solution)/shard_map/ppermute | solution.py:193
  35.4 0.0 collective-permute-done.9
  35.4 0.0 collective-permute-done.10
  35.4 0.1 add_convert_fusion.4
  35.5 1.6 %collective-permute-start.12 = (bf16[864,128]{1,0:T(8,128)(2,1)S(1)}, bf16[864,128]{1,0:T(8,128)(2,1)S(1)}, u32[]{:S(2)}, u32[]{:S(2)}) collective-permute-start(bf16[864,128]{1,0:T(8,128)(2,1)S(1)} %add_convert_fusion.4), channel_id=1, source_target_pairs={{0,2},{1,5},{2,0},{3,7},{4,6},{5,1},{6,4},{7,3},{8,10},{9,13},{10,... | collective-permute-start | bytes 663560 | tf_op jit(solution)/shard_map/ppermute | solution.py:193
  37.1 1.0 %collective-permute-done.13 = bf16[1152,128]{1,0:T(8,128)(2,1)S(1)} collective-permute-done((bf16[1152,128]{1,0:T(8,128)(2,1)S(1)}, bf16[1152,128]{1,0:T(8,128)(2,1)S(1)}, u32[]{:S(2)}, u32[]{:S(2)}) %collective-permute-start.13) | collective-permute-done | bytes 294944 | tf_op jit(solution)/shard_map/ppermute | solution.py:193
  38.2 2.4 %collective-permute-start.11 = (bf16[576,128]{1,0:T(8,128)(2,1)S(1)}, bf16[576,128]{1,0:T(8,128)(2,1)S(1)}, u32[]{:S(2)}, u32[]{:S(2)}) collective-permute-start(bf16[576,128]{1,0:T(8,128)(2,1)S(1)} %add_convert_fusion.7), channel_id=1, source_target_pairs={{0,2},{1,3},{2,0},{3,1},{4,6},{5,7},{6,4},{7,5},{8,10},{9,11},{10,... | collective-permute-start | bytes 442376 | tf_op jit(solution)/shard_map/ppermute | solution.py:193
  40.6 0.1 add_convert_fusion.6
  40.7 2.8 %collective-permute-start.15 = (bf16[576,128]{1,0:T(8,128)(2,1)S(1)}, bf16[576,128]{1,0:T(8,128)(2,1)S(1)}, u32[]{:S(2)}, u32[]{:S(2)}) collective-permute-start(bf16[576,128]{1,0:T(8,128)(2,1)S(1)} %add_convert_fusion.6), channel_id=1, source_target_pairs={{0,4},{1,5},{2,6},{3,7},{4,0},{5,1},{6,2},{7,3},{8,12},{9,13},{10,... | collective-permute-start | bytes 442376 | tf_op jit(solution)/shard_map/ppermute | solution.py:193
  43.4 0.1 convert_add_fusion.1
  43.5 2.6 %collective-permute-start.16 = (bf16[432,128]{1,0:T(8,128)(2,1)S(1)}, bf16[432,128]{1,0:T(8,128)(2,1)S(1)}, u32[]{:S(2)}, u32[]{:S(2)}) collective-permute-start(bf16[432,128]{1,0:T(8,128)(2,1)S(1)} %get-tuple-element.59), channel_id=1, source_target_pairs={{0,8},{1,9},{2,10},{3,11},{4,12},{5,13},{6,14},{7,15},{8,0},{9,1},... | collective-permute-start | bytes 331784 | tf_op jit(solution)/shard_map/ppermute | solution.py:193
  46.2 1.8 %collective-permute-start.14 = (bf16[288,128]{1,0:T(8,128)(2,1)S(1)}, bf16[288,128]{1,0:T(8,128)(2,1)S(1)}, u32[]{:S(2)}, u32[]{:S(2)}) collective-permute-start(bf16[288,128]{1,0:T(8,128)(2,1)S(1)} %add_convert_fusion.11), channel_id=1, source_target_pairs={{0,4},{1,5},{2,6},{3,7},{4,0},{5,1},{6,2},{7,3},{8,12},{9,13},{10,... | collective-permute-start | bytes 221192 | tf_op jit(solution)/shard_map/ppermute | solution.py:193
  48.0 1.8 %collective-permute-done.15 = bf16[576,128]{1,0:T(8,128)(2,1)S(1)} collective-permute-done((bf16[576,128]{1,0:T(8,128)(2,1)S(1)}, bf16[576,128]{1,0:T(8,128)(2,1)S(1)}, u32[]{:S(2)}, u32[]{:S(2)}) %collective-permute-start.15) | collective-permute-done | bytes 147488 | tf_op jit(solution)/shard_map/ppermute | solution.py:193
  49.9 0.1 convert_add_fusion.2
  49.9 1.0 %collective-permute-start.17 = (bf16[288,128]{1,0:T(8,128)(2,1)S(1)}, bf16[288,128]{1,0:T(8,128)(2,1)S(1)}, u32[]{:S(2)}, u32[]{:S(2)}) collective-permute-start(bf16[288,128]{1,0:T(8,128)(2,1)S(1)} %get-tuple-element.61), channel_id=1, source_target_pairs={{0,8},{1,9},{2,10},{3,11},{4,12},{5,13},{6,14},{7,15},{8,0},{9,1},... | collective-permute-start | bytes 221192 | tf_op jit(solution)/shard_map/ppermute | solution.py:193
  50.9 0.5 collective-permute-done.14
  51.5 3.6 %collective-permute-start.18 = (bf16[144,128]{1,0:T(8,128)(2,1)S(1)}, bf16[144,128]{1,0:T(8,128)(2,1)S(1)}, u32[]{:S(2)}, u32[]{:S(2)}) collective-permute-start(bf16[144,128]{1,0:T(8,128)(2,1)S(1)} %get-tuple-element.63), channel_id=1, source_target_pairs={{0,8},{1,9},{2,10},{3,11},{4,12},{5,13},{6,14},{7,15},{8,0},{9,1},... | collective-permute-start | bytes 110600 | tf_op jit(solution)/shard_map/ppermute | solution.py:193
  55.1 0.0 collective-permute-done.8.refs_3_
  55.1 0.0 collective-permute-done.6.refs_1_
  55.1 0.7 %shard_map.115 = bf16[1,69,1536]{2,1,0:T(8,128)(2,1)} custom-call(f32[720,128]{1,0:T(8,128)S(1)} %get-tuple-element.57.refs_0_, bf16[720,128]{1,0:T(8,128)(2,1)S(1)} %collective-permute-done.6.refs_1_, f32[144,128]{1,0:T(8,128)S(1)} %get-tuple-element.64.refs_2_, bf16[144,128]{1,0:T(8,128)(2,1)S(1)} %collective-permute-done.8.refs_3_), custom_call_target="tpu_custom_call" | custom-call | tf_op jit(solution)/shard_map/pallas_call | solution.py:247
  55.9 0.0 collective-permute-done.16.refs_1_
  55.9 1.7 %collective-permute-done.17.refs_3_ = bf16[288,128]{1,0:T(8,128)(2,1)S(1)} collective-permute-done((bf16[288,128]{1,0:T(8,128)(2,1)S(1)}, bf16[288,128]{1,0:T(8,128)(2,1)S(1)}, u32[]{:S(2)}, u32[]{:S(2)}) %collective-permute-start.17) | collective-permute-done | bytes 73760 | tf_op jit(solution)/shard_map/ppermute | solution.py:193
  57.6 0.8 %collective-permute-done.18.refs_5_ = bf16[144,128]{1,0:T(8,128)(2,1)S(1)} collective-permute-done((bf16[144,128]{1,0:T(8,128)(2,1)S(1)}, bf16[144,128]{1,0:T(8,128)(2,1)S(1)}, u32[]{:S(2)}, u32[]{:S(2)}) %collective-permute-start.18) | collective-permute-done | bytes 36896 | tf_op jit(solution)/shard_map/ppermute | solution.py:193
  58.4 0.7 %shard_map.116 = bf16[1,69,1536]{2,1,0:T(8,128)(2,1)} custom-call(f32[432,128]{1,0:T(8,128)S(1)} %get-tuple-element.58.refs_0_, bf16[432,128]{1,0:T(8,128)(2,1)S(1)} %collective-permute-done.16.refs_1_, f32[288,128]{1,0:T(8,128)S(1)} %get-tuple-element.60.refs_2_, bf16[288,128]{1,0:T(8,128)(2,1)S(1)} %collective-permute-done.17.refs_3_, ...), custom_call_target="tpu_custom_call" | custom-call | tf_op jit(solution)/shard_map/pallas_call | solution.py:247
  (9 shorter events, 0.2 us)
Async XLA Ops:
  5.3 2.6 %collective-permute-start.1 = (bf16[3456,128]{1,0:T(8,128)(2,1)S(1)}, bf16[3456,128]{1,0:T(8,128)(2,1)S(1)}, u32[]{:S(2)}, u32[]{:S(2)}) collective-permute-start(bf16[3456,128]{1,0:T(8,128)(2,1)S(1)} %get-tuple-element.31), channel_id=1, source_target_pairs={{0,1},{1,0},{2,3},{3,2},{4,5},{5,4},{6,7},{7,6},{8,9},{9,8},{10,11... | collective-permute-start | bytes 2654216 | tf_op jit(solution)/shard_map/ppermute | solution.py:193
  5.8 5.3 %collective-permute-start = (bf16[3456,128]{1,0:T(8,128)(2,1)S(1)}, bf16[3456,128]{1,0:T(8,128)(2,1)S(1)}, u32[]{:S(2)}, u32[]{:S(2)}) collective-permute-start(bf16[3456,128]{1,0:T(8,128)(2,1)S(1)} %get-tuple-element.30), channel_id=1, source_target_pairs={{0,1},{1,0},{2,3},{3,2},{4,5},{5,4},{6,7},{7,6},{8,9},{9,8},{10,11... | collective-permute-start | bytes 2654216 | tf_op jit(solution)/shard_map/ppermute | solution.py:193
  8.0 12.5 %collective-permute-start.2 = (bf16[2880,128]{1,0:T(8,128)(2,1)S(1)}, bf16[2880,128]{1,0:T(8,128)(2,1)S(1)}, u32[]{:S(2)}, u32[]{:S(2)}) collective-permute-start(bf16[2880,128]{1,0:T(8,128)(2,1)S(1)} %add_convert_fusion), channel_id=1, source_target_pairs={{0,4},{1,3},{2,6},{3,1},{4,0},{5,7},{6,2},{7,5},{8,12},{9,11},{10,... | collective-permute-start | bytes 2211848 | tf_op jit(solution)/shard_map/ppermute | solution.py:193
  15.7 8.3 %collective-permute-start.4 = (bf16[3456,128]{1,0:T(8,128)(2,1)S(1)}, bf16[3456,128]{1,0:T(8,128)(2,1)S(1)}, u32[]{:S(2)}, u32[]{:S(2)}) collective-permute-start(bf16[3456,128]{1,0:T(8,128)(2,1)S(1)} %get-tuple-element.36), channel_id=1, source_target_pairs={{0,1},{1,0},{2,3},{3,2},{4,5},{5,4},{6,7},{7,6},{8,9},{9,8},{10,11... | collective-permute-start | bytes 2654216 | tf_op jit(solution)/shard_map/ppermute | solution.py:193
  15.8 6.8 %collective-permute-start.5 = (bf16[576,128]{1,0:T(8,128)(2,1)S(1)}, bf16[576,128]{1,0:T(8,128)(2,1)S(1)}, u32[]{:S(2)}, u32[]{:S(2)}) collective-permute-start(bf16[576,128]{1,0:T(8,128)(2,1)S(1)} %add_convert_fusion.8), channel_id=1, source_target_pairs={{0,4},{1,3},{2,6},{3,1},{4,0},{5,7},{6,2},{7,5},{8,12},{9,11},{10,... | collective-permute-start | bytes 442376 | tf_op jit(solution)/shard_map/ppermute | solution.py:193
  17.1 18.3 %collective-permute-start.9 = (bf16[3456,128]{1,0:T(8,128)(2,1)S(1)}, bf16[3456,128]{1,0:T(8,128)(2,1)S(1)}, u32[]{:S(2)}, u32[]{:S(2)}) collective-permute-start(bf16[3456,128]{1,0:T(8,128)(2,1)S(1)} %get-tuple-element.35), channel_id=1, source_target_pairs={{0,1},{1,0},{2,3},{3,2},{4,5},{5,4},{6,7},{7,6},{8,9},{9,8},{10,11... | collective-permute-start | bytes 2654216 | tf_op jit(solution)/shard_map/ppermute | solution.py:193
  20.6 9.7 %collective-permute-start.3 = (bf16[1440,128]{1,0:T(8,128)(2,1)S(1)}, bf16[1440,128]{1,0:T(8,128)(2,1)S(1)}, u32[]{:S(2)}, u32[]{:S(2)}) collective-permute-start(bf16[1440,128]{1,0:T(8,128)(2,1)S(1)} %add_convert_fusion.2), channel_id=1, source_target_pairs={{0,2},{1,5},{2,0},{3,7},{4,6},{5,1},{6,4},{7,3},{8,10},{9,13},{10,... | collective-permute-start | bytes 1105928 | tf_op jit(solution)/shard_map/ppermute | solution.py:193
  22.6 11.4 %collective-permute-start.7 = (bf16[288,128]{1,0:T(8,128)(2,1)S(1)}, bf16[288,128]{1,0:T(8,128)(2,1)S(1)}, u32[]{:S(2)}, u32[]{:S(2)}) collective-permute-start(bf16[288,128]{1,0:T(8,128)(2,1)S(1)} %add_convert_fusion.12), channel_id=1, source_target_pairs={{0,2},{1,5},{2,0},{3,7},{4,6},{5,1},{6,4},{7,3},{8,10},{9,13},{10,... | collective-permute-start | bytes 221192 | tf_op jit(solution)/shard_map/ppermute | solution.py:193
  24.2 11.2 %collective-permute-start.10 = (bf16[1728,128]{1,0:T(8,128)(2,1)S(1)}, bf16[1728,128]{1,0:T(8,128)(2,1)S(1)}, u32[]{:S(2)}, u32[]{:S(2)}) collective-permute-start(bf16[1728,128]{1,0:T(8,128)(2,1)S(1)} %add_convert_fusion.1), channel_id=1, source_target_pairs={{0,4},{1,3},{2,6},{3,1},{4,0},{5,7},{6,2},{7,5},{8,12},{9,11},{10,... | collective-permute-start | bytes 1327112 | tf_op jit(solution)/shard_map/ppermute | solution.py:193
  25.9 12.3 %collective-permute-start.13 = (bf16[1152,128]{1,0:T(8,128)(2,1)S(1)}, bf16[1152,128]{1,0:T(8,128)(2,1)S(1)}, u32[]{:S(2)}, u32[]{:S(2)}) collective-permute-start(bf16[1152,128]{1,0:T(8,128)(2,1)S(1)} %add_convert_fusion.3), channel_id=1, source_target_pairs={{0,2},{1,3},{2,0},{3,1},{4,6},{5,7},{6,4},{7,5},{8,10},{9,11},{10,... | collective-permute-start | bytes 884744 | tf_op jit(solution)/shard_map/ppermute | solution.py:193
  30.4 24.7 %collective-permute-start.6 = (bf16[720,128]{1,0:T(8,128)(2,1)S(1)}, bf16[720,128]{1,0:T(8,128)(2,1)S(1)}, u32[]{:S(2)}, u32[]{:S(2)}) collective-permute-start(bf16[720,128]{1,0:T(8,128)(2,1)S(1)} %get-tuple-element.56), channel_id=1, source_target_pairs={{0,8},{1,9},{2,10},{3,11},{4,12},{5,13},{6,14},{7,15},{8,0},{9,1},... | collective-permute-start | bytes 552968 | tf_op jit(solution)/shard_map/ppermute | solution.py:193
  34.0 21.1 %collective-permute-start.8 = (bf16[144,128]{1,0:T(8,128)(2,1)S(1)}, bf16[144,128]{1,0:T(8,128)(2,1)S(1)}, u32[]{:S(2)}, u32[]{:S(2)}) collective-permute-start(bf16[144,128]{1,0:T(8,128)(2,1)S(1)} %get-tuple-element.65), channel_id=1, source_target_pairs={{0,8},{1,9},{2,10},{3,11},{4,12},{5,13},{6,14},{7,15},{8,0},{9,1},... | collective-permute-start | bytes 110600 | tf_op jit(solution)/shard_map/ppermute | solution.py:193
  35.5 7.9 %collective-permute-start.12 = (bf16[864,128]{1,0:T(8,128)(2,1)S(1)}, bf16[864,128]{1,0:T(8,128)(2,1)S(1)}, u32[]{:S(2)}, u32[]{:S(2)}) collective-permute-start(bf16[864,128]{1,0:T(8,128)(2,1)S(1)} %add_convert_fusion.4), channel_id=1, source_target_pairs={{0,2},{1,5},{2,0},{3,7},{4,6},{5,1},{6,4},{7,3},{8,10},{9,13},{10,... | collective-permute-start | bytes 663560 | tf_op jit(solution)/shard_map/ppermute | solution.py:193
  38.2 8.0 %collective-permute-start.11 = (bf16[576,128]{1,0:T(8,128)(2,1)S(1)}, bf16[576,128]{1,0:T(8,128)(2,1)S(1)}, u32[]{:S(2)}, u32[]{:S(2)}) collective-permute-start(bf16[576,128]{1,0:T(8,128)(2,1)S(1)} %add_convert_fusion.7), channel_id=1, source_target_pairs={{0,2},{1,3},{2,0},{3,1},{4,6},{5,7},{6,4},{7,5},{8,10},{9,11},{10,... | collective-permute-start | bytes 442376 | tf_op jit(solution)/shard_map/ppermute | solution.py:193
  40.7 9.2 %collective-permute-start.15 = (bf16[576,128]{1,0:T(8,128)(2,1)S(1)}, bf16[576,128]{1,0:T(8,128)(2,1)S(1)}, u32[]{:S(2)}, u32[]{:S(2)}) collective-permute-start(bf16[576,128]{1,0:T(8,128)(2,1)S(1)} %add_convert_fusion.6), channel_id=1, source_target_pairs={{0,4},{1,5},{2,6},{3,7},{4,0},{5,1},{6,2},{7,3},{8,12},{9,13},{10,... | collective-permute-start | bytes 442376 | tf_op jit(solution)/shard_map/ppermute | solution.py:193
  43.5 12.3 %collective-permute-start.16 = (bf16[432,128]{1,0:T(8,128)(2,1)S(1)}, bf16[432,128]{1,0:T(8,128)(2,1)S(1)}, u32[]{:S(2)}, u32[]{:S(2)}) collective-permute-start(bf16[432,128]{1,0:T(8,128)(2,1)S(1)} %get-tuple-element.59), channel_id=1, source_target_pairs={{0,8},{1,9},{2,10},{3,11},{4,12},{5,13},{6,14},{7,15},{8,0},{9,1},... | collective-permute-start | bytes 331784 | tf_op jit(solution)/shard_map/ppermute | solution.py:193
  46.2 5.2 %collective-permute-start.14 = (bf16[288,128]{1,0:T(8,128)(2,1)S(1)}, bf16[288,128]{1,0:T(8,128)(2,1)S(1)}, u32[]{:S(2)}, u32[]{:S(2)}) collective-permute-start(bf16[288,128]{1,0:T(8,128)(2,1)S(1)} %add_convert_fusion.11), channel_id=1, source_target_pairs={{0,4},{1,5},{2,6},{3,7},{4,0},{5,1},{6,2},{7,3},{8,12},{9,13},{10,... | collective-permute-start | bytes 221192 | tf_op jit(solution)/shard_map/ppermute | solution.py:193
  49.9 7.7 %collective-permute-start.17 = (bf16[288,128]{1,0:T(8,128)(2,1)S(1)}, bf16[288,128]{1,0:T(8,128)(2,1)S(1)}, u32[]{:S(2)}, u32[]{:S(2)}) collective-permute-start(bf16[288,128]{1,0:T(8,128)(2,1)S(1)} %get-tuple-element.61), channel_id=1, source_target_pairs={{0,8},{1,9},{2,10},{3,11},{4,12},{5,13},{6,14},{7,15},{8,0},{9,1},... | collective-permute-start | bytes 221192 | tf_op jit(solution)/shard_map/ppermute | solution.py:193
  51.5 6.9 %collective-permute-start.18 = (bf16[144,128]{1,0:T(8,128)(2,1)S(1)}, bf16[144,128]{1,0:T(8,128)(2,1)S(1)}, u32[]{:S(2)}, u32[]{:S(2)}) collective-permute-start(bf16[144,128]{1,0:T(8,128)(2,1)S(1)} %get-tuple-element.63), channel_id=1, source_target_pairs={{0,8},{1,9},{2,10},{3,11},{4,12},{5,13},{6,14},{7,15},{8,0},{9,1},... | collective-permute-start | bytes 110600 | tf_op jit(solution)/shard_map/ppermute | solution.py:193

commit v19 on v16

--- a/solution.py
+++ b/solution.py
@@ -61,7 +61,7 @@
 
 
 STRAIGHT = ((0, 1, 2, 3), (0, 1, 2, 3))
-MIXED = ((0, 2, 1, 3), (0, 1, 2, 3))
+MIXED = ((0, 1, 2, 3), (0, 2, 1, 3))
 BITS = 4
 
 

time: 57.5 us -> 57.6 us (level)
  waiting for transfers between devices: 18.9 us -> 10.3 us
  starting transfers between devices: 25.9 us -> 34.1 us
    ppermute x19, waiting for transfers between devices: 18.9 us -> 10.3 us  [exchange(): return lax.ppermute(value, 'curve', pairs)]
    ppermute x19, starting transfers between devices: 25.9 us -> 34.1 us  [exchange(): return lax.ppermute(value, 'curve', pairs)]
where the time goes in v19:
time: 57.6 us; the launch traced here: 57 us
  starting transfers between devices  34.1 us (59%)
  Pallas kernels  10.8 us (19%)
  waiting for transfers between devices  10.3 us (18%)
  other arithmetic  1.09 us (2%)
  between operations  0.74 us (1%)
    ppermute x19, starting transfers between devices, exchange(): return lax.ppermute(value, 'curve', pairs)  34.1 us
    ppermute x19, waiting for transfers between devices, exchange(): return lax.ppermute(value, 'curve', pairs)  10.3 us
    pallas_call x2, Pallas kernels, products(): pl.pallas_call(functools.partial(product_kernel, channels, pitch, chunks,...  9.28 us
    pallas_call x2, Pallas kernels, final_sum(): pl.pallas_call(functools.partial(final_kernel, like_shape[1], pitch, part...  1.48 us
  transfers between devices with their start and end apart: 19, of which 10 were waited for; matrix products, arithmetic and copies ran while one was open for 2% of the time, Pallas kernels for 9%

profile of v19, /device:TPU:0, one launch (start us, length us, event | category | flops | bytes accessed | tf_op | source)
XLA Modules:
  0.0 57.0 jit_solution(16763749133442811512)
XLA Ops:
  0.6 4.6 %shard_map.113 = (f32[13824,128]{1,0:T(8,128)S(1)}, bf16[3456,128]{1,0:T(8,128)(2,1)S(1)}, bf16[3456,128]{1,0:T(8,128)(2,1)S(1)}) custom-call(s32[144]{0:T(256)} %source_hbm.2, s32[144]{0:T(256)} %target_hbm.2, s32[1,16]{1,0:T(1,128)} %counts_hbm.2, bf16[1,69,1536]{2,1,0:T(8,128)(2,1)} %x_hbm.1, bf16[144,128,128]{2,1,0:T(8,128)(2,1)} %w_hbm.2), custom_call_target="tpu_custom_call" | custom-call | flops 325582848 | bytes 13565952 | tf_op jit(solution)/shard_map/pallas_call | solution.py:163
  5.2 0.5 collective-permute-start.1
  5.8 0.1 collective-permute-start
  5.9 2.0 %collective-permute-done.1 = bf16[3456,128]{1,0:T(8,128)(2,1)S(1)} collective-permute-done((bf16[3456,128]{1,0:T(8,128)(2,1)S(1)}, bf16[3456,128]{1,0:T(8,128)(2,1)S(1)}, u32[]{:S(2)}, u32[]{:S(2)}) %collective-permute-start.1) | collective-permute-done | bytes 884768 | tf_op jit(solution)/shard_map/ppermute | solution.py:193
  7.8 0.1 add_convert_fusion
  8.0 3.0 %collective-permute-start.2 = (bf16[2592,128]{1,0:T(8,128)(2,1)S(1)}, bf16[2592,128]{1,0:T(8,128)(2,1)S(1)}, u32[]{:S(2)}, u32[]{:S(2)}) collective-permute-start(bf16[2592,128]{1,0:T(8,128)(2,1)S(1)} %add_convert_fusion), channel_id=1, source_target_pairs={{0,2},{1,5},{2,0},{3,7},{4,6},{5,1},{6,4},{7,3},{8,10},{9,13},{10,... | collective-permute-start | bytes 1990664 | tf_op jit(solution)/shard_map/ppermute | solution.py:193
  11.0 0.0 collective-permute-done
  11.0 4.7 %shard_map.114 = (f32[13824,128]{1,0:T(8,128)S(1)}, bf16[3456,128]{1,0:T(8,128)(2,1)S(1)}, bf16[3456,128]{1,0:T(8,128)(2,1)S(1)}) custom-call(s32[144]{0:T(256)} %source_hbm.3, s32[144]{0:T(256)} %target_hbm.3, s32[1,16]{1,0:T(1,128)} %counts_hbm.3, bf16[1,69,1536]{2,1,0:T(8,128)(2,1)} %x_hbm.2, bf16[144,128,128]{2,1,0:T(8,128)(2,1)} %w_hbm.3), custom_call_target="tpu_custom_call" | custom-call | flops 325582848 | bytes 13565952 | tf_op jit(solution)/shard_map/pallas_call | solution.py:163
  15.7 0.1 collective-permute-start.4
  15.7 1.4 %collective-permute-start.5 = (bf16[864,128]{1,0:T(8,128)(2,1)S(1)}, bf16[864,128]{1,0:T(8,128)(2,1)S(1)}, u32[]{:S(2)}, u32[]{:S(2)}) collective-permute-start(bf16[864,128]{1,0:T(8,128)(2,1)S(1)} %add_convert_fusion.5), channel_id=1, source_target_pairs={{0,2},{1,5},{2,0},{3,7},{4,6},{5,1},{6,4},{7,3},{8,10},{9,13},{10,... | collective-permute-start | bytes 663560 | tf_op jit(solution)/shard_map/ppermute | solution.py:193
  17.2 0.4 collective-permute-start.9
  17.5 2.0 %collective-permute-done.2 = bf16[2592,128]{1,0:T(8,128)(2,1)S(1)} collective-permute-done((bf16[2592,128]{1,0:T(8,128)(2,1)S(1)}, bf16[2592,128]{1,0:T(8,128)(2,1)S(1)}, u32[]{:S(2)}, u32[]{:S(2)}) %collective-permute-start.2) | collective-permute-done | bytes 663584 | tf_op jit(solution)/shard_map/ppermute | solution.py:193
  19.6 0.1 add_convert_fusion.2
  19.7 2.1 %collective-permute-start.3 = (bf16[1296,128]{1,0:T(8,128)(2,1)S(1)}, bf16[1296,128]{1,0:T(8,128)(2,1)S(1)}, u32[]{:S(2)}, u32[]{:S(2)}) collective-permute-start(bf16[1296,128]{1,0:T(8,128)(2,1)S(1)} %add_convert_fusion.2), channel_id=1, source_target_pairs={{0,4},{1,3},{2,6},{3,1},{4,0},{5,7},{6,2},{7,5},{8,12},{9,11},{10,... | collective-permute-start | bytes 995336 | tf_op jit(solution)/shard_map/ppermute | solution.py:193
  21.8 0.1 collective-permute-done.5
  21.9 0.1 add_convert_fusion.10
  22.0 2.4 %collective-permute-start.7 = (bf16[432,128]{1,0:T(8,128)(2,1)S(1)}, bf16[432,128]{1,0:T(8,128)(2,1)S(1)}, u32[]{:S(2)}, u32[]{:S(2)}) collective-permute-start(bf16[432,128]{1,0:T(8,128)(2,1)S(1)} %add_convert_fusion.10), channel_id=1, source_target_pairs={{0,4},{1,3},{2,6},{3,1},{4,0},{5,7},{6,2},{7,5},{8,12},{9,11},{10,... | collective-permute-start | bytes 331784 | tf_op jit(solution)/shard_map/ppermute | solution.py:193
  24.4 0.1 add_convert_fusion.3
  24.5 0.1 add_convert_fusion.1
  24.6 1.6 %collective-permute-start.10 = (bf16[1728,128]{1,0:T(8,128)(2,1)S(1)}, bf16[1728,128]{1,0:T(8,128)(2,1)S(1)}, u32[]{:S(2)}, u32[]{:S(2)}) collective-permute-start(bf16[1728,128]{1,0:T(8,128)(2,1)S(1)} %add_convert_fusion.1), channel_id=1, source_target_pairs={{0,2},{1,5},{2,0},{3,7},{4,6},{5,1},{6,4},{7,3},{8,10},{9,13},{10,... | collective-permute-start | bytes 1327112 | tf_op jit(solution)/shard_map/ppermute | solution.py:193
  26.2 0.6 collective-permute-start.13
  26.7 1.1 %collective-permute-done.3 = bf16[1296,128]{1,0:T(8,128)(2,1)S(1)} collective-permute-done((bf16[1296,128]{1,0:T(8,128)(2,1)S(1)}, bf16[1296,128]{1,0:T(8,128)(2,1)S(1)}, u32[]{:S(2)}, u32[]{:S(2)}) %collective-permute-start.3) | collective-permute-done | bytes 331808 | tf_op jit(solution)/shard_map/ppermute | solution.py:193
  27.9 0.1 add_convert_fusion.6
  28.0 3.5 %collective-permute-start.6 = (bf16[648,128]{1,0:T(8,128)(2,1)S(1)}, bf16[648,128]{1,0:T(8,128)(2,1)S(1)}, u32[]{:S(2)}, u32[]{:S(2)}) collective-permute-start(bf16[648,128]{1,0:T(8,128)(2,1)S(1)} %get-tuple-element.56), channel_id=1, source_target_pairs={{0,8},{1,9},{2,10},{3,11},{4,12},{5,13},{6,14},{7,15},{8,0},{9,1},... | collective-permute-start | bytes 497672 | tf_op jit(solution)/shard_map/ppermute | solution.py:193
  31.5 0.5 collective-permute-done.7
  32.0 0.1 convert_add_fusion.3
  32.1 3.3 %collective-permute-start.8 = (bf16[216,128]{1,0:T(8,128)(2,1)S(1)}, bf16[216,128]{1,0:T(8,128)(2,1)S(1)}, u32[]{:S(2)}, u32[]{:S(2)}) collective-permute-start(bf16[216,128]{1,0:T(8,128)(2,1)S(1)} %get-tuple-element.63), channel_id=1, source_target_pairs={{0,8},{1,9},{2,10},{3,11},{4,12},{5,13},{6,14},{7,15},{8,0},{9,1},... | collective-permute-start | bytes 165896 | tf_op jit(solution)/shard_map/ppermute | solution.py:193
  35.4 0.0 collective-permute-done.9
  35.4 0.1 add_convert_fusion.4
  35.5 2.6 %collective-permute-start.12 = (bf16[864,128]{1,0:T(8,128)(2,1)S(1)}, bf16[864,128]{1,0:T(8,128)(2,1)S(1)}, u32[]{:S(2)}, u32[]{:S(2)}) collective-permute-start(bf16[864,128]{1,0:T(8,128)(2,1)S(1)} %add_convert_fusion.4), channel_id=1, source_target_pairs={{0,4},{1,3},{2,6},{3,1},{4,0},{5,7},{6,2},{7,5},{8,12},{9,11},{10,... | collective-permute-start | bytes 663560 | tf_op jit(solution)/shard_map/ppermute | solution.py:193
  38.0 0.3 collective-permute-done.13
  38.4 2.1 %collective-permute-start.11 = (bf16[576,128]{1,0:T(8,128)(2,1)S(1)}, bf16[576,128]{1,0:T(8,128)(2,1)S(1)}, u32[]{:S(2)}, u32[]{:S(2)}) collective-permute-start(bf16[576,128]{1,0:T(8,128)(2,1)S(1)} %add_convert_fusion.8), channel_id=1, source_target_pairs={{0,2},{1,3},{2,0},{3,1},{4,6},{5,7},{6,4},{7,5},{8,10},{9,11},{10,... | collective-permute-start | bytes 442376 | tf_op jit(solution)/shard_map/ppermute | solution.py:193
  40.5 0.1 add_convert_fusion.7
  40.6 2.5 %collective-permute-start.15 = (bf16[576,128]{1,0:T(8,128)(2,1)S(1)}, bf16[576,128]{1,0:T(8,128)(2,1)S(1)}, u32[]{:S(2)}, u32[]{:S(2)}) collective-permute-start(bf16[576,128]{1,0:T(8,128)(2,1)S(1)} %add_convert_fusion.7), channel_id=1, source_target_pairs={{0,4},{1,5},{2,6},{3,7},{4,0},{5,1},{6,2},{7,3},{8,12},{9,13},{10,... | collective-permute-start | bytes 442376 | tf_op jit(solution)/shard_map/ppermute | solution.py:193
  43.1 0.3 collective-permute-done.12
  43.3 0.1 convert_add_fusion.1
  43.4 2.6 %collective-permute-start.16 = (bf16[432,128]{1,0:T(8,128)(2,1)S(1)}, bf16[432,128]{1,0:T(8,128)(2,1)S(1)}, u32[]{:S(2)}, u32[]{:S(2)}) collective-permute-start(bf16[432,128]{1,0:T(8,128)(2,1)S(1)} %get-tuple-element.59), channel_id=1, source_target_pairs={{0,8},{1,9},{2,10},{3,11},{4,12},{5,13},{6,14},{7,15},{8,0},{9,1},... | collective-permute-start | bytes 331784 | tf_op jit(solution)/shard_map/ppermute | solution.py:193
  46.0 0.0 collective-permute-done.11
  46.0 2.5 %collective-permute-start.14 = (bf16[288,128]{1,0:T(8,128)(2,1)S(1)}, bf16[288,128]{1,0:T(8,128)(2,1)S(1)}, u32[]{:S(2)}, u32[]{:S(2)}) collective-permute-start(bf16[288,128]{1,0:T(8,128)(2,1)S(1)} %add_convert_fusion.12), channel_id=1, source_target_pairs={{0,4},{1,5},{2,6},{3,7},{4,0},{5,1},{6,2},{7,3},{8,12},{9,13},{10,... | collective-permute-start | bytes 221192 | tf_op jit(solution)/shard_map/ppermute | solution.py:193
  48.6 0.0 collective-permute-done.15
  48.6 0.1 convert_add_fusion.2
  48.6 1.1 %collective-permute-start.17 = (bf16[288,128]{1,0:T(8,128)(2,1)S(1)}, bf16[288,128]{1,0:T(8,128)(2,1)S(1)}, u32[]{:S(2)}, u32[]{:S(2)}) collective-permute-start(bf16[288,128]{1,0:T(8,128)(2,1)S(1)} %get-tuple-element.61), channel_id=1, source_target_pairs={{0,8},{1,9},{2,10},{3,11},{4,12},{5,13},{6,14},{7,15},{8,0},{9,1},... | collective-permute-start | bytes 221192 | tf_op jit(solution)/shard_map/ppermute | solution.py:193
  49.7 1.6 %collective-permute-done.14 = bf16[288,128]{1,0:T(8,128)(2,1)S(1)} collective-permute-done((bf16[288,128]{1,0:T(8,128)(2,1)S(1)}, bf16[288,128]{1,0:T(8,128)(2,1)S(1)}, u32[]{:S(2)}, u32[]{:S(2)}) %collective-permute-start.14) | collective-permute-done | bytes 73760 | tf_op jit(solution)/shard_map/ppermute | solution.py:193
  51.3 1.8 %collective-permute-start.18 = (bf16[144,128]{1,0:T(8,128)(2,1)S(1)}, bf16[144,128]{1,0:T(8,128)(2,1)S(1)}, u32[]{:S(2)}, u32[]{:S(2)}) collective-permute-start(bf16[144,128]{1,0:T(8,128)(2,1)S(1)} %get-tuple-element.65), channel_id=1, source_target_pairs={{0,8},{1,9},{2,10},{3,11},{4,12},{5,13},{6,14},{7,15},{8,0},{9,1},... | collective-permute-start | bytes 110600 | tf_op jit(solution)/shard_map/ppermute | solution.py:193
  53.1 0.7 %shard_map.115 = bf16[1,69,1536]{2,1,0:T(8,128)(2,1)} custom-call(f32[648,128]{1,0:T(8,128)S(1)} %get-tuple-element.57.refs_0_, bf16[648,128]{1,0:T(8,128)(2,1)S(1)} %collective-permute-done.6.refs_1_, f32[216,128]{1,0:T(8,128)S(1)} %get-tuple-element.62.refs_2_, bf16[216,128]{1,0:T(8,128)(2,1)S(1)} %collective-permute-done.8.refs_3_), custom_call_target="tpu_custom_call" | custom-call | tf_op jit(solution)/shard_map/pallas_call | solution.py:247
  53.8 1.7 %collective-permute-done.17.refs_3_ = bf16[288,128]{1,0:T(8,128)(2,1)S(1)} collective-permute-done((bf16[288,128]{1,0:T(8,128)(2,1)S(1)}, bf16[288,128]{1,0:T(8,128)(2,1)S(1)}, u32[]{:S(2)}, u32[]{:S(2)}) %collective-permute-start.17) | collective-permute-done | bytes 73760 | tf_op jit(solution)/shard_map/ppermute | solution.py:193
  55.5 0.7 %collective-permute-done.18.refs_5_ = bf16[144,128]{1,0:T(8,128)(2,1)S(1)} collective-permute-done((bf16[144,128]{1,0:T(8,128)(2,1)S(1)}, bf16[144,128]{1,0:T(8,128)(2,1)S(1)}, u32[]{:S(2)}, u32[]{:S(2)}) %collective-permute-start.18) | collective-permute-done | bytes 36896 | tf_op jit(solution)/shard_map/ppermute | solution.py:193
  56.3 0.7 %shard_map.116 = bf16[1,69,1536]{2,1,0:T(8,128)(2,1)} custom-call(f32[432,128]{1,0:T(8,128)S(1)} %get-tuple-element.58.refs_0_, bf16[432,128]{1,0:T(8,128)(2,1)S(1)} %collective-permute-done.16.refs_1_, f32[288,128]{1,0:T(8,128)S(1)} %get-tuple-element.60.refs_2_, bf16[288,128]{1,0:T(8,128)(2,1)S(1)} %collective-permute-done.17.refs_3_, ...), custom_call_target="tpu_custom_call" | custom-call | tf_op jit(solution)/shard_map/pallas_call | solution.py:247
  (9 shorter events, 0.2 us)
Async XLA Ops:
  5.2 2.6 %collective-permute-start.1 = (bf16[3456,128]{1,0:T(8,128)(2,1)S(1)}, bf16[3456,128]{1,0:T(8,128)(2,1)S(1)}, u32[]{:S(2)}, u32[]{:S(2)}) collective-permute-start(bf16[3456,128]{1,0:T(8,128)(2,1)S(1)} %get-tuple-element.31), channel_id=1, source_target_pairs={{0,1},{1,0},{2,3},{3,2},{4,5},{5,4},{6,7},{7,6},{8,9},{9,8},{10,11... | collective-permute-start | bytes 2654216 | tf_op jit(solution)/shard_map/ppermute | solution.py:193
  5.8 5.2 %collective-permute-start = (bf16[3456,128]{1,0:T(8,128)(2,1)S(1)}, bf16[3456,128]{1,0:T(8,128)(2,1)S(1)}, u32[]{:S(2)}, u32[]{:S(2)}) collective-permute-start(bf16[3456,128]{1,0:T(8,128)(2,1)S(1)} %get-tuple-element.30), channel_id=1, source_target_pairs={{0,1},{1,0},{2,3},{3,2},{4,5},{5,4},{6,7},{7,6},{8,9},{9,8},{10,11... | collective-permute-start | bytes 2654216 | tf_op jit(solution)/shard_map/ppermute | solution.py:193
  8.0 11.6 %collective-permute-start.2 = (bf16[2592,128]{1,0:T(8,128)(2,1)S(1)}, bf16[2592,128]{1,0:T(8,128)(2,1)S(1)}, u32[]{:S(2)}, u32[]{:S(2)}) collective-permute-start(bf16[2592,128]{1,0:T(8,128)(2,1)S(1)} %add_convert_fusion), channel_id=1, source_target_pairs={{0,2},{1,5},{2,0},{3,7},{4,6},{5,1},{6,4},{7,3},{8,10},{9,13},{10,... | collective-permute-start | bytes 1990664 | tf_op jit(solution)/shard_map/ppermute | solution.py:193
  15.7 8.7 %collective-permute-start.4 = (bf16[3456,128]{1,0:T(8,128)(2,1)S(1)}, bf16[3456,128]{1,0:T(8,128)(2,1)S(1)}, u32[]{:S(2)}, u32[]{:S(2)}) collective-permute-start(bf16[3456,128]{1,0:T(8,128)(2,1)S(1)} %get-tuple-element.36), channel_id=1, source_target_pairs={{0,1},{1,0},{2,3},{3,2},{4,5},{5,4},{6,7},{7,6},{8,9},{9,8},{10,11... | collective-permute-start | bytes 2654216 | tf_op jit(solution)/shard_map/ppermute | solution.py:193
  15.7 6.2 %collective-permute-start.5 = (bf16[864,128]{1,0:T(8,128)(2,1)S(1)}, bf16[864,128]{1,0:T(8,128)(2,1)S(1)}, u32[]{:S(2)}, u32[]{:S(2)}) collective-permute-start(bf16[864,128]{1,0:T(8,128)(2,1)S(1)} %add_convert_fusion.5), channel_id=1, source_target_pairs={{0,2},{1,5},{2,0},{3,7},{4,6},{5,1},{6,4},{7,3},{8,10},{9,13},{10,... | collective-permute-start | bytes 663560 | tf_op jit(solution)/shard_map/ppermute | solution.py:193
  17.2 18.2 %collective-permute-start.9 = (bf16[3456,128]{1,0:T(8,128)(2,1)S(1)}, bf16[3456,128]{1,0:T(8,128)(2,1)S(1)}, u32[]{:S(2)}, u32[]{:S(2)}) collective-permute-start(bf16[3456,128]{1,0:T(8,128)(2,1)S(1)} %get-tuple-element.35), channel_id=1, source_target_pairs={{0,1},{1,0},{2,3},{3,2},{4,5},{5,4},{6,7},{7,6},{8,9},{9,8},{10,11... | collective-permute-start | bytes 2654216 | tf_op jit(solution)/shard_map/ppermute | solution.py:193
  19.7 8.2 %collective-permute-start.3 = (bf16[1296,128]{1,0:T(8,128)(2,1)S(1)}, bf16[1296,128]{1,0:T(8,128)(2,1)S(1)}, u32[]{:S(2)}, u32[]{:S(2)}) collective-permute-start(bf16[1296,128]{1,0:T(8,128)(2,1)S(1)} %add_convert_fusion.2), channel_id=1, source_target_pairs={{0,4},{1,3},{2,6},{3,1},{4,0},{5,7},{6,2},{7,5},{8,12},{9,11},{10,... | collective-permute-start | bytes 995336 | tf_op jit(solution)/shard_map/ppermute | solution.py:193
  22.0 10.0 %collective-permute-start.7 = (bf16[432,128]{1,0:T(8,128)(2,1)S(1)}, bf16[432,128]{1,0:T(8,128)(2,1)S(1)}, u32[]{:S(2)}, u32[]{:S(2)}) collective-permute-start(bf16[432,128]{1,0:T(8,128)(2,1)S(1)} %add_convert_fusion.10), channel_id=1, source_target_pairs={{0,4},{1,3},{2,6},{3,1},{4,0},{5,7},{6,2},{7,5},{8,12},{9,11},{10,... | collective-permute-start | bytes 331784 | tf_op jit(solution)/shard_map/ppermute | solution.py:193
  24.6 10.8 %collective-permute-start.10 = (bf16[1728,128]{1,0:T(8,128)(2,1)S(1)}, bf16[1728,128]{1,0:T(8,128)(2,1)S(1)}, u32[]{:S(2)}, u32[]{:S(2)}) collective-permute-start(bf16[1728,128]{1,0:T(8,128)(2,1)S(1)} %add_convert_fusion.1), channel_id=1, source_target_pairs={{0,2},{1,5},{2,0},{3,7},{4,6},{5,1},{6,4},{7,3},{8,10},{9,13},{10,... | collective-permute-start | bytes 1327112 | tf_op jit(solution)/shard_map/ppermute | solution.py:193
  26.2 12.2 %collective-permute-start.13 = (bf16[1152,128]{1,0:T(8,128)(2,1)S(1)}, bf16[1152,128]{1,0:T(8,128)(2,1)S(1)}, u32[]{:S(2)}, u32[]{:S(2)}) collective-permute-start(bf16[1152,128]{1,0:T(8,128)(2,1)S(1)} %add_convert_fusion.3), channel_id=1, source_target_pairs={{0,2},{1,3},{2,0},{3,1},{4,6},{5,7},{6,4},{7,5},{8,10},{9,11},{10,... | collective-permute-start | bytes 884744 | tf_op jit(solution)/shard_map/ppermute | solution.py:193
  28.0 25.1 %collective-permute-start.6 = (bf16[648,128]{1,0:T(8,128)(2,1)S(1)}, bf16[648,128]{1,0:T(8,128)(2,1)S(1)}, u32[]{:S(2)}, u32[]{:S(2)}) collective-permute-start(bf16[648,128]{1,0:T(8,128)(2,1)S(1)} %get-tuple-element.56), channel_id=1, source_target_pairs={{0,8},{1,9},{2,10},{3,11},{4,12},{5,13},{6,14},{7,15},{8,0},{9,1},... | collective-permute-start | bytes 497672 | tf_op jit(solution)/shard_map/ppermute | solution.py:193
  32.1 21.0 %collective-permute-start.8 = (bf16[216,128]{1,0:T(8,128)(2,1)S(1)}, bf16[216,128]{1,0:T(8,128)(2,1)S(1)}, u32[]{:S(2)}, u32[]{:S(2)}) collective-permute-start(bf16[216,128]{1,0:T(8,128)(2,1)S(1)} %get-tuple-element.63), channel_id=1, source_target_pairs={{0,8},{1,9},{2,10},{3,11},{4,12},{5,13},{6,14},{7,15},{8,0},{9,1},... | collective-permute-start | bytes 165896 | tf_op jit(solution)/shard_map/ppermute | solution.py:193
  35.5 7.9 %collective-permute-start.12 = (bf16[864,128]{1,0:T(8,128)(2,1)S(1)}, bf16[864,128]{1,0:T(8,128)(2,1)S(1)}, u32[]{:S(2)}, u32[]{:S(2)}) collective-permute-start(bf16[864,128]{1,0:T(8,128)(2,1)S(1)} %add_convert_fusion.4), channel_id=1, source_target_pairs={{0,4},{1,3},{2,6},{3,1},{4,0},{5,7},{6,2},{7,5},{8,12},{9,11},{10,... | collective-permute-start | bytes 663560 | tf_op jit(solution)/shard_map/ppermute | solution.py:193
  38.4 7.6 %collective-permute-start.11 = (bf16[576,128]{1,0:T(8,128)(2,1)S(1)}, bf16[576,128]{1,0:T(8,128)(2,1)S(1)}, u32[]{:S(2)}, u32[]{:S(2)}) collective-permute-start(bf16[576,128]{1,0:T(8,128)(2,1)S(1)} %add_convert_fusion.8), channel_id=1, source_target_pairs={{0,2},{1,3},{2,0},{3,1},{4,6},{5,7},{6,4},{7,5},{8,10},{9,11},{10,... | collective-permute-start | bytes 442376 | tf_op jit(solution)/shard_map/ppermute | solution.py:193
  40.6 8.0 %collective-permute-start.15 = (bf16[576,128]{1,0:T(8,128)(2,1)S(1)}, bf16[576,128]{1,0:T(8,128)(2,1)S(1)}, u32[]{:S(2)}, u32[]{:S(2)}) collective-permute-start(bf16[576,128]{1,0:T(8,128)(2,1)S(1)} %add_convert_fusion.7), channel_id=1, source_target_pairs={{0,4},{1,5},{2,6},{3,7},{4,0},{5,1},{6,2},{7,3},{8,12},{9,13},{10,... | collective-permute-start | bytes 442376 | tf_op jit(solution)/shard_map/ppermute | solution.py:193
  43.4 10.4 %collective-permute-start.16 = (bf16[432,128]{1,0:T(8,128)(2,1)S(1)}, bf16[432,128]{1,0:T(8,128)(2,1)S(1)}, u32[]{:S(2)}, u32[]{:S(2)}) collective-permute-start(bf16[432,128]{1,0:T(8,128)(2,1)S(1)} %get-tuple-element.59), channel_id=1, source_target_pairs={{0,8},{1,9},{2,10},{3,11},{4,12},{5,13},{6,14},{7,15},{8,0},{9,1},... | collective-permute-start | bytes 331784 | tf_op jit(solution)/shard_map/ppermute | solution.py:193
  46.0 5.3 %collective-permute-start.14 = (bf16[288,128]{1,0:T(8,128)(2,1)S(1)}, bf16[288,128]{1,0:T(8,128)(2,1)S(1)}, u32[]{:S(2)}, u32[]{:S(2)}) collective-permute-start(bf16[288,128]{1,0:T(8,128)(2,1)S(1)} %add_convert_fusion.12), channel_id=1, source_target_pairs={{0,4},{1,5},{2,6},{3,7},{4,0},{5,1},{6,2},{7,3},{8,12},{9,13},{10,... | collective-permute-start | bytes 221192 | tf_op jit(solution)/shard_map/ppermute | solution.py:193
  48.6 6.9 %collective-permute-start.17 = (bf16[288,128]{1,0:T(8,128)(2,1)S(1)}, bf16[288,128]{1,0:T(8,128)(2,1)S(1)}, u32[]{:S(2)}, u32[]{:S(2)}) collective-permute-start(bf16[288,128]{1,0:T(8,128)(2,1)S(1)} %get-tuple-element.61), channel_id=1, source_target_pairs={{0,8},{1,9},{2,10},{3,11},{4,12},{5,13},{6,14},{7,15},{8,0},{9,1},... | collective-permute-start | bytes 221192 | tf_op jit(solution)/shard_map/ppermute | solution.py:193
  51.3 4.9 %collective-permute-start.18 = (bf16[144,128]{1,0:T(8,128)(2,1)S(1)}, bf16[144,128]{1,0:T(8,128)(2,1)S(1)}, u32[]{:S(2)}, u32[]{:S(2)}) collective-permute-start(bf16[144,128]{1,0:T(8,128)(2,1)S(1)} %get-tuple-element.65), channel_id=1, source_target_pairs={{0,8},{1,9},{2,10},{3,11},{4,12},{5,13},{6,14},{7,15},{8,0},{9,1},... | collective-permute-start | bytes 110600 | tf_op jit(solution)/shard_map/ppermute | solution.py:193
